TPU v7x, 512 devices: a whole 4x8x8 slice. The times are simulated.
512 devices in a mesh: dp: 32 (over z, x), ctx: 16 (over y, core).
Axes of the slice: x: 4, y: 8, z: 8, core: 2. Of those that a mesh axis runs over, the one named last changes fastest.
Arguments:
- item_ids: int32 [2, 32, 2048], P(None, 'dp', 'ctx'), may hold values from 0 to 16383, as said below
- segments: int32 [32, 2048], P('dp', 'ctx'), may hold values from 0 to 31, never falling along the last dimension, each value on 1 to 512 neighbouring positions
- touched_rows: bfloat16 [16384, 512], P('dp'), may hold values from -6 to 6
- w_in: bfloat16 [512, 2048], replicated, may hold values from -0.25 to 0.25
- w_out: bfloat16 [512, 512], replicated, may hold values from -0.25 to 0.25
- out_grad: bfloat16 [32, 2048, 512], P('dp', 'ctx'), may hold values from -6 to 6
Outputs:
- layer_out: bfloat16 [32, 2048, 512], P('dp', 'ctx')
- table_grad: float32 [16384, 512], P('dp', 'ctx')
- w_in_grad: float32 [512, 2048], P('ctx', 'dp')
- w_out_grad: float32 [512, 512], P('ctx', 'dp')
Inputs may be any that keep to these rules, and one draw needn't show every extreme that they name: `item_ids`: row r is held by owner r // 512. Among the 256 lookups of one device (both hashes of its events), no owner is named more than 32 times, and one owner exactly 32 times. `segments`: each user's events form one contiguous run of at most 512 events, and in every group one user has exactly 512.
All inputs are finite; a program needn't handle non-finite values.
Results may differ from a plain program's by a relative error of at most 0.034.
Values may be sent and summed in bfloat16 or wider, within the bound.
No kernel may reach another device: no remote copies, remote signals or barrier semaphores. Data moves between devices by JAX's collectives and lax.ppermute only.
A program may use at most 64 MiB of HBM per device.

v0:
```python
import math

import jax
import jax.numpy as jnp
from jax import lax
from jax.sharding import PartitionSpec as P

H = 8
DH = 64


epsilon = 1e-05


def passed_along(block, axis, distance):
    devices = range(lax.axis_size(axis))
    route = [(i - distance, i) for i in devices if i - distance in devices]
    return lax.ppermute(block, axis, route)


def layer_norm(values):
    centered = values - jnp.mean(values, axis=-1, keepdims=True)
    inverse = lax.rsqrt(jnp.mean(centered * centered, axis=-1, keepdims=True) + epsilon)
    return (centered * inverse, inverse)


def norm_backward(normed, inverse, upstream):
    first_mean = jnp.mean(upstream, axis=-1, keepdims=True)
    second_mean = jnp.mean(upstream * normed, axis=-1, keepdims=True)
    return inverse * (upstream - first_mean - normed * second_mean)


def silu_slope(values):
    sigmoid = jax.nn.sigmoid(values)
    return sigmoid * (1.0 + values * (1.0 - sigmoid))


def local(item_ids, segments, touched_rows, w_in, w_out, out_grad):
    rows_dev = segments.shape[1]
    model_width = w_in.shape[0]
    table_dev = touched_rows.shape[0]
    owners_count = lax.axis_size("dp")
    ctx_count = lax.axis_size("ctx")
    capacity = max(rows_dev // 4, 6 * rows_dev // owners_count + 2)
    reach_blocks = min(4, ctx_count // 2)
    margin = reach_blocks * rows_dev
    score_scale = 1.0 / math.sqrt(DH)
    lookups = item_ids.reshape(2 * rows_dev)
    owner_of = lookups // table_dev
    local_row = lookups % table_dev
    member = (owner_of[:, None] == jnp.arange(owners_count, dtype=jnp.int32)[None, :]).astype(
        jnp.int32
    )
    slot_rank = jnp.sum(jnp.cumsum(member, axis=0) * member, axis=1) - 1
    slot_index = owner_of * capacity + slot_rank
    requests = jnp.full((owners_count * capacity,), -1, jnp.int32).at[slot_index].set(local_row)
    requests = requests.reshape(owners_count, capacity)
    asked_rows = lax.all_to_all(requests, "dp", split_axis=0, concat_axis=0, tiled=True)
    present = asked_rows >= 0
    found_rows = jnp.take(touched_rows, jnp.maximum(asked_rows, 0), axis=0)
    found_rows = jnp.where(present[..., None], found_rows, jnp.zeros((), found_rows.dtype))
    fetched = lax.all_to_all(found_rows, "dp", split_axis=0, concat_axis=0, tiled=True)
    embedded = jnp.take(
        fetched.reshape(owners_count * capacity, model_width), slot_index, axis=0
    ).astype(jnp.float32)
    inputs = (embedded[:rows_dev] + embedded[rows_dev:]).astype(jnp.bfloat16)
    inputs_f = inputs.astype(jnp.float32)
    input_hat, input_inv = layer_norm(inputs_f)
    normed = input_hat.astype(jnp.bfloat16)
    projected = jnp.dot(normed, w_in, preferred_element_type=jnp.float32)
    activated = jax.nn.silu(projected).astype(jnp.bfloat16)
    gates = activated[:, :model_width].astype(jnp.float32)
    value_rows = activated[:, model_width : 2 * model_width]
    query_rows = activated[:, 2 * model_width : 3 * model_width]
    key_rows = activated[:, 3 * model_width :]
    user_plus = segments[0] + 1
    far_keys = []
    far_values = []
    far_users = []
    for offset in range(reach_blocks, 0, -1):
        got_keys, got_values, got_users = passed_along(
            (key_rows, value_rows, user_plus), "ctx", offset
        )
        far_keys.append(got_keys)
        far_values.append(got_values)
        far_users.append(got_users)
    key_heads = jnp.concatenate(far_keys + [key_rows]).reshape(-1, H, DH)
    value_heads = jnp.concatenate(far_values + [value_rows]).reshape(-1, H, DH)
    key_users = jnp.concatenate(far_users + [user_plus])
    query_heads = query_rows.reshape(rows_dev, H, DH)
    row_index = jnp.arange(rows_dev, dtype=jnp.int32)[:, None]
    col_index = jnp.arange(margin + rows_dev, dtype=jnp.int32)[None, :]
    allowed = (user_plus[:, None] == key_users[None, :]) & (col_index <= row_index + margin)
    scores = (
        jnp.einsum("qhd,khd->hqk", query_heads, key_heads, preferred_element_type=jnp.float32)
        * score_scale
    )
    weights = jnp.where(allowed[None], jax.nn.silu(scores), 0.0).astype(jnp.bfloat16)
    attended = jnp.einsum(
        "hqk,khd->qhd", weights, value_heads, preferred_element_type=jnp.float32
    ).reshape(rows_dev, model_width)
    att_hat, att_inv = layer_norm(attended)
    mixed = (att_hat * gates).astype(jnp.bfloat16)
    grad_rows = out_grad[0]
    layer_out = (inputs_f + jnp.dot(mixed, w_out, preferred_element_type=jnp.float32)).astype(
        jnp.bfloat16
    )
    mixed_grad = jnp.einsum("re,de->rd", grad_rows, w_out, preferred_element_type=jnp.float32)
    gate_grad = mixed_grad * att_hat
    attended_grad = norm_backward(att_hat, att_inv, mixed_grad * gates).astype(jnp.bfloat16)
    grad_heads = attended_grad.reshape(rows_dev, H, DH)
    prob_grad = jnp.einsum(
        "qhd,khd->hqk", grad_heads, value_heads, preferred_element_type=jnp.float32
    )
    score_grad = jnp.where(allowed[None], prob_grad * silu_slope(scores), 0.0).astype(jnp.bfloat16)
    query_grad = (
        jnp.einsum("hqk,khd->qhd", score_grad, key_heads, preferred_element_type=jnp.float32)
        * score_scale
    ).reshape(rows_dev, model_width)
    key_all = (
        jnp.einsum("hqk,qhd->khd", score_grad, query_heads, preferred_element_type=jnp.float32)
        * score_scale
    ).reshape(-1, model_width)
    value_all = jnp.einsum(
        "hqk,qhd->khd", weights, grad_heads, preferred_element_type=jnp.float32
    ).reshape(-1, model_width)
    key_grad = key_all[margin:]
    value_grad = value_all[margin:]
    for offset in range(1, reach_blocks + 1):
        block_start = (reach_blocks - offset) * rows_dev
        back_keys, back_values = (
            passed_along(
                key_all[block_start : block_start + rows_dev].astype(jnp.bfloat16), "ctx", -offset
            ).astype(jnp.float32),
            passed_along(
                value_all[block_start : block_start + rows_dev].astype(jnp.bfloat16), "ctx", -offset
            ).astype(jnp.float32),
        )
        key_grad = key_grad + back_keys
        value_grad = value_grad + back_values
    joined = jnp.concatenate([gate_grad, value_grad, query_grad, key_grad], axis=1)
    projected_grad = (joined * silu_slope(projected)).astype(jnp.bfloat16)
    normed_grad = jnp.einsum("re,de->rd", projected_grad, w_in, preferred_element_type=jnp.float32)
    inputs_grad = (
        grad_rows.astype(jnp.float32) + norm_backward(input_hat, input_inv, normed_grad)
    ).astype(jnp.bfloat16)
    w_in_part = jnp.einsum("rd,re->de", normed, projected_grad, preferred_element_type=jnp.float32)
    w_out_part = jnp.einsum("rd,re->de", mixed, grad_rows, preferred_element_type=jnp.float32)
    in_share, out_share = (
        lax.psum_scatter(
            w_in_part.astype(jnp.bfloat16), "ctx", scatter_dimension=0, tiled=True
        ).astype(jnp.float32),
        lax.psum_scatter(
            w_out_part.astype(jnp.bfloat16), "ctx", scatter_dimension=0, tiled=True
        ).astype(jnp.float32),
    )
    w_in_grad, w_out_grad = (
        lax.psum_scatter(
            in_share.astype(jnp.bfloat16), "dp", scatter_dimension=1, tiled=True
        ).astype(jnp.float32),
        lax.psum_scatter(
            out_share.astype(jnp.bfloat16), "dp", scatter_dimension=1, tiled=True
        ).astype(jnp.float32),
    )
    lookup_grads = jnp.concatenate([inputs_grad, inputs_grad])
    outgoing = (
        jnp.zeros((owners_count * capacity, model_width), jnp.bfloat16)
        .at[slot_index]
        .set(lookup_grads)
    )
    outgoing = outgoing.reshape(owners_count, capacity, model_width)
    arrived = lax.all_to_all(outgoing, "dp", split_axis=0, concat_axis=0, tiled=True)
    targets = jnp.where(asked_rows >= 0, asked_rows, table_dev).reshape(-1)
    accumulated = jax.ops.segment_sum(
        arrived.reshape(-1, model_width).astype(jnp.float32), targets, num_segments=table_dev + 1
    )[:table_dev]
    table_grad = lax.psum_scatter(
        accumulated.astype(jnp.bfloat16), "ctx", scatter_dimension=1, tiled=True
    ).astype(jnp.float32)
    return (layer_out[None], table_grad, w_in_grad, w_out_grad)


def solution(mesh):
    return jax.shard_map(
        local,
        mesh=mesh,
        in_specs=(
            P(None, "dp", "ctx"),
            P("dp", "ctx"),
            P("dp", None),
            P(),
            P(),
            P("dp", "ctx", None),
        ),
        out_specs=(P("dp", "ctx", None), P("dp", "ctx"), P("ctx", "dp"), P("ctx", "dp")),
        check_vma=False,
    )
```

profile of v0, /device:TPU:1, one launch (start us, length us, event | category | flops | bytes accessed | tf_op | source)
XLA Modules:
  0.0 753.2 jit_solution(17172278742148855600)
XLA Ops:
  11.9 22.1 %all_to_all.22 = s32[32,1,32]{2,1,0:T(1,128)S(1)} all-to-all(s32[32,1,32]{2,1,0:T(1,128)S(1)} %all_to_all.14), channel_id=1, replica_groups=mesh['dp'=32,'ctx'=16] {'dp'}, dimensions={0} | all-to-all | bytes 8192 | tf_op jit(solution)/shard_map/all_to_all | solution.py:58
  34.1 5.1 gather_fusion
  40.4 3.9 all-to-all-start.1
  44.4 5.2 collective-permute-start.7
  49.6 3.2 collective-permute-start.6
  52.8 3.2 collective-permute-start.5
  56.1 4.5 collective-permute-start.4
  61.4 8.2 %all-to-all-done.1 = bf16[32,32,512]{2,1,0:T(8,128)(2,1)S(1)} async-done(((bf16[32,32,512]{2,1,0:T(8,128)(2,1)}), bf16[32,32,512]{2,1,0:T(8,128)(2,1)S(1)}, u32[]{:S(2)}, u32[]{:S(2)}) %all-to-all-start.1) | async-done | bytes 1048608 | tf_op jit(solution)/shard_map/all_to_all | solution.py:62
  72.8 4.2 collective-permute-start.8
  77.0 5.4 collective-permute-start
  83.2 6.8 collective-permute-start.11
  90.1 2.3 collective-permute-start.10
  92.4 2.3 collective-permute-start.9
  94.7 1.9 collective-permute-start.1
  96.7 2.8 collective-permute-start.2
  101.1 5.8 collective-permute-start.3
  113.4 3.7 select_convert_fusion.1
  122.5 2.0 multiply_convert_fusion.1
  126.1 3.4 select_convert_fusion
  136.0 2.2 convolution_convert_fusion.1
  149.7 2.1 collective-permute-start.16
  169.9 8.4 %collective-permute-done.14 = bf16[128,512]{1,0:T(8,128)(2,1)S(1)} collective-permute-done((bf16[128,512]{1,0:T(8,128)(2,1)}, bf16[128,512]{1,0:T(8,128)(2,1)S(1)}, u32[]{:S(2)}, u32[]{:S(2)}) %collective-permute-start.14) | collective-permute-done | bytes 131104 | tf_op jit(solution)/shard_map/ppermute | solution.py:18
  178.3 4.8 collective-permute-done.15
  185.7 2.2 convolution_convert_fusion
  189.0 2.8 scatter_custom_fusion.1
  191.8 5.4 all-to-all-start.2
  200.1 23.3 %all-to-all-done.2 = bf16[32,32,512]{2,1,0:T(8,128)(2,1)S(1)} async-done(((bf16[32,32,512]{2,1,0:T(8,128)(2,1)}), bf16[32,32,512]{2,1,0:T(8,128)(2,1)S(1)}, u32[]{:S(2)}, u32[]{:S(2)}) %all-to-all-start.2) | async-done | bytes 1048608 | tf_op jit(solution)/shard_map/all_to_all | solution.py:172
  223.4 8.1 %scatter_custom_fusion.2 = f32[513,512]{1,0:T(8,128)} fusion(s32[1024]{0:T(1024)S(1)} %bitcast.152, bf16[1024,512]{1,0:T(8,128)(2,1)S(1)} %bitcast.116, f32[]{:T(128)} %constant.96.clone.1), kind=kCustom, calls=%fused_computation.9 | custom fusion | flops 1048576 | bytes 2099204 | tf_op jit(solution)/shard_map/scatter-add | solution.py:174
  233.9 30.0 %reduce-scatter.12.cloned.1.call-done = bf16[32,2048]{1,0:T(8,128)(2,1)} async-done(((bf16[512,2048]{1,0:T(8,128)(2,1)}), bf16[32,2048]{1,0:T(8,128)(2,1)}) %reduce-scatter.12.cloned.1.call-update) | async-done | bytes 131088 | tf_op jit(solution)/shard_map/reduce_scatter | solution.py:150
  266.8 195.9 %reduce-scatter.20.cloned.1.call-done = bf16[16,32]{1,0:T(8,128)(2,1)} async-done(((bf16[512,32]{1,0:T(8,128)(2,1)}), bf16[16,32]{1,0:T(8,128)(2,1)}) %reduce-scatter.20.cloned.1.call-update) | async-done | bytes 1040
  464.1 61.5 %reduce-scatter.16.cloned.1.call-done = bf16[32,512]{1,0:T(8,128)(2,1)} async-done(((bf16[512,512]{1,0:T(8,128)(2,1)}), bf16[32,512]{1,0:T(8,128)(2,1)}) %reduce-scatter.16.cloned.1.call-update) | async-done | bytes 32784
  527.2 218.1 %reduce-scatter.18.cloned.1.call-done = bf16[64,32]{1,0:T(8,128)(2,1)} async-done(((bf16[2048,32]{1,0:T(8,128)(2,1)}), bf16[64,32]{1,0:T(8,128)(2,1)}) %reduce-scatter.18.cloned.1.call-update) | async-done | bytes 4112
  (184 shorter events, 77.9 us)
Async XLA Ops:
  7.2 64.0 %copy-start = (bf16[512,2048]{1,0:T(8,128)(2,1)S(1)}, bf16[512,2048]{1,0:T(8,128)(2,1)}, u32[]{:S(2)}) copy-start(bf16[512,2048]{1,0:T(8,128)(2,1)} %param.9) | copy-start | bytes 6291460
  10.3 50.3 %copy-start.21 = (s32[256,1]{0,1:T(1,128)}, s32[256,1]{0,1:T(1,128)S(1)}, u32[]{:S(2)}) copy-start(s32[256,1]{0,1:T(1,128)S(1)} %compare_select_fusion.1) | copy-start | bytes 3076
  40.4 29.2 %all-to-all-start.1 = ((bf16[32,32,512]{2,1,0:T(8,128)(2,1)}), bf16[32,32,512]{2,1,0:T(8,128)(2,1)S(1)}, u32[]{:S(2)}, u32[]{:S(2)}) async-start(bf16[32,32,512]{2,1,0:T(8,128)(2,1)} %select_select_fusion), calls=%async_computation.1 | async-start | bytes 2097152 | tf_op jit(solution)/shard_map/all_to_all | solution.py:62
  44.4 154.2 %reduce-scatter.14.cloned.1.call-start = ((), (), s32[]{:S(2)}) async-start(), calls=%async_computation.9 | async-start | bytes 557056 | tf_op jit(solution)/shard_map/reduce_scatter | solution.py:153
  44.4 16.9 %collective-permute-start.7 = (s32[128]{0:T(128)S(1)}, s32[128]{0:T(128)S(1)}, u32[]{:S(2)}, u32[]{:S(2)}) collective-permute-start(s32[128]{0:T(128)S(1)} %add_bitcast_fusion.1), channel_id=1, source_target_pairs={{0,1},{1,2},{2,3},{3,4},{4,5},{5,6},{6,7},{7,8},{8,9},{9,10},{10,1... | collective-permute-start | bytes 1544 | tf_op jit(solution)/shard_map/ppermute | solution.py:18
  49.6 11.7 %collective-permute-start.6 = (s32[128]{0:T(128)S(1)}, s32[128]{0:T(128)S(1)}, u32[]{:S(2)}, u32[]{:S(2)}) collective-permute-start(s32[128]{0:T(128)S(1)} %add_bitcast_fusion.1), channel_id=1, source_target_pairs={{0,2},{1,3},{2,4},{3,5},{4,6},{5,7},{6,8},{7,9},{8,10},{9,11},{10,... | collective-permute-start | bytes 1544 | tf_op jit(solution)/shard_map/ppermute | solution.py:18
  52.8 8.5 %collective-permute-start.5 = (s32[128]{0:T(128)S(1)}, s32[128]{0:T(128)S(1)}, u32[]{:S(2)}, u32[]{:S(2)}) collective-permute-start(s32[128]{0:T(128)S(1)} %add_bitcast_fusion.1), channel_id=1, source_target_pairs={{0,3},{1,4},{2,5},{3,6},{4,7},{5,8},{6,9},{7,10},{8,11},{9,12},{10... | collective-permute-start | bytes 1544 | tf_op jit(solution)/shard_map/ppermute | solution.py:18
  56.1 5.2 collective-permute-start.4
  72.8 36.2 %copy-start.7 = (bf16[128,2048]{1,0:T(8,128)(2,1)}, bf16[128,2048]{1,0:T(8,128)(2,1)S(1)}, u32[]{:S(2)}) copy-start(bf16[128,2048]{1,0:T(8,128)(2,1)S(1)} %get-tuple-element.46) | copy-start | bytes 1572868
  72.8 23.9 %collective-permute-start.8 = (bf16[128,512]{1,0:T(8,128)(2,1)S(1)}, bf16[128,512]{1,0:T(8,128)(2,1)S(1)}, u32[]{:S(2)}, u32[]{:S(2)}) collective-permute-start(bf16[128,512]{1,0:T(8,128)(2,1)S(1)} %get-tuple-element.40), channel_id=1, source_target_pairs={{0,4},{1,5},{2,6},{3,7},{4,8},{5,9},{6,10},{7,11},{8,12},{9,13},{1... | collective-permute-start | bytes 393224 | tf_op jit(solution)/shard_map/ppermute | solution.py:18
  77.0 17.7 %collective-permute-start = (bf16[128,512]{1,0:T(8,128)(2,1)S(1)}, bf16[128,512]{1,0:T(8,128)(2,1)S(1)}, u32[]{:S(2)}, u32[]{:S(2)}) collective-permute-start(bf16[128,512]{1,0:T(8,128)(2,1)S(1)} %get-tuple-element.41), channel_id=1, source_target_pairs={{0,4},{1,5},{2,6},{3,7},{4,8},{5,9},{6,10},{7,11},{8,12},{9,13},{1... | collective-permute-start | bytes 393224 | tf_op jit(solution)/shard_map/ppermute | solution.py:18
  83.2 25.6 %collective-permute-start.11 = (bf16[128,512]{1,0:T(8,128)(2,1)S(1)}, bf16[128,512]{1,0:T(8,128)(2,1)S(1)}, u32[]{:S(2)}, u32[]{:S(2)}) collective-permute-start(bf16[128,512]{1,0:T(8,128)(2,1)S(1)} %get-tuple-element.40), channel_id=1, source_target_pairs={{0,1},{1,2},{2,3},{3,4},{4,5},{5,6},{6,7},{7,8},{8,9},{9,10},{10,1... | collective-permute-start | bytes 393224 | tf_op jit(solution)/shard_map/ppermute | solution.py:18
  90.1 18.8 %collective-permute-start.10 = (bf16[128,512]{1,0:T(8,128)(2,1)S(1)}, bf16[128,512]{1,0:T(8,128)(2,1)S(1)}, u32[]{:S(2)}, u32[]{:S(2)}) collective-permute-start(bf16[128,512]{1,0:T(8,128)(2,1)S(1)} %get-tuple-element.40), channel_id=1, source_target_pairs={{0,2},{1,3},{2,4},{3,5},{4,6},{5,7},{6,8},{7,9},{8,10},{9,11},{10,... | collective-permute-start | bytes 393224 | tf_op jit(solution)/shard_map/ppermute | solution.py:18
  92.4 16.4 %collective-permute-start.9 = (bf16[128,512]{1,0:T(8,128)(2,1)S(1)}, bf16[128,512]{1,0:T(8,128)(2,1)S(1)}, u32[]{:S(2)}, u32[]{:S(2)}) collective-permute-start(bf16[128,512]{1,0:T(8,128)(2,1)S(1)} %get-tuple-element.40), channel_id=1, source_target_pairs={{0,3},{1,4},{2,5},{3,6},{4,7},{5,8},{6,9},{7,10},{8,11},{9,12},{10... | collective-permute-start | bytes 393224 | tf_op jit(solution)/shard_map/ppermute | solution.py:18
  94.7 6.4 collective-permute-start.1
  96.7 10.2 %collective-permute-start.2 = (bf16[128,512]{1,0:T(8,128)(2,1)S(1)}, bf16[128,512]{1,0:T(8,128)(2,1)S(1)}, u32[]{:S(2)}, u32[]{:S(2)}) collective-permute-start(bf16[128,512]{1,0:T(8,128)(2,1)S(1)} %get-tuple-element.41), channel_id=1, source_target_pairs={{0,2},{1,3},{2,4},{3,5},{4,6},{5,7},{6,8},{7,9},{8,10},{9,11},{10,... | collective-permute-start | bytes 393224 | tf_op jit(solution)/shard_map/ppermute | solution.py:18
  101.1 7.7 %collective-permute-start.3 = (bf16[128,512]{1,0:T(8,128)(2,1)S(1)}, bf16[128,512]{1,0:T(8,128)(2,1)S(1)}, u32[]{:S(2)}, u32[]{:S(2)}) collective-permute-start(bf16[128,512]{1,0:T(8,128)(2,1)S(1)} %get-tuple-element.41), channel_id=1, source_target_pairs={{0,1},{1,2},{2,3},{3,4},{4,5},{5,6},{6,7},{7,8},{8,9},{9,10},{10,1... | collective-permute-start | bytes 393224 | tf_op jit(solution)/shard_map/ppermute | solution.py:18
  138.2 125.7 %reduce-scatter.12.cloned.1.call-start = ((), (), s32[]{:S(2)}) async-start(), calls=%async_computation.8 | async-start | bytes 2228224 | tf_op jit(solution)/shard_map/reduce_scatter | solution.py:150
  145.8 17.1 %collective-permute-start.17 = (bf16[128,512]{1,0:T(8,128)(2,1)}, bf16[128,512]{1,0:T(8,128)(2,1)}, u32[]{:S(2)}, u32[]{:S(2)}) collective-permute-start(bf16[128,512]{1,0:T(8,128)(2,1)} %copy.84), channel_id=1, source_target_pairs={{2,0},{3,1},{4,2},{5,3},{6,4},{7,5},{8,6},{9,7},{10,8},{11,9},{12,... | collective-permute-start | bytes 393224 | tf_op jit(solution)/shard_map/ppermute | solution.py:18
  147.1 17.1 %collective-permute-start.18 = (bf16[128,512]{1,0:T(8,128)(2,1)}, bf16[128,512]{1,0:T(8,128)(2,1)}, u32[]{:S(2)}, u32[]{:S(2)}) collective-permute-start(bf16[128,512]{1,0:T(8,128)(2,1)} %copy.85), channel_id=1, source_target_pairs={{3,0},{4,1},{5,2},{6,3},{7,4},{8,5},{9,6},{10,7},{11,8},{12,9},{13... | collective-permute-start | bytes 393224 | tf_op jit(solution)/shard_map/ppermute | solution.py:18
  148.4 17.1 %collective-permute-start.19 = (bf16[128,512]{1,0:T(8,128)(2,1)}, bf16[128,512]{1,0:T(8,128)(2,1)}, u32[]{:S(2)}, u32[]{:S(2)}) collective-permute-start(bf16[128,512]{1,0:T(8,128)(2,1)} %copy.86), channel_id=1, source_target_pairs={{4,0},{5,1},{6,2},{7,3},{8,4},{9,5},{10,6},{11,7},{12,8},{13,9},{1... | collective-permute-start | bytes 393224 | tf_op jit(solution)/shard_map/ppermute | solution.py:18
  149.7 17.8 %collective-permute-start.16 = (bf16[128,512]{1,0:T(8,128)(2,1)}, bf16[128,512]{1,0:T(8,128)(2,1)}, u32[]{:S(2)}, u32[]{:S(2)}) collective-permute-start(bf16[128,512]{1,0:T(8,128)(2,1)} %copy.82), channel_id=1, source_target_pairs={{1,0},{2,1},{3,2},{4,3},{5,4},{6,5},{7,6},{8,7},{9,8},{10,9},{11,1... | collective-permute-start | bytes 393224 | tf_op jit(solution)/shard_map/ppermute | solution.py:18
  160.5 9.4 %collective-permute-start.13 = (bf16[128,512]{1,0:T(8,128)(2,1)}, bf16[128,512]{1,0:T(8,128)(2,1)}, u32[]{:S(2)}, u32[]{:S(2)}) collective-permute-start(bf16[128,512]{1,0:T(8,128)(2,1)} %copy.79), channel_id=1, source_target_pairs={{2,0},{3,1},{4,2},{5,3},{6,4},{7,5},{8,6},{9,7},{10,8},{11,9},{12,... | collective-permute-start | bytes 393224 | tf_op jit(solution)/shard_map/ppermute | solution.py:18
  162.9 15.4 %collective-permute-start.14 = (bf16[128,512]{1,0:T(8,128)(2,1)}, bf16[128,512]{1,0:T(8,128)(2,1)S(1)}, u32[]{:S(2)}, u32[]{:S(2)}) collective-permute-start(bf16[128,512]{1,0:T(8,128)(2,1)} %copy.80), channel_id=1, source_target_pairs={{3,0},{4,1},{5,2},{6,3},{7,4},{8,5},{9,6},{10,7},{11,8},{12,9},{13... | collective-permute-start | bytes 393224 | tf_op jit(solution)/shard_map/ppermute | solution.py:18
  164.2 18.9 %collective-permute-start.15 = (bf16[128,512]{1,0:T(8,128)(2,1)}, bf16[128,512]{1,0:T(8,128)(2,1)S(1)}, u32[]{:S(2)}, u32[]{:S(2)}) collective-permute-start(bf16[128,512]{1,0:T(8,128)(2,1)} %copy.81), channel_id=1, source_target_pairs={{4,0},{5,1},{6,2},{7,3},{8,4},{9,5},{10,6},{11,7},{12,8},{13,9},{1... | collective-permute-start | bytes 393224 | tf_op jit(solution)/shard_map/ppermute | solution.py:18
  165.5 17.6 %collective-permute-start.12 = (bf16[128,512]{1,0:T(8,128)(2,1)}, bf16[128,512]{1,0:T(8,128)(2,1)S(1)}, u32[]{:S(2)}, u32[]{:S(2)}) collective-permute-start(bf16[128,512]{1,0:T(8,128)(2,1)} %copy.77), channel_id=1, source_target_pairs={{1,0},{2,1},{3,2},{4,3},{5,4},{6,5},{7,6},{8,7},{9,8},{10,9},{11,1... | collective-permute-start | bytes 393224 | tf_op jit(solution)/shard_map/ppermute | solution.py:18
  191.8 31.6 %all-to-all-start.2 = ((bf16[32,32,512]{2,1,0:T(8,128)(2,1)}), bf16[32,32,512]{2,1,0:T(8,128)(2,1)S(1)}, u32[]{:S(2)}, u32[]{:S(2)}) async-start(bf16[32,32,512]{2,1,0:T(8,128)(2,1)} %bitcast.117), calls=%async_computation.2 | async-start | bytes 2097152 | tf_op jit(solution)/shard_map/all_to_all | solution.py:172
  197.2 265.5 %reduce-scatter.20.cloned.1.call-start = ((), (), s32[]{:S(2)}) async-start(), calls=%async_computation.12 | async-start | bytes 135168
  200.0 325.6 %reduce-scatter.16.cloned.1.call-start = ((), (), s32[]{:S(2)}) async-start(), calls=%async_computation.10 | async-start | bytes 557056
  231.5 34.4 %copy-start.6 = (bf16[512,512]{1,0:T(8,128)(2,1)S(1)}, bf16[512,512]{1,0:T(8,128)(2,1)}, u32[]{:S(2)}) copy-start(bf16[512,512]{1,0:T(8,128)(2,1)} %param.10) | copy-start | bytes 1572868
  231.5 34.4 %copy-start.9 = (bf16[128,512]{1,0:T(8,128)(2,1)S(1)}, bf16[128,512]{1,0:T(8,128)(2,1)}, u32[]{:S(2)}) copy-start(bf16[128,512]{1,0:T(8,128)(2,1)} %get-tuple-element.27) | copy-start | bytes 393220
  233.9 511.4 %reduce-scatter.18.cloned.1.call-start = ((), (), s32[]{:S(2)}) async-start(), calls=%async_computation.11 | async-start | bytes 540672
  (21 other events, 206.2 us)
Sparse Core Ops, SparseCore 0:
  138.3 58.5 reduce-scatter.13
  200.0 63.8 reduce-scatter.11
  268.7 193.8 reduce-scatter.19
  465.3 60.2 reduce-scatter.15
  530.5 214.7 reduce-scatter.17
where the time goes:
time: 759 us; the launch traced here: 753 us
  waiting for transfers between devices  555 us (73%)
  starting transfers between devices  69 us (9%)
  local copies, waits for them, and re-layouts  46.2 us (6%)
  other arithmetic  24.6 us (3%)
  blocking collectives  22.1 us (3%)
  matrix products  21.6 us (3%)
  between operations  14.6 us (2%)
    unnamed x8, waiting for transfers between devices  476 us
    ppermute x20, starting transfers between devices, passed_along(): return lax.ppermute(block, axis, route)  59.5 us
    reduce_scatter x1, waiting for transfers between devices, local(): lax.psum_scatter(w_in_part.astype(jnp.bfloat16), 'ctx', scatter_dimension...  30 us
    all_to_all x1, waiting for transfers between devices, local(): lax.all_to_all(outgoing, 'dp', split_axis=0, concat_axis=0, tiled=True)  23.3 us
    all_to_all x1, blocking collectives, local(): lax.all_to_all(requests, 'dp', split_axis=0, concat_axis=0, tiled=True)  22.1 us
    ppermute x20, waiting for transfers between devices, passed_along(): return lax.ppermute(block, axis, route)  18.1 us
  transfers between devices with their start and end apart: 27, of which 12 were waited for; matrix products, arithmetic and copies ran while one was open for 6% of the time, Pallas kernels for 0%

commit v1 on v0

--- a/solution.py
+++ b/solution.py
@@ -33,6 +33,22 @@
 def silu_slope(values):
     sigmoid = jax.nn.sigmoid(values)
     return sigmoid * (1.0 + values * (1.0 - sigmoid))
+
+
+def scatter_ctx(terms, core):
+    devices = lax.axis_size("ctx")
+    chips = devices // 2
+    rows = terms.shape[0] // devices
+    slabs = terms.reshape(chips, 2, rows, terms.shape[1])
+    kept = lax.dynamic_index_in_dim(slabs, core, 1, keepdims=False)
+    sent = lax.dynamic_index_in_dim(slabs, 1 - core, 1, keepdims=False)
+    got = lax.ppermute(sent, "ctx", [(i, i ^ 1) for i in range(devices)])
+    chip_sum = (kept.astype(jnp.float32) + got.astype(jnp.float32)).astype(jnp.bfloat16)
+    groups = [list(range(first, devices, 2)) for first in range(2)]
+    spread = lax.all_to_all(
+        chip_sum, "ctx", split_axis=0, concat_axis=0, tiled=True, axis_index_groups=groups
+    )
+    return jnp.sum(spread.astype(jnp.float32), axis=0)
 
 
 def local(item_ids, segments, touched_rows, w_in, w_out, out_grad):
@@ -146,22 +162,18 @@
     ).astype(jnp.bfloat16)
     w_in_part = jnp.einsum("rd,re->de", normed, projected_grad, preferred_element_type=jnp.float32)
     w_out_part = jnp.einsum("rd,re->de", mixed, grad_rows, preferred_element_type=jnp.float32)
-    in_share, out_share = (
-        lax.psum_scatter(
-            w_in_part.astype(jnp.bfloat16), "ctx", scatter_dimension=0, tiled=True
-        ).astype(jnp.float32),
-        lax.psum_scatter(
-            w_out_part.astype(jnp.bfloat16), "ctx", scatter_dimension=0, tiled=True
-        ).astype(jnp.float32),
-    )
-    w_in_grad, w_out_grad = (
-        lax.psum_scatter(
-            in_share.astype(jnp.bfloat16), "dp", scatter_dimension=1, tiled=True
-        ).astype(jnp.float32),
-        lax.psum_scatter(
-            out_share.astype(jnp.bfloat16), "dp", scatter_dimension=1, tiled=True
-        ).astype(jnp.float32),
-    )
+    core = lax.axis_index("ctx") % 2
+    w_part = jnp.concatenate([w_in_part, w_out_part], axis=1).astype(jnp.bfloat16)
+    w_share = scatter_ctx(w_part, core)
+    w_cols = w_share.astype(jnp.bfloat16)
+    width = w_in.shape[1]
+    dp_in = w_cols[:, :width].reshape(-1, owners_count, width // owners_count)
+    dp_out = w_cols[:, width:].reshape(-1, owners_count, model_width // owners_count)
+    dp_send = jnp.concatenate([dp_in, dp_out], axis=2).transpose(1, 0, 2)
+    dp_got = lax.all_to_all(dp_send, "dp", split_axis=0, concat_axis=0, tiled=True)
+    w_total = jnp.sum(dp_got.astype(jnp.float32), axis=0)
+    w_in_grad = w_total[:, : width // owners_count]
+    w_out_grad = w_total[:, width // owners_count :]
     lookup_grads = jnp.concatenate([inputs_grad, inputs_grad])
     outgoing = (
         jnp.zeros((owners_count * capacity, model_width), jnp.bfloat16)
@@ -170,13 +182,12 @@
     )
     outgoing = outgoing.reshape(owners_count, capacity, model_width)
     arrived = lax.all_to_all(outgoing, "dp", split_axis=0, concat_axis=0, tiled=True)
-    targets = jnp.where(asked_rows >= 0, asked_rows, table_dev).reshape(-1)
-    accumulated = jax.ops.segment_sum(
-        arrived.reshape(-1, model_width).astype(jnp.float32), targets, num_segments=table_dev + 1
-    )[:table_dev]
-    table_grad = lax.psum_scatter(
-        accumulated.astype(jnp.bfloat16), "ctx", scatter_dimension=1, tiled=True
-    ).astype(jnp.float32)
+    row_of = jnp.arange(table_dev, dtype=jnp.int32)[None, :]
+    hits = (asked_rows.reshape(-1)[:, None] == row_of).astype(jnp.bfloat16)
+    accumulated = jnp.einsum(
+        "sd,sr->dr", arrived.reshape(-1, model_width), hits, preferred_element_type=jnp.float32
+    )
+    table_grad = scatter_ctx(accumulated.astype(jnp.bfloat16), core).T
     return (layer_out[None], table_grad, w_in_grad, w_out_grad)
 
 

time: 759 us -> 297 us (0.39)
  waiting for transfers between devices: 555 us -> 91.5 us
  starting transfers between devices: 69 us -> 95.3 us
  between operations: 14.6 us -> 1.59 us
    unnamed x8 -> x0, waiting for transfers between devices: 476 us -> none
    all_to_all x0 -> x3, waiting for transfers between devices: none -> 41 us  [the longest x2 32.3 us: scatter_ctx(): lax.all_to_all(chip_sum, 'ctx', split_axis=0, concat_axis=0, tiled=True,...]
    reduce_scatter x2 -> x0, waiting for transfers between devices: 30 us -> none  [the longest x1 30 us: local(): lax.psum_scatter(w_in_part.astype(jnp.bfloat16), 'ctx', scatter_dimension...]
    all_to_all x0 -> x3, starting transfers between devices: none -> 19.9 us  [the longest x2 14.2 us: scatter_ctx(): lax.all_to_all(chip_sum, 'ctx', split_axis=0, concat_axis=0, tiled=True,...]
    scatter-add x1 -> x0, other arithmetic: 8.08 us -> none  [local(): jax.ops.segment_sum(arrived.reshape(-1, model_width).astype(jnp.float32),...]
  transfers between devices with their start and end apart: 27 -> 27, of which waited for: 12 -> 11; matrix products, arithmetic and copies ran while one was open for 6% -> 10% of each run, Pallas kernels for 0% -> 0%
where the time goes in v1:
time: 297 us; the launch traced here: 296 us
  starting transfers between devices  95.3 us (32%)
  waiting for transfers between devices  91.5 us (31%)
  local copies, waits for them, and re-layouts  40.7 us (14%)
  other arithmetic  23.9 us (8%)
  blocking collectives  22.1 us (7%)
  matrix products  20.4 us (7%)
    ppermute x20, starting transfers between devices, passed_along(): return lax.ppermute(block, axis, route)  59.6 us
    all_to_all x2, waiting for transfers between devices, scatter_ctx(): lax.all_to_all(chip_sum, 'ctx', split_axis=0, concat_axis=0, tiled=True,...  32.3 us
    all_to_all x1, waiting for transfers between devices, local(): lax.all_to_all(outgoing, 'dp', split_axis=0, concat_axis=0, tiled=True)  24.1 us
    all_to_all x1, blocking collectives, local(): lax.all_to_all(requests, 'dp', split_axis=0, concat_axis=0, tiled=True)  22.1 us
    ppermute x20, waiting for transfers between devices, passed_along(): return lax.ppermute(block, axis, route)  17.1 us
    all_to_all x2, starting transfers between devices, scatter_ctx(): lax.all_to_all(chip_sum, 'ctx', split_axis=0, concat_axis=0, tiled=True,...  14.2 us
    all_to_all x1, waiting for transfers between devices, local(): lax.all_to_all(dp_send, 'dp', split_axis=0, concat_axis=0, tiled=True)  8.69 us
    all_to_all x1, waiting for transfers between devices, local(): lax.all_to_all(found_rows, 'dp', split_axis=0, concat_axis=0, tiled=True)  8.23 us
  transfers between devices with their start and end apart: 27, of which 11 were waited for; matrix products, arithmetic and copies ran while one was open for 10% of the time, Pallas kernels for 0%

profile of v1, /device:TPU:1, one launch (start us, length us, event | category | flops | bytes accessed | tf_op | source)
XLA Modules:
  0.0 295.6 jit_solution(8360616722166680244)
XLA Ops:
  5.3 22.1 %all_to_all.34 = s32[32,1,32]{2,1,0:T(1,128)S(1)} all-to-all(s32[32,1,32]{2,1,0:T(1,128)S(1)} %all_to_all.21), channel_id=1, replica_groups=mesh['dp'=32,'ctx'=16] {'dp'}, dimensions={0} | all-to-all | bytes 8192 | tf_op jit(solution)/shard_map/all_to_all | solution.py:74
  27.5 5.1 %gather_fusion = bf16[1024,512]{1,0:T(8,128)(2,1)S(1)} fusion(bf16[512,512]{1,0:T(8,128)(2,1)} %param.8, s32[1024]{0:T(1024)S(1)} %broadcast_clamp_fusion), kind=kCustom, calls=%fused_computation | custom fusion | bytes 2101248 | tf_op jit(solution)/shard_map/jit(_take)/gather | solution.py:76
  33.9 3.9 %all-to-all-start.1 = ((bf16[32,32,512]{2,1,0:T(8,128)(2,1)}), bf16[32,32,512]{2,1,0:T(8,128)(2,1)S(1)}, u32[]{:S(2)}, u32[]{:S(2)}) async-start(bf16[32,32,512]{2,1,0:T(8,128)(2,1)} %select_select_fusion), calls=%async_computation.1 | async-start | bytes 2097152 | tf_op jit(solution)/shard_map/all_to_all | solution.py:78
  37.9 5.2 %collective-permute-start.7 = (s32[128]{0:T(128)S(1)}, s32[128]{0:T(128)S(1)}, u32[]{:S(2)}, u32[]{:S(2)}) collective-permute-start(s32[128]{0:T(128)S(1)} %add_bitcast_fusion.1), channel_id=1, source_target_pairs={{0,1},{1,2},{2,3},{3,4},{4,5},{5,6},{6,7},{7,8},{8,9},{9,10},{10,1... | collective-permute-start | bytes 1544 | tf_op jit(solution)/shard_map/ppermute | solution.py:18
  43.1 3.2 %collective-permute-start.6 = (s32[128]{0:T(128)S(1)}, s32[128]{0:T(128)S(1)}, u32[]{:S(2)}, u32[]{:S(2)}) collective-permute-start(s32[128]{0:T(128)S(1)} %add_bitcast_fusion.1), channel_id=1, source_target_pairs={{0,2},{1,3},{2,4},{3,5},{4,6},{5,7},{6,8},{7,9},{8,10},{9,11},{10,... | collective-permute-start | bytes 1544 | tf_op jit(solution)/shard_map/ppermute | solution.py:18
  46.3 3.2 %collective-permute-start.5 = (s32[128]{0:T(128)S(1)}, s32[128]{0:T(128)S(1)}, u32[]{:S(2)}, u32[]{:S(2)}) collective-permute-start(s32[128]{0:T(128)S(1)} %add_bitcast_fusion.1), channel_id=1, source_target_pairs={{0,3},{1,4},{2,5},{3,6},{4,7},{5,8},{6,9},{7,10},{8,11},{9,12},{10... | collective-permute-start | bytes 1544 | tf_op jit(solution)/shard_map/ppermute | solution.py:18
  49.5 4.5 %collective-permute-start.4 = (s32[128]{0:T(128)S(1)}, s32[128]{0:T(128)S(1)}, u32[]{:S(2)}, u32[]{:S(2)}) collective-permute-start(s32[128]{0:T(128)S(1)} %add_bitcast_fusion.1), channel_id=1, source_target_pairs={{0,4},{1,5},{2,6},{3,7},{4,8},{5,9},{6,10},{7,11},{8,12},{9,13},{1... | collective-permute-start | bytes 1544 | tf_op jit(solution)/shard_map/ppermute | solution.py:18
  54.8 8.2 %all-to-all-done.1 = bf16[32,32,512]{2,1,0:T(8,128)(2,1)S(1)} async-done(((bf16[32,32,512]{2,1,0:T(8,128)(2,1)}), bf16[32,32,512]{2,1,0:T(8,128)(2,1)S(1)}, u32[]{:S(2)}, u32[]{:S(2)}) %all-to-all-start.1) | async-done | bytes 1048608 | tf_op jit(solution)/shard_map/all_to_all | solution.py:78
  66.3 4.2 %collective-permute-start.8 = (bf16[128,512]{1,0:T(8,128)(2,1)S(1)}, bf16[128,512]{1,0:T(8,128)(2,1)S(1)}, u32[]{:S(2)}, u32[]{:S(2)}) collective-permute-start(bf16[128,512]{1,0:T(8,128)(2,1)S(1)} %get-tuple-element.48), channel_id=1, source_target_pairs={{0,4},{1,5},{2,6},{3,7},{4,8},{5,9},{6,10},{7,11},{8,12},{9,13},{1... | collective-permute-start | bytes 393224 | tf_op jit(solution)/shard_map/ppermute | solution.py:18
  70.5 5.4 %collective-permute-start = (bf16[128,512]{1,0:T(8,128)(2,1)S(1)}, bf16[128,512]{1,0:T(8,128)(2,1)S(1)}, u32[]{:S(2)}, u32[]{:S(2)}) collective-permute-start(bf16[128,512]{1,0:T(8,128)(2,1)S(1)} %get-tuple-element.49), channel_id=1, source_target_pairs={{0,4},{1,5},{2,6},{3,7},{4,8},{5,9},{6,10},{7,11},{8,12},{9,13},{1... | collective-permute-start | bytes 393224 | tf_op jit(solution)/shard_map/ppermute | solution.py:18
  76.7 6.8 %collective-permute-start.11 = (bf16[128,512]{1,0:T(8,128)(2,1)S(1)}, bf16[128,512]{1,0:T(8,128)(2,1)S(1)}, u32[]{:S(2)}, u32[]{:S(2)}) collective-permute-start(bf16[128,512]{1,0:T(8,128)(2,1)S(1)} %get-tuple-element.48), channel_id=1, source_target_pairs={{0,1},{1,2},{2,3},{3,4},{4,5},{5,6},{6,7},{7,8},{8,9},{9,10},{10,1... | collective-permute-start | bytes 393224 | tf_op jit(solution)/shard_map/ppermute | solution.py:18
  83.6 2.3 collective-permute-start.10
  85.9 2.3 collective-permute-start.9
  90.2 2.8 collective-permute-start.2
  94.6 5.8 %collective-permute-start.3 = (bf16[128,512]{1,0:T(8,128)(2,1)S(1)}, bf16[128,512]{1,0:T(8,128)(2,1)S(1)}, u32[]{:S(2)}, u32[]{:S(2)}) collective-permute-start(bf16[128,512]{1,0:T(8,128)(2,1)S(1)} %get-tuple-element.49), channel_id=1, source_target_pairs={{0,1},{1,2},{2,3},{3,4},{4,5},{5,6},{6,7},{7,8},{8,9},{9,10},{10,1... | collective-permute-start | bytes 393224 | tf_op jit(solution)/shard_map/ppermute | solution.py:18
  106.9 3.7 %select_convert_fusion.1 = (bf16[8,128,640]{2,1,0:T(8,128)(2,1)S(1)}, f32[8,128,640]{2,1,0:T(8,128)}) fusion(pred[128,640]{1,0:T(8,128)(4,1)} %fusion.15, bf16[128,8,64]{0,2,1:T(8,128)(2,1)} %bitcast.162, bf16[640,8,64]{0,2,1:T(8,128)(2,1)} %bitcast.143), kind=kOutput, calls=%fused_computation.10 | convolution fusion | flops 88473600 | bytes 4800512 | tf_op jit(solution)/shard_map/qhd,khd->hqk/dot_general | solution.py:111
  119.6 3.4 %select_convert_fusion = bf16[8,128,640]{2,1,0:T(8,128)(2,1)S(1)} fusion(f32[8,128,640]{2,1,0:T(8,128)} %get-tuple-element.57, bf16[128,8,64]{0,2,1:T(8,128)(2,1)} %bitcast.164, bf16[640,8,64]{0,2,1:T(8,128)(2,1)} %bitcast.141, pred[128,640]{1,0:T(8,128)(4,1)} %fusion.15), kind=kOutput, calls=%fused_computation.9 | convolution fusion | flops 91095040 | bytes 4800512 | tf_op jit(solution)/shard_map/qhd,khd->hqk/dot_general | solution.py:128
  140.2 2.1 collective-permute-start.16
  159.3 9.4 %collective-permute-done.14 = bf16[128,512]{1,0:T(8,128)(2,1)S(1)} collective-permute-done((bf16[128,512]{1,0:T(8,128)(2,1)}, bf16[128,512]{1,0:T(8,128)(2,1)S(1)}, u32[]{:S(2)}, u32[]{:S(2)}) %collective-permute-start.14) | collective-permute-done | bytes 131104 | tf_op jit(solution)/shard_map/ppermute | solution.py:18
  168.7 4.0 %collective-permute-done.15 = bf16[128,512]{1,0:T(8,128)(2,1)S(1)} collective-permute-done((bf16[128,512]{1,0:T(8,128)(2,1)}, bf16[128,512]{1,0:T(8,128)(2,1)S(1)}, u32[]{:S(2)}, u32[]{:S(2)}) %collective-permute-start.15) | collective-permute-done | bytes 131104 | tf_op jit(solution)/shard_map/ppermute | solution.py:18
  178.6 2.6 collective-permute-start.21
  181.4 2.8 scatter_custom_fusion.1
  184.1 5.3 %all-to-all-start.2 = ((bf16[32,32,512]{2,1,0:T(8,128)(2,1)}), bf16[32,32,512]{2,1,0:T(8,128)(2,1)}, u32[]{:S(2)}, u32[]{:S(2)}) async-start(bf16[32,32,512]{2,1,0:T(8,128)(2,1)} %bitcast.140), calls=%async_computation.2 | async-start | bytes 2097152 | tf_op jit(solution)/shard_map/all_to_all | solution.py:184
  189.5 3.1 %fusion = bf16[8,32,2560]{2,1,0:T(8,128)(2,1)} fusion(bf16[8,32,2560]{2,1,0:T(8,128)(2,1)} %collective-permute-done.21, s32[]{:T(128)S(6)} %select_n.96, bf16[8,2,32,2048]{3,2,1,0:T(8,128)(2,1)} %bitcast.137, bf16[8,2,32,512]{3,2,1,0:T(8,128)(2,1)S(1)} %convolution_convert_fusion.1), kind=kLoop, calls=%fused_computation.8 | loop fusion | flops 5242880 | bytes 5242884 | tf_op jit(solution)/shard_map/convert_element_type | solution.py:46
  192.6 24.1 %all-to-all-done.2 = bf16[32,32,512]{2,1,0:T(8,128)(2,1)} async-done(((bf16[32,32,512]{2,1,0:T(8,128)(2,1)}), bf16[32,32,512]{2,1,0:T(8,128)(2,1)}, u32[]{:S(2)}, u32[]{:S(2)}) %all-to-all-start.2) | async-done | bytes 1048608 | tf_op jit(solution)/shard_map/all_to_all | solution.py:184
  216.7 10.2 %all-to-all-start.4 = ((bf16[8,32,2560]{2,1,0:T(8,128)(2,1)}), bf16[8,32,2560]{2,1,0:T(8,128)(2,1)S(1)}, u32[]{:S(2)}, u32[]{:S(2)}) async-start(bf16[8,32,2560]{2,1,0:T(8,128)(2,1)} %fusion), calls=%async_computation.4 | async-start | bytes 2621440 | tf_op jit(solution)/shard_map/all_to_all | solution.py:48
  231.6 3.9 %collective-permute-start.20 = (bf16[8,32,512]{2,1,0:T(8,128)(2,1)S(1)}, bf16[8,32,512]{2,1,0:T(8,128)(2,1)S(1)}, u32[]{:S(2)}, u32[]{:S(2)}) collective-permute-start(bf16[8,32,512]{2,1,0:T(8,128)(2,1)S(1)} %dynamic-slice_bitcast_fusion), channel_id=1, source_target_pairs={{0,1},{1,0},{2,3},{3,2},{4,5},{5,4},{6,7},{7,6},{8,9},{9,8},{10,11... | collective-permute-start | bytes 786440 | tf_op jit(solution)/shard_map/ppermute | solution.py:45
  237.3 24.3 %all-to-all-done.4 = bf16[8,32,2560]{2,1,0:T(8,128)(2,1)S(1)} async-done(((bf16[8,32,2560]{2,1,0:T(8,128)(2,1)}), bf16[8,32,2560]{2,1,0:T(8,128)(2,1)S(1)}, u32[]{:S(2)}, u32[]{:S(2)}) %all-to-all-start.4) | async-done | bytes 1310752 | tf_op jit(solution)/shard_map/all_to_all | solution.py:48
  261.7 4.1 %all-to-all-start.3 = ((bf16[8,32,512]{2,1,0:T(8,128)(2,1)}), bf16[8,32,512]{2,1,0:T(8,128)(2,1)}, u32[]{:S(2)}, u32[]{:S(2)}) async-start(bf16[8,32,512]{2,1,0:T(8,128)(2,1)} %fusion.12), calls=%async_computation.3 | async-start | bytes 524288 | tf_op jit(solution)/shard_map/all_to_all | solution.py:48
  269.9 7.9 %all-to-all-done.3 = bf16[8,32,512]{2,1,0:T(8,128)(2,1)} async-done(((bf16[8,32,512]{2,1,0:T(8,128)(2,1)}), bf16[8,32,512]{2,1,0:T(8,128)(2,1)}, u32[]{:S(2)}, u32[]{:S(2)}) %all-to-all-start.3) | async-done | bytes 262176 | tf_op jit(solution)/shard_map/all_to_all | solution.py:48
  277.8 5.7 %all-to-all-start.5 = ((bf16[32,32,80]{2,1,0:T(8,128)(2,1)}), bf16[32,32,80]{2,1,0:T(8,128)(2,1)S(1)}, u32[]{:S(2)}, u32[]{:S(2)}) async-start(bf16[32,32,80]{2,1,0:T(8,128)(2,1)} %maximum_bitcast_fusion), calls=%async_computation.5 | async-start | bytes 524288 | tf_op jit(solution)/shard_map/all_to_all | solution.py:173
  286.1 8.7 %all-to-all-done.5 = bf16[32,32,80]{2,1,0:T(8,128)(2,1)S(1)} async-done(((bf16[32,32,80]{2,1,0:T(8,128)(2,1)}), bf16[32,32,80]{2,1,0:T(8,128)(2,1)S(1)}, u32[]{:S(2)}, u32[]{:S(2)}) %all-to-all-start.5) | async-done | bytes 163872 | tf_op jit(solution)/shard_map/all_to_all | solution.py:173
  (189 shorter events, 83.5 us)
Async XLA Ops:
  0.6 64.0 %copy-start = (bf16[512,2048]{1,0:T(8,128)(2,1)S(1)}, bf16[512,2048]{1,0:T(8,128)(2,1)}, u32[]{:S(2)}) copy-start(bf16[512,2048]{1,0:T(8,128)(2,1)} %param.9) | copy-start | bytes 6291460
  3.8 50.8 %copy-start.23 = (s32[256,1]{0,1:T(1,128)}, s32[256,1]{0,1:T(1,128)S(1)}, u32[]{:S(2)}) copy-start(s32[256,1]{0,1:T(1,128)S(1)} %compare_select_fusion) | copy-start | bytes 3076
  33.9 29.2 %all-to-all-start.1 = ((bf16[32,32,512]{2,1,0:T(8,128)(2,1)}), bf16[32,32,512]{2,1,0:T(8,128)(2,1)S(1)}, u32[]{:S(2)}, u32[]{:S(2)}) async-start(bf16[32,32,512]{2,1,0:T(8,128)(2,1)} %select_select_fusion), calls=%async_computation.1 | async-start | bytes 2097152 | tf_op jit(solution)/shard_map/all_to_all | solution.py:78
  37.9 26.4 %copy-start.24 = (s32[128]{0:T(128)}, s32[128]{0:T(128)S(1)}, u32[]{:S(2)}) copy-start(s32[128]{0:T(128)S(1)} %add_bitcast_fusion.1) | copy-start | bytes 1540
  37.9 16.9 %collective-permute-start.7 = (s32[128]{0:T(128)S(1)}, s32[128]{0:T(128)S(1)}, u32[]{:S(2)}, u32[]{:S(2)}) collective-permute-start(s32[128]{0:T(128)S(1)} %add_bitcast_fusion.1), channel_id=1, source_target_pairs={{0,1},{1,2},{2,3},{3,4},{4,5},{5,6},{6,7},{7,8},{8,9},{9,10},{10,1... | collective-permute-start | bytes 1544 | tf_op jit(solution)/shard_map/ppermute | solution.py:18
  43.1 11.7 %collective-permute-start.6 = (s32[128]{0:T(128)S(1)}, s32[128]{0:T(128)S(1)}, u32[]{:S(2)}, u32[]{:S(2)}) collective-permute-start(s32[128]{0:T(128)S(1)} %add_bitcast_fusion.1), channel_id=1, source_target_pairs={{0,2},{1,3},{2,4},{3,5},{4,6},{5,7},{6,8},{7,9},{8,10},{9,11},{10,... | collective-permute-start | bytes 1544 | tf_op jit(solution)/shard_map/ppermute | solution.py:18
  46.3 8.5 %collective-permute-start.5 = (s32[128]{0:T(128)S(1)}, s32[128]{0:T(128)S(1)}, u32[]{:S(2)}, u32[]{:S(2)}) collective-permute-start(s32[128]{0:T(128)S(1)} %add_bitcast_fusion.1), channel_id=1, source_target_pairs={{0,3},{1,4},{2,5},{3,6},{4,7},{5,8},{6,9},{7,10},{8,11},{9,12},{10... | collective-permute-start | bytes 1544 | tf_op jit(solution)/shard_map/ppermute | solution.py:18
  49.5 5.2 %collective-permute-start.4 = (s32[128]{0:T(128)S(1)}, s32[128]{0:T(128)S(1)}, u32[]{:S(2)}, u32[]{:S(2)}) collective-permute-start(s32[128]{0:T(128)S(1)} %add_bitcast_fusion.1), channel_id=1, source_target_pairs={{0,4},{1,5},{2,6},{3,7},{4,8},{5,9},{6,10},{7,11},{8,12},{9,13},{1... | collective-permute-start | bytes 1544 | tf_op jit(solution)/shard_map/ppermute | solution.py:18
  66.2 36.2 %copy-start.7 = (bf16[128,2048]{1,0:T(8,128)(2,1)}, bf16[128,2048]{1,0:T(8,128)(2,1)S(1)}, u32[]{:S(2)}) copy-start(bf16[128,2048]{1,0:T(8,128)(2,1)S(1)} %get-tuple-element.54) | copy-start | bytes 1572868
  66.3 23.9 %collective-permute-start.8 = (bf16[128,512]{1,0:T(8,128)(2,1)S(1)}, bf16[128,512]{1,0:T(8,128)(2,1)S(1)}, u32[]{:S(2)}, u32[]{:S(2)}) collective-permute-start(bf16[128,512]{1,0:T(8,128)(2,1)S(1)} %get-tuple-element.48), channel_id=1, source_target_pairs={{0,4},{1,5},{2,6},{3,7},{4,8},{5,9},{6,10},{7,11},{8,12},{9,13},{1... | collective-permute-start | bytes 393224 | tf_op jit(solution)/shard_map/ppermute | solution.py:18
  70.5 17.7 %collective-permute-start = (bf16[128,512]{1,0:T(8,128)(2,1)S(1)}, bf16[128,512]{1,0:T(8,128)(2,1)S(1)}, u32[]{:S(2)}, u32[]{:S(2)}) collective-permute-start(bf16[128,512]{1,0:T(8,128)(2,1)S(1)} %get-tuple-element.49), channel_id=1, source_target_pairs={{0,4},{1,5},{2,6},{3,7},{4,8},{5,9},{6,10},{7,11},{8,12},{9,13},{1... | collective-permute-start | bytes 393224 | tf_op jit(solution)/shard_map/ppermute | solution.py:18
  76.7 25.6 %collective-permute-start.11 = (bf16[128,512]{1,0:T(8,128)(2,1)S(1)}, bf16[128,512]{1,0:T(8,128)(2,1)S(1)}, u32[]{:S(2)}, u32[]{:S(2)}) collective-permute-start(bf16[128,512]{1,0:T(8,128)(2,1)S(1)} %get-tuple-element.48), channel_id=1, source_target_pairs={{0,1},{1,2},{2,3},{3,4},{4,5},{5,6},{6,7},{7,8},{8,9},{9,10},{10,1... | collective-permute-start | bytes 393224 | tf_op jit(solution)/shard_map/ppermute | solution.py:18
  83.6 18.8 %collective-permute-start.10 = (bf16[128,512]{1,0:T(8,128)(2,1)S(1)}, bf16[128,512]{1,0:T(8,128)(2,1)S(1)}, u32[]{:S(2)}, u32[]{:S(2)}) collective-permute-start(bf16[128,512]{1,0:T(8,128)(2,1)S(1)} %get-tuple-element.48), channel_id=1, source_target_pairs={{0,2},{1,3},{2,4},{3,5},{4,6},{5,7},{6,8},{7,9},{8,10},{9,11},{10,... | collective-permute-start | bytes 393224 | tf_op jit(solution)/shard_map/ppermute | solution.py:18
  85.9 16.4 %collective-permute-start.9 = (bf16[128,512]{1,0:T(8,128)(2,1)S(1)}, bf16[128,512]{1,0:T(8,128)(2,1)S(1)}, u32[]{:S(2)}, u32[]{:S(2)}) collective-permute-start(bf16[128,512]{1,0:T(8,128)(2,1)S(1)} %get-tuple-element.48), channel_id=1, source_target_pairs={{0,3},{1,4},{2,5},{3,6},{4,7},{5,8},{6,9},{7,10},{8,11},{9,12},{10... | collective-permute-start | bytes 393224 | tf_op jit(solution)/shard_map/ppermute | solution.py:18
  88.2 6.4 %collective-permute-start.1 = (bf16[128,512]{1,0:T(8,128)(2,1)S(1)}, bf16[128,512]{1,0:T(8,128)(2,1)S(1)}, u32[]{:S(2)}, u32[]{:S(2)}) collective-permute-start(bf16[128,512]{1,0:T(8,128)(2,1)S(1)} %get-tuple-element.49), channel_id=1, source_target_pairs={{0,3},{1,4},{2,5},{3,6},{4,7},{5,8},{6,9},{7,10},{8,11},{9,12},{10... | collective-permute-start | bytes 393224 | tf_op jit(solution)/shard_map/ppermute | solution.py:18
  90.2 10.2 %collective-permute-start.2 = (bf16[128,512]{1,0:T(8,128)(2,1)S(1)}, bf16[128,512]{1,0:T(8,128)(2,1)S(1)}, u32[]{:S(2)}, u32[]{:S(2)}) collective-permute-start(bf16[128,512]{1,0:T(8,128)(2,1)S(1)} %get-tuple-element.49), channel_id=1, source_target_pairs={{0,2},{1,3},{2,4},{3,5},{4,6},{5,7},{6,8},{7,9},{8,10},{9,11},{10,... | collective-permute-start | bytes 393224 | tf_op jit(solution)/shard_map/ppermute | solution.py:18
  94.6 7.7 %collective-permute-start.3 = (bf16[128,512]{1,0:T(8,128)(2,1)S(1)}, bf16[128,512]{1,0:T(8,128)(2,1)S(1)}, u32[]{:S(2)}, u32[]{:S(2)}) collective-permute-start(bf16[128,512]{1,0:T(8,128)(2,1)S(1)} %get-tuple-element.49), channel_id=1, source_target_pairs={{0,1},{1,2},{2,3},{3,4},{4,5},{5,6},{6,7},{7,8},{8,9},{9,10},{10,1... | collective-permute-start | bytes 393224 | tf_op jit(solution)/shard_map/ppermute | solution.py:18
  136.3 17.0 %collective-permute-start.17 = (bf16[128,512]{1,0:T(8,128)(2,1)}, bf16[128,512]{1,0:T(8,128)(2,1)}, u32[]{:S(2)}, u32[]{:S(2)}) collective-permute-start(bf16[128,512]{1,0:T(8,128)(2,1)} %copy.142), channel_id=1, source_target_pairs={{2,0},{3,1},{4,2},{5,3},{6,4},{7,5},{8,6},{9,7},{10,8},{11,9},{12,... | collective-permute-start | bytes 393224 | tf_op jit(solution)/shard_map/ppermute | solution.py:18
  137.6 17.2 %collective-permute-start.18 = (bf16[128,512]{1,0:T(8,128)(2,1)}, bf16[128,512]{1,0:T(8,128)(2,1)}, u32[]{:S(2)}, u32[]{:S(2)}) collective-permute-start(bf16[128,512]{1,0:T(8,128)(2,1)} %copy.143), channel_id=1, source_target_pairs={{3,0},{4,1},{5,2},{6,3},{7,4},{8,5},{9,6},{10,7},{11,8},{12,9},{13... | collective-permute-start | bytes 393224 | tf_op jit(solution)/shard_map/ppermute | solution.py:18
  138.9 17.2 %collective-permute-start.19 = (bf16[128,512]{1,0:T(8,128)(2,1)}, bf16[128,512]{1,0:T(8,128)(2,1)}, u32[]{:S(2)}, u32[]{:S(2)}) collective-permute-start(bf16[128,512]{1,0:T(8,128)(2,1)} %copy.144), channel_id=1, source_target_pairs={{4,0},{5,1},{6,2},{7,3},{8,4},{9,5},{10,6},{11,7},{12,8},{13,9},{1... | collective-permute-start | bytes 393224 | tf_op jit(solution)/shard_map/ppermute | solution.py:18
  140.2 17.9 %collective-permute-start.16 = (bf16[128,512]{1,0:T(8,128)(2,1)}, bf16[128,512]{1,0:T(8,128)(2,1)}, u32[]{:S(2)}, u32[]{:S(2)}) collective-permute-start(bf16[128,512]{1,0:T(8,128)(2,1)} %copy.140), channel_id=1, source_target_pairs={{1,0},{2,1},{3,2},{4,3},{5,4},{6,5},{7,6},{8,7},{9,8},{10,9},{11,1... | collective-permute-start | bytes 393224 | tf_op jit(solution)/shard_map/ppermute | solution.py:18
  148.2 25.6 %copy-start.11 = (f32[128,512]{1,0:T(8,128)S(1)}, f32[128,512]{1,0:T(8,128)}, u32[]{:S(2)}) copy-start(f32[128,512]{1,0:T(8,128)} %get-tuple-element.44) | copy-start | bytes 786436
  149.9 9.4 %collective-permute-start.13 = (bf16[128,512]{1,0:T(8,128)(2,1)}, bf16[128,512]{1,0:T(8,128)(2,1)}, u32[]{:S(2)}, u32[]{:S(2)}) collective-permute-start(bf16[128,512]{1,0:T(8,128)(2,1)} %copy.137), channel_id=1, source_target_pairs={{2,0},{3,1},{4,2},{5,3},{6,4},{7,5},{8,6},{9,7},{10,8},{11,9},{12,... | collective-permute-start | bytes 393224 | tf_op jit(solution)/shard_map/ppermute | solution.py:18
  153.3 15.3 %collective-permute-start.14 = (bf16[128,512]{1,0:T(8,128)(2,1)}, bf16[128,512]{1,0:T(8,128)(2,1)S(1)}, u32[]{:S(2)}, u32[]{:S(2)}) collective-permute-start(bf16[128,512]{1,0:T(8,128)(2,1)} %copy.138), channel_id=1, source_target_pairs={{3,0},{4,1},{5,2},{6,3},{7,4},{8,5},{9,6},{10,7},{11,8},{12,9},{13... | collective-permute-start | bytes 393224 | tf_op jit(solution)/shard_map/ppermute | solution.py:18
  154.8 17.9 %collective-permute-start.15 = (bf16[128,512]{1,0:T(8,128)(2,1)}, bf16[128,512]{1,0:T(8,128)(2,1)S(1)}, u32[]{:S(2)}, u32[]{:S(2)}) collective-permute-start(bf16[128,512]{1,0:T(8,128)(2,1)} %copy.139), channel_id=1, source_target_pairs={{4,0},{5,1},{6,2},{7,3},{8,4},{9,5},{10,6},{11,7},{12,8},{13,9},{1... | collective-permute-start | bytes 393224 | tf_op jit(solution)/shard_map/ppermute | solution.py:18
  156.1 16.6 %collective-permute-start.12 = (bf16[128,512]{1,0:T(8,128)(2,1)}, bf16[128,512]{1,0:T(8,128)(2,1)S(1)}, u32[]{:S(2)}, u32[]{:S(2)}) collective-permute-start(bf16[128,512]{1,0:T(8,128)(2,1)} %copy.135), channel_id=1, source_target_pairs={{1,0},{2,1},{3,2},{4,3},{5,4},{6,5},{7,6},{8,7},{9,8},{10,9},{11,1... | collective-permute-start | bytes 393224 | tf_op jit(solution)/shard_map/ppermute | solution.py:18
  178.6 10.9 %collective-permute-start.21 = (bf16[8,32,2560]{2,1,0:T(8,128)(2,1)}, bf16[8,32,2560]{2,1,0:T(8,128)(2,1)}, u32[]{:S(2)}, u32[]{:S(2)}) collective-permute-start(bf16[8,32,2560]{2,1,0:T(8,128)(2,1)} %fusion.4), channel_id=1, source_target_pairs={{0,1},{1,0},{2,3},{3,2},{4,5},{5,4},{6,7},{7,6},{8,9},{9,8},{10,11... | collective-permute-start | bytes 3932168 | tf_op jit(solution)/shard_map/ppermute | solution.py:45
  184.1 32.6 %all-to-all-start.2 = ((bf16[32,32,512]{2,1,0:T(8,128)(2,1)}), bf16[32,32,512]{2,1,0:T(8,128)(2,1)}, u32[]{:S(2)}, u32[]{:S(2)}) async-start(bf16[32,32,512]{2,1,0:T(8,128)(2,1)} %bitcast.140), calls=%async_computation.2 | async-start | bytes 2097152 | tf_op jit(solution)/shard_map/all_to_all | solution.py:184
  216.7 45.0 %all-to-all-start.4 = ((bf16[8,32,2560]{2,1,0:T(8,128)(2,1)}), bf16[8,32,2560]{2,1,0:T(8,128)(2,1)S(1)}, u32[]{:S(2)}, u32[]{:S(2)}) async-start(bf16[8,32,2560]{2,1,0:T(8,128)(2,1)} %fusion), calls=%async_computation.4 | async-start | bytes 2621440 | tf_op jit(solution)/shard_map/all_to_all | solution.py:48
  231.6 5.0 %collective-permute-start.20 = (bf16[8,32,512]{2,1,0:T(8,128)(2,1)S(1)}, bf16[8,32,512]{2,1,0:T(8,128)(2,1)S(1)}, u32[]{:S(2)}, u32[]{:S(2)}) collective-permute-start(bf16[8,32,512]{2,1,0:T(8,128)(2,1)S(1)} %dynamic-slice_bitcast_fusion), channel_id=1, source_target_pairs={{0,1},{1,0},{2,3},{3,2},{4,5},{5,4},{6,7},{7,6},{8,9},{9,8},{10,11... | collective-permute-start | bytes 786440 | tf_op jit(solution)/shard_map/ppermute | solution.py:45
  261.7 16.1 %all-to-all-start.3 = ((bf16[8,32,512]{2,1,0:T(8,128)(2,1)}), bf16[8,32,512]{2,1,0:T(8,128)(2,1)}, u32[]{:S(2)}, u32[]{:S(2)}) async-start(bf16[8,32,512]{2,1,0:T(8,128)(2,1)} %fusion.12), calls=%async_computation.3 | async-start | bytes 524288 | tf_op jit(solution)/shard_map/all_to_all | solution.py:48
  277.8 17.0 %all-to-all-start.5 = ((bf16[32,32,80]{2,1,0:T(8,128)(2,1)}), bf16[32,32,80]{2,1,0:T(8,128)(2,1)S(1)}, u32[]{:S(2)}, u32[]{:S(2)}) async-start(bf16[32,32,80]{2,1,0:T(8,128)(2,1)} %maximum_bitcast_fusion), calls=%async_computation.5 | async-start | bytes 524288 | tf_op jit(solution)/shard_map/all_to_all | solution.py:173
  (23 other events, 185.4 us)

commit v2 on v0

v2 whole, which is shorter than its diff:
```python
import math

import jax
import jax.numpy as jnp
from jax import lax
from jax.experimental import pallas as pl
from jax.experimental.pallas import tpu as pltpu
from jax.sharding import PartitionSpec as P

H = 8
DH = 64
X_CHIPS = 4
REACH = 4
USER_ROWS = 16

epsilon = 1e-05
f32 = jnp.float32
bf16 = jnp.bfloat16


def passed_along(block, axis, distance):
    devices = range(lax.axis_size(axis))
    route = [(i - distance, i) for i in devices if i - distance in devices]
    return lax.ppermute(block, axis, route)


def layer_norm(values):
    centered = values - jnp.mean(values, axis=-1, keepdims=True)
    inverse = lax.rsqrt(jnp.mean(centered * centered, axis=-1, keepdims=True) + epsilon)
    return (centered * inverse, inverse)


def norm_backward(normed, inverse, upstream):
    first_mean = jnp.mean(upstream, axis=-1, keepdims=True)
    second_mean = jnp.mean(upstream * normed, axis=-1, keepdims=True)
    return inverse * (upstream - first_mean - normed * second_mean)


def sigmoid(values):
    return 0.5 * jnp.tanh(0.5 * values) + 0.5


def silu_slope(values):
    sig = sigmoid(values)
    return sig * (1.0 + values * (1.0 - sig))


def iota(shape, dim):
    return lax.broadcasted_iota(jnp.int32, shape, dim)


def dot(left, right):
    return jnp.dot(left, right, preferred_element_type=f32)


def dot_nt(left, right):
    return lax.dot_general(left, right, (((1,), (1,)), ((), ())), preferred_element_type=f32)


def dot_tn(left, right):
    return lax.dot_general(left, right, (((0,), (0,)), ((), ())), preferred_element_type=f32)


def hot(condition):
    return condition.astype(f32).astype(bf16)


def as_column(row):
    length = row.shape[1]
    eye = iota((length, length), 0) == iota((length, length), 1)
    return jnp.sum(jnp.where(eye, jnp.broadcast_to(row, (length, length)), 0.0), axis=1, keepdims=True)


def both_heads(pair):
    low = iota(pair.shape, 1) < DH
    zero = jnp.zeros_like(pair)
    return jnp.concatenate([jnp.where(low, pair, zero), jnp.where(low, zero, pair)], axis=0)


def one_pair(stacked):
    rows = stacked.shape[0] // 2
    low = iota((rows, stacked.shape[1]), 1) < DH
    return jnp.where(low, stacked[:rows], stacked[rows:])


def call(body, outs, *operands, flops=0, moved=0):
    return pl.pallas_call(
        body,
        out_shape=[jax.ShapeDtypeStruct(shape, kind) for shape, kind in outs],
        compiler_params=pltpu.CompilerParams(vmem_limit_bytes=40 * 1024 * 1024),
        cost_estimate=pl.CostEstimate(flops=flops, bytes_accessed=moved, transcendentals=0),
    )(*operands)


def route_body(table_dev, ids_ref, request_ref, slot_ref):
    owners, capacity = request_ref.shape
    ids = ids_ref[...]
    count = ids.shape[0]
    shift = table_dev.bit_length() - 1
    owner = jnp.right_shift(ids, shift)
    row = jnp.bitwise_and(ids, table_dev - 1)
    member_f = (owner == iota((count, owners), 1)).astype(f32)
    member = member_f.astype(bf16)
    earlier = hot(iota((count, count), 0) > iota((count, count), 1))
    rank = jnp.sum(dot(earlier, member) * member_f, axis=1, keepdims=True).astype(jnp.int32)
    rank_hot = hot(rank == iota((count, capacity), 1))
    high = (member_f * jnp.right_shift(row, 4).astype(f32)).astype(bf16)
    low = (member_f * jnp.bitwise_and(row, 15).astype(f32)).astype(bf16)
    found = 16.0 * dot_tn(high, rank_hot) + dot_tn(low, rank_hot) + dot_tn(member, rank_hot)
    request_ref[...] = found.astype(jnp.int32) - 1
    slot_ref[...] = owner * capacity + rank


def gather_body(asked_ref, table_ref, found_ref):
    slots = asked_ref.shape[1]
    hits = hot(iota((table_ref.shape[0], slots), 0) == asked_ref[...])
    found_ref[...] = dot_tn(hits, table_ref[...]).astype(bf16)


def slot_matrix(slot, slots):
    events = slot.shape[0] // 2
    places = iota((events, slots), 1)
    return hot((slot[:events] == places) | (slot[events:] == places))


def embed_body(slot_ref, fetched_ref, user_ref, inputs_ref, packed_ref):
    rows = inputs_ref.shape[0]
    places = slot_matrix(slot_ref[...], fetched_ref.shape[0])
    inputs = dot(places, fetched_ref[...]).astype(bf16)
    inputs_ref[...] = inputs
    packed_ref[:rows, :] = layer_norm(inputs.astype(f32))[0].astype(bf16)
    packed_ref[rows:, :] = user_rows(user_ref[...], packed_ref.shape[1])


def user_rows(user, width):
    wide = jnp.concatenate([user, jnp.zeros((1, width - user.shape[1]), f32)], axis=1)
    return jnp.broadcast_to(wide, (USER_ROWS, width)).astype(bf16)


def project_body(
    packed_ref, w_in_ref, w_out_ref, grad_ref, user_ref,
    projected_ref, gates_ref, values_ref, queries_ref, keys_ref, mixed_grad_ref,
):
    rows = grad_ref.shape[0]
    width = grad_ref.shape[1]
    normed = packed_ref[:rows, :]
    for part, out_ref in enumerate((gates_ref, values_ref, queries_ref, keys_ref)):
        columns = slice(part * width, (part + 1) * width)
        projected = dot(normed, w_in_ref[:, columns])
        projected_ref[:, columns] = projected
        out_ref[:rows, :] = (projected * sigmoid(projected)).astype(bf16)
    queries_ref[rows:, :] = user_rows(user_ref[...], width)
    mixed_grad_ref[...] = dot_nt(grad_ref[...], w_out_ref[...])


def window_mask(user_row, key_user_row, margin):
    rows = user_row.shape[1]
    columns = key_user_row.shape[1]
    user_column = as_column(user_row)
    allowed = (user_column == key_user_row) & (
        iota((rows, columns), 1) <= iota((rows, columns), 0) + margin
    )
    weight = allowed.astype(f32)
    return jnp.concatenate([weight, weight], axis=0) > 0.0


def forward_body(
    halo4_ref, halo3_ref, halo2_ref, halo1_ref, values_ref, keys_ref, queries_ref, gates_ref,
    inputs_ref, mixed_grad_ref, w_in_ref, w_out_ref, user_ref,
    out_ref, mixed_ref, gate_grad_ref, att_grad_ref, all_keys_ref, all_values_ref, key_user_ref,
):
    rows, width = inputs_ref.shape
    score_scale = 1.0 / math.sqrt(DH)
    halos = (halo4_ref, halo3_ref, halo2_ref, halo1_ref)
    far = jnp.concatenate([halo[:rows, :] for halo in halos], axis=0)
    margin = far.shape[0]
    for part, own_ref, all_ref in ((1, values_ref, all_values_ref), (3, keys_ref, all_keys_ref)):
        projected = dot(far, w_in_ref[:, part * width : (part + 1) * width])
        all_ref[:margin, :] = (projected * sigmoid(projected)).astype(bf16)
        all_ref[margin:, :] = own_ref[...]
    user_row = user_ref[...]
    key_user = jnp.concatenate(
        [halo[rows : rows + 1, :rows].astype(f32) for halo in halos] + [user_row], axis=1
    )
    key_user_ref[...] = key_user
    allowed = window_mask(user_row, key_user, margin)
    parts = []
    for pair in range(H // 2):
        columns = slice(2 * DH * pair, 2 * DH * (pair + 1))
        scores = dot_nt(both_heads(queries_ref[:rows, columns]), all_keys_ref[:, columns]) * score_scale
        weights = jnp.where(allowed, scores * sigmoid(scores), 0.0).astype(bf16)
        parts.append(one_pair(dot(weights, all_values_ref[:, columns])))
    att_hat, att_inv = layer_norm(jnp.concatenate(parts, axis=1))
    gates = gates_ref[...].astype(f32)
    mixed = (att_hat * gates).astype(bf16)
    mixed_ref[...] = mixed
    out_ref[...] = (inputs_ref[...].astype(f32) + dot(mixed, w_out_ref[...])).astype(bf16)
    mixed_grad = mixed_grad_ref[...]
    gate_grad_ref[...] = mixed_grad * att_hat
    att_grad_ref[...] = norm_backward(att_hat, att_inv, mixed_grad * gates).astype(bf16)


def split_by_core(core, section, terms, kept_ref, sent_ref):
    devices = 2 * kept_ref.shape[1]
    rows = terms.shape[0] // devices
    lanes = terms.shape[1] // X_CHIPS
    even = core == 0
    for x in range(X_CHIPS):
        for chip in range(devices // 2):
            first = terms[2 * chip * rows : (2 * chip + 1) * rows, x * lanes : (x + 1) * lanes]
            second = terms[(2 * chip + 1) * rows : (2 * chip + 2) * rows, x * lanes : (x + 1) * lanes]
            place = (x, chip, slice(None), slice(section * lanes, (section + 1) * lanes))
            kept_ref[place] = jnp.where(even, first, second).astype(bf16)
            sent_ref[place] = jnp.where(even, second, first).astype(bf16)


def order_by_x(block, piece):
    width = block.shape[1]
    old = iota((width, width), 0)
    new = iota((width, width), 1)
    per_x = width // X_CHIPS
    inner = jnp.bitwise_and(old, piece - 1)
    owner = jnp.right_shift(old, piece.bit_length() - 1)
    x = jnp.bitwise_and(owner, X_CHIPS - 1)
    z = jnp.right_shift(owner, X_CHIPS.bit_length() - 1)
    return dot(block, hot(new == x * per_x + z * piece + inner)).astype(bf16)


def query_body(
    piece_in, piece_out, core_ref, queries_ref, all_keys_ref, all_values_ref, att_grad_ref, gate_grad_ref,
    projected_ref, user_ref, key_user_ref, packed_ref, mixed_ref, grad_ref,
    gate_query_ref, kept_ref, sent_ref,
):
    rows, width = grad_ref.shape
    score_scale = 1.0 / math.sqrt(DH)
    margin = all_keys_ref.shape[0] - rows
    allowed = window_mask(user_ref[...], key_user_ref[...], margin)
    parts = []
    for pair in range(H // 2):
        columns = slice(2 * DH * pair, 2 * DH * (pair + 1))
        keys = all_keys_ref[:, columns]
        scores = dot_nt(both_heads(queries_ref[:rows, columns]), keys) * score_scale
        prob_grad = dot_nt(both_heads(att_grad_ref[:, columns]), all_values_ref[:, columns])
        score_grad = jnp.where(allowed, prob_grad * silu_slope(scores), 0.0).astype(bf16)
        parts.append(one_pair(dot(score_grad, keys)) * score_scale)
    query_grad = jnp.concatenate(parts, axis=1)
    core = core_ref[0]
    normed = packed_ref[:rows, :]
    gate_part = (gate_grad_ref[...] * silu_slope(projected_ref[:, :width])).astype(bf16)
    query_part = (query_grad * silu_slope(projected_ref[:, 2 * width : 3 * width])).astype(bf16)
    gate_query_ref[:, :width] = gate_part
    gate_query_ref[:, width:] = query_part
    split_by_core(core, 0, dot_tn(normed, order_by_x(gate_part, piece_in)), kept_ref, sent_ref)
    split_by_core(core, 1, dot_tn(normed, order_by_x(query_part, piece_in)), kept_ref, sent_ref)
    split_by_core(core, 2, dot_tn(mixed_ref[...], order_by_x(grad_ref[...], piece_out)), kept_ref, sent_ref)


def key_body(
    query0_ref, query1_ref, query2_ref, query3_ref, query4_ref,
    grad0_ref, grad1_ref, grad2_ref, grad3_ref, grad4_ref,
    keys_ref, values_ref, projected_ref, gate_query_ref, w_in_ref, inputs_ref, out_grad_ref, slot_ref, user_ref,
    value_key_ref, outgoing_ref,
):
    rows, width = inputs_ref.shape
    score_scale = 1.0 / math.sqrt(DH)
    query_refs = (query0_ref, query1_ref, query2_ref, query3_ref, query4_ref)
    grad_refs = (grad0_ref, grad1_ref, grad2_ref, grad3_ref, grad4_ref)
    user_row = user_ref[...]
    query_user = jnp.concatenate(
        [as_column(ref[rows : rows + 1, :rows].astype(f32)) for ref in query_refs], axis=0
    )
    total = query_user.shape[0]
    allowed = (query_user == user_row) & (iota((total, rows), 1) <= iota((total, rows), 0))
    weight = allowed.astype(f32)
    allowed = jnp.concatenate([weight, weight], axis=0) > 0.0
    key_parts = []
    value_parts = []
    for pair in range(H // 2):
        columns = slice(2 * DH * pair, 2 * DH * (pair + 1))
        queries = both_heads(jnp.concatenate([ref[:rows, columns] for ref in query_refs], axis=0))
        grads = both_heads(jnp.concatenate([ref[:, columns] for ref in grad_refs], axis=0))
        scores = dot_nt(queries, keys_ref[:, columns]) * score_scale
        sig = sigmoid(scores)
        raw = scores * sig
        weights = jnp.where(allowed, raw, 0.0).astype(bf16)
        prob_grad = dot_nt(grads, values_ref[:, columns])
        score_grad = jnp.where(allowed, prob_grad * (sig + raw * (1.0 - sig)), 0.0).astype(bf16)
        key_parts.append(dot_tn(score_grad, queries) * score_scale)
        value_parts.append(dot_tn(weights, grads))
    key_grad = jnp.concatenate(key_parts, axis=1)
    value_grad = jnp.concatenate(value_parts, axis=1)
    value_part = (value_grad * silu_slope(projected_ref[:, width : 2 * width])).astype(bf16)
    key_part = (key_grad * silu_slope(projected_ref[:, 3 * width :])).astype(bf16)
    value_key_ref[:, :width] = value_part
    value_key_ref[:, width:] = key_part
    joined = jnp.concatenate(
        [gate_query_ref[:, :width], value_part, gate_query_ref[:, width:], key_part], axis=1
    )
    normed_grad = dot_nt(joined, w_in_ref[...])
    input_hat, input_inv = layer_norm(inputs_ref[...].astype(f32))
    inputs_grad = (
        out_grad_ref[...].astype(f32) + norm_backward(input_hat, input_inv, normed_grad)
    ).astype(bf16)
    places = slot_matrix(slot_ref[...], outgoing_ref.shape[0])
    outgoing_ref[...] = dot_tn(places, inputs_grad).astype(bf16)


def late_weights_body(piece_in, core_ref, packed_ref, value_key_ref, kept_ref, sent_ref):
    rows = value_key_ref.shape[0]
    width = value_key_ref.shape[1] // 2
    core = core_ref[0]
    normed = packed_ref[:rows, :]
    for section in range(2):
        part = value_key_ref[:, section * width : (section + 1) * width]
        split_by_core(core, section, dot_tn(normed, order_by_x(part, piece_in)), kept_ref, sent_ref)


def table_body(core_ref, asked_ref, arrived_ref, kept_ref, sent_ref):
    slots = asked_ref.shape[1]
    table_dev = kept_ref.shape[2]
    hits = hot(iota((table_dev, slots), 0) == asked_ref[...])
    sums = dot(hits, arrived_ref[...]).T
    rows = kept_ref.shape[1]
    even = core_ref[0] == 0
    for chip in range(kept_ref.shape[0]):
        first = sums[2 * chip * rows : (2 * chip + 1) * rows]
        second = sums[(2 * chip + 1) * rows : (2 * chip + 2) * rows]
        kept_ref[chip] = jnp.where(even, first, second).astype(bf16)
        sent_ref[chip] = jnp.where(even, second, first).astype(bf16)


def pair_sum(kept, sent):
    devices = lax.axis_size("ctx")
    got = lax.ppermute(sent, "ctx", [(i, i ^ 1) for i in range(devices)])
    return (kept.astype(f32) + got.astype(f32)).astype(bf16)


def chips_along_y():
    devices = lax.axis_size("ctx")
    return [list(range(first, devices, 2)) for first in range(2)]


def spread(block, axis, groups):
    return lax.all_to_all(
        block, axis, split_axis=0, concat_axis=0, tiled=True, axis_index_groups=groups
    )


def total_of(blocks):
    return jnp.sum(blocks.astype(f32), axis=0)


def sum_along_x(block):
    count = lax.axis_size("dp")
    me = lax.axis_index("dp") % X_CHIPS
    own = lax.dynamic_index_in_dim(block, me, 0, keepdims=False).astype(f32)
    for step in range(1, X_CHIPS):
        route = [(i, i - i % X_CHIPS + (i + step) % X_CHIPS) for i in range(count)]
        piece = lax.dynamic_index_in_dim(block, (me + step) % X_CHIPS, 0, keepdims=False)
        own = own + lax.ppermute(piece, "dp", route).astype(f32)
    return own.astype(bf16)


def reduce_weights(early, late, owners):
    xs = [list(range(first, first + X_CHIPS)) for first in range(0, owners, X_CHIPS)]
    zs = [list(range(first, owners, X_CHIPS)) for first in range(X_CHIPS)]
    z_chips = owners // X_CHIPS
    early_x = total_of(spread(early, "dp", xs)).astype(bf16)
    late_x = sum_along_x(late)
    both = jnp.concatenate([early_x, late_x], axis=2)
    along_y = total_of(spread(both, "ctx", chips_along_y())).astype(bf16)
    rows = along_y.shape[0]
    gate, query, out, value, key = jnp.split(along_y, 5, axis=1)
    wide = jnp.concatenate([gate, value, query, key], axis=1).reshape(rows, z_chips, -1)
    thin = out.reshape(rows, z_chips, -1)
    send = jnp.concatenate([wide, thin], axis=2).transpose(1, 0, 2)
    summed = total_of(spread(send, "dp", zs))
    return (summed[:, : wide.shape[2]], summed[:, wide.shape[2] :])


def local(item_ids, segments, touched_rows, w_in, w_out, out_grad):
    rows_dev = segments.shape[1]
    model_width = w_in.shape[0]
    table_dev = touched_rows.shape[0]
    owners = lax.axis_size("dp")
    capacity = max(rows_dev // 4, 6 * rows_dev // owners + 2)
    slots = owners * capacity
    core = (lax.axis_index("ctx") % 2).astype(jnp.int32).reshape(1)
    piece_in = w_in.shape[1] // owners
    piece_out = model_width // owners
    block = (rows_dev, model_width)
    packed_block = (rows_dev + USER_ROWS, model_width)
    reach_block = ((REACH + 1) * rows_dev, model_width)
    chips = lax.axis_size("ctx") // 2
    weight_rows = model_width // (2 * chips)

    user = (segments + 1).astype(f32)
    grad_rows = out_grad[0]
    requests, slot = call(
        lambda *refs: route_body(table_dev, *refs),
        [((owners, capacity), jnp.int32), ((2 * rows_dev, 1), jnp.int32)],
        item_ids.reshape(2 * rows_dev, 1),
    )
    asked = lax.all_to_all(requests, "dp", split_axis=0, concat_axis=0, tiled=True).reshape(1, slots)
    (found,) = call(gather_body, [((slots, model_width), bf16)], asked, touched_rows)
    fetched = lax.all_to_all(
        found.reshape(owners, capacity, model_width), "dp", split_axis=0, concat_axis=0, tiled=True
    ).reshape(slots, model_width)
    inputs, packed = call(
        embed_body, [(block, bf16), (packed_block, bf16)], slot, fetched, user
    )
    halos = [passed_along(packed, "ctx", offset) for offset in range(REACH, 0, -1)]
    projected, gates, values, queries, keys, mixed_grad = call(
        project_body,
        [
            ((rows_dev, 4 * model_width), f32), (block, bf16), (block, bf16),
            (packed_block, bf16), (block, bf16), (block, f32),
        ],
        packed, w_in, w_out, grad_rows, user,
        flops=400_000_000, moved=6_000_000,
    )
    later_queries = [passed_along(queries, "ctx", -offset) for offset in range(1, REACH + 1)]
    layer_out, mixed, gate_grad, att_grad, all_keys, all_values, key_user = call(
        forward_body,
        [
            (block, bf16), (block, bf16), (block, f32), (block, bf16),
            (reach_block, bf16), (reach_block, bf16), ((1, (REACH + 1) * rows_dev), f32),
        ],
        *halos, values, keys, queries, gates, inputs, mixed_grad, w_in, w_out, user,
        flops=1_000_000_000, moved=8_000_000,
    )
    later_grads = [passed_along(att_grad, "ctx", -offset) for offset in range(1, REACH + 1)]
    early_block = (X_CHIPS, chips, weight_rows, 3 * model_width // X_CHIPS)
    gate_query, early_kept, early_sent = call(
        lambda *refs: query_body(piece_in, piece_out, *refs),
        [((rows_dev, 2 * model_width), bf16), (early_block, bf16), (early_block, bf16)],
        core, queries, all_keys, all_values, att_grad, gate_grad, projected, user, key_user,
        packed, mixed, grad_rows,
        flops=1_000_000_000, moved=8_000_000,
    )
    early = pair_sum(early_kept, early_sent)
    value_key, outgoing = call(
        key_body,
        [((rows_dev, 2 * model_width), bf16), ((slots, model_width), bf16)],
        queries, *later_queries, att_grad, *later_grads, keys, values, projected, gate_query,
        w_in, inputs, grad_rows, slot, user,
        flops=1_000_000_000, moved=8_000_000,
    )
    arrived = lax.all_to_all(
        outgoing.reshape(owners, capacity, model_width), "dp", split_axis=0, concat_axis=0, tiled=True
    ).reshape(slots, model_width)
    late_block = (X_CHIPS, chips, weight_rows, 2 * model_width // X_CHIPS)
    late_kept, late_sent = call(
        lambda *refs: late_weights_body(piece_in, *refs),
        [(late_block, bf16), (late_block, bf16)],
        core, packed, value_key,
        flops=400_000_000, moved=3_000_000,
    )
    late = pair_sum(late_kept, late_sent)
    w_in_grad, w_out_grad = reduce_weights(early, late, owners)
    table_block = (chips, model_width // (2 * chips), table_dev)
    table_kept, table_sent = call(
        table_body, [(table_block, bf16), (table_block, bf16)], core, asked, arrived
    )
    table_sum = pair_sum(table_kept, table_sent)
    table_grad = total_of(spread(table_sum, "ctx", chips_along_y())).T
    return (layer_out[None], table_grad, w_in_grad, w_out_grad)


def solution(mesh):
    return jax.shard_map(
        local,
        mesh=mesh,
        in_specs=(
            P(None, "dp", "ctx"),
            P("dp", "ctx"),
            P("dp", None),
            P(),
            P(),
            P("dp", "ctx", None),
        ),
        out_specs=(P("dp", "ctx", None), P("dp", "ctx"), P("ctx", "dp"), P("ctx", "dp")),
        check_vma=False,
    )
```

time: 759 us -> 246 us (0.32)
  waiting for transfers between devices: 555 us -> 94 us
  local copies, waits for them, and re-layouts: 46.2 us -> 7.28 us
  matrix products: 21.6 us -> 0 us
  Pallas kernels: 0 us -> 19.8 us
  blocking collectives: 22.1 us -> 41.4 us
  other arithmetic: 24.6 us -> 5.99 us
  between operations: 14.6 us -> 1.13 us
    unnamed x8 -> x0, waiting for transfers between devices: 476 us -> none
    all_to_all x2 -> x5, waiting for transfers between devices: 31.5 us -> 65.2 us  [the longest x1 25.2 us: local(): lax.all_to_all(found.reshape(owners, capacity, model_width), 'dp', split_...]
    reduce_scatter x2 -> x0, waiting for transfers between devices: 30 us -> none  [the longest x1 30 us: local(): lax.psum_scatter(w_in_part.astype(jnp.bfloat16), 'ctx', scatter_dimension...]
    ppermute x20 -> x12, starting transfers between devices: 59.5 us -> 30.2 us  [passed_along(): return lax.ppermute(block, axis, route)]
    ppermute x0 -> x6, starting transfers between devices: none -> 22.5 us  [the longest x3 11.7 us: pair_sum(): got = lax.ppermute(sent, 'ctx', [(i, i ^ 1) for i in range(devices)])]
    dot_general x12 -> x0, matrix products: 21.6 us -> none  [the longest x1 3.67 us: local(): jnp.einsum('qhd,khd->hqk', query_heads, key_heads, preferred_element_type...]
    pallas_call x0 -> x9, Pallas kernels: none -> 19.8 us  [call(): pl.pallas_call(body, out_shape=[jax.ShapeDtypeStruct(shape, kind) for sha...]
    all_to_all x0 -> x1, blocking collectives: none -> 19.3 us  [spread(): lax.all_to_all(block, axis, split_axis=0, concat_axis=0, tiled=True, axis...]
  transfers between devices with their start and end apart: 27 -> 23, of which waited for: 12 -> 13; matrix products, arithmetic and copies ran while one was open for 6% -> 3% of each run, Pallas kernels for 0% -> 3%
where the time goes in v2:
time: 246 us; the launch traced here: 244 us
  waiting for transfers between devices  94 us (38%)
  starting transfers between devices  74 us (30%)
  blocking collectives  41.4 us (17%)
  Pallas kernels  19.8 us (8%)
  local copies, waits for them, and re-layouts  7.28 us (3%)
  other arithmetic  5.99 us (2%)
    ppermute x12, starting transfers between devices, passed_along(): return lax.ppermute(block, axis, route)  30.2 us
    all_to_all x1, waiting for transfers between devices, local(): lax.all_to_all(found.reshape(owners, capacity, model_width), 'dp', split_...  25.2 us
    all_to_all x1, waiting for transfers between devices, local(): lax.all_to_all(outgoing.reshape(owners, capacity, model_width), 'dp', spl...  24.6 us
    ppermute x12, waiting for transfers between devices, passed_along(): return lax.ppermute(block, axis, route)  23.1 us
    all_to_all x1, blocking collectives, local(): lax.all_to_all(requests, 'dp', split_axis=0, concat_axis=0, tiled=True)  22.1 us
    pallas_call x9, Pallas kernels, call(): pl.pallas_call(body, out_shape=[jax.ShapeDtypeStruct(shape, kind) for sha...  19.8 us
    all_to_all x1, blocking collectives, spread(): lax.all_to_all(block, axis, split_axis=0, concat_axis=0, tiled=True, axis...  19.3 us
    all_to_all x3, waiting for transfers between devices, spread(): lax.all_to_all(block, axis, split_axis=0, concat_axis=0, tiled=True, axis...  15.3 us
  transfers between devices with their start and end apart: 23, of which 13 were waited for; matrix products, arithmetic and copies ran while one was open for 3% of the time, Pallas kernels for 3%

profile of v2, /device:TPU:1, one launch (start us, length us, event | category | flops | bytes accessed | tf_op | source)
XLA Modules:
  0.0 243.5 jit_solution(16812645642877022967)
XLA Ops:
  2.0 22.1 %all_to_all.39 = s32[32,1,32]{2,1,0:T(1,128)S(1)} all-to-all(s32[32,1,32]{2,1,0:T(1,128)S(1)} %bitcast.31), channel_id=1, replica_groups=mesh['dp'=32,'ctx'=16] {'dp'}, dimensions={0} | all-to-all | bytes 8192 | tf_op jit(solution)/shard_map/all_to_all | solution.py:404
  28.2 4.1 %all-to-all-start.1 = ((bf16[32,32,512]{2,1,0:T(8,128)(2,1)}), bf16[32,32,512]{2,1,0:T(8,128)(2,1)S(1)}, u32[]{:S(2)}, u32[]{:S(2)}) async-start(bf16[32,32,512]{2,1,0:T(8,128)(2,1)} %bitcast.27), calls=%async_computation.1 | async-start | bytes 2097152 | tf_op jit(solution)/shard_map/all_to_all | solution.py:406
  32.3 25.2 %all-to-all-done.1 = bf16[32,32,512]{2,1,0:T(8,128)(2,1)S(1)} async-done(((bf16[32,32,512]{2,1,0:T(8,128)(2,1)}), bf16[32,32,512]{2,1,0:T(8,128)(2,1)S(1)}, u32[]{:S(2)}, u32[]{:S(2)}) %all-to-all-start.1) | async-done | bytes 1048608 | tf_op jit(solution)/shard_map/all_to_all | solution.py:406
  58.7 4.2 %collective-permute-start = (bf16[144,512]{1,0:T(8,128)(2,1)}, bf16[144,512]{1,0:T(8,128)(2,1)S(1)}, u32[]{:S(2)}, u32[]{:S(2)}) collective-permute-start(bf16[144,512]{1,0:T(8,128)(2,1)} %get-tuple-element.32.packed_ref.refs_9_.refs_1_), channel_id=1, source_target_pairs={{0,4},{1,5},{2,6},{3,7},{4,8},{5,9},{6,10},{7,11},{8,12},{9,13},{1... | collective-permute-start | bytes 442376 | tf_op jit(solution)/shard_map/ppermute | solution.py:24
  62.9 9.7 %collective-permute-start.1 = (bf16[144,512]{1,0:T(8,128)(2,1)}, bf16[144,512]{1,0:T(8,128)(2,1)S(1)}, u32[]{:S(2)}, u32[]{:S(2)}) collective-permute-start(bf16[144,512]{1,0:T(8,128)(2,1)} %get-tuple-element.32.packed_ref.refs_9_.refs_1_), channel_id=1, source_target_pairs={{0,3},{1,4},{2,5},{3,6},{4,7},{5,8},{6,9},{7,10},{8,11},{9,12},{10... | collective-permute-start | bytes 442376 | tf_op jit(solution)/shard_map/ppermute | solution.py:24
  72.6 2.3 collective-permute-start.2
  80.7 3.1 %shard_map.97 = (bf16[128,512]{1,0:T(8,128)(2,1)}, bf16[128,512]{1,0:T(8,128)(2,1)S(1)}, f32[128,512]{1,0:T(8,128)S(1)}, bf16[128,512]{1,0:T(8,128)(2,1)S(1)}, b...) custom-call(bf16[144,512]{1,0:T(8,128)(2,1)S(1)} %collective-permute-done.halo4_ref, ...), custom_call_target="tpu_custom_call" | custom-call | flops 1000000000 | bytes 8000000 | tf_op jit(solution)/shard_map/pallas_call | solution.py:87
  83.8 5.1 %shard_map.98 = (bf16[128,1024]{1,0:T(8,128)(2,1)S(1)}, bf16[4,8,32,384]{3,2,1,0:T(8,128)(2,1)S(1)}, bf16[4,8,32,384]{3,2,1,0:T(8,128)(2,1)}) custom-call(s32[1]{0:T(128)} %bitcast.7.refs_0_.core_ref, bf16[144,512]{1,0:T(8,128)(2,1)S(1)} %get-tuple-element.35.queries_ref.refs_1_.query0_ref, bf16[640,512]{1,0:T(8,128)(2,1)S(1)} %get-tuple-element.42.refs_2_, ...), custom_call_target="tpu_custom_call" | custom-call | flops 1000000000 | bytes 8000000 | tf_op jit(solution)/shard_map/pallas_call | solution.py:87
  88.9 2.2 collective-permute-start.13
  91.1 2.1 collective-permute-start.4
  99.6 2.1 collective-permute-done.5.query2_ref
  103.1 5.6 %collective-permute-done.6.query3_ref = bf16[144,512]{1,0:T(8,128)(2,1)S(1)} collective-permute-done((bf16[144,512]{1,0:T(8,128)(2,1)S(1)}, bf16[144,512]{1,0:T(8,128)(2,1)S(1)}, u32[]{:S(2)}, u32[]{:S(2)}) %collective-permute-start.6) | collective-permute-done | bytes 147488 | tf_op jit(solution)/shard_map/ppermute | solution.py:24
  110.6 5.6 %collective-permute-done.7.query4_ref = bf16[144,512]{1,0:T(8,128)(2,1)S(1)} collective-permute-done((bf16[144,512]{1,0:T(8,128)(2,1)S(1)}, bf16[144,512]{1,0:T(8,128)(2,1)S(1)}, u32[]{:S(2)}, u32[]{:S(2)}) %collective-permute-start.7) | collective-permute-done | bytes 147488 | tf_op jit(solution)/shard_map/ppermute | solution.py:24
  117.7 4.6 %collective-permute-done.10.grad3_ref = bf16[128,512]{1,0:T(8,128)(2,1)S(1)} collective-permute-done((bf16[128,512]{1,0:T(8,128)(2,1)S(1)}, bf16[128,512]{1,0:T(8,128)(2,1)S(1)}, u32[]{:S(2)}, u32[]{:S(2)}) %collective-permute-start.10) | collective-permute-done | bytes 131104 | tf_op jit(solution)/shard_map/ppermute | solution.py:24
  122.3 2.7 %collective-permute-done.11.grad4_ref = bf16[128,512]{1,0:T(8,128)(2,1)S(1)} collective-permute-done((bf16[128,512]{1,0:T(8,128)(2,1)S(1)}, bf16[128,512]{1,0:T(8,128)(2,1)S(1)}, u32[]{:S(2)}, u32[]{:S(2)}) %collective-permute-start.11) | collective-permute-done | bytes 131104 | tf_op jit(solution)/shard_map/ppermute | solution.py:24
  126.1 4.9 %shard_map.99 = (bf16[128,1024]{1,0:T(8,128)(2,1)S(1)}, bf16[1024,512]{1,0:T(8,128)(2,1)}) custom-call(bf16[144,512]{1,0:T(8,128)(2,1)S(1)} %get-tuple-element.35.queries_ref.refs_1_.query0_ref, bf16[144,512]{1,0:T(8,128)(2,1)S(1)} %collective-permute-done.4.query1_ref, bf16[144,512]{1,0:T(8,128)(2,1)S(1)} %collective-permute-done.5.query2_ref, ...), custom_call_target="tpu_custom_call" | custom-call | flops 1000000000 | bytes 8000000 | tf_op jit(solution)/shard_map/pallas_call | solution.py:87
  132.9 3.3 %collective-permute-start.14 = (bf16[4,8,32,256]{3,2,1,0:T(8,128)(2,1)S(1)}, bf16[4,8,32,256]{3,2,1,0:T(8,128)(2,1)}, u32[]{:S(2)}, u32[]{:S(2)}) collective-permute-start(bf16[4,8,32,256]{3,2,1,0:T(8,128)(2,1)S(1)} %get-tuple-element.55), channel_id=1, source_target_pairs={{0,1},{1,0},{2,3},{3,2},{4,5},{5,4},{6,7},{7,6},{8,9},{9,8},{10,11... | collective-permute-start | bytes 1572872 | tf_op jit(solution)/shard_map/ppermute | solution.py:334
  136.3 2.2 add_convert_fusion
  138.5 3.9 %all-to-all-start.4 = ((bf16[4,8,32,384]{3,2,1,0:T(8,128)(2,1)}), bf16[4,8,32,384]{3,2,1,0:T(8,128)(2,1)S(1)}, u32[]{:S(2)}, u32[]{:S(2)}) async-start(bf16[4,8,32,384]{3,2,1,0:T(8,128)(2,1)} %add_convert_fusion), calls=%async_computation.4 | async-start | bytes 1572864 | tf_op jit(solution)/shard_map/all_to_all | solution.py:344
  143.7 3.4 %collective-permute-start.15 = (bf16[8,32,256]{2,1,0:T(8,128)(2,1)S(1)}, bf16[8,32,256]{2,1,0:T(8,128)(2,1)S(1)}, u32[]{:S(2)}, u32[]{:S(2)}) collective-permute-start(bf16[8,32,256]{2,1,0:T(8,128)(2,1)S(1)} %get-tuple-element.80), channel_id=1, source_target_pairs={{0,16},{16,32},{32,48},{48,0},{64,80},{80,96},{96,112},{112,64},{1... | collective-permute-start | bytes 393224 | tf_op jit(solution)/shard_map/ppermute | solution.py:360
  147.1 4.3 %collective-permute-start.16 = (bf16[8,32,256]{2,1,0:T(8,128)(2,1)S(1)}, bf16[8,32,256]{2,1,0:T(8,128)(2,1)S(1)}, u32[]{:S(2)}, u32[]{:S(2)}) collective-permute-start(bf16[8,32,256]{2,1,0:T(8,128)(2,1)S(1)} %get-tuple-element.82), channel_id=1, source_target_pairs={{0,32},{16,48},{32,0},{48,16},{64,96},{80,112},{96,64},{112,80},{1... | collective-permute-start | bytes 393224 | tf_op jit(solution)/shard_map/ppermute | solution.py:360
  151.4 3.1 %collective-permute-start.17 = (bf16[8,32,256]{2,1,0:T(8,128)(2,1)S(1)}, bf16[8,32,256]{2,1,0:T(8,128)(2,1)S(1)}, u32[]{:S(2)}, u32[]{:S(2)}) collective-permute-start(bf16[8,32,256]{2,1,0:T(8,128)(2,1)S(1)} %get-tuple-element.81), channel_id=1, source_target_pairs={{0,48},{16,0},{32,16},{48,32},{64,112},{80,64},{96,80},{112,96},{1... | collective-permute-start | bytes 393224 | tf_op jit(solution)/shard_map/ppermute | solution.py:360
  154.5 2.6 %collective-permute-done.15 = bf16[8,32,256]{2,1,0:T(8,128)(2,1)S(1)} collective-permute-done((bf16[8,32,256]{2,1,0:T(8,128)(2,1)S(1)}, bf16[8,32,256]{2,1,0:T(8,128)(2,1)S(1)}, u32[]{:S(2)}, u32[]{:S(2)}) %collective-permute-start.15) | collective-permute-done | bytes 131104 | tf_op jit(solution)/shard_map/ppermute | solution.py:360
  157.1 3.1 %collective-permute-done.16 = bf16[8,32,256]{2,1,0:T(8,128)(2,1)S(1)} collective-permute-done((bf16[8,32,256]{2,1,0:T(8,128)(2,1)S(1)}, bf16[8,32,256]{2,1,0:T(8,128)(2,1)S(1)}, u32[]{:S(2)}, u32[]{:S(2)}) %collective-permute-start.16) | collective-permute-done | bytes 131104 | tf_op jit(solution)/shard_map/ppermute | solution.py:360
  160.5 19.3 %all_to_all.40 = bf16[8,32,640]{2,1,0:T(8,128)(2,1)S(1)} all-to-all(bf16[8,32,640]{2,1,0:T(8,128)(2,1)S(1)} %pad_maximum_fusion), channel_id=1, replica_groups={{0,2,4,6,8,10,12,14},{1,3,5,7,9,11,13,15},{16,18,20,22,24,26,28,30},{17..., dimensions={0} | all-to-all | bytes 655360 | tf_op jit(solution)/shard_map/all_to_all | solution.py:344
  179.8 6.1 %all-to-all-start.2 = ((bf16[32,32,512]{2,1,0:T(8,128)(2,1)}), bf16[32,32,512]{2,1,0:T(8,128)(2,1)S(1)}, u32[]{:S(2)}, u32[]{:S(2)}) async-start(bf16[32,32,512]{2,1,0:T(8,128)(2,1)} %bitcast.8), calls=%async_computation.2 | async-start | bytes 2097152 | tf_op jit(solution)/shard_map/all_to_all | solution.py:449
  185.9 24.6 %all-to-all-done.2 = bf16[32,32,512]{2,1,0:T(8,128)(2,1)S(1)} async-done(((bf16[32,32,512]{2,1,0:T(8,128)(2,1)}), bf16[32,32,512]{2,1,0:T(8,128)(2,1)S(1)}, u32[]{:S(2)}, u32[]{:S(2)}) %all-to-all-start.2) | async-done | bytes 1048608 | tf_op jit(solution)/shard_map/all_to_all | solution.py:449
  211.4 6.2 %collective-permute-start.12 = (bf16[8,32,512]{2,1,0:T(8,128)(2,1)S(1)}, bf16[8,32,512]{2,1,0:T(8,128)(2,1)S(1)}, u32[]{:S(2)}, u32[]{:S(2)}) collective-permute-start(bf16[8,32,512]{2,1,0:T(8,128)(2,1)S(1)} %get-tuple-element.50), channel_id=1, source_target_pairs={{0,1},{1,0},{2,3},{3,2},{4,5},{5,4},{6,7},{7,6},{8,9},{9,8},{10,11... | collective-permute-start | bytes 786440 | tf_op jit(solution)/shard_map/ppermute | solution.py:334
  218.7 3.8 %all-to-all-start.6 = ((bf16[8,32,80]{2,1,0:T(8,128)(2,1)}), bf16[8,32,80]{2,1,0:T(8,128)(2,1)S(1)}, u32[]{:S(2)}, u32[]{:S(2)}) async-start(bf16[8,32,80]{2,1,0:T(8,128)(2,1)} %copy.40), calls=%async_computation.6 | async-start | bytes 131072 | tf_op jit(solution)/shard_map/all_to_all | solution.py:344
  223.3 6.4 %all-to-all-done.6 = bf16[8,32,80]{2,1,0:T(8,128)(2,1)S(1)} async-done(((bf16[8,32,80]{2,1,0:T(8,128)(2,1)}), bf16[8,32,80]{2,1,0:T(8,128)(2,1)S(1)}, u32[]{:S(2)}, u32[]{:S(2)}) %all-to-all-start.6) | async-done | bytes 40992 | tf_op jit(solution)/shard_map/all_to_all | solution.py:344
  229.7 3.4 %all-to-all-start.3 = ((bf16[8,32,512]{2,1,0:T(8,128)(2,1)}), bf16[8,32,512]{2,1,0:T(8,128)(2,1)S(1)}, u32[]{:S(2)}, u32[]{:S(2)}) async-start(bf16[8,32,512]{2,1,0:T(8,128)(2,1)} %add_convert_fusion.2), calls=%async_computation.3 | async-start | bytes 524288 | tf_op jit(solution)/shard_map/all_to_all | solution.py:344
  233.9 9.0 %all-to-all-done.3 = bf16[8,32,512]{2,1,0:T(8,128)(2,1)S(1)} async-done(((bf16[8,32,512]{2,1,0:T(8,128)(2,1)}), bf16[8,32,512]{2,1,0:T(8,128)(2,1)S(1)}, u32[]{:S(2)}, u32[]{:S(2)}) %all-to-all-start.3) | async-done | bytes 262176 | tf_op jit(solution)/shard_map/all_to_all | solution.py:344
  (65 shorter events, 32.1 us)
Async XLA Ops:
  25.4 1.0 copy-start.4
  26.5 5.8 %copy-start.7 = (s32[1,128]{1,0:T(1,128)S(1)}, s32[1,128]{1,0:T(1,128)}, u32[]{:S(2)}) copy-start(s32[1,128]{1,0:T(1,128)} %param.7) | copy-start | bytes 1540
  27.2 1.0 copy-start.1
  28.2 48.8 %copy-start = (bf16[512,2048]{1,0:T(8,128)(2,1)S(1)}, bf16[512,2048]{1,0:T(8,128)(2,1)}, u32[]{:S(2)}) copy-start(bf16[512,2048]{1,0:T(8,128)(2,1)} %w_in_ref.5) | copy-start | bytes 6291460
  28.2 48.8 %copy-start.5 = (bf16[1,128,512]{2,1,0:T(8,128)(2,1)S(1)}, bf16[1,128,512]{2,1,0:T(8,128)(2,1)}, u32[]{:S(2)}) copy-start(bf16[1,128,512]{2,1,0:T(8,128)(2,1)} %param.11) | copy-start | bytes 393220
  28.2 29.3 %all-to-all-start.1 = ((bf16[32,32,512]{2,1,0:T(8,128)(2,1)}), bf16[32,32,512]{2,1,0:T(8,128)(2,1)S(1)}, u32[]{:S(2)}, u32[]{:S(2)}) async-start(bf16[32,32,512]{2,1,0:T(8,128)(2,1)} %bitcast.27), calls=%async_computation.1 | async-start | bytes 2097152 | tf_op jit(solution)/shard_map/all_to_all | solution.py:406
  58.7 20.9 %collective-permute-start = (bf16[144,512]{1,0:T(8,128)(2,1)}, bf16[144,512]{1,0:T(8,128)(2,1)S(1)}, u32[]{:S(2)}, u32[]{:S(2)}) collective-permute-start(bf16[144,512]{1,0:T(8,128)(2,1)} %get-tuple-element.32.packed_ref.refs_9_.refs_1_), channel_id=1, source_target_pairs={{0,4},{1,5},{2,6},{3,7},{4,8},{5,9},{6,10},{7,11},{8,12},{9,13},{1... | collective-permute-start | bytes 442376 | tf_op jit(solution)/shard_map/ppermute | solution.py:24
  62.9 16.7 %collective-permute-start.1 = (bf16[144,512]{1,0:T(8,128)(2,1)}, bf16[144,512]{1,0:T(8,128)(2,1)S(1)}, u32[]{:S(2)}, u32[]{:S(2)}) collective-permute-start(bf16[144,512]{1,0:T(8,128)(2,1)} %get-tuple-element.32.packed_ref.refs_9_.refs_1_), channel_id=1, source_target_pairs={{0,3},{1,4},{2,5},{3,6},{4,7},{5,8},{6,9},{7,10},{8,11},{9,12},{10... | collective-permute-start | bytes 442376 | tf_op jit(solution)/shard_map/ppermute | solution.py:24
  72.6 7.0 %collective-permute-start.2 = (bf16[144,512]{1,0:T(8,128)(2,1)}, bf16[144,512]{1,0:T(8,128)(2,1)S(1)}, u32[]{:S(2)}, u32[]{:S(2)}) collective-permute-start(bf16[144,512]{1,0:T(8,128)(2,1)} %get-tuple-element.32.packed_ref.refs_9_.refs_1_), channel_id=1, source_target_pairs={{0,2},{1,3},{2,4},{3,5},{4,6},{5,7},{6,8},{7,9},{8,10},{9,11},{10,... | collective-permute-start | bytes 442376 | tf_op jit(solution)/shard_map/ppermute | solution.py:24
  74.9 4.7 %collective-permute-start.3 = (bf16[144,512]{1,0:T(8,128)(2,1)}, bf16[144,512]{1,0:T(8,128)(2,1)S(1)}, u32[]{:S(2)}, u32[]{:S(2)}) collective-permute-start(bf16[144,512]{1,0:T(8,128)(2,1)} %get-tuple-element.32.packed_ref.refs_9_.refs_1_), channel_id=1, source_target_pairs={{0,1},{1,2},{2,3},{3,4},{4,5},{5,6},{6,7},{7,8},{8,9},{9,10},{10,1... | collective-permute-start | bytes 442376 | tf_op jit(solution)/shard_map/ppermute | solution.py:24
  77.0 1.0 copy-start.2
  79.7 1.0 copy-start.3
  88.9 47.4 %collective-permute-start.13 = (bf16[4,8,32,384]{3,2,1,0:T(8,128)(2,1)}, bf16[4,8,32,384]{3,2,1,0:T(8,128)(2,1)}, u32[]{:S(2)}, u32[]{:S(2)}) collective-permute-start(bf16[4,8,32,384]{3,2,1,0:T(8,128)(2,1)} %get-tuple-element.52), channel_id=1, source_target_pairs={{0,1},{1,0},{2,3},{3,2},{4,5},{5,4},{6,7},{7,6},{8,9},{9,8},{10,11... | collective-permute-start | bytes 2359304 | tf_op jit(solution)/shard_map/ppermute | solution.py:334
  91.1 7.2 %collective-permute-start.4 = (bf16[144,512]{1,0:T(8,128)(2,1)S(1)}, bf16[144,512]{1,0:T(8,128)(2,1)S(1)}, u32[]{:S(2)}, u32[]{:S(2)}) collective-permute-start(bf16[144,512]{1,0:T(8,128)(2,1)S(1)} %get-tuple-element.35.queries_ref.refs_1_.query0_ref), channel_id=1, source_target_pairs={{1,0},{2,1},{3,2},{4,3},{5,4},{6,5},{7,6},{8,7},{9,8},{10,9},{11,1... | collective-permute-start | bytes 442376 | tf_op jit(solution)/shard_map/ppermute | solution.py:24
  93.2 8.6 %collective-permute-start.5 = (bf16[144,512]{1,0:T(8,128)(2,1)S(1)}, bf16[144,512]{1,0:T(8,128)(2,1)S(1)}, u32[]{:S(2)}, u32[]{:S(2)}) collective-permute-start(bf16[144,512]{1,0:T(8,128)(2,1)S(1)} %get-tuple-element.35.queries_ref.refs_1_.query0_ref), channel_id=1, source_target_pairs={{2,0},{3,1},{4,2},{5,3},{6,4},{7,5},{8,6},{9,7},{10,8},{11,9},{12,... | collective-permute-start | bytes 442376 | tf_op jit(solution)/shard_map/ppermute | solution.py:24
  94.5 14.2 %collective-permute-start.6 = (bf16[144,512]{1,0:T(8,128)(2,1)S(1)}, bf16[144,512]{1,0:T(8,128)(2,1)S(1)}, u32[]{:S(2)}, u32[]{:S(2)}) collective-permute-start(bf16[144,512]{1,0:T(8,128)(2,1)S(1)} %get-tuple-element.35.queries_ref.refs_1_.query0_ref), channel_id=1, source_target_pairs={{3,0},{4,1},{5,2},{6,3},{7,4},{8,5},{9,6},{10,7},{11,8},{12,9},{13... | collective-permute-start | bytes 442376 | tf_op jit(solution)/shard_map/ppermute | solution.py:24
  95.8 20.4 %collective-permute-start.7 = (bf16[144,512]{1,0:T(8,128)(2,1)S(1)}, bf16[144,512]{1,0:T(8,128)(2,1)S(1)}, u32[]{:S(2)}, u32[]{:S(2)}) collective-permute-start(bf16[144,512]{1,0:T(8,128)(2,1)S(1)} %get-tuple-element.35.queries_ref.refs_1_.query0_ref), channel_id=1, source_target_pairs={{4,0},{5,1},{6,2},{7,3},{8,4},{9,5},{10,6},{11,7},{12,8},{13,9},{1... | collective-permute-start | bytes 442376 | tf_op jit(solution)/shard_map/ppermute | solution.py:24
  98.4 23.9 %collective-permute-start.10 = (bf16[128,512]{1,0:T(8,128)(2,1)S(1)}, bf16[128,512]{1,0:T(8,128)(2,1)S(1)}, u32[]{:S(2)}, u32[]{:S(2)}) collective-permute-start(bf16[128,512]{1,0:T(8,128)(2,1)S(1)} %get-tuple-element.40.refs_4_.grad0_ref), channel_id=1, source_target_pairs={{3,0},{4,1},{5,2},{6,3},{7,4},{8,5},{9,6},{10,7},{11,8},{12,9},{13... | collective-permute-start | bytes 393224 | tf_op jit(solution)/shard_map/ppermute | solution.py:24
  101.8 23.2 %collective-permute-start.11 = (bf16[128,512]{1,0:T(8,128)(2,1)S(1)}, bf16[128,512]{1,0:T(8,128)(2,1)S(1)}, u32[]{:S(2)}, u32[]{:S(2)}) collective-permute-start(bf16[128,512]{1,0:T(8,128)(2,1)S(1)} %get-tuple-element.40.refs_4_.grad0_ref), channel_id=1, source_target_pairs={{4,0},{5,1},{6,2},{7,3},{8,4},{9,5},{10,6},{11,7},{12,8},{13,9},{1... | collective-permute-start | bytes 393224 | tf_op jit(solution)/shard_map/ppermute | solution.py:24
  108.7 16.3 %collective-permute-start.8 = (bf16[128,512]{1,0:T(8,128)(2,1)S(1)}, bf16[128,512]{1,0:T(8,128)(2,1)S(1)}, u32[]{:S(2)}, u32[]{:S(2)}) collective-permute-start(bf16[128,512]{1,0:T(8,128)(2,1)S(1)} %get-tuple-element.40.refs_4_.grad0_ref), channel_id=1, source_target_pairs={{1,0},{2,1},{3,2},{4,3},{5,4},{6,5},{7,6},{8,7},{9,8},{10,9},{11,1... | collective-permute-start | bytes 393224 | tf_op jit(solution)/shard_map/ppermute | solution.py:24
  116.2 9.9 %collective-permute-start.9 = (bf16[128,512]{1,0:T(8,128)(2,1)S(1)}, bf16[128,512]{1,0:T(8,128)(2,1)S(1)}, u32[]{:S(2)}, u32[]{:S(2)}) collective-permute-start(bf16[128,512]{1,0:T(8,128)(2,1)S(1)} %get-tuple-element.40.refs_4_.grad0_ref), channel_id=1, source_target_pairs={{2,0},{3,1},{4,2},{5,3},{6,4},{7,5},{8,6},{9,7},{10,8},{11,9},{12,... | collective-permute-start | bytes 393224 | tf_op jit(solution)/shard_map/ppermute | solution.py:24
  132.9 9.5 %collective-permute-start.14 = (bf16[4,8,32,256]{3,2,1,0:T(8,128)(2,1)S(1)}, bf16[4,8,32,256]{3,2,1,0:T(8,128)(2,1)}, u32[]{:S(2)}, u32[]{:S(2)}) collective-permute-start(bf16[4,8,32,256]{3,2,1,0:T(8,128)(2,1)S(1)} %get-tuple-element.55), channel_id=1, source_target_pairs={{0,1},{1,0},{2,3},{3,2},{4,5},{5,4},{6,7},{7,6},{8,9},{9,8},{10,11... | collective-permute-start | bytes 1572872 | tf_op jit(solution)/shard_map/ppermute | solution.py:334
  138.5 21.8 %all-to-all-start.4 = ((bf16[4,8,32,384]{3,2,1,0:T(8,128)(2,1)}), bf16[4,8,32,384]{3,2,1,0:T(8,128)(2,1)S(1)}, u32[]{:S(2)}, u32[]{:S(2)}) async-start(bf16[4,8,32,384]{3,2,1,0:T(8,128)(2,1)} %add_convert_fusion), calls=%async_computation.4 | async-start | bytes 1572864 | tf_op jit(solution)/shard_map/all_to_all | solution.py:344
  143.7 13.4 %collective-permute-start.15 = (bf16[8,32,256]{2,1,0:T(8,128)(2,1)S(1)}, bf16[8,32,256]{2,1,0:T(8,128)(2,1)S(1)}, u32[]{:S(2)}, u32[]{:S(2)}) collective-permute-start(bf16[8,32,256]{2,1,0:T(8,128)(2,1)S(1)} %get-tuple-element.80), channel_id=1, source_target_pairs={{0,16},{16,32},{32,48},{48,0},{64,80},{80,96},{96,112},{112,64},{1... | collective-permute-start | bytes 393224 | tf_op jit(solution)/shard_map/ppermute | solution.py:360
  147.1 13.1 %collective-permute-start.16 = (bf16[8,32,256]{2,1,0:T(8,128)(2,1)S(1)}, bf16[8,32,256]{2,1,0:T(8,128)(2,1)S(1)}, u32[]{:S(2)}, u32[]{:S(2)}) collective-permute-start(bf16[8,32,256]{2,1,0:T(8,128)(2,1)S(1)} %get-tuple-element.82), channel_id=1, source_target_pairs={{0,32},{16,48},{32,0},{48,16},{64,96},{80,112},{96,64},{112,80},{1... | collective-permute-start | bytes 393224 | tf_op jit(solution)/shard_map/ppermute | solution.py:360
  151.4 8.8 %collective-permute-start.17 = (bf16[8,32,256]{2,1,0:T(8,128)(2,1)S(1)}, bf16[8,32,256]{2,1,0:T(8,128)(2,1)S(1)}, u32[]{:S(2)}, u32[]{:S(2)}) collective-permute-start(bf16[8,32,256]{2,1,0:T(8,128)(2,1)S(1)} %get-tuple-element.81), channel_id=1, source_target_pairs={{0,48},{16,0},{32,16},{48,32},{64,112},{80,64},{96,80},{112,96},{1... | collective-permute-start | bytes 393224 | tf_op jit(solution)/shard_map/ppermute | solution.py:360
  179.8 30.7 %all-to-all-start.2 = ((bf16[32,32,512]{2,1,0:T(8,128)(2,1)}), bf16[32,32,512]{2,1,0:T(8,128)(2,1)S(1)}, u32[]{:S(2)}, u32[]{:S(2)}) async-start(bf16[32,32,512]{2,1,0:T(8,128)(2,1)} %bitcast.8), calls=%async_computation.2 | async-start | bytes 2097152 | tf_op jit(solution)/shard_map/all_to_all | solution.py:449
  211.4 11.2 %collective-permute-start.12 = (bf16[8,32,512]{2,1,0:T(8,128)(2,1)S(1)}, bf16[8,32,512]{2,1,0:T(8,128)(2,1)S(1)}, u32[]{:S(2)}, u32[]{:S(2)}) collective-permute-start(bf16[8,32,512]{2,1,0:T(8,128)(2,1)S(1)} %get-tuple-element.50), channel_id=1, source_target_pairs={{0,1},{1,0},{2,3},{3,2},{4,5},{5,4},{6,7},{7,6},{8,9},{9,8},{10,11... | collective-permute-start | bytes 786440 | tf_op jit(solution)/shard_map/ppermute | solution.py:334
  218.7 11.0 %all-to-all-start.6 = ((bf16[8,32,80]{2,1,0:T(8,128)(2,1)}), bf16[8,32,80]{2,1,0:T(8,128)(2,1)S(1)}, u32[]{:S(2)}, u32[]{:S(2)}) async-start(bf16[8,32,80]{2,1,0:T(8,128)(2,1)} %copy.40), calls=%async_computation.6 | async-start | bytes 131072 | tf_op jit(solution)/shard_map/all_to_all | solution.py:344
  229.7 13.2 %all-to-all-start.3 = ((bf16[8,32,512]{2,1,0:T(8,128)(2,1)}), bf16[8,32,512]{2,1,0:T(8,128)(2,1)S(1)}, u32[]{:S(2)}, u32[]{:S(2)}) async-start(bf16[8,32,512]{2,1,0:T(8,128)(2,1)} %add_convert_fusion.2), calls=%async_computation.3 | async-start | bytes 524288 | tf_op jit(solution)/shard_map/all_to_all | solution.py:344
  233.1 10.4 %copy-start.6 = (f32[32,80]{1,0:T(8,128)}, f32[32,80]{1,0:T(8,128)S(1)}, u32[]{:S(2)}) copy-start(f32[32,80]{1,0:T(8,128)S(1)} %convert_reduce_fusion.1) | copy-start | bytes 30724

commit v3 on v2

--- a/solution.py
+++ b/solution.py
@@ -87,14 +87,15 @@
     return pl.pallas_call(
         body,
         out_shape=[jax.ShapeDtypeStruct(shape, kind) for shape, kind in outs],
-        compiler_params=pltpu.CompilerParams(vmem_limit_bytes=40 * 1024 * 1024),
+        compiler_params=pltpu.CompilerParams(vmem_limit_bytes=16 * 1024 * 1024),
         cost_estimate=pl.CostEstimate(flops=flops, bytes_accessed=moved, transcendentals=0),
     )(*operands)
 
 
 def route_body(table_dev, ids_ref, request_ref, slot_ref):
     owners, capacity = request_ref.shape
-    ids = ids_ref[...]
+    ids = jnp.concatenate([as_column(ids_ref[h : h + 1, :].astype(f32)) for h in range(2)], axis=0)
+    ids = ids.astype(jnp.int32)
     count = ids.shape[0]
     shift = table_dev.bit_length() - 1
     owner = jnp.right_shift(ids, shift)
@@ -111,9 +112,14 @@
     slot_ref[...] = owner * capacity + rank
 
 
-def gather_body(asked_ref, table_ref, found_ref):
-    slots = asked_ref.shape[1]
-    hits = hot(iota((table_ref.shape[0], slots), 0) == asked_ref[...])
+def gather_body(asked_ref, table_ref, found_ref, asked_row_ref):
+    asked_rows = asked_ref[...]
+    asked_row = jnp.concatenate(
+        [asked_rows[g : g + 1, :] for g in range(asked_rows.shape[0])], axis=1
+    )
+    asked_row_ref[...] = asked_row
+    slots = asked_row.shape[1]
+    hits = hot(iota((table_ref.shape[0], slots), 0) == asked_row)
     found_ref[...] = dot_tn(hits, table_ref[...]).astype(bf16)
 
 
@@ -200,6 +206,15 @@
     att_grad_ref[...] = norm_backward(att_hat, att_inv, mixed_grad * gates).astype(bf16)
 
 
+def halving_place(chip, chips):
+    place = 0
+    while chips > 1:
+        place = 2 * place + chip % 2
+        chip //= 2
+        chips //= 2
+    return place
+
+
 def split_by_core(core, section, terms, kept_ref, sent_ref):
     devices = 2 * kept_ref.shape[1]
     rows = terms.shape[0] // devices
@@ -209,7 +224,7 @@
         for chip in range(devices // 2):
             first = terms[2 * chip * rows : (2 * chip + 1) * rows, x * lanes : (x + 1) * lanes]
             second = terms[(2 * chip + 1) * rows : (2 * chip + 2) * rows, x * lanes : (x + 1) * lanes]
-            place = (x, chip, slice(None), slice(section * lanes, (section + 1) * lanes))
+            place = (x, halving_place(chip, devices // 2), slice(None), slice(section * lanes, (section + 1) * lanes))
             kept_ref[place] = jnp.where(even, first, second).astype(bf16)
             sent_ref[place] = jnp.where(even, second, first).astype(bf16)
 
@@ -227,11 +242,10 @@
 
 
 def query_body(
-    piece_in, piece_out, core_ref, queries_ref, all_keys_ref, all_values_ref, att_grad_ref, gate_grad_ref,
-    projected_ref, user_ref, key_user_ref, packed_ref, mixed_ref, grad_ref,
-    gate_query_ref, kept_ref, sent_ref,
+    queries_ref, all_keys_ref, all_values_ref, att_grad_ref, gate_grad_ref,
+    projected_ref, user_ref, key_user_ref, gate_query_ref,
 ):
-    rows, width = grad_ref.shape
+    rows, width = gate_grad_ref.shape
     score_scale = 1.0 / math.sqrt(DH)
     margin = all_keys_ref.shape[0] - rows
     allowed = window_mask(user_ref[...], key_user_ref[...], margin)
@@ -244,15 +258,10 @@
         score_grad = jnp.where(allowed, prob_grad * silu_slope(scores), 0.0).astype(bf16)
         parts.append(one_pair(dot(score_grad, keys)) * score_scale)
     query_grad = jnp.concatenate(parts, axis=1)
-    core = core_ref[0]
-    normed = packed_ref[:rows, :]
-    gate_part = (gate_grad_ref[...] * silu_slope(projected_ref[:, :width])).astype(bf16)
-    query_part = (query_grad * silu_slope(projected_ref[:, 2 * width : 3 * width])).astype(bf16)
-    gate_query_ref[:, :width] = gate_part
-    gate_query_ref[:, width:] = query_part
-    split_by_core(core, 0, dot_tn(normed, order_by_x(gate_part, piece_in)), kept_ref, sent_ref)
-    split_by_core(core, 1, dot_tn(normed, order_by_x(query_part, piece_in)), kept_ref, sent_ref)
-    split_by_core(core, 2, dot_tn(mixed_ref[...], order_by_x(grad_ref[...], piece_out)), kept_ref, sent_ref)
+    gate_part = gate_grad_ref[...] * silu_slope(projected_ref[:, :width])
+    query_part = query_grad * silu_slope(projected_ref[:, 2 * width : 3 * width])
+    gate_query_ref[:, :width] = gate_part.astype(bf16)
+    gate_query_ref[:, width:] = query_part.astype(bf16)
 
 
 def key_body(
@@ -305,14 +314,21 @@
     outgoing_ref[...] = dot_tn(places, inputs_grad).astype(bf16)
 
 
-def late_weights_body(piece_in, core_ref, packed_ref, value_key_ref, kept_ref, sent_ref):
-    rows = value_key_ref.shape[0]
-    width = value_key_ref.shape[1] // 2
+def weights_body(
+    piece_in, piece_out, core_ref, packed_ref, gate_query_ref, value_key_ref, mixed_ref, grad_ref,
+    kept_ref, sent_ref,
+):
+    rows, width = grad_ref.shape
     core = core_ref[0]
     normed = packed_ref[:rows, :]
-    for section in range(2):
-        part = value_key_ref[:, section * width : (section + 1) * width]
+    parts = (
+        gate_query_ref[:, :width], value_key_ref[:, :width],
+        gate_query_ref[:, width:], value_key_ref[:, width:],
+    )
+    for section, part in enumerate(parts):
         split_by_core(core, section, dot_tn(normed, order_by_x(part, piece_in)), kept_ref, sent_ref)
+    last = dot_tn(mixed_ref[...], order_by_x(grad_ref[...], piece_out))
+    split_by_core(core, len(parts), last, kept_ref, sent_ref)
 
 
 def table_body(core_ref, asked_ref, arrived_ref, kept_ref, sent_ref):
@@ -361,21 +377,33 @@
     return own.astype(bf16)
 
 
-def reduce_weights(early, late, owners):
-    xs = [list(range(first, first + X_CHIPS)) for first in range(0, owners, X_CHIPS)]
+def sum_along_y(block):
+    count = lax.axis_size("ctx")
+    me = lax.axis_index("ctx")
+    distance = 2
+    while block.shape[0] > 1:
+        half = block.shape[0] // 2
+        bit = (me // distance) % 2
+        sent = lax.dynamic_slice_in_dim(block, (1 - bit) * half, half, 0)
+        kept = lax.dynamic_slice_in_dim(block, bit * half, half, 0)
+        got = lax.ppermute(sent, "ctx", [(i, i ^ distance) for i in range(count)])
+        block = (kept.astype(f32) + got.astype(f32)).astype(bf16)
+        distance *= 2
+    return block[0]
+
+
+def weights_to_z(along_y, owners):
+    rows = along_y.shape[0]
+    z_chips = owners // X_CHIPS
+    wide_width = along_y.shape[1] * 4 // 5
+    wide = along_y[:, :wide_width].reshape(rows, z_chips, -1)
+    thin = along_y[:, wide_width:].reshape(rows, z_chips, -1)
+    return jnp.concatenate([wide, thin], axis=2).transpose(1, 0, 2), wide.shape[2]
+
+
+def sum_along_z(send, owners):
     zs = [list(range(first, owners, X_CHIPS)) for first in range(X_CHIPS)]
-    z_chips = owners // X_CHIPS
-    early_x = total_of(spread(early, "dp", xs)).astype(bf16)
-    late_x = sum_along_x(late)
-    both = jnp.concatenate([early_x, late_x], axis=2)
-    along_y = total_of(spread(both, "ctx", chips_along_y())).astype(bf16)
-    rows = along_y.shape[0]
-    gate, query, out, value, key = jnp.split(along_y, 5, axis=1)
-    wide = jnp.concatenate([gate, value, query, key], axis=1).reshape(rows, z_chips, -1)
-    thin = out.reshape(rows, z_chips, -1)
-    send = jnp.concatenate([wide, thin], axis=2).transpose(1, 0, 2)
-    summed = total_of(spread(send, "dp", zs))
-    return (summed[:, : wide.shape[2]], summed[:, wide.shape[2] :])
+    return total_of(spread(send, "dp", zs))
 
 
 def local(item_ids, segments, touched_rows, w_in, w_out, out_grad):
@@ -399,10 +427,12 @@
     requests, slot = call(
         lambda *refs: route_body(table_dev, *refs),
         [((owners, capacity), jnp.int32), ((2 * rows_dev, 1), jnp.int32)],
-        item_ids.reshape(2 * rows_dev, 1),
-    )
-    asked = lax.all_to_all(requests, "dp", split_axis=0, concat_axis=0, tiled=True).reshape(1, slots)
-    (found,) = call(gather_body, [((slots, model_width), bf16)], asked, touched_rows)
+        item_ids.reshape(2, rows_dev),
+    )
+    asked = lax.all_to_all(requests, "dp", split_axis=0, concat_axis=0, tiled=True)
+    found, asked_row = call(
+        gather_body, [((slots, model_width), bf16), ((1, slots), jnp.int32)], asked, touched_rows
+    )
     fetched = lax.all_to_all(
         found.reshape(owners, capacity, model_width), "dp", split_axis=0, concat_axis=0, tiled=True
     ).reshape(slots, model_width)
@@ -417,9 +447,10 @@
             (packed_block, bf16), (block, bf16), (block, f32),
         ],
         packed, w_in, w_out, grad_rows, user,
-        flops=400_000_000, moved=6_000_000,
+        flops=1_500_000_000, moved=6_000_000,
     )
     later_queries = [passed_along(queries, "ctx", -offset) for offset in range(1, REACH + 1)]
+    halos, later_queries = lax.optimization_barrier((halos, later_queries))
     layer_out, mixed, gate_grad, att_grad, all_keys, all_values, key_user = call(
         forward_body,
         [
@@ -427,44 +458,41 @@
             (reach_block, bf16), (reach_block, bf16), ((1, (REACH + 1) * rows_dev), f32),
         ],
         *halos, values, keys, queries, gates, inputs, mixed_grad, w_in, w_out, user,
-        flops=1_000_000_000, moved=8_000_000,
+        flops=4_000_000_000, moved=8_000_000,
     )
     later_grads = [passed_along(att_grad, "ctx", -offset) for offset in range(1, REACH + 1)]
-    early_block = (X_CHIPS, chips, weight_rows, 3 * model_width // X_CHIPS)
-    gate_query, early_kept, early_sent = call(
-        lambda *refs: query_body(piece_in, piece_out, *refs),
-        [((rows_dev, 2 * model_width), bf16), (early_block, bf16), (early_block, bf16)],
-        core, queries, all_keys, all_values, att_grad, gate_grad, projected, user, key_user,
-        packed, mixed, grad_rows,
-        flops=1_000_000_000, moved=8_000_000,
-    )
-    early = pair_sum(early_kept, early_sent)
+    (gate_query,) = call(
+        query_body, [((rows_dev, 2 * model_width), bf16)],
+        queries, all_keys, all_values, att_grad, gate_grad, projected, user, key_user,
+        flops=4_000_000_000, moved=8_000_000,
+    )
     value_key, outgoing = call(
         key_body,
         [((rows_dev, 2 * model_width), bf16), ((slots, model_width), bf16)],
         queries, *later_queries, att_grad, *later_grads, keys, values, projected, gate_query,
         w_in, inputs, grad_rows, slot, user,
-        flops=1_000_000_000, moved=8_000_000,
+        flops=4_000_000_000, moved=8_000_000,
     )
     arrived = lax.all_to_all(
         outgoing.reshape(owners, capacity, model_width), "dp", split_axis=0, concat_axis=0, tiled=True
     ).reshape(slots, model_width)
-    late_block = (X_CHIPS, chips, weight_rows, 2 * model_width // X_CHIPS)
-    late_kept, late_sent = call(
-        lambda *refs: late_weights_body(piece_in, *refs),
-        [(late_block, bf16), (late_block, bf16)],
-        core, packed, value_key,
-        flops=400_000_000, moved=3_000_000,
-    )
-    late = pair_sum(late_kept, late_sent)
-    w_in_grad, w_out_grad = reduce_weights(early, late, owners)
+    weight_block = (X_CHIPS, chips, weight_rows, 5 * model_width // X_CHIPS)
+    weight_kept, weight_sent = call(
+        lambda *refs: weights_body(piece_in, piece_out, *refs),
+        [(weight_block, bf16), (weight_block, bf16)],
+        core, packed, gate_query, value_key, mixed, grad_rows,
+        flops=4_000_000_000, moved=6_000_000,
+    )
+    z_send, wide = weights_to_z(sum_along_y(sum_along_x(pair_sum(weight_kept, weight_sent))), owners)
+    arrived, z_send = lax.optimization_barrier((arrived, z_send))
     table_block = (chips, model_width // (2 * chips), table_dev)
     table_kept, table_sent = call(
-        table_body, [(table_block, bf16), (table_block, bf16)], core, asked, arrived
+        table_body, [(table_block, bf16), (table_block, bf16)], core, asked_row, arrived
     )
     table_sum = pair_sum(table_kept, table_sent)
     table_grad = total_of(spread(table_sum, "ctx", chips_along_y())).T
-    return (layer_out[None], table_grad, w_in_grad, w_out_grad)
+    summed = sum_along_z(z_send, owners)
+    return (layer_out[None], table_grad, summed[:, :wide], summed[:, wide:])
 
 
 def solution(mesh):

time: 246 us -> 230 us (0.935)
  blocking collectives: 41.4 us -> 22.1 us
  starting transfers between devices: 74 us -> 90.4 us
  waiting for transfers between devices: 94 us -> 81.1 us
    all_to_all x1, waiting for transfers between devices: 24.6 us -> 0.01 us  [local(): lax.all_to_all(outgoing.reshape(owners, capacity, model_width), 'dp', spl...]
    all_to_all x1 -> x0, blocking collectives: 19.3 us -> none  [spread(): lax.all_to_all(block, axis, split_axis=0, concat_axis=0, tiled=True, axis...]
    ppermute x0 -> x3, starting transfers between devices: none -> 18.5 us  [sum_along_y(): got = lax.ppermute(sent, 'ctx', [(i, i ^ distance) for i in range(count)])]
    ppermute x3, waiting for transfers between devices: 5.73 us -> 18.4 us  [sum_along_x(): own = own + lax.ppermute(piece, 'dp', route).astype(f32)]
    ppermute x12, waiting for transfers between devices: 23.1 us -> 12.9 us  [passed_along(): return lax.ppermute(block, axis, route)]
    ppermute x0 -> x3, waiting for transfers between devices: none -> 9.72 us  [sum_along_y(): got = lax.ppermute(sent, 'ctx', [(i, i ^ distance) for i in range(count)])]
    ppermute x3 -> x2, starting transfers between devices: 11.7 us -> 6.85 us  [pair_sum(): got = lax.ppermute(sent, 'ctx', [(i, i ^ 1) for i in range(devices)])]
    ppermute x12, starting transfers between devices: 30.2 us -> 33.9 us  [passed_along(): return lax.ppermute(block, axis, route)]
  transfers between devices with their start and end apart: 23 -> 24, of which waited for: 13 -> 12; matrix products, arithmetic and copies ran while one was open for 3% -> 3% of each run, Pallas kernels for 3% -> 1%
where the time goes in v3:
time: 230 us; the launch traced here: 226 us
  starting transfers between devices  90.4 us (39%)
  waiting for transfers between devices  81.1 us (35%)
  blocking collectives  22.1 us (10%)
  Pallas kernels  17.8 us (8%)
  local copies, waits for them, and re-layouts  8.24 us (4%)
  other arithmetic  5.17 us (2%)
    ppermute x12, starting transfers between devices, passed_along(): return lax.ppermute(block, axis, route)  33.9 us
    all_to_all x1, waiting for transfers between devices, local(): lax.all_to_all(found.reshape(owners, capacity, model_width), 'dp', split_...  25.2 us
    all_to_all x1, blocking collectives, local(): lax.all_to_all(requests, 'dp', split_axis=0, concat_axis=0, tiled=True)  22.1 us
    ppermute x3, starting transfers between devices, sum_along_y(): got = lax.ppermute(sent, 'ctx', [(i, i ^ distance) for i in range(count)])  18.5 us
    ppermute x3, waiting for transfers between devices, sum_along_x(): own = own + lax.ppermute(piece, 'dp', route).astype(f32)  18.4 us
    pallas_call x9, Pallas kernels, call(): pl.pallas_call(body, out_shape=[jax.ShapeDtypeStruct(shape, kind) for sha...  17.8 us
    all_to_all x2, waiting for transfers between devices, spread(): lax.all_to_all(block, axis, split_axis=0, concat_axis=0, tiled=True, axis...  14.9 us
    ppermute x12, waiting for transfers between devices, passed_along(): return lax.ppermute(block, axis, route)  12.9 us
  transfers between devices with their start and end apart: 24, of which 12 were waited for; matrix products, arithmetic and copies ran while one was open for 3% of the time, Pallas kernels for 1%

profile of v3, /device:TPU:1, one launch (start us, length us, event | category | flops | bytes accessed | tf_op | source)
XLA Modules:
  0.0 226.1 jit_solution(13480474192274939111)
XLA Ops:
  1.9 22.1 %all_to_all.31 = s32[32,1,32]{2,1,0:T(1,128)S(1)} all-to-all(s32[32,1,32]{2,1,0:T(1,128)S(1)} %bitcast.31), channel_id=1, replica_groups=mesh['dp'=32,'ctx'=16] {'dp'}, dimensions={0} | all-to-all | bytes 8192 | tf_op jit(solution)/shard_map/all_to_all | solution.py:432
  27.0 4.1 %all-to-all-start.1 = ((bf16[32,32,512]{2,1,0:T(8,128)(2,1)}), bf16[32,32,512]{2,1,0:T(8,128)(2,1)S(1)}, u32[]{:S(2)}, u32[]{:S(2)}) async-start(bf16[32,32,512]{2,1,0:T(8,128)(2,1)} %bitcast.4), calls=%async_computation.1 | async-start | bytes 2097152 | tf_op jit(solution)/shard_map/all_to_all | solution.py:436
  31.1 25.2 %all-to-all-done.1 = bf16[32,32,512]{2,1,0:T(8,128)(2,1)S(1)} async-done(((bf16[32,32,512]{2,1,0:T(8,128)(2,1)}), bf16[32,32,512]{2,1,0:T(8,128)(2,1)S(1)}, u32[]{:S(2)}, u32[]{:S(2)}) %all-to-all-start.1) | async-done | bytes 1048608 | tf_op jit(solution)/shard_map/all_to_all | solution.py:436
  60.1 6.0 %collective-permute-start.4 = (bf16[144,512]{1,0:T(8,128)(2,1)S(1)}, bf16[144,512]{1,0:T(8,128)(2,1)S(1)}, u32[]{:S(2)}, u32[]{:S(2)}) collective-permute-start(bf16[144,512]{1,0:T(8,128)(2,1)S(1)} %get-tuple-element.43.queries_ref.query0_ref), channel_id=1, source_target_pairs={{1,0},{2,1},{3,2},{4,3},{5,4},{6,5},{7,6},{8,7},{9,8},{10,9},{11,1... | collective-permute-start | bytes 442376 | tf_op jit(solution)/shard_map/ppermute | solution.py:24
  70.0 6.3 %collective-permute-start = (bf16[144,512]{1,0:T(8,128)(2,1)S(1)}, bf16[144,512]{1,0:T(8,128)(2,1)S(1)}, u32[]{:S(2)}, u32[]{:S(2)}) collective-permute-start(bf16[144,512]{1,0:T(8,128)(2,1)S(1)} %get-tuple-element.42.packed_ref.refs_1_), channel_id=1, source_target_pairs={{0,4},{1,5},{2,6},{3,7},{4,8},{5,9},{6,10},{7,11},{8,12},{9,13},{1... | collective-permute-start | bytes 442376 | tf_op jit(solution)/shard_map/ppermute | solution.py:24
  76.3 6.2 %collective-permute-start.1 = (bf16[144,512]{1,0:T(8,128)(2,1)S(1)}, bf16[144,512]{1,0:T(8,128)(2,1)S(1)}, u32[]{:S(2)}, u32[]{:S(2)}) collective-permute-start(bf16[144,512]{1,0:T(8,128)(2,1)S(1)} %get-tuple-element.42.packed_ref.refs_1_), channel_id=1, source_target_pairs={{0,3},{1,4},{2,5},{3,6},{4,7},{5,8},{6,9},{7,10},{8,11},{9,12},{10... | collective-permute-start | bytes 442376 | tf_op jit(solution)/shard_map/ppermute | solution.py:24
  82.5 3.4 %collective-permute-start.2 = (bf16[144,512]{1,0:T(8,128)(2,1)S(1)}, bf16[144,512]{1,0:T(8,128)(2,1)S(1)}, u32[]{:S(2)}, u32[]{:S(2)}) collective-permute-start(bf16[144,512]{1,0:T(8,128)(2,1)S(1)} %get-tuple-element.42.packed_ref.refs_1_), channel_id=1, source_target_pairs={{0,2},{1,3},{2,4},{3,5},{4,6},{5,7},{6,8},{7,9},{8,10},{9,11},{10,... | collective-permute-start | bytes 442376 | tf_op jit(solution)/shard_map/ppermute | solution.py:24
  85.9 2.2 collective-permute-start.3
  91.9 3.1 %shard_map.97 = (bf16[128,512]{1,0:T(8,128)(2,1)}, bf16[128,512]{1,0:T(8,128)(2,1)S(1)}, f32[128,512]{1,0:T(8,128)S(1)}, bf16[128,512]{1,0:T(8,128)(2,1)S(1)}, b...) custom-call(bf16[144,512]{1,0:T(8,128)(2,1)S(1)} %collective-permute-done.halo4_ref, ...), custom_call_target="tpu_custom_call" | custom-call | flops 4000000000 | bytes 8000000 | tf_op jit(solution)/shard_map/pallas_call | solution.py:87
  101.1 2.1 shard_map.98.gate_query_ref.refs_2_
  103.1 3.4 %collective-permute-done.10.grad3_ref = bf16[128,512]{1,0:T(8,128)(2,1)S(1)} collective-permute-done((bf16[128,512]{1,0:T(8,128)(2,1)S(1)}, bf16[128,512]{1,0:T(8,128)(2,1)S(1)}, u32[]{:S(2)}, u32[]{:S(2)}) %collective-permute-start.10) | collective-permute-done | bytes 131104 | tf_op jit(solution)/shard_map/ppermute | solution.py:24
  106.5 7.3 %collective-permute-done.11.grad4_ref = bf16[128,512]{1,0:T(8,128)(2,1)S(1)} collective-permute-done((bf16[128,512]{1,0:T(8,128)(2,1)S(1)}, bf16[128,512]{1,0:T(8,128)(2,1)S(1)}, u32[]{:S(2)}, u32[]{:S(2)}) %collective-permute-start.11) | collective-permute-done | bytes 131104 | tf_op jit(solution)/shard_map/ppermute | solution.py:24
  113.8 5.0 %shard_map.99 = (bf16[128,1024]{1,0:T(8,128)(2,1)S(1)}, bf16[1024,512]{1,0:T(8,128)(2,1)}) custom-call(bf16[144,512]{1,0:T(8,128)(2,1)S(1)} %get-tuple-element.43.queries_ref.query0_ref, bf16[144,512]{1,0:T(8,128)(2,1)S(1)} %collective-permute-done.4.query1_ref, bf16[144,512]{1,0:T(8,128)(2,1)S(1)} %collective-permute-done.5.query2_ref, ...), custom_call_target="tpu_custom_call" | custom-call | flops 4000000000 | bytes 8000000 | tf_op jit(solution)/shard_map/pallas_call | solution.py:87
  118.8 3.2 %shard_map.100 = (bf16[4,8,32,640]{3,2,1,0:T(8,128)(2,1)S(1)}, bf16[4,8,32,640]{3,2,1,0:T(8,128)(2,1)}) custom-call(s32[1]{0:T(128)} %bitcast.8.refs_0_.core_ref, bf16[144,512]{1,0:T(8,128)(2,1)S(1)} %get-tuple-element.42.packed_ref.refs_1_, bf16[128,1024]{1,0:T(8,128)(2,1)S(1)} %shard_map.98.gate_query_ref.refs_2_, ...), custom_call_target="tpu_custom_call" | custom-call | flops 4000000000 | bytes 6000000 | tf_op jit(solution)/shard_map/pallas_call | solution.py:87
  122.0 2.3 %collective-permute-start.12 = (bf16[4,8,32,640]{3,2,1,0:T(8,128)(2,1)}, bf16[4,8,32,640]{3,2,1,0:T(8,128)(2,1)}, u32[]{:S(2)}, u32[]{:S(2)}) collective-permute-start(bf16[4,8,32,640]{3,2,1,0:T(8,128)(2,1)} %get-tuple-element.69), channel_id=1, source_target_pairs={{0,1},{1,0},{2,3},{3,2},{4,5},{5,4},{6,7},{7,6},{8,9},{9,8},{10,11... | collective-permute-start | bytes 3932168 | tf_op jit(solution)/shard_map/ppermute | solution.py:350
  124.3 5.0 %all-to-all-start.2 = ((bf16[32,32,512]{2,1,0:T(8,128)(2,1)}), bf16[32,32,512]{2,1,0:T(8,128)(2,1)S(1)}, u32[]{:S(2)}, u32[]{:S(2)}) async-start(bf16[32,32,512]{2,1,0:T(8,128)(2,1)} %bitcast.9), calls=%async_computation.2 | async-start | bytes 2097152 | tf_op jit(solution)/shard_map/all_to_all | solution.py:476
  132.3 3.1 %collective-permute-start.13 = (bf16[8,32,640]{2,1,0:T(8,128)(2,1)S(1)}, bf16[8,32,640]{2,1,0:T(8,128)(2,1)S(1)}, u32[]{:S(2)}, u32[]{:S(2)}) collective-permute-start(bf16[8,32,640]{2,1,0:T(8,128)(2,1)S(1)} %get-tuple-element.86), channel_id=1, source_target_pairs={{0,16},{16,32},{32,48},{48,0},{64,80},{80,96},{96,112},{112,64},{1... | collective-permute-start | bytes 983048 | tf_op jit(solution)/shard_map/ppermute | solution.py:376
  135.5 4.3 %collective-permute-start.14 = (bf16[8,32,640]{2,1,0:T(8,128)(2,1)S(1)}, bf16[8,32,640]{2,1,0:T(8,128)(2,1)S(1)}, u32[]{:S(2)}, u32[]{:S(2)}) collective-permute-start(bf16[8,32,640]{2,1,0:T(8,128)(2,1)S(1)} %get-tuple-element.88), channel_id=1, source_target_pairs={{0,32},{16,48},{32,0},{48,16},{64,96},{80,112},{96,64},{112,80},{1... | collective-permute-start | bytes 983048 | tf_op jit(solution)/shard_map/ppermute | solution.py:376
  139.8 3.1 %collective-permute-start.15 = (bf16[8,32,640]{2,1,0:T(8,128)(2,1)S(1)}, bf16[8,32,640]{2,1,0:T(8,128)(2,1)S(1)}, u32[]{:S(2)}, u32[]{:S(2)}) collective-permute-start(bf16[8,32,640]{2,1,0:T(8,128)(2,1)S(1)} %get-tuple-element.87), channel_id=1, source_target_pairs={{0,48},{16,0},{32,16},{48,32},{64,112},{80,64},{96,80},{112,96},{1... | collective-permute-start | bytes 983048 | tf_op jit(solution)/shard_map/ppermute | solution.py:376
  142.9 6.9 %collective-permute-done.13 = bf16[8,32,640]{2,1,0:T(8,128)(2,1)S(1)} collective-permute-done((bf16[8,32,640]{2,1,0:T(8,128)(2,1)S(1)}, bf16[8,32,640]{2,1,0:T(8,128)(2,1)S(1)}, u32[]{:S(2)}, u32[]{:S(2)}) %collective-permute-start.13) | collective-permute-done | bytes 327712 | tf_op jit(solution)/shard_map/ppermute | solution.py:376
  149.8 11.5 %collective-permute-done.14 = bf16[8,32,640]{2,1,0:T(8,128)(2,1)S(1)} collective-permute-done((bf16[8,32,640]{2,1,0:T(8,128)(2,1)S(1)}, bf16[8,32,640]{2,1,0:T(8,128)(2,1)S(1)}, u32[]{:S(2)}, u32[]{:S(2)}) %collective-permute-start.14) | collective-permute-done | bytes 327712 | tf_op jit(solution)/shard_map/ppermute | solution.py:376
  162.5 6.5 %collective-permute-start.16 = (bf16[4,32,640]{2,1,0:T(8,128)(2,1)S(1)}, bf16[4,32,640]{2,1,0:T(8,128)(2,1)S(1)}, u32[]{:S(2)}, u32[]{:S(2)}) collective-permute-start(bf16[4,32,640]{2,1,0:T(8,128)(2,1)S(1)} %constant_dynamic-slice_fusion.2), channel_id=1, source_target_pairs={{0,2},{1,3},{2,0},{3,1},{4,6},{5,7},{6,4},{7,5},{8,10},{9,11},{10,... | collective-permute-start | bytes 491528 | tf_op jit(solution)/shard_map/ppermute | solution.py:389
  169.0 3.2 %collective-permute-done.16 = bf16[4,32,640]{2,1,0:T(8,128)(2,1)S(1)} collective-permute-done((bf16[4,32,640]{2,1,0:T(8,128)(2,1)S(1)}, bf16[4,32,640]{2,1,0:T(8,128)(2,1)S(1)}, u32[]{:S(2)}, u32[]{:S(2)}) %collective-permute-start.16) | collective-permute-done | bytes 163872 | tf_op jit(solution)/shard_map/ppermute | solution.py:389
  172.2 6.9 %collective-permute-start.17 = (bf16[2,32,640]{2,1,0:T(8,128)(2,1)S(1)}, bf16[2,32,640]{2,1,0:T(8,128)(2,1)S(1)}, u32[]{:S(2)}, u32[]{:S(2)}) collective-permute-start(bf16[2,32,640]{2,1,0:T(8,128)(2,1)S(1)} %constant_dynamic-slice_fusion.1), channel_id=1, source_target_pairs={{0,4},{1,5},{2,6},{3,7},{4,0},{5,1},{6,2},{7,3},{8,12},{9,13},{10,... | collective-permute-start | bytes 245768 | tf_op jit(solution)/shard_map/ppermute | solution.py:389
  179.2 2.7 %collective-permute-done.17 = bf16[2,32,640]{2,1,0:T(8,128)(2,1)S(1)} collective-permute-done((bf16[2,32,640]{2,1,0:T(8,128)(2,1)S(1)}, bf16[2,32,640]{2,1,0:T(8,128)(2,1)S(1)}, u32[]{:S(2)}, u32[]{:S(2)}) %collective-permute-start.17) | collective-permute-done | bytes 81952 | tf_op jit(solution)/shard_map/ppermute | solution.py:389
  181.9 5.2 %collective-permute-start.18 = (bf16[1,32,640]{2,1,0:T(8,128)(2,1)S(1)}, bf16[1,32,640]{2,1,0:T(8,128)(2,1)S(1)}, u32[]{:S(2)}, u32[]{:S(2)}) collective-permute-start(bf16[1,32,640]{2,1,0:T(8,128)(2,1)S(1)} %constant_dynamic-slice_fusion), channel_id=1, source_target_pairs={{0,8},{1,9},{2,10},{3,11},{4,12},{5,13},{6,14},{7,15},{8,0},{9,1},... | collective-permute-start | bytes 122888 | tf_op jit(solution)/shard_map/ppermute | solution.py:389
  187.1 3.9 %collective-permute-done.18 = bf16[1,32,640]{2,1,0:T(8,128)(2,1)S(1)} collective-permute-done((bf16[1,32,640]{2,1,0:T(8,128)(2,1)S(1)}, bf16[1,32,640]{2,1,0:T(8,128)(2,1)S(1)}, u32[]{:S(2)}, u32[]{:S(2)}) %collective-permute-start.18) | collective-permute-done | bytes 40992 | tf_op jit(solution)/shard_map/ppermute | solution.py:389
  192.9 4.6 %collective-permute-start.19 = (bf16[8,32,512]{2,1,0:T(8,128)(2,1)S(1)}, bf16[8,32,512]{2,1,0:T(8,128)(2,1)S(1)}, u32[]{:S(2)}, u32[]{:S(2)}) collective-permute-start(bf16[8,32,512]{2,1,0:T(8,128)(2,1)S(1)} %get-tuple-element.72), channel_id=1, source_target_pairs={{0,1},{1,0},{2,3},{3,2},{4,5},{5,4},{6,7},{7,6},{8,9},{9,8},{10,11... | collective-permute-start | bytes 786440 | tf_op jit(solution)/shard_map/ppermute | solution.py:350
  197.5 5.3 %all-to-all-start.4 = ((bf16[8,32,80]{2,1,0:T(8,128)(2,1)}), bf16[8,32,80]{2,1,0:T(8,128)(2,1)S(1)}, u32[]{:S(2)}, u32[]{:S(2)}) async-start(bf16[8,32,80]{2,1,0:T(8,128)(2,1)} %maximum_bitcast_fusion), calls=%async_computation.4 | async-start | bytes 131072 | tf_op jit(solution)/shard_map/all_to_all | solution.py:360
  203.6 6.4 %all-to-all-done.4 = bf16[8,32,80]{2,1,0:T(8,128)(2,1)S(1)} async-done(((bf16[8,32,80]{2,1,0:T(8,128)(2,1)}), bf16[8,32,80]{2,1,0:T(8,128)(2,1)S(1)}, u32[]{:S(2)}, u32[]{:S(2)}) %all-to-all-start.4) | async-done | bytes 40992 | tf_op jit(solution)/shard_map/all_to_all | solution.py:360
  209.9 6.2 %all-to-all-start.3 = ((bf16[8,32,512]{2,1,0:T(8,128)(2,1)}), bf16[8,32,512]{2,1,0:T(8,128)(2,1)S(1)}, u32[]{:S(2)}, u32[]{:S(2)}) async-start(bf16[8,32,512]{2,1,0:T(8,128)(2,1)} %add_convert_fusion.1), calls=%async_computation.3 | async-start | bytes 524288 | tf_op jit(solution)/shard_map/all_to_all | solution.py:360
  216.9 8.5 %all-to-all-done.3 = bf16[8,32,512]{2,1,0:T(8,128)(2,1)S(1)} async-done(((bf16[8,32,512]{2,1,0:T(8,128)(2,1)}), bf16[8,32,512]{2,1,0:T(8,128)(2,1)S(1)}, u32[]{:S(2)}, u32[]{:S(2)}) %all-to-all-start.3) | async-done | bytes 262176 | tf_op jit(solution)/shard_map/all_to_all | solution.py:360
  (72 shorter events, 30.0 us)
Async XLA Ops:
  25.1 6.0 %copy-start.11 = (s32[1,128]{1,0:T(1,128)S(1)}, s32[1,128]{1,0:T(1,128)}, u32[]{:S(2)}) copy-start(s32[1,128]{1,0:T(1,128)} %param.7) | copy-start | bytes 1540
  27.0 29.8 %copy-start.4 = (bf16[512,512]{1,0:T(8,128)(2,1)S(1)}, bf16[512,512]{1,0:T(8,128)(2,1)}, u32[]{:S(2)}) copy-start(bf16[512,512]{1,0:T(8,128)(2,1)} %w_out_ref.3) | copy-start | bytes 1572868
  27.0 29.8 %copy-start.5 = (bf16[1,128,512]{2,1,0:T(8,128)(2,1)S(1)}, bf16[1,128,512]{2,1,0:T(8,128)(2,1)}, u32[]{:S(2)}) copy-start(bf16[1,128,512]{2,1,0:T(8,128)(2,1)} %param.11) | copy-start | bytes 393220
  27.0 29.3 %all-to-all-start.1 = ((bf16[32,32,512]{2,1,0:T(8,128)(2,1)}), bf16[32,32,512]{2,1,0:T(8,128)(2,1)S(1)}, u32[]{:S(2)}, u32[]{:S(2)}) async-start(bf16[32,32,512]{2,1,0:T(8,128)(2,1)} %bitcast.4), calls=%async_computation.1 | async-start | bytes 2097152 | tf_op jit(solution)/shard_map/all_to_all | solution.py:436
  56.9 1.6 copy-start.1
  60.1 16.2 %collective-permute-start.4 = (bf16[144,512]{1,0:T(8,128)(2,1)S(1)}, bf16[144,512]{1,0:T(8,128)(2,1)S(1)}, u32[]{:S(2)}, u32[]{:S(2)}) collective-permute-start(bf16[144,512]{1,0:T(8,128)(2,1)S(1)} %get-tuple-element.43.queries_ref.query0_ref), channel_id=1, source_target_pairs={{1,0},{2,1},{3,2},{4,3},{5,4},{6,5},{7,6},{8,7},{9,8},{10,9},{11,1... | collective-permute-start | bytes 442376 | tf_op jit(solution)/shard_map/ppermute | solution.py:24
  66.1 16.4 %collective-permute-start.5 = (bf16[144,512]{1,0:T(8,128)(2,1)S(1)}, bf16[144,512]{1,0:T(8,128)(2,1)S(1)}, u32[]{:S(2)}, u32[]{:S(2)}) collective-permute-start(bf16[144,512]{1,0:T(8,128)(2,1)S(1)} %get-tuple-element.43.queries_ref.query0_ref), channel_id=1, source_target_pairs={{2,0},{3,1},{4,2},{5,3},{6,4},{7,5},{8,6},{9,7},{10,8},{11,9},{12,... | collective-permute-start | bytes 442376 | tf_op jit(solution)/shard_map/ppermute | solution.py:24
  67.4 18.5 %collective-permute-start.6 = (bf16[144,512]{1,0:T(8,128)(2,1)S(1)}, bf16[144,512]{1,0:T(8,128)(2,1)S(1)}, u32[]{:S(2)}, u32[]{:S(2)}) collective-permute-start(bf16[144,512]{1,0:T(8,128)(2,1)S(1)} %get-tuple-element.43.queries_ref.query0_ref), channel_id=1, source_target_pairs={{3,0},{4,1},{5,2},{6,3},{7,4},{8,5},{9,6},{10,7},{11,8},{12,9},{13... | collective-permute-start | bytes 442376 | tf_op jit(solution)/shard_map/ppermute | solution.py:24
  68.7 19.4 %collective-permute-start.7 = (bf16[144,512]{1,0:T(8,128)(2,1)S(1)}, bf16[144,512]{1,0:T(8,128)(2,1)S(1)}, u32[]{:S(2)}, u32[]{:S(2)}) collective-permute-start(bf16[144,512]{1,0:T(8,128)(2,1)S(1)} %get-tuple-element.43.queries_ref.query0_ref), channel_id=1, source_target_pairs={{4,0},{5,1},{6,2},{7,3},{8,4},{9,5},{10,6},{11,7},{12,8},{13,9},{1... | collective-permute-start | bytes 442376 | tf_op jit(solution)/shard_map/ppermute | solution.py:24
  70.0 18.1 %collective-permute-start = (bf16[144,512]{1,0:T(8,128)(2,1)S(1)}, bf16[144,512]{1,0:T(8,128)(2,1)S(1)}, u32[]{:S(2)}, u32[]{:S(2)}) collective-permute-start(bf16[144,512]{1,0:T(8,128)(2,1)S(1)} %get-tuple-element.42.packed_ref.refs_1_), channel_id=1, source_target_pairs={{0,4},{1,5},{2,6},{3,7},{4,8},{5,9},{6,10},{7,11},{8,12},{9,13},{1... | collective-permute-start | bytes 442376 | tf_op jit(solution)/shard_map/ppermute | solution.py:24
  76.3 11.9 %collective-permute-start.1 = (bf16[144,512]{1,0:T(8,128)(2,1)S(1)}, bf16[144,512]{1,0:T(8,128)(2,1)S(1)}, u32[]{:S(2)}, u32[]{:S(2)}) collective-permute-start(bf16[144,512]{1,0:T(8,128)(2,1)S(1)} %get-tuple-element.42.packed_ref.refs_1_), channel_id=1, source_target_pairs={{0,3},{1,4},{2,5},{3,6},{4,7},{5,8},{6,9},{7,10},{8,11},{9,12},{10... | collective-permute-start | bytes 442376 | tf_op jit(solution)/shard_map/ppermute | solution.py:24
  82.5 6.3 %collective-permute-start.2 = (bf16[144,512]{1,0:T(8,128)(2,1)S(1)}, bf16[144,512]{1,0:T(8,128)(2,1)S(1)}, u32[]{:S(2)}, u32[]{:S(2)}) collective-permute-start(bf16[144,512]{1,0:T(8,128)(2,1)S(1)} %get-tuple-element.42.packed_ref.refs_1_), channel_id=1, source_target_pairs={{0,2},{1,3},{2,4},{3,5},{4,6},{5,7},{6,8},{7,9},{8,10},{9,11},{10,... | collective-permute-start | bytes 442376 | tf_op jit(solution)/shard_map/ppermute | solution.py:24
  85.9 4.5 %collective-permute-start.3 = (bf16[144,512]{1,0:T(8,128)(2,1)S(1)}, bf16[144,512]{1,0:T(8,128)(2,1)S(1)}, u32[]{:S(2)}, u32[]{:S(2)}) collective-permute-start(bf16[144,512]{1,0:T(8,128)(2,1)S(1)} %get-tuple-element.42.packed_ref.refs_1_), channel_id=1, source_target_pairs={{0,1},{1,2},{2,3},{3,4},{4,5},{5,6},{6,7},{7,8},{8,9},{9,10},{10,1... | collective-permute-start | bytes 442376 | tf_op jit(solution)/shard_map/ppermute | solution.py:24
  90.4 1.6 copy-start.2
  91.9 9.1 %copy-start.8 = (f32[128,2048]{1,0:T(8,128)S(1)}, f32[128,2048]{1,0:T(8,128)}, u32[]{:S(2)}) copy-start(f32[128,2048]{1,0:T(8,128)} %copy-done.7) | copy-start | bytes 3145732
  95.0 11.4 %collective-permute-start.10 = (bf16[128,512]{1,0:T(8,128)(2,1)S(1)}, bf16[128,512]{1,0:T(8,128)(2,1)S(1)}, u32[]{:S(2)}, u32[]{:S(2)}) collective-permute-start(bf16[128,512]{1,0:T(8,128)(2,1)S(1)} %get-tuple-element.59.att_grad_ref.grad0_ref), channel_id=1, source_target_pairs={{3,0},{4,1},{5,2},{6,3},{7,4},{8,5},{9,6},{10,7},{11,8},{12,9},{13... | collective-permute-start | bytes 393224 | tf_op jit(solution)/shard_map/ppermute | solution.py:24
  96.3 17.5 %collective-permute-start.11 = (bf16[128,512]{1,0:T(8,128)(2,1)S(1)}, bf16[128,512]{1,0:T(8,128)(2,1)S(1)}, u32[]{:S(2)}, u32[]{:S(2)}) collective-permute-start(bf16[128,512]{1,0:T(8,128)(2,1)S(1)} %get-tuple-element.59.att_grad_ref.grad0_ref), channel_id=1, source_target_pairs={{4,0},{5,1},{6,2},{7,3},{8,4},{9,5},{10,6},{11,7},{12,8},{13,9},{1... | collective-permute-start | bytes 393224 | tf_op jit(solution)/shard_map/ppermute | solution.py:24
  97.6 16.2 %collective-permute-start.8 = (bf16[128,512]{1,0:T(8,128)(2,1)S(1)}, bf16[128,512]{1,0:T(8,128)(2,1)S(1)}, u32[]{:S(2)}, u32[]{:S(2)}) collective-permute-start(bf16[128,512]{1,0:T(8,128)(2,1)S(1)} %get-tuple-element.59.att_grad_ref.grad0_ref), channel_id=1, source_target_pairs={{1,0},{2,1},{3,2},{4,3},{5,4},{6,5},{7,6},{8,7},{9,8},{10,9},{11,1... | collective-permute-start | bytes 393224 | tf_op jit(solution)/shard_map/ppermute | solution.py:24
  99.6 14.2 %collective-permute-start.9 = (bf16[128,512]{1,0:T(8,128)(2,1)S(1)}, bf16[128,512]{1,0:T(8,128)(2,1)S(1)}, u32[]{:S(2)}, u32[]{:S(2)}) collective-permute-start(bf16[128,512]{1,0:T(8,128)(2,1)S(1)} %get-tuple-element.59.att_grad_ref.grad0_ref), channel_id=1, source_target_pairs={{2,0},{3,1},{4,2},{5,3},{6,4},{7,5},{8,6},{9,7},{10,8},{11,9},{12,... | collective-permute-start | bytes 393224 | tf_op jit(solution)/shard_map/ppermute | solution.py:24
  101.0 12.8 %copy-start.3 = (bf16[512,2048]{1,0:T(8,128)(2,1)S(1)}, bf16[512,2048]{1,0:T(8,128)(2,1)}, u32[]{:S(2)}) copy-start(bf16[512,2048]{1,0:T(8,128)(2,1)} %w_in_ref.5) | copy-start | bytes 6291460
  122.0 7.4 %collective-permute-start.12 = (bf16[4,8,32,640]{3,2,1,0:T(8,128)(2,1)}, bf16[4,8,32,640]{3,2,1,0:T(8,128)(2,1)}, u32[]{:S(2)}, u32[]{:S(2)}) collective-permute-start(bf16[4,8,32,640]{3,2,1,0:T(8,128)(2,1)} %get-tuple-element.69), channel_id=1, source_target_pairs={{0,1},{1,0},{2,3},{3,2},{4,5},{5,4},{6,7},{7,6},{8,9},{9,8},{10,11... | collective-permute-start | bytes 3932168 | tf_op jit(solution)/shard_map/ppermute | solution.py:350
  124.3 67.8 %all-to-all-start.2 = ((bf16[32,32,512]{2,1,0:T(8,128)(2,1)}), bf16[32,32,512]{2,1,0:T(8,128)(2,1)S(1)}, u32[]{:S(2)}, u32[]{:S(2)}) async-start(bf16[32,32,512]{2,1,0:T(8,128)(2,1)} %bitcast.9), calls=%async_computation.2 | async-start | bytes 2097152 | tf_op jit(solution)/shard_map/all_to_all | solution.py:476
  132.3 17.5 %collective-permute-start.13 = (bf16[8,32,640]{2,1,0:T(8,128)(2,1)S(1)}, bf16[8,32,640]{2,1,0:T(8,128)(2,1)S(1)}, u32[]{:S(2)}, u32[]{:S(2)}) collective-permute-start(bf16[8,32,640]{2,1,0:T(8,128)(2,1)S(1)} %get-tuple-element.86), channel_id=1, source_target_pairs={{0,16},{16,32},{32,48},{48,0},{64,80},{80,96},{96,112},{112,64},{1... | collective-permute-start | bytes 983048 | tf_op jit(solution)/shard_map/ppermute | solution.py:376
  135.5 25.8 %collective-permute-start.14 = (bf16[8,32,640]{2,1,0:T(8,128)(2,1)S(1)}, bf16[8,32,640]{2,1,0:T(8,128)(2,1)S(1)}, u32[]{:S(2)}, u32[]{:S(2)}) collective-permute-start(bf16[8,32,640]{2,1,0:T(8,128)(2,1)S(1)} %get-tuple-element.88), channel_id=1, source_target_pairs={{0,32},{16,48},{32,0},{48,16},{64,96},{80,112},{96,64},{112,80},{1... | collective-permute-start | bytes 983048 | tf_op jit(solution)/shard_map/ppermute | solution.py:376
  139.8 21.5 %collective-permute-start.15 = (bf16[8,32,640]{2,1,0:T(8,128)(2,1)S(1)}, bf16[8,32,640]{2,1,0:T(8,128)(2,1)S(1)}, u32[]{:S(2)}, u32[]{:S(2)}) collective-permute-start(bf16[8,32,640]{2,1,0:T(8,128)(2,1)S(1)} %get-tuple-element.87), channel_id=1, source_target_pairs={{0,48},{16,0},{32,16},{48,32},{64,112},{80,64},{96,80},{112,96},{1... | collective-permute-start | bytes 983048 | tf_op jit(solution)/shard_map/ppermute | solution.py:376
  162.5 9.7 %collective-permute-start.16 = (bf16[4,32,640]{2,1,0:T(8,128)(2,1)S(1)}, bf16[4,32,640]{2,1,0:T(8,128)(2,1)S(1)}, u32[]{:S(2)}, u32[]{:S(2)}) collective-permute-start(bf16[4,32,640]{2,1,0:T(8,128)(2,1)S(1)} %constant_dynamic-slice_fusion.2), channel_id=1, source_target_pairs={{0,2},{1,3},{2,0},{3,1},{4,6},{5,7},{6,4},{7,5},{8,10},{9,11},{10,... | collective-permute-start | bytes 491528 | tf_op jit(solution)/shard_map/ppermute | solution.py:389
  172.2 9.6 %collective-permute-start.17 = (bf16[2,32,640]{2,1,0:T(8,128)(2,1)S(1)}, bf16[2,32,640]{2,1,0:T(8,128)(2,1)S(1)}, u32[]{:S(2)}, u32[]{:S(2)}) collective-permute-start(bf16[2,32,640]{2,1,0:T(8,128)(2,1)S(1)} %constant_dynamic-slice_fusion.1), channel_id=1, source_target_pairs={{0,4},{1,5},{2,6},{3,7},{4,0},{5,1},{6,2},{7,3},{8,12},{9,13},{10,... | collective-permute-start | bytes 245768 | tf_op jit(solution)/shard_map/ppermute | solution.py:389
  181.9 9.1 %collective-permute-start.18 = (bf16[1,32,640]{2,1,0:T(8,128)(2,1)S(1)}, bf16[1,32,640]{2,1,0:T(8,128)(2,1)S(1)}, u32[]{:S(2)}, u32[]{:S(2)}) collective-permute-start(bf16[1,32,640]{2,1,0:T(8,128)(2,1)S(1)} %constant_dynamic-slice_fusion), channel_id=1, source_target_pairs={{0,8},{1,9},{2,10},{3,11},{4,12},{5,13},{6,14},{7,15},{8,0},{9,1},... | collective-permute-start | bytes 122888 | tf_op jit(solution)/shard_map/ppermute | solution.py:389
  192.9 9.9 %collective-permute-start.19 = (bf16[8,32,512]{2,1,0:T(8,128)(2,1)S(1)}, bf16[8,32,512]{2,1,0:T(8,128)(2,1)S(1)}, u32[]{:S(2)}, u32[]{:S(2)}) collective-permute-start(bf16[8,32,512]{2,1,0:T(8,128)(2,1)S(1)} %get-tuple-element.72), channel_id=1, source_target_pairs={{0,1},{1,0},{2,3},{3,2},{4,5},{5,4},{6,7},{7,6},{8,9},{9,8},{10,11... | collective-permute-start | bytes 786440 | tf_op jit(solution)/shard_map/ppermute | solution.py:350
  197.5 12.5 %all-to-all-start.4 = ((bf16[8,32,80]{2,1,0:T(8,128)(2,1)}), bf16[8,32,80]{2,1,0:T(8,128)(2,1)S(1)}, u32[]{:S(2)}, u32[]{:S(2)}) async-start(bf16[8,32,80]{2,1,0:T(8,128)(2,1)} %maximum_bitcast_fusion), calls=%async_computation.4 | async-start | bytes 131072 | tf_op jit(solution)/shard_map/all_to_all | solution.py:360
  209.9 15.5 %all-to-all-start.3 = ((bf16[8,32,512]{2,1,0:T(8,128)(2,1)}), bf16[8,32,512]{2,1,0:T(8,128)(2,1)S(1)}, u32[]{:S(2)}, u32[]{:S(2)}) async-start(bf16[8,32,512]{2,1,0:T(8,128)(2,1)} %add_convert_fusion.1), calls=%async_computation.3 | async-start | bytes 524288 | tf_op jit(solution)/shard_map/all_to_all | solution.py:360
  216.1 10.0 %copy-start.10 = (f32[32,80]{1,0:T(8,128)}, f32[32,80]{1,0:T(8,128)S(1)}, u32[]{:S(2)}) copy-start(f32[32,80]{1,0:T(8,128)S(1)} %convert_reduce_fusion.1) | copy-start | bytes 30724
  (4 other events, 3.8 us)

commit v4 on v3

--- a/solution.py
+++ b/solution.py
@@ -24,6 +24,38 @@
     return lax.ppermute(block, axis, route)
 
 
+def swapped(block, senders=(0, 1)):
+    devices = range(lax.axis_size("ctx"))
+    return lax.ppermute(block, "ctx", [(i, i ^ 1) for i in devices if i % 2 in senders])
+
+
+def halo(block, direction, own):
+    two = passed_along(block, "ctx", 2 * direction)
+    four = passed_along(block, "ctx", 4 * direction)
+    far_sender = 1 if direction > 0 else 0
+    return (four, swapped(four, (far_sender,)), two, swapped(two), own)
+
+
+def nearest_last(core, four, mate_four, two, mate_two, mate_own):
+    even = core == 0
+    return (
+        four,
+        jnp.where(even, mate_four, mate_two),
+        two,
+        jnp.where(even, mate_two, mate_own),
+    )
+
+
+def nearest_first(core, four, mate_four, two, mate_two, mate_own):
+    even = core == 0
+    return (
+        jnp.where(even, mate_own, mate_two),
+        two,
+        jnp.where(even, mate_two, mate_four),
+        four,
+    )
+
+
 def layer_norm(values):
     centered = values - jnp.mean(values, axis=-1, keepdims=True)
     inverse = lax.rsqrt(jnp.mean(centered * centered, axis=-1, keepdims=True) + epsilon)
@@ -83,10 +115,15 @@
     return jnp.where(low, stacked[:rows], stacked[rows:])
 
 
-def call(body, outs, *operands, flops=0, moved=0):
+def call(body, outs, *operands, core=None, flops=0, moved=0):
+    in_specs = [pl.BlockSpec(memory_space=pltpu.VMEM)] * len(operands)
+    if core is not None:
+        in_specs = [pl.BlockSpec(memory_space=pltpu.SMEM)] + in_specs
+        operands = (core,) + operands
     return pl.pallas_call(
         body,
         out_shape=[jax.ShapeDtypeStruct(shape, kind) for shape, kind in outs],
+        in_specs=in_specs,
         compiler_params=pltpu.CompilerParams(vmem_limit_bytes=16 * 1024 * 1024),
         cost_estimate=pl.CostEstimate(flops=flops, bytes_accessed=moved, transcendentals=0),
     )(*operands)
@@ -144,7 +181,7 @@
 
 
 def project_body(
-    packed_ref, w_in_ref, w_out_ref, grad_ref, user_ref,
+    packed_ref, w_in_ref, w_out_ref, grad_ref,
     projected_ref, gates_ref, values_ref, queries_ref, keys_ref, mixed_grad_ref,
 ):
     rows = grad_ref.shape[0]
@@ -154,8 +191,7 @@
         columns = slice(part * width, (part + 1) * width)
         projected = dot(normed, w_in_ref[:, columns])
         projected_ref[:, columns] = projected
-        out_ref[:rows, :] = (projected * sigmoid(projected)).astype(bf16)
-    queries_ref[rows:, :] = user_rows(user_ref[...], width)
+        out_ref[...] = (projected * sigmoid(projected)).astype(bf16)
     mixed_grad_ref[...] = dot_nt(grad_ref[...], w_out_ref[...])
 
 
@@ -171,14 +207,16 @@
 
 
 def forward_body(
-    halo4_ref, halo3_ref, halo2_ref, halo1_ref, values_ref, keys_ref, queries_ref, gates_ref,
+    core_ref, four_ref, mate_four_ref, two_ref, mate_two_ref, mate_own_ref, values_ref, keys_ref, queries_ref, gates_ref,
     inputs_ref, mixed_grad_ref, w_in_ref, w_out_ref, user_ref,
     out_ref, mixed_ref, gate_grad_ref, att_grad_ref, all_keys_ref, all_values_ref, key_user_ref,
 ):
     rows, width = inputs_ref.shape
     score_scale = 1.0 / math.sqrt(DH)
-    halos = (halo4_ref, halo3_ref, halo2_ref, halo1_ref)
-    far = jnp.concatenate([halo[:rows, :] for halo in halos], axis=0)
+    halos = nearest_last(
+        core_ref[0], four_ref[...], mate_four_ref[...], two_ref[...], mate_two_ref[...], mate_own_ref[...]
+    )
+    far = jnp.concatenate([block[:rows, :] for block in halos], axis=0)
     margin = far.shape[0]
     for part, own_ref, all_ref in ((1, values_ref, all_values_ref), (3, keys_ref, all_keys_ref)):
         projected = dot(far, w_in_ref[:, part * width : (part + 1) * width])
@@ -186,14 +224,14 @@
         all_ref[margin:, :] = own_ref[...]
     user_row = user_ref[...]
     key_user = jnp.concatenate(
-        [halo[rows : rows + 1, :rows].astype(f32) for halo in halos] + [user_row], axis=1
+        [block[rows : rows + 1, :rows].astype(f32) for block in halos] + [user_row], axis=1
     )
     key_user_ref[...] = key_user
     allowed = window_mask(user_row, key_user, margin)
     parts = []
     for pair in range(H // 2):
         columns = slice(2 * DH * pair, 2 * DH * (pair + 1))
-        scores = dot_nt(both_heads(queries_ref[:rows, columns]), all_keys_ref[:, columns]) * score_scale
+        scores = dot_nt(both_heads(queries_ref[:, columns]), all_keys_ref[:, columns]) * score_scale
         weights = jnp.where(allowed, scores * sigmoid(scores), 0.0).astype(bf16)
         parts.append(one_pair(dot(weights, all_values_ref[:, columns])))
     att_hat, att_inv = layer_norm(jnp.concatenate(parts, axis=1))
@@ -206,44 +244,36 @@
     att_grad_ref[...] = norm_backward(att_hat, att_inv, mixed_grad * gates).astype(bf16)
 
 
-def halving_place(chip, chips):
-    place = 0
-    while chips > 1:
-        place = 2 * place + chip % 2
-        chip //= 2
-        chips //= 2
-    return place
-
-
-def split_by_core(core, section, terms, kept_ref, sent_ref):
-    devices = 2 * kept_ref.shape[1]
-    rows = terms.shape[0] // devices
-    lanes = terms.shape[1] // X_CHIPS
-    even = core == 0
-    for x in range(X_CHIPS):
-        for chip in range(devices // 2):
-            first = terms[2 * chip * rows : (2 * chip + 1) * rows, x * lanes : (x + 1) * lanes]
-            second = terms[(2 * chip + 1) * rows : (2 * chip + 2) * rows, x * lanes : (x + 1) * lanes]
-            place = (x, halving_place(chip, devices // 2), slice(None), slice(section * lanes, (section + 1) * lanes))
-            kept_ref[place] = jnp.where(even, first, second).astype(bf16)
-            sent_ref[place] = jnp.where(even, second, first).astype(bf16)
-
-
-def order_by_x(block, piece):
+def core_first(block, rows):
     width = block.shape[1]
     old = iota((width, width), 0)
     new = iota((width, width), 1)
-    per_x = width // X_CHIPS
-    inner = jnp.bitwise_and(old, piece - 1)
-    owner = jnp.right_shift(old, piece.bit_length() - 1)
-    x = jnp.bitwise_and(owner, X_CHIPS - 1)
-    z = jnp.right_shift(owner, X_CHIPS.bit_length() - 1)
-    return dot(block, hot(new == x * per_x + z * piece + inner)).astype(bf16)
+    inner = jnp.bitwise_and(old, rows - 1)
+    device = jnp.right_shift(old, rows.bit_length() - 1)
+    place = jnp.bitwise_and(device, 1) * (width // 2) + jnp.right_shift(device, 1) * rows + inner
+    return dot(block, hot(new == place)).astype(bf16)
+
+
+def split_by_core(core, terms, first_owner, piece, first_row, stride, kept_ref, sent_ref):
+    half = terms.shape[1] // 2
+    even = core == 0
+    for local_owner in range(terms.shape[0] // piece):
+        owner = first_owner + local_owner
+        rows = terms[local_owner * piece : (local_owner + 1) * piece]
+        place = first_row + (local_owner // X_CHIPS) * stride
+        kept_ref[owner % X_CHIPS, place : place + piece, :] = jnp.where(
+            even, rows[:, :half], rows[:, half:]
+        ).astype(bf16)
+        sent_ref[owner % X_CHIPS, place : place + piece, :] = jnp.where(
+            even, rows[:, half:], rows[:, :half]
+        ).astype(bf16)
 
 
 def query_body(
-    queries_ref, all_keys_ref, all_values_ref, att_grad_ref, gate_grad_ref,
-    projected_ref, user_ref, key_user_ref, gate_query_ref,
+    core_ref, queries_ref, all_keys_ref, all_values_ref, att_grad_ref, gate_grad_ref,
+    projected_ref, user_ref, key_user_ref,
+    four_ref, mate_four_ref, two_ref, mate_two_ref, mate_own_ref, w_in_ref,
+    gate_query_ref, all_queries_ref, query_user_ref,
 ):
     rows, width = gate_grad_ref.shape
     score_scale = 1.0 / math.sqrt(DH)
@@ -253,7 +283,7 @@
     for pair in range(H // 2):
         columns = slice(2 * DH * pair, 2 * DH * (pair + 1))
         keys = all_keys_ref[:, columns]
-        scores = dot_nt(both_heads(queries_ref[:rows, columns]), keys) * score_scale
+        scores = dot_nt(both_heads(queries_ref[:, columns]), keys) * score_scale
         prob_grad = dot_nt(both_heads(att_grad_ref[:, columns]), all_values_ref[:, columns])
         score_grad = jnp.where(allowed, prob_grad * silu_slope(scores), 0.0).astype(bf16)
         parts.append(one_pair(dot(score_grad, keys)) * score_scale)
@@ -262,22 +292,34 @@
     query_part = query_grad * silu_slope(projected_ref[:, 2 * width : 3 * width])
     gate_query_ref[:, :width] = gate_part.astype(bf16)
     gate_query_ref[:, width:] = query_part.astype(bf16)
+    halos = nearest_first(
+        core_ref[0], four_ref[...], mate_four_ref[...], two_ref[...], mate_two_ref[...], mate_own_ref[...]
+    )
+    far = jnp.concatenate([block[:rows, :] for block in halos], axis=0)
+    projected = dot(far, w_in_ref[:, 2 * width : 3 * width])
+    all_queries_ref[:rows, :] = queries_ref[...]
+    all_queries_ref[rows:, :] = (projected * sigmoid(projected)).astype(bf16)
+    query_user_ref[...] = jnp.concatenate(
+        [as_column(user_ref[...])]
+        + [as_column(block[rows : rows + 1, :rows].astype(f32)) for block in halos],
+        axis=0,
+    )
 
 
 def key_body(
-    query0_ref, query1_ref, query2_ref, query3_ref, query4_ref,
-    grad0_ref, grad1_ref, grad2_ref, grad3_ref, grad4_ref,
+    core_ref, all_queries_ref, query_user_ref, att_grad_ref,
+    four_ref, mate_four_ref, two_ref, mate_two_ref, mate_own_ref,
     keys_ref, values_ref, projected_ref, gate_query_ref, w_in_ref, inputs_ref, out_grad_ref, slot_ref, user_ref,
     value_key_ref, outgoing_ref,
 ):
     rows, width = inputs_ref.shape
     score_scale = 1.0 / math.sqrt(DH)
-    query_refs = (query0_ref, query1_ref, query2_ref, query3_ref, query4_ref)
-    grad_refs = (grad0_ref, grad1_ref, grad2_ref, grad3_ref, grad4_ref)
     user_row = user_ref[...]
-    query_user = jnp.concatenate(
-        [as_column(ref[rows : rows + 1, :rows].astype(f32)) for ref in query_refs], axis=0
-    )
+    query_user = query_user_ref[...]
+    halos = nearest_first(
+        core_ref[0], four_ref[...], mate_four_ref[...], two_ref[...], mate_two_ref[...], mate_own_ref[...]
+    )
+    all_grads = jnp.concatenate((att_grad_ref[...],) + halos, axis=0)
     total = query_user.shape[0]
     allowed = (query_user == user_row) & (iota((total, rows), 1) <= iota((total, rows), 0))
     weight = allowed.astype(f32)
@@ -286,8 +328,8 @@
     value_parts = []
     for pair in range(H // 2):
         columns = slice(2 * DH * pair, 2 * DH * (pair + 1))
-        queries = both_heads(jnp.concatenate([ref[:rows, columns] for ref in query_refs], axis=0))
-        grads = both_heads(jnp.concatenate([ref[:, columns] for ref in grad_refs], axis=0))
+        queries = both_heads(all_queries_ref[:, columns])
+        grads = both_heads(all_grads[:, columns])
         scores = dot_nt(queries, keys_ref[:, columns]) * score_scale
         sig = sigmoid(scores)
         raw = scores * sig
@@ -314,21 +356,37 @@
     outgoing_ref[...] = dot_tn(places, inputs_grad).astype(bf16)
 
 
-def weights_body(
-    piece_in, piece_out, core_ref, packed_ref, gate_query_ref, value_key_ref, mixed_ref, grad_ref,
-    kept_ref, sent_ref,
+def early_body(
+    piece_in, piece_out, weight_rows,
+    core_ref, packed_ref, gate_query_ref, mixed_ref, grad_ref, kept_ref, sent_ref,
 ):
     rows, width = grad_ref.shape
     core = core_ref[0]
-    normed = packed_ref[:rows, :]
-    parts = (
-        gate_query_ref[:, :width], value_key_ref[:, :width],
-        gate_query_ref[:, width:], value_key_ref[:, width:],
-    )
-    for section, part in enumerate(parts):
-        split_by_core(core, section, dot_tn(normed, order_by_x(part, piece_in)), kept_ref, sent_ref)
-    last = dot_tn(mixed_ref[...], order_by_x(grad_ref[...], piece_out))
-    split_by_core(core, len(parts), last, kept_ref, sent_ref)
+    per_part = width // piece_in
+    in_rows = piece_in * per_part // X_CHIPS
+    normed = core_first(packed_ref[:rows, :], weight_rows)
+    for section, first_owner in ((0, 0), (1, 2 * per_part)):
+        terms = dot_tn(gate_query_ref[:, section * width : (section + 1) * width], normed)
+        split_by_core(
+            core, terms, first_owner, piece_in, section * in_rows, piece_in, kept_ref, sent_ref
+        )
+    terms = dot_tn(grad_ref[...], core_first(mixed_ref[...], weight_rows))
+    split_by_core(core, terms, 0, piece_out, 2 * in_rows, piece_out, kept_ref, sent_ref)
+
+
+def late_body(piece_in, weight_rows, core_ref, packed_ref, value_key_ref, kept_ref, sent_ref):
+    rows = value_key_ref.shape[0]
+    width = value_key_ref.shape[1] // 2
+    core = core_ref[0]
+    per_part = width // piece_in
+    in_rows = piece_in * per_part // X_CHIPS
+    normed = core_first(packed_ref[:rows, :], weight_rows)
+    for section in range(2):
+        terms = dot_tn(value_key_ref[:, section * width : (section + 1) * width], normed)
+        split_by_core(
+            core, terms, (2 * section + 1) * per_part, piece_in, section * in_rows, piece_in,
+            kept_ref, sent_ref,
+        )
 
 
 def table_body(core_ref, asked_ref, arrived_ref, kept_ref, sent_ref):
@@ -366,44 +424,34 @@
     return jnp.sum(blocks.astype(f32), axis=0)
 
 
-def sum_along_x(block):
-    count = lax.axis_size("dp")
-    me = lax.axis_index("dp") % X_CHIPS
+def sum_along(block, axis_at, stride, count):
+    devices = lax.axis_size("dp")
+    me = axis_at % count
     own = lax.dynamic_index_in_dim(block, me, 0, keepdims=False).astype(f32)
-    for step in range(1, X_CHIPS):
-        route = [(i, i - i % X_CHIPS + (i + step) % X_CHIPS) for i in range(count)]
-        piece = lax.dynamic_index_in_dim(block, (me + step) % X_CHIPS, 0, keepdims=False)
+    for step in range(1, count):
+        route = []
+        for i in range(devices):
+            at = i // stride % count
+            route.append((i, i + ((at + step) % count - at) * stride))
+        piece = lax.dynamic_index_in_dim(block, (me + step) % count, 0, keepdims=False)
         own = own + lax.ppermute(piece, "dp", route).astype(f32)
     return own.astype(bf16)
 
 
-def sum_along_y(block):
-    count = lax.axis_size("ctx")
-    me = lax.axis_index("ctx")
-    distance = 2
-    while block.shape[0] > 1:
-        half = block.shape[0] // 2
-        bit = (me // distance) % 2
-        sent = lax.dynamic_slice_in_dim(block, (1 - bit) * half, half, 0)
-        kept = lax.dynamic_slice_in_dim(block, bit * half, half, 0)
-        got = lax.ppermute(sent, "ctx", [(i, i ^ distance) for i in range(count)])
-        block = (kept.astype(f32) + got.astype(f32)).astype(bf16)
-        distance *= 2
-    return block[0]
-
-
-def weights_to_z(along_y, owners):
-    rows = along_y.shape[0]
+def sum_along_x(block):
+    return sum_along(block, lax.axis_index("dp"), 1, X_CHIPS)
+
+
+def sum_along_z(early, late, piece_in, piece_out, owners):
     z_chips = owners // X_CHIPS
-    wide_width = along_y.shape[1] * 4 // 5
-    wide = along_y[:, :wide_width].reshape(rows, z_chips, -1)
-    thin = along_y[:, wide_width:].reshape(rows, z_chips, -1)
-    return jnp.concatenate([wide, thin], axis=2).transpose(1, 0, 2), wide.shape[2]
-
-
-def sum_along_z(send, owners):
-    zs = [list(range(first, owners, X_CHIPS)) for first in range(X_CHIPS)]
-    return total_of(spread(send, "dp", zs))
+    width = early.shape[1]
+    half = early.shape[0] - z_chips * piece_out
+    first = early[:half].reshape(2, -1, piece_in, width)
+    second = late.reshape(2, -1, piece_in, width)
+    wide = jnp.concatenate([first, second], axis=1).reshape(z_chips, piece_in, width)
+    thin = early[half:].reshape(z_chips, piece_out, width)
+    both = jnp.concatenate([wide, thin], axis=1)
+    return sum_along(both, lax.axis_index("dp") // X_CHIPS, X_CHIPS, z_chips)
 
 
 def local(item_ids, segments, touched_rows, w_in, w_out, out_grad):
@@ -439,60 +487,83 @@
     inputs, packed = call(
         embed_body, [(block, bf16), (packed_block, bf16)], slot, fetched, user
     )
-    halos = [passed_along(packed, "ctx", offset) for offset in range(REACH, 0, -1)]
+    own = swapped(packed)
+    earlier = halo(packed, 1, own)
+    later = halo(packed, -1, own)
     projected, gates, values, queries, keys, mixed_grad = call(
         project_body,
         [
             ((rows_dev, 4 * model_width), f32), (block, bf16), (block, bf16),
-            (packed_block, bf16), (block, bf16), (block, f32),
+            (block, bf16), (block, bf16), (block, f32),
         ],
-        packed, w_in, w_out, grad_rows, user,
+        packed, w_in, w_out, grad_rows,
         flops=1_500_000_000, moved=6_000_000,
     )
-    later_queries = [passed_along(queries, "ctx", -offset) for offset in range(1, REACH + 1)]
-    halos, later_queries = lax.optimization_barrier((halos, later_queries))
     layer_out, mixed, gate_grad, att_grad, all_keys, all_values, key_user = call(
         forward_body,
         [
             (block, bf16), (block, bf16), (block, f32), (block, bf16),
             (reach_block, bf16), (reach_block, bf16), ((1, (REACH + 1) * rows_dev), f32),
         ],
-        *halos, values, keys, queries, gates, inputs, mixed_grad, w_in, w_out, user,
-        flops=4_000_000_000, moved=8_000_000,
-    )
-    later_grads = [passed_along(att_grad, "ctx", -offset) for offset in range(1, REACH + 1)]
-    (gate_query,) = call(
-        query_body, [((rows_dev, 2 * model_width), bf16)],
-        queries, all_keys, all_values, att_grad, gate_grad, projected, user, key_user,
-        flops=4_000_000_000, moved=8_000_000,
-    )
+        *earlier, values, keys, queries, gates, inputs, mixed_grad, w_in, w_out, user,
+        core=core, flops=4_000_000_000, moved=8_000_000,
+    )
+    later_grads = halo(att_grad, -1, swapped(att_grad, (1,)))
+    four, mate_four, two, mate_two, mate_own = later_grads
+    gate_grad, mate_own = lax.optimization_barrier((gate_grad, mate_own))
+    mixed, four, mate_two = lax.optimization_barrier((mixed, four, mate_two))
+    later_grads = (four, mate_four, two, mate_two, mate_own)
+    gate_query, all_queries, query_user = call(
+        query_body,
+        [
+            ((rows_dev, 2 * model_width), bf16), (reach_block, bf16),
+            (((REACH + 1) * rows_dev, 1), f32),
+        ],
+        queries, all_keys, all_values, att_grad, gate_grad, projected, user, key_user, *later, w_in,
+        core=core, flops=4_000_000_000, moved=8_000_000,
+    )
+    half_width = model_width // 2
+    early_block = (X_CHIPS, 3 * model_width // X_CHIPS, half_width)
+    early_kept, early_sent = call(
+        lambda *refs: early_body(piece_in, piece_out, weight_rows, *refs),
+        [(early_block, bf16), (early_block, bf16)],
+        packed, gate_query, mixed, grad_rows,
+        core=core, flops=2_000_000_000, moved=4_000_000,
+    )
+    early_pair = pair_sum(early_kept, early_sent)
+    gate_query, early_pair = lax.optimization_barrier((gate_query, early_pair))
+    early = sum_along_x(early_pair)
     value_key, outgoing = call(
         key_body,
         [((rows_dev, 2 * model_width), bf16), ((slots, model_width), bf16)],
-        queries, *later_queries, att_grad, *later_grads, keys, values, projected, gate_query,
+        all_queries, query_user, att_grad, *later_grads, keys, values, projected, gate_query,
         w_in, inputs, grad_rows, slot, user,
-        flops=4_000_000_000, moved=8_000_000,
+        core=core, flops=4_000_000_000, moved=8_000_000,
     )
     arrived = lax.all_to_all(
         outgoing.reshape(owners, capacity, model_width), "dp", split_axis=0, concat_axis=0, tiled=True
     ).reshape(slots, model_width)
-    weight_block = (X_CHIPS, chips, weight_rows, 5 * model_width // X_CHIPS)
-    weight_kept, weight_sent = call(
-        lambda *refs: weights_body(piece_in, piece_out, *refs),
-        [(weight_block, bf16), (weight_block, bf16)],
-        core, packed, gate_query, value_key, mixed, grad_rows,
-        flops=4_000_000_000, moved=6_000_000,
-    )
-    z_send, wide = weights_to_z(sum_along_y(sum_along_x(pair_sum(weight_kept, weight_sent))), owners)
-    arrived, z_send = lax.optimization_barrier((arrived, z_send))
+    late_block = (X_CHIPS, 2 * model_width // X_CHIPS, half_width)
+    late_kept, late_sent = call(
+        lambda *refs: late_body(piece_in, weight_rows, *refs),
+        [(late_block, bf16), (late_block, bf16)],
+        packed, value_key,
+        core=core, flops=1_500_000_000, moved=3_000_000,
+    )
+    late = sum_along_x(pair_sum(late_kept, late_sent))
+    along_dp = sum_along_z(early, late, piece_in, piece_out, owners)
+    weight_terms = along_dp.T.reshape(chips, weight_rows, piece_in + piece_out)
     table_block = (chips, model_width // (2 * chips), table_dev)
     table_kept, table_sent = call(
-        table_body, [(table_block, bf16), (table_block, bf16)], core, asked_row, arrived
+        table_body, [(table_block, bf16), (table_block, bf16)], asked_row, arrived, core=core
     )
     table_sum = pair_sum(table_kept, table_sent)
-    table_grad = total_of(spread(table_sum, "ctx", chips_along_y())).T
-    summed = sum_along_z(z_send, owners)
-    return (layer_out[None], table_grad, summed[:, :wide], summed[:, wide:])
+    last = jnp.concatenate([table_sum, weight_terms], axis=2)
+    summed = total_of(spread(last, "ctx", chips_along_y()))
+    table_grad = summed[:, :table_dev].T
+    w_in_grad = summed[:, table_dev : table_dev + piece_in]
+    w_out_grad = summed[:, table_dev + piece_in :]
+    return (layer_out[None], table_grad, w_in_grad, w_out_grad)
 
 
 def solution(mesh):

time: 230 us -> 212 us (0.922)
  waiting for transfers between devices: 81.1 us -> 46 us
  blocking collectives: 22.1 us -> 40.6 us
  starting transfers between devices: 90.4 us -> 95.2 us
    ppermute x6 -> x21, starting transfers between devices: 29.1 us -> 64.6 us  [the longest x13 44.3 us: sum_along(): own = own + lax.ppermute(piece, 'dp', route).astype(f32)]
    ppermute x12 -> x6, starting transfers between devices: 33.9 us -> 12.6 us  [passed_along(): return lax.ppermute(block, axis, route)]
    all_to_all x0 -> x1, blocking collectives: none -> 18.5 us  [spread(): lax.all_to_all(block, axis, split_axis=0, concat_axis=0, tiled=True, axis...]
    ppermute x6 -> x21, waiting for transfers between devices: 28.1 us -> 11.4 us  [the longest x13 10.3 us: sum_along(): own = own + lax.ppermute(piece, 'dp', route).astype(f32)]
    all_to_all x2 -> x0, waiting for transfers between devices: 14.9 us -> none  [spread(): lax.all_to_all(block, axis, split_axis=0, concat_axis=0, tiled=True, axis...]
    all_to_all x2 -> x0, starting transfers between devices: 11.5 us -> none  [spread(): lax.all_to_all(block, axis, split_axis=0, concat_axis=0, tiled=True, axis...]
    ppermute x12 -> x6, waiting for transfers between devices: 12.9 us -> 7.98 us  [passed_along(): return lax.ppermute(block, axis, route)]
    unnamed x25 -> x15, local copies, waits for them, and re-layouts: 7.67 us -> 3.99 us
  transfers between devices with their start and end apart: 24 -> 32, of which waited for: 12 -> 10; matrix products, arithmetic and copies ran while one was open for 3% -> 2% of each run, Pallas kernels for 1% -> 4%
where the time goes in v4:
time: 212 us; the launch traced here: 210 us
  starting transfers between devices  95.2 us (45%)
  waiting for transfers between devices  46 us (22%)
  blocking collectives  40.6 us (19%)
  Pallas kernels  16.8 us (8%)
  local copies, waits for them, and re-layouts  6.66 us (3%)
  other arithmetic  3.19 us (2%)
    ppermute x13, starting transfers between devices, sum_along(): own = own + lax.ppermute(piece, 'dp', route).astype(f32)  44.3 us
    all_to_all x1, waiting for transfers between devices, local(): lax.all_to_all(found.reshape(owners, capacity, model_width), 'dp', split_...  25.2 us
    all_to_all x1, blocking collectives, local(): lax.all_to_all(requests, 'dp', split_axis=0, concat_axis=0, tiled=True)  22.1 us
    ppermute x8, starting transfers between devices, swapped(): lax.ppermute(block, 'ctx', [(i, i ^ 1) for i in devices if i % 2 in sende...  20.4 us
    all_to_all x1, blocking collectives, spread(): lax.all_to_all(block, axis, split_axis=0, concat_axis=0, tiled=True, axis...  18.5 us
    pallas_call x10, Pallas kernels, call(): pl.pallas_call(body, out_shape=[jax.ShapeDtypeStruct(shape, kind) for sha...  16.8 us
    ppermute x6, starting transfers between devices, passed_along(): return lax.ppermute(block, axis, route)  12.6 us
    ppermute x13, waiting for transfers between devices, sum_along(): own = own + lax.ppermute(piece, 'dp', route).astype(f32)  10.3 us
  transfers between devices with their start and end apart: 32, of which 10 were waited for; matrix products, arithmetic and copies ran while one was open for 2% of the time, Pallas kernels for 4%

profile of v4, /device:TPU:1, one launch (start us, length us, event | category | flops | bytes accessed | tf_op | source)
XLA Modules:
  0.0 209.9 jit_solution(13078096747896521678)
XLA Ops:
  1.9 22.1 %all_to_all.26 = s32[32,1,32]{2,1,0:T(1,128)S(1)} all-to-all(s32[32,1,32]{2,1,0:T(1,128)S(1)} %bitcast.59), channel_id=1, replica_groups=mesh['dp'=32,'ctx'=16] {'dp'}, dimensions={0} | all-to-all | bytes 8192 | tf_op jit(solution)/shard_map/all_to_all | solution.py:480
  27.0 4.1 %all-to-all-start.1 = ((bf16[32,32,512]{2,1,0:T(8,128)(2,1)}), bf16[32,32,512]{2,1,0:T(8,128)(2,1)S(1)}, u32[]{:S(2)}, u32[]{:S(2)}) async-start(bf16[32,32,512]{2,1,0:T(8,128)(2,1)} %bitcast.5), calls=%async_computation.1 | async-start | bytes 2097152 | tf_op jit(solution)/shard_map/all_to_all | solution.py:484
  31.1 25.2 %all-to-all-done.1 = bf16[32,32,512]{2,1,0:T(8,128)(2,1)S(1)} async-done(((bf16[32,32,512]{2,1,0:T(8,128)(2,1)}), bf16[32,32,512]{2,1,0:T(8,128)(2,1)S(1)}, u32[]{:S(2)}, u32[]{:S(2)}) %all-to-all-start.1) | async-done | bytes 1048608 | tf_op jit(solution)/shard_map/all_to_all | solution.py:484
  56.9 4.2 %collective-permute-start = (bf16[144,512]{1,0:T(8,128)(2,1)S(1)}, bf16[144,512]{1,0:T(8,128)(2,1)S(1)}, u32[]{:S(2)}, u32[]{:S(2)}) collective-permute-start(bf16[144,512]{1,0:T(8,128)(2,1)S(1)} %get-tuple-element.44.packed_ref.refs_1_), channel_id=1, source_target_pairs={{0,4},{1,5},{2,6},{3,7},{4,8},{5,9},{6,10},{7,11},{8,12},{9,13},{1... | collective-permute-start | bytes 442376 | tf_op jit(solution)/shard_map/ppermute | solution.py:24
  61.1 3.2 %collective-permute-start.2 = (bf16[144,512]{1,0:T(8,128)(2,1)S(1)}, bf16[144,512]{1,0:T(8,128)(2,1)S(1)}, u32[]{:S(2)}, u32[]{:S(2)}) collective-permute-start(bf16[144,512]{1,0:T(8,128)(2,1)S(1)} %get-tuple-element.44.packed_ref.refs_1_), channel_id=1, source_target_pairs={{0,2},{1,3},{2,4},{3,5},{4,6},{5,7},{6,8},{7,9},{8,10},{9,11},{10,... | collective-permute-start | bytes 442376 | tf_op jit(solution)/shard_map/ppermute | solution.py:24
  65.6 6.6 %collective-permute-start.4 = (bf16[144,512]{1,0:T(8,128)(2,1)S(1)}, bf16[144,512]{1,0:T(8,128)(2,1)S(1)}, u32[]{:S(2)}, u32[]{:S(2)}) collective-permute-start(bf16[144,512]{1,0:T(8,128)(2,1)S(1)} %get-tuple-element.44.packed_ref.refs_1_), channel_id=1, source_target_pairs={{0,1},{1,0},{2,3},{3,2},{4,5},{5,4},{6,7},{7,6},{8,9},{9,8},{10,11... | collective-permute-start | bytes 442376 | tf_op jit(solution)/shard_map/ppermute | solution.py:29
  80.9 3.0 %collective-permute-start.9 = (bf16[144,512]{1,0:T(8,128)(2,1)S(1)}, bf16[144,512]{1,0:T(8,128)(2,1)S(1)}, u32[]{:S(2)}, u32[]{:S(2)}) collective-permute-start(bf16[144,512]{1,0:T(8,128)(2,1)S(1)} %collective-permute-done.8.two_ref), channel_id=1, source_target_pairs={{0,1},{1,0},{2,3},{3,2},{4,5},{5,4},{6,7},{7,6},{8,9},{9,8},{10,11... | collective-permute-start | bytes 442376 | tf_op jit(solution)/shard_map/ppermute | solution.py:29
  84.0 3.1 %shard_map.97 = (bf16[128,512]{1,0:T(8,128)(2,1)}, bf16[128,512]{1,0:T(8,128)(2,1)S(1)}, f32[128,512]{1,0:T(8,128)S(1)}, bf16[128,512]{1,0:T(8,128)(2,1)S(1)}, b...) custom-call(s32[1]{0:T(128)} %bitcast.core_ref.refs_0_, ...), custom_call_target="tpu_custom_call" | custom-call | flops 4000000000 | bytes 8000000 | tf_op jit(solution)/shard_map/pallas_call | solution.py:123
  91.7 5.7 %collective-permute-done.11.two_ref = bf16[128,512]{1,0:T(8,128)(2,1)S(1)} collective-permute-done((bf16[128,512]{1,0:T(8,128)(2,1)S(1)}, bf16[128,512]{1,0:T(8,128)(2,1)S(1)}, u32[]{:S(2)}, u32[]{:S(2)}) %collective-permute-start.11) | collective-permute-done | bytes 131104 | tf_op jit(solution)/shard_map/ppermute | solution.py:24
  97.4 2.2 %collective-permute-start.12 = (bf16[128,512]{1,0:T(8,128)(2,1)S(1)}, bf16[128,512]{1,0:T(8,128)(2,1)S(1)}, u32[]{:S(2)}, u32[]{:S(2)}) collective-permute-start(bf16[128,512]{1,0:T(8,128)(2,1)S(1)} %collective-permute-done.11.two_ref), channel_id=1, source_target_pairs={{0,1},{1,0},{2,3},{3,2},{4,5},{5,4},{6,7},{7,6},{8,9},{9,8},{10,11... | collective-permute-start | bytes 393224 | tf_op jit(solution)/shard_map/ppermute | solution.py:29
  99.7 2.5 %shard_map.98 = (bf16[128,1024]{1,0:T(8,128)(2,1)S(1)}, bf16[640,512]{1,0:T(8,128)(2,1)S(1)}, f32[640,1]{1,0:T(8,128)S(1)}) custom-call(s32[1]{0:T(128)} %bitcast.core_ref.refs_0_, bf16[128,512]{1,0:T(8,128)(2,1)S(1)} %get-tuple-element.47.queries_ref, bf16[640,512]{1,0:T(8,128)(2,1)S(1)} %get-tuple-element.53.all_keys_ref, ...), custom_call_target="tpu_custom_call" | custom-call | flops 4000000000 | bytes 8000000 | tf_op jit(solution)/shard_map/pallas_call | solution.py:123
  105.5 2.2 %collective-permute-start.14 = (bf16[4,384,256]{2,1,0:T(8,128)(2,1)S(1)}, bf16[4,384,256]{2,1,0:T(8,128)(2,1)S(1)}, u32[]{:S(2)}, u32[]{:S(2)}) collective-permute-start(bf16[4,384,256]{2,1,0:T(8,128)(2,1)S(1)} %get-tuple-element.69), channel_id=1, source_target_pairs={{0,1},{1,0},{2,3},{3,2},{4,5},{5,4},{6,7},{7,6},{8,9},{9,8},{10,11... | collective-permute-start | bytes 2359304 | tf_op jit(solution)/shard_map/ppermute | solution.py:408
  111.0 4.9 %shard_map.100 = (bf16[128,1024]{1,0:T(8,128)(2,1)S(1)}, bf16[1024,512]{1,0:T(8,128)(2,1)}) custom-call(s32[1]{0:T(128)} %bitcast.core_ref.refs_0_, bf16[640,512]{1,0:T(8,128)(2,1)S(1)} %get-tuple-element.60.all_queries_ref, f32[640,1]{1,0:T(8,128)S(1)} %get-tuple-element.61.query_user_ref, bf16[128,512]{1,0:T(8,128)(2,1)S(1)} %get-tuple-element.55.att_grad_ref, ...), custom_call_target="tpu_custom_call" | custom-call | flops 4000000000 | bytes 8000000 | tf_op jit(solution)/shard_map/pallas_call | solution.py:123
  115.9 5.0 %all-to-all-start.2 = ((bf16[32,32,512]{2,1,0:T(8,128)(2,1)}), bf16[32,32,512]{2,1,0:T(8,128)(2,1)S(1)}, u32[]{:S(2)}, u32[]{:S(2)}) async-start(bf16[32,32,512]{2,1,0:T(8,128)(2,1)} %bitcast.9), calls=%async_computation.2 | async-start | bytes 2097152 | tf_op jit(solution)/shard_map/all_to_all | solution.py:543
  121.6 2.3 %collective-permute-start.19 = (bf16[4,256,256]{2,1,0:T(8,128)(2,1)S(1)}, bf16[4,256,256]{2,1,0:T(8,128)(2,1)}, u32[]{:S(2)}, u32[]{:S(2)}) collective-permute-start(bf16[4,256,256]{2,1,0:T(8,128)(2,1)S(1)} %get-tuple-element.77), channel_id=1, source_target_pairs={{0,1},{1,0},{2,3},{3,2},{4,5},{5,4},{6,7},{7,6},{8,9},{9,8},{10,11... | collective-permute-start | bytes 1572872 | tf_op jit(solution)/shard_map/ppermute | solution.py:408
  124.2 4.6 %collective-permute-start.18 = (bf16[384,256]{1,0:T(8,128)(2,1)S(1)}, bf16[384,256]{1,0:T(8,128)(2,1)S(1)}, u32[]{:S(2)}, u32[]{:S(2)}) collective-permute-start(bf16[384,256]{1,0:T(8,128)(2,1)S(1)} %get-tuple-element.93), channel_id=1, source_target_pairs={{0,48},{16,0},{32,16},{48,32},{64,112},{80,64},{96,80},{112,96},{1... | collective-permute-start | bytes 589832 | tf_op jit(solution)/shard_map/ppermute | solution.py:437
  128.8 2.5 %collective-permute-start.17 = (bf16[384,256]{1,0:T(8,128)(2,1)S(1)}, bf16[384,256]{1,0:T(8,128)(2,1)S(1)}, u32[]{:S(2)}, u32[]{:S(2)}) collective-permute-start(bf16[384,256]{1,0:T(8,128)(2,1)S(1)} %get-tuple-element.94), channel_id=1, source_target_pairs={{0,32},{16,48},{32,0},{48,16},{64,96},{80,112},{96,64},{112,80},{1... | collective-permute-start | bytes 589832 | tf_op jit(solution)/shard_map/ppermute | solution.py:437
  131.3 2.5 %collective-permute-start.16 = (bf16[384,256]{1,0:T(8,128)(2,1)S(1)}, bf16[384,256]{1,0:T(8,128)(2,1)S(1)}, u32[]{:S(2)}, u32[]{:S(2)}) collective-permute-start(bf16[384,256]{1,0:T(8,128)(2,1)S(1)} %get-tuple-element.92), channel_id=1, source_target_pairs={{0,16},{16,32},{32,48},{48,0},{64,80},{80,96},{96,112},{112,64},{1... | collective-permute-start | bytes 589832 | tf_op jit(solution)/shard_map/ppermute | solution.py:437
  135.8 4.0 %collective-permute-start.22 = (bf16[256,256]{1,0:T(8,128)(2,1)}, bf16[256,256]{1,0:T(8,128)(2,1)S(1)}, u32[]{:S(2)}, u32[]{:S(2)}) collective-permute-start(bf16[256,256]{1,0:T(8,128)(2,1)} %get-tuple-element.96), channel_id=1, source_target_pairs={{0,48},{16,0},{32,16},{48,32},{64,112},{80,64},{96,80},{112,96},{1... | collective-permute-start | bytes 393224 | tf_op jit(solution)/shard_map/ppermute | solution.py:437
  139.8 3.1 %collective-permute-start.21 = (bf16[256,256]{1,0:T(8,128)(2,1)}, bf16[256,256]{1,0:T(8,128)(2,1)}, u32[]{:S(2)}, u32[]{:S(2)}) collective-permute-start(bf16[256,256]{1,0:T(8,128)(2,1)} %get-tuple-element.97), channel_id=1, source_target_pairs={{0,32},{16,48},{32,0},{48,16},{64,96},{80,112},{96,64},{112,80},{1... | collective-permute-start | bytes 393224 | tf_op jit(solution)/shard_map/ppermute | solution.py:437
  145.5 4.0 %collective-permute-done.16 = bf16[384,256]{1,0:T(8,128)(2,1)S(1)} collective-permute-done((bf16[384,256]{1,0:T(8,128)(2,1)S(1)}, bf16[384,256]{1,0:T(8,128)(2,1)S(1)}, u32[]{:S(2)}, u32[]{:S(2)}) %collective-permute-start.16) | collective-permute-done | bytes 196640 | tf_op jit(solution)/shard_map/ppermute | solution.py:437
  150.0 2.3 %collective-permute-done.21 = bf16[256,256]{1,0:T(8,128)(2,1)} collective-permute-done((bf16[256,256]{1,0:T(8,128)(2,1)}, bf16[256,256]{1,0:T(8,128)(2,1)}, u32[]{:S(2)}, u32[]{:S(2)}) %collective-permute-start.21) | collective-permute-done | bytes 131104 | tf_op jit(solution)/shard_map/ppermute | solution.py:437
  152.2 3.2 %collective-permute-done.20 = bf16[256,256]{1,0:T(8,128)(2,1)} collective-permute-done((bf16[256,256]{1,0:T(8,128)(2,1)S(1)}, bf16[256,256]{1,0:T(8,128)(2,1)}, u32[]{:S(2)}, u32[]{:S(2)}) %collective-permute-start.20) | collective-permute-done | bytes 131104 | tf_op jit(solution)/shard_map/ppermute | solution.py:437
  156.9 3.2 %collective-permute-start.29 = (bf16[80,256]{0,1:T(8,128)(2,1)S(1)}, bf16[80,256]{0,1:T(8,128)(2,1)S(1)}, u32[]{:S(2)}, u32[]{:S(2)}) collective-permute-start(bf16[80,256]{0,1:T(8,128)(2,1)S(1)} %fusion.27), channel_id=1, source_target_pairs={{0,448},{16,464},{32,480},{48,496},{64,0},{80,16},{96,32},{112,48}... | collective-permute-start | bytes 122888 | tf_op jit(solution)/shard_map/ppermute | solution.py:437
  160.4 4.3 %collective-permute-start.28 = (bf16[80,256]{0,1:T(8,128)(2,1)S(1)}, bf16[80,256]{0,1:T(8,128)(2,1)S(1)}, u32[]{:S(2)}, u32[]{:S(2)}) collective-permute-start(bf16[80,256]{0,1:T(8,128)(2,1)S(1)} %get-tuple-element.91), channel_id=1, source_target_pairs={{0,384},{16,400},{32,416},{48,432},{64,448},{80,464},{96,480},{112... | collective-permute-start | bytes 122888 | tf_op jit(solution)/shard_map/ppermute | solution.py:437
  164.6 4.0 %collective-permute-start.27 = (bf16[80,256]{0,1:T(8,128)(2,1)S(1)}, bf16[80,256]{0,1:T(8,128)(2,1)S(1)}, u32[]{:S(2)}, u32[]{:S(2)}) collective-permute-start(bf16[80,256]{0,1:T(8,128)(2,1)S(1)} %get-tuple-element.90), channel_id=1, source_target_pairs={{0,320},{16,336},{32,352},{48,368},{64,384},{80,400},{96,416},{112... | collective-permute-start | bytes 122888 | tf_op jit(solution)/shard_map/ppermute | solution.py:437
  168.7 4.0 %collective-permute-start.26 = (bf16[80,256]{0,1:T(8,128)(2,1)S(1)}, bf16[80,256]{0,1:T(8,128)(2,1)S(1)}, u32[]{:S(2)}, u32[]{:S(2)}) collective-permute-start(bf16[80,256]{0,1:T(8,128)(2,1)S(1)} %get-tuple-element.89), channel_id=1, source_target_pairs={{0,256},{16,272},{32,288},{48,304},{64,320},{80,336},{96,352},{112... | collective-permute-start | bytes 122888 | tf_op jit(solution)/shard_map/ppermute | solution.py:437
  172.7 2.8 %collective-permute-start.25 = (bf16[80,256]{0,1:T(8,128)(2,1)S(1)}, bf16[80,256]{0,1:T(8,128)(2,1)S(1)}, u32[]{:S(2)}, u32[]{:S(2)}) collective-permute-start(bf16[80,256]{0,1:T(8,128)(2,1)S(1)} %get-tuple-element.88), channel_id=1, source_target_pairs={{0,192},{16,208},{32,224},{48,240},{64,256},{80,272},{96,288},{112... | collective-permute-start | bytes 122888 | tf_op jit(solution)/shard_map/ppermute | solution.py:437
  175.5 5.0 %collective-permute-start.24 = (bf16[80,256]{0,1:T(8,128)(2,1)S(1)}, bf16[80,256]{0,1:T(8,128)(2,1)S(1)}, u32[]{:S(2)}, u32[]{:S(2)}) collective-permute-start(bf16[80,256]{0,1:T(8,128)(2,1)S(1)} %get-tuple-element.87), channel_id=1, source_target_pairs={{0,128},{16,144},{32,160},{48,176},{64,192},{80,208},{96,224},{112... | collective-permute-start | bytes 122888 | tf_op jit(solution)/shard_map/ppermute | solution.py:437
  180.6 2.3 %collective-permute-start.23 = (bf16[80,256]{0,1:T(8,128)(2,1)S(1)}, bf16[80,256]{0,1:T(8,128)(2,1)S(1)}, u32[]{:S(2)}, u32[]{:S(2)}) collective-permute-start(bf16[80,256]{0,1:T(8,128)(2,1)S(1)} %get-tuple-element.86), channel_id=1, source_target_pairs={{0,64},{16,80},{32,96},{48,112},{64,128},{80,144},{96,160},{112,17... | collective-permute-start | bytes 122888 | tf_op jit(solution)/shard_map/ppermute | solution.py:437
  183.7 4.4 %collective-permute-start.15 = (bf16[8,32,512]{2,1,0:T(8,128)(2,1)S(1)}, bf16[8,32,512]{2,1,0:T(8,128)(2,1)S(1)}, u32[]{:S(2)}, u32[]{:S(2)}) collective-permute-start(bf16[8,32,512]{2,1,0:T(8,128)(2,1)S(1)} %get-tuple-element.73), channel_id=1, source_target_pairs={{0,1},{1,0},{2,3},{3,2},{4,5},{5,4},{6,7},{7,6},{8,9},{9,8},{10,11... | collective-permute-start | bytes 786440 | tf_op jit(solution)/shard_map/ppermute | solution.py:408
  189.3 18.5 %all_to_all.27 = bf16[8,32,592]{2,1,0:T(8,128)(2,1)S(1)} all-to-all(bf16[8,32,592]{2,1,0:T(8,128)(2,1)S(1)} %pad_maximum_fusion), channel_id=1, replica_groups={{0,2,4,6,8,10,12,14},{1,3,5,7,9,11,13,15},{16,18,20,22,24,26,28,30},{17..., dimensions={0} | all-to-all | bytes 606208 | tf_op jit(solution)/shard_map/all_to_all | solution.py:418
  (80 shorter events, 37.3 us)
Async XLA Ops:
  27.0 29.3 %all-to-all-start.1 = ((bf16[32,32,512]{2,1,0:T(8,128)(2,1)}), bf16[32,32,512]{2,1,0:T(8,128)(2,1)S(1)}, u32[]{:S(2)}, u32[]{:S(2)}) async-start(bf16[32,32,512]{2,1,0:T(8,128)(2,1)} %bitcast.5), calls=%async_computation.1 | async-start | bytes 2097152 | tf_op jit(solution)/shard_map/all_to_all | solution.py:484
  56.9 16.6 %collective-permute-start = (bf16[144,512]{1,0:T(8,128)(2,1)S(1)}, bf16[144,512]{1,0:T(8,128)(2,1)S(1)}, u32[]{:S(2)}, u32[]{:S(2)}) collective-permute-start(bf16[144,512]{1,0:T(8,128)(2,1)S(1)} %get-tuple-element.44.packed_ref.refs_1_), channel_id=1, source_target_pairs={{0,4},{1,5},{2,6},{3,7},{4,8},{5,9},{6,10},{7,11},{8,12},{9,13},{1... | collective-permute-start | bytes 442376 | tf_op jit(solution)/shard_map/ppermute | solution.py:24
  61.1 14.3 %collective-permute-start.2 = (bf16[144,512]{1,0:T(8,128)(2,1)S(1)}, bf16[144,512]{1,0:T(8,128)(2,1)S(1)}, u32[]{:S(2)}, u32[]{:S(2)}) collective-permute-start(bf16[144,512]{1,0:T(8,128)(2,1)S(1)} %get-tuple-element.44.packed_ref.refs_1_), channel_id=1, source_target_pairs={{0,2},{1,3},{2,4},{3,5},{4,6},{5,7},{6,8},{7,9},{8,10},{9,11},{10,... | collective-permute-start | bytes 442376 | tf_op jit(solution)/shard_map/ppermute | solution.py:24
  64.3 15.3 %collective-permute-start.6 = (bf16[144,512]{1,0:T(8,128)(2,1)S(1)}, bf16[144,512]{1,0:T(8,128)(2,1)S(1)}, u32[]{:S(2)}, u32[]{:S(2)}) collective-permute-start(bf16[144,512]{1,0:T(8,128)(2,1)S(1)} %get-tuple-element.44.packed_ref.refs_1_), channel_id=1, source_target_pairs={{4,0},{5,1},{6,2},{7,3},{8,4},{9,5},{10,6},{11,7},{12,8},{13,9},{1... | collective-permute-start | bytes 442376 | tf_op jit(solution)/shard_map/ppermute | solution.py:24
  65.6 18.4 %collective-permute-start.4 = (bf16[144,512]{1,0:T(8,128)(2,1)S(1)}, bf16[144,512]{1,0:T(8,128)(2,1)S(1)}, u32[]{:S(2)}, u32[]{:S(2)}) collective-permute-start(bf16[144,512]{1,0:T(8,128)(2,1)S(1)} %get-tuple-element.44.packed_ref.refs_1_), channel_id=1, source_target_pairs={{0,1},{1,0},{2,3},{3,2},{4,5},{5,4},{6,7},{7,6},{8,9},{9,8},{10,11... | collective-permute-start | bytes 442376 | tf_op jit(solution)/shard_map/ppermute | solution.py:29
  72.2 8.8 %collective-permute-start.8 = (bf16[144,512]{1,0:T(8,128)(2,1)S(1)}, bf16[144,512]{1,0:T(8,128)(2,1)S(1)}, u32[]{:S(2)}, u32[]{:S(2)}) collective-permute-start(bf16[144,512]{1,0:T(8,128)(2,1)S(1)} %get-tuple-element.44.packed_ref.refs_1_), channel_id=1, source_target_pairs={{2,0},{3,1},{4,2},{5,3},{6,4},{7,5},{8,6},{9,7},{10,8},{11,9},{12,... | collective-permute-start | bytes 442376 | tf_op jit(solution)/shard_map/ppermute | solution.py:24
  73.5 10.5 %collective-permute-start.1 = (bf16[144,512]{1,0:T(8,128)(2,1)S(1)}, bf16[144,512]{1,0:T(8,128)(2,1)S(1)}, u32[]{:S(2)}, u32[]{:S(2)}) collective-permute-start(bf16[144,512]{1,0:T(8,128)(2,1)S(1)} %collective-permute-done.four_ref), channel_id=1, source_target_pairs={{1,0},{3,2},{5,4},{7,6},{9,8},{11,10},{13,12},{15,14},{17,16},{19,... | collective-permute-start | bytes 442376 | tf_op jit(solution)/shard_map/ppermute | solution.py:29
  75.4 8.6 %collective-permute-start.3 = (bf16[144,512]{1,0:T(8,128)(2,1)S(1)}, bf16[144,512]{1,0:T(8,128)(2,1)S(1)}, u32[]{:S(2)}, u32[]{:S(2)}) collective-permute-start(bf16[144,512]{1,0:T(8,128)(2,1)S(1)} %collective-permute-done.2.two_ref), channel_id=1, source_target_pairs={{0,1},{1,0},{2,3},{3,2},{4,5},{5,4},{6,7},{7,6},{8,9},{9,8},{10,11... | collective-permute-start | bytes 442376 | tf_op jit(solution)/shard_map/ppermute | solution.py:29
  79.6 20.0 %collective-permute-start.7 = (bf16[144,512]{1,0:T(8,128)(2,1)S(1)}, bf16[144,512]{1,0:T(8,128)(2,1)S(1)}, u32[]{:S(2)}, u32[]{:S(2)}) collective-permute-start(bf16[144,512]{1,0:T(8,128)(2,1)S(1)} %collective-permute-done.6.four_ref), channel_id=1, source_target_pairs={{0,1},{2,3},{4,5},{6,7},{8,9},{10,11},{12,13},{14,15},{16,17},{18,... | collective-permute-start | bytes 442376 | tf_op jit(solution)/shard_map/ppermute | solution.py:29
  80.9 18.7 %collective-permute-start.9 = (bf16[144,512]{1,0:T(8,128)(2,1)S(1)}, bf16[144,512]{1,0:T(8,128)(2,1)S(1)}, u32[]{:S(2)}, u32[]{:S(2)}) collective-permute-start(bf16[144,512]{1,0:T(8,128)(2,1)S(1)} %collective-permute-done.8.two_ref), channel_id=1, source_target_pairs={{0,1},{1,0},{2,3},{3,2},{4,5},{5,4},{6,7},{7,6},{8,9},{9,8},{10,11... | collective-permute-start | bytes 442376 | tf_op jit(solution)/shard_map/ppermute | solution.py:29
  87.1 4.5 %collective-permute-start.5 = (bf16[128,512]{1,0:T(8,128)(2,1)S(1)}, bf16[128,512]{1,0:T(8,128)(2,1)S(1)}, u32[]{:S(2)}, u32[]{:S(2)}) collective-permute-start(bf16[128,512]{1,0:T(8,128)(2,1)S(1)} %get-tuple-element.55.att_grad_ref), channel_id=1, source_target_pairs={{1,0},{3,2},{5,4},{7,6},{9,8},{11,10},{13,12},{15,14},{17,16},{19,... | collective-permute-start | bytes 393224 | tf_op jit(solution)/shard_map/ppermute | solution.py:29
  89.1 8.4 %collective-permute-start.11 = (bf16[128,512]{1,0:T(8,128)(2,1)S(1)}, bf16[128,512]{1,0:T(8,128)(2,1)S(1)}, u32[]{:S(2)}, u32[]{:S(2)}) collective-permute-start(bf16[128,512]{1,0:T(8,128)(2,1)S(1)} %get-tuple-element.55.att_grad_ref), channel_id=1, source_target_pairs={{2,0},{3,1},{4,2},{5,3},{6,4},{7,5},{8,6},{9,7},{10,8},{11,9},{12,... | collective-permute-start | bytes 393224 | tf_op jit(solution)/shard_map/ppermute | solution.py:24
  90.4 14.0 %collective-permute-start.10 = (bf16[128,512]{1,0:T(8,128)(2,1)S(1)}, bf16[128,512]{1,0:T(8,128)(2,1)S(1)}, u32[]{:S(2)}, u32[]{:S(2)}) collective-permute-start(bf16[128,512]{1,0:T(8,128)(2,1)S(1)} %get-tuple-element.55.att_grad_ref), channel_id=1, source_target_pairs={{4,0},{5,1},{6,2},{7,3},{8,4},{9,5},{10,6},{11,7},{12,8},{13,9},{1... | collective-permute-start | bytes 393224 | tf_op jit(solution)/shard_map/ppermute | solution.py:24
  97.4 7.0 %collective-permute-start.12 = (bf16[128,512]{1,0:T(8,128)(2,1)S(1)}, bf16[128,512]{1,0:T(8,128)(2,1)S(1)}, u32[]{:S(2)}, u32[]{:S(2)}) collective-permute-start(bf16[128,512]{1,0:T(8,128)(2,1)S(1)} %collective-permute-done.11.two_ref), channel_id=1, source_target_pairs={{0,1},{1,0},{2,3},{3,2},{4,5},{5,4},{6,7},{7,6},{8,9},{9,8},{10,11... | collective-permute-start | bytes 393224 | tf_op jit(solution)/shard_map/ppermute | solution.py:29
  105.5 4.2 %collective-permute-start.14 = (bf16[4,384,256]{2,1,0:T(8,128)(2,1)S(1)}, bf16[4,384,256]{2,1,0:T(8,128)(2,1)S(1)}, u32[]{:S(2)}, u32[]{:S(2)}) collective-permute-start(bf16[4,384,256]{2,1,0:T(8,128)(2,1)S(1)} %get-tuple-element.69), channel_id=1, source_target_pairs={{0,1},{1,0},{2,3},{3,2},{4,5},{5,4},{6,7},{7,6},{8,9},{9,8},{10,11... | collective-permute-start | bytes 2359304 | tf_op jit(solution)/shard_map/ppermute | solution.py:408
  107.8 3.2 %collective-permute-start.13 = (bf16[128,512]{1,0:T(8,128)(2,1)S(1)}, bf16[128,512]{1,0:T(8,128)(2,1)S(1)}, u32[]{:S(2)}, u32[]{:S(2)}) collective-permute-start(bf16[128,512]{1,0:T(8,128)(2,1)S(1)} %collective-permute-done.10.four_ref), channel_id=1, source_target_pairs={{0,1},{2,3},{4,5},{6,7},{8,9},{10,11},{12,13},{14,15},{16,17},{18,... | collective-permute-start | bytes 393224 | tf_op jit(solution)/shard_map/ppermute | solution.py:29
  115.9 67.0 %all-to-all-start.2 = ((bf16[32,32,512]{2,1,0:T(8,128)(2,1)}), bf16[32,32,512]{2,1,0:T(8,128)(2,1)S(1)}, u32[]{:S(2)}, u32[]{:S(2)}) async-start(bf16[32,32,512]{2,1,0:T(8,128)(2,1)} %bitcast.9), calls=%async_computation.2 | async-start | bytes 2097152 | tf_op jit(solution)/shard_map/all_to_all | solution.py:543
  121.6 12.3 %collective-permute-start.19 = (bf16[4,256,256]{2,1,0:T(8,128)(2,1)S(1)}, bf16[4,256,256]{2,1,0:T(8,128)(2,1)}, u32[]{:S(2)}, u32[]{:S(2)}) collective-permute-start(bf16[4,256,256]{2,1,0:T(8,128)(2,1)S(1)} %get-tuple-element.77), channel_id=1, source_target_pairs={{0,1},{1,0},{2,3},{3,2},{4,5},{5,4},{6,7},{7,6},{8,9},{9,8},{10,11... | collective-permute-start | bytes 1572872 | tf_op jit(solution)/shard_map/ppermute | solution.py:408
  124.2 19.4 %collective-permute-start.18 = (bf16[384,256]{1,0:T(8,128)(2,1)S(1)}, bf16[384,256]{1,0:T(8,128)(2,1)S(1)}, u32[]{:S(2)}, u32[]{:S(2)}) collective-permute-start(bf16[384,256]{1,0:T(8,128)(2,1)S(1)} %get-tuple-element.93), channel_id=1, source_target_pairs={{0,48},{16,0},{32,16},{48,32},{64,112},{80,64},{96,80},{112,96},{1... | collective-permute-start | bytes 589832 | tf_op jit(solution)/shard_map/ppermute | solution.py:437
  128.8 16.7 %collective-permute-start.17 = (bf16[384,256]{1,0:T(8,128)(2,1)S(1)}, bf16[384,256]{1,0:T(8,128)(2,1)S(1)}, u32[]{:S(2)}, u32[]{:S(2)}) collective-permute-start(bf16[384,256]{1,0:T(8,128)(2,1)S(1)} %get-tuple-element.94), channel_id=1, source_target_pairs={{0,32},{16,48},{32,0},{48,16},{64,96},{80,112},{96,64},{112,80},{1... | collective-permute-start | bytes 589832 | tf_op jit(solution)/shard_map/ppermute | solution.py:437
  131.3 18.2 %collective-permute-start.16 = (bf16[384,256]{1,0:T(8,128)(2,1)S(1)}, bf16[384,256]{1,0:T(8,128)(2,1)S(1)}, u32[]{:S(2)}, u32[]{:S(2)}) collective-permute-start(bf16[384,256]{1,0:T(8,128)(2,1)S(1)} %get-tuple-element.92), channel_id=1, source_target_pairs={{0,16},{16,32},{32,48},{48,0},{64,80},{80,96},{96,112},{112,64},{1... | collective-permute-start | bytes 589832 | tf_op jit(solution)/shard_map/ppermute | solution.py:437
  135.8 14.2 %collective-permute-start.22 = (bf16[256,256]{1,0:T(8,128)(2,1)}, bf16[256,256]{1,0:T(8,128)(2,1)S(1)}, u32[]{:S(2)}, u32[]{:S(2)}) collective-permute-start(bf16[256,256]{1,0:T(8,128)(2,1)} %get-tuple-element.96), channel_id=1, source_target_pairs={{0,48},{16,0},{32,16},{48,32},{64,112},{80,64},{96,80},{112,96},{1... | collective-permute-start | bytes 393224 | tf_op jit(solution)/shard_map/ppermute | solution.py:437
  139.8 12.5 %collective-permute-start.21 = (bf16[256,256]{1,0:T(8,128)(2,1)}, bf16[256,256]{1,0:T(8,128)(2,1)}, u32[]{:S(2)}, u32[]{:S(2)}) collective-permute-start(bf16[256,256]{1,0:T(8,128)(2,1)} %get-tuple-element.97), channel_id=1, source_target_pairs={{0,32},{16,48},{32,0},{48,16},{64,96},{80,112},{96,64},{112,80},{1... | collective-permute-start | bytes 393224 | tf_op jit(solution)/shard_map/ppermute | solution.py:437
  143.6 11.8 %collective-permute-start.20 = (bf16[256,256]{1,0:T(8,128)(2,1)S(1)}, bf16[256,256]{1,0:T(8,128)(2,1)}, u32[]{:S(2)}, u32[]{:S(2)}) collective-permute-start(bf16[256,256]{1,0:T(8,128)(2,1)S(1)} %get-tuple-element.95), channel_id=1, source_target_pairs={{0,16},{16,32},{32,48},{48,0},{64,80},{80,96},{96,112},{112,64},{1... | collective-permute-start | bytes 393224 | tf_op jit(solution)/shard_map/ppermute | solution.py:437
  156.9 18.6 %collective-permute-start.29 = (bf16[80,256]{0,1:T(8,128)(2,1)S(1)}, bf16[80,256]{0,1:T(8,128)(2,1)S(1)}, u32[]{:S(2)}, u32[]{:S(2)}) collective-permute-start(bf16[80,256]{0,1:T(8,128)(2,1)S(1)} %fusion.27), channel_id=1, source_target_pairs={{0,448},{16,464},{32,480},{48,496},{64,0},{80,16},{96,32},{112,48}... | collective-permute-start | bytes 122888 | tf_op jit(solution)/shard_map/ppermute | solution.py:437
  160.4 20.2 %collective-permute-start.28 = (bf16[80,256]{0,1:T(8,128)(2,1)S(1)}, bf16[80,256]{0,1:T(8,128)(2,1)S(1)}, u32[]{:S(2)}, u32[]{:S(2)}) collective-permute-start(bf16[80,256]{0,1:T(8,128)(2,1)S(1)} %get-tuple-element.91), channel_id=1, source_target_pairs={{0,384},{16,400},{32,416},{48,432},{64,448},{80,464},{96,480},{112... | collective-permute-start | bytes 122888 | tf_op jit(solution)/shard_map/ppermute | solution.py:437
  164.6 19.1 %collective-permute-start.27 = (bf16[80,256]{0,1:T(8,128)(2,1)S(1)}, bf16[80,256]{0,1:T(8,128)(2,1)S(1)}, u32[]{:S(2)}, u32[]{:S(2)}) collective-permute-start(bf16[80,256]{0,1:T(8,128)(2,1)S(1)} %get-tuple-element.90), channel_id=1, source_target_pairs={{0,320},{16,336},{32,352},{48,368},{64,384},{80,400},{96,416},{112... | collective-permute-start | bytes 122888 | tf_op jit(solution)/shard_map/ppermute | solution.py:437
  168.7 19.4 %collective-permute-start.26 = (bf16[80,256]{0,1:T(8,128)(2,1)S(1)}, bf16[80,256]{0,1:T(8,128)(2,1)S(1)}, u32[]{:S(2)}, u32[]{:S(2)}) collective-permute-start(bf16[80,256]{0,1:T(8,128)(2,1)S(1)} %get-tuple-element.89), channel_id=1, source_target_pairs={{0,256},{16,272},{32,288},{48,304},{64,320},{80,336},{96,352},{112... | collective-permute-start | bytes 122888 | tf_op jit(solution)/shard_map/ppermute | solution.py:437
  172.7 15.4 %collective-permute-start.25 = (bf16[80,256]{0,1:T(8,128)(2,1)S(1)}, bf16[80,256]{0,1:T(8,128)(2,1)S(1)}, u32[]{:S(2)}, u32[]{:S(2)}) collective-permute-start(bf16[80,256]{0,1:T(8,128)(2,1)S(1)} %get-tuple-element.88), channel_id=1, source_target_pairs={{0,192},{16,208},{32,224},{48,240},{64,256},{80,272},{96,288},{112... | collective-permute-start | bytes 122888 | tf_op jit(solution)/shard_map/ppermute | solution.py:437
  175.5 12.6 %collective-permute-start.24 = (bf16[80,256]{0,1:T(8,128)(2,1)S(1)}, bf16[80,256]{0,1:T(8,128)(2,1)S(1)}, u32[]{:S(2)}, u32[]{:S(2)}) collective-permute-start(bf16[80,256]{0,1:T(8,128)(2,1)S(1)} %get-tuple-element.87), channel_id=1, source_target_pairs={{0,128},{16,144},{32,160},{48,176},{64,192},{80,208},{96,224},{112... | collective-permute-start | bytes 122888 | tf_op jit(solution)/shard_map/ppermute | solution.py:437
  180.6 7.6 %collective-permute-start.23 = (bf16[80,256]{0,1:T(8,128)(2,1)S(1)}, bf16[80,256]{0,1:T(8,128)(2,1)S(1)}, u32[]{:S(2)}, u32[]{:S(2)}) collective-permute-start(bf16[80,256]{0,1:T(8,128)(2,1)S(1)} %get-tuple-element.86), channel_id=1, source_target_pairs={{0,64},{16,80},{32,96},{48,112},{64,128},{80,144},{96,160},{112,17... | collective-permute-start | bytes 122888 | tf_op jit(solution)/shard_map/ppermute | solution.py:437
  183.7 5.5 %collective-permute-start.15 = (bf16[8,32,512]{2,1,0:T(8,128)(2,1)S(1)}, bf16[8,32,512]{2,1,0:T(8,128)(2,1)S(1)}, u32[]{:S(2)}, u32[]{:S(2)}) collective-permute-start(bf16[8,32,512]{2,1,0:T(8,128)(2,1)S(1)} %get-tuple-element.73), channel_id=1, source_target_pairs={{0,1},{1,0},{2,3},{3,2},{4,5},{5,4},{6,7},{7,6},{8,9},{9,8},{10,11... | collective-permute-start | bytes 786440 | tf_op jit(solution)/shard_map/ppermute | solution.py:408
  (7 other events, 139.5 us)

commit v5 on v4

--- a/solution.py
+++ b/solution.py
@@ -29,11 +29,16 @@
     return lax.ppermute(block, "ctx", [(i, i ^ 1) for i in devices if i % 2 in senders])
 
 
-def halo(block, direction, own):
-    two = passed_along(block, "ctx", 2 * direction)
-    four = passed_along(block, "ctx", 4 * direction)
+def halo_across(block, direction):
+    return (
+        passed_along(block, "ctx", 4 * direction),
+        passed_along(block, "ctx", 2 * direction),
+    )
+
+
+def halo_inside(four, two, direction):
     far_sender = 1 if direction > 0 else 0
-    return (four, swapped(four, (far_sender,)), two, swapped(two), own)
+    return (swapped(four, (far_sender,)), swapped(two))
 
 
 def nearest_last(core, four, mate_four, two, mate_two, mate_own):
@@ -182,7 +187,7 @@
 
 def project_body(
     packed_ref, w_in_ref, w_out_ref, grad_ref,
-    projected_ref, gates_ref, values_ref, queries_ref, keys_ref, mixed_grad_ref,
+    gates_ref, values_ref, queries_ref, keys_ref, mixed_grad_ref,
 ):
     rows = grad_ref.shape[0]
     width = grad_ref.shape[1]
@@ -190,7 +195,6 @@
     for part, out_ref in enumerate((gates_ref, values_ref, queries_ref, keys_ref)):
         columns = slice(part * width, (part + 1) * width)
         projected = dot(normed, w_in_ref[:, columns])
-        projected_ref[:, columns] = projected
         out_ref[...] = (projected * sigmoid(projected)).astype(bf16)
     mixed_grad_ref[...] = dot_nt(grad_ref[...], w_out_ref[...])
 
@@ -271,9 +275,9 @@
 
 def query_body(
     core_ref, queries_ref, all_keys_ref, all_values_ref, att_grad_ref, gate_grad_ref,
-    projected_ref, user_ref, key_user_ref,
+    packed_ref, user_ref, key_user_ref,
     four_ref, mate_four_ref, two_ref, mate_two_ref, mate_own_ref, w_in_ref,
-    gate_query_ref, all_queries_ref, query_user_ref,
+    gate_query_ref, value_key_slope_ref, all_queries_ref, query_user_ref,
 ):
     rows, width = gate_grad_ref.shape
     score_scale = 1.0 / math.sqrt(DH)
@@ -288,8 +292,14 @@
         score_grad = jnp.where(allowed, prob_grad * silu_slope(scores), 0.0).astype(bf16)
         parts.append(one_pair(dot(score_grad, keys)) * score_scale)
     query_grad = jnp.concatenate(parts, axis=1)
-    gate_part = gate_grad_ref[...] * silu_slope(projected_ref[:, :width])
-    query_part = query_grad * silu_slope(projected_ref[:, 2 * width : 3 * width])
+    normed = packed_ref[:rows, :]
+    gate_slope, value_slope, query_slope, key_slope = [
+        silu_slope(dot(normed, w_in_ref[:, part * width : (part + 1) * width])) for part in range(4)
+    ]
+    value_key_slope_ref[:, :width] = value_slope
+    value_key_slope_ref[:, width:] = key_slope
+    gate_part = gate_grad_ref[...] * gate_slope
+    query_part = query_grad * query_slope
     gate_query_ref[:, :width] = gate_part.astype(bf16)
     gate_query_ref[:, width:] = query_part.astype(bf16)
     halos = nearest_first(
@@ -309,7 +319,7 @@
 def key_body(
     core_ref, all_queries_ref, query_user_ref, att_grad_ref,
     four_ref, mate_four_ref, two_ref, mate_two_ref, mate_own_ref,
-    keys_ref, values_ref, projected_ref, gate_query_ref, w_in_ref, inputs_ref, out_grad_ref, slot_ref, user_ref,
+    keys_ref, values_ref, value_key_slope_ref, gate_query_ref, w_in_ref, inputs_ref, out_grad_ref, slot_ref, user_ref,
     value_key_ref, outgoing_ref,
 ):
     rows, width = inputs_ref.shape
@@ -340,8 +350,8 @@
         value_parts.append(dot_tn(weights, grads))
     key_grad = jnp.concatenate(key_parts, axis=1)
     value_grad = jnp.concatenate(value_parts, axis=1)
-    value_part = (value_grad * silu_slope(projected_ref[:, width : 2 * width])).astype(bf16)
-    key_part = (key_grad * silu_slope(projected_ref[:, 3 * width :])).astype(bf16)
+    value_part = (value_grad * value_key_slope_ref[:, :width]).astype(bf16)
+    key_part = (key_grad * value_key_slope_ref[:, width:]).astype(bf16)
     value_key_ref[:, :width] = value_part
     value_key_ref[:, width:] = key_part
     joined = jnp.concatenate(
@@ -374,18 +384,29 @@
     split_by_core(core, terms, 0, piece_out, 2 * in_rows, piece_out, kept_ref, sent_ref)
 
 
-def late_body(piece_in, weight_rows, core_ref, packed_ref, value_key_ref, kept_ref, sent_ref):
+def late_body(
+    piece_in, piece_out, weight_rows,
+    core_ref, packed_ref, value_key_ref, early_kept_ref, early_sent_ref, kept_ref, sent_ref,
+):
     rows = value_key_ref.shape[0]
     width = value_key_ref.shape[1] // 2
     core = core_ref[0]
-    per_part = width // piece_in
-    in_rows = piece_in * per_part // X_CHIPS
+    piece = piece_in + piece_out
+    z_part = width // piece_in // X_CHIPS
+    z_chips = kept_ref.shape[1] // piece
+    for early_ref, ref in ((early_kept_ref, kept_ref), (early_sent_ref, sent_ref)):
+        for z in range(z_chips):
+            section, inner = divmod(z, z_part)
+            if section % 2 == 0:
+                old = (section // 2 * z_part + inner) * piece_in
+                ref[:, z * piece : z * piece + piece_in, :] = early_ref[:, old : old + piece_in, :]
+            old = 2 * z_part * piece_in + z * piece_out
+            ref[:, z * piece + piece_in : (z + 1) * piece, :] = early_ref[:, old : old + piece_out, :]
     normed = core_first(packed_ref[:rows, :], weight_rows)
     for section in range(2):
         terms = dot_tn(value_key_ref[:, section * width : (section + 1) * width], normed)
         split_by_core(
-            core, terms, (2 * section + 1) * per_part, piece_in, section * in_rows, piece_in,
-            kept_ref, sent_ref,
+            core, terms, 0, piece_in, (2 * section + 1) * z_part * piece, piece, kept_ref, sent_ref
         )
 
 
@@ -424,34 +445,19 @@
     return jnp.sum(blocks.astype(f32), axis=0)
 
 
-def sum_along(block, axis_at, stride, count):
+def sum_along_x(block):
     devices = lax.axis_size("dp")
-    me = axis_at % count
+    me = lax.axis_index("dp") % X_CHIPS
     own = lax.dynamic_index_in_dim(block, me, 0, keepdims=False).astype(f32)
-    for step in range(1, count):
-        route = []
-        for i in range(devices):
-            at = i // stride % count
-            route.append((i, i + ((at + step) % count - at) * stride))
-        piece = lax.dynamic_index_in_dim(block, (me + step) % count, 0, keepdims=False)
+    for step in range(1, X_CHIPS):
+        route = [(i, i - i % X_CHIPS + (i + step) % X_CHIPS) for i in range(devices)]
+        piece = lax.dynamic_index_in_dim(block, (me + step) % X_CHIPS, 0, keepdims=False)
         own = own + lax.ppermute(piece, "dp", route).astype(f32)
     return own.astype(bf16)
 
 
-def sum_along_x(block):
-    return sum_along(block, lax.axis_index("dp"), 1, X_CHIPS)
-
-
-def sum_along_z(early, late, piece_in, piece_out, owners):
-    z_chips = owners // X_CHIPS
-    width = early.shape[1]
-    half = early.shape[0] - z_chips * piece_out
-    first = early[:half].reshape(2, -1, piece_in, width)
-    second = late.reshape(2, -1, piece_in, width)
-    wide = jnp.concatenate([first, second], axis=1).reshape(z_chips, piece_in, width)
-    thin = early[half:].reshape(z_chips, piece_out, width)
-    both = jnp.concatenate([wide, thin], axis=1)
-    return sum_along(both, lax.axis_index("dp") // X_CHIPS, X_CHIPS, z_chips)
+def chips_along_z(owners):
+    return [list(range(first, owners, X_CHIPS)) for first in range(X_CHIPS)]
 
 
 def local(item_ids, segments, touched_rows, w_in, w_out, out_grad):
@@ -487,18 +493,24 @@
     inputs, packed = call(
         embed_body, [(block, bf16), (packed_block, bf16)], slot, fetched, user
     )
-    own = swapped(packed)
-    earlier = halo(packed, 1, own)
-    later = halo(packed, -1, own)
-    projected, gates, values, queries, keys, mixed_grad = call(
+    mate_own = swapped(packed)
+    earlier_four, earlier_two = halo_across(packed, 1)
+    later_four, later_two = halo_across(packed, -1)
+    gates, values, queries, keys, mixed_grad = call(
         project_body,
         [
-            ((rows_dev, 4 * model_width), f32), (block, bf16), (block, bf16),
-            (block, bf16), (block, bf16), (block, f32),
+            (block, bf16), (block, bf16), (block, bf16), (block, bf16), (block, f32),
         ],
         packed, w_in, w_out, grad_rows,
         flops=1_500_000_000, moved=6_000_000,
     )
+    earlier_four, later_four, later_two, mate_own, mixed_grad = lax.optimization_barrier(
+        (earlier_four, later_four, later_two, mate_own, mixed_grad)
+    )
+    inside = halo_inside(earlier_four, earlier_two, 1) + halo_inside(later_four, later_two, -1)
+    mate_four, mate_two, later_mate_four, later_mate_two = lax.optimization_barrier(inside)
+    earlier = (earlier_four, mate_four, earlier_two, mate_two, mate_own)
+    later = (later_four, later_mate_four, later_two, later_mate_two, mate_own)
     layer_out, mixed, gate_grad, att_grad, all_keys, all_values, key_user = call(
         forward_body,
         [
@@ -508,18 +520,19 @@
         *earlier, values, keys, queries, gates, inputs, mixed_grad, w_in, w_out, user,
         core=core, flops=4_000_000_000, moved=8_000_000,
     )
-    later_grads = halo(att_grad, -1, swapped(att_grad, (1,)))
-    four, mate_four, two, mate_two, mate_own = later_grads
-    gate_grad, mate_own = lax.optimization_barrier((gate_grad, mate_own))
-    mixed, four, mate_two = lax.optimization_barrier((mixed, four, mate_two))
-    later_grads = (four, mate_four, two, mate_two, mate_own)
-    gate_query, all_queries, query_user = call(
+    own_grad = swapped(att_grad, (1,))
+    grad_four, grad_two = halo_across(att_grad, -1)
+    grad_mate_four, grad_mate_two = halo_inside(grad_four, grad_two, -1)
+    gate_grad, own_grad, grad_two = lax.optimization_barrier((gate_grad, own_grad, grad_two))
+    mixed, grad_four, grad_mate_two = lax.optimization_barrier((mixed, grad_four, grad_mate_two))
+    later_grads = (grad_four, grad_mate_four, grad_two, grad_mate_two, own_grad)
+    gate_query, value_key_slope, all_queries, query_user = call(
         query_body,
         [
-            ((rows_dev, 2 * model_width), bf16), (reach_block, bf16),
+            ((rows_dev, 2 * model_width), bf16), ((rows_dev, 2 * model_width), f32), (reach_block, bf16),
             (((REACH + 1) * rows_dev, 1), f32),
         ],
-        queries, all_keys, all_values, att_grad, gate_grad, projected, user, key_user, *later, w_in,
+        queries, all_keys, all_values, att_grad, gate_grad, packed, user, key_user, *later, w_in,
         core=core, flops=4_000_000_000, moved=8_000_000,
     )
     half_width = model_width // 2
@@ -530,29 +543,32 @@
         packed, gate_query, mixed, grad_rows,
         core=core, flops=2_000_000_000, moved=4_000_000,
     )
-    early_pair = pair_sum(early_kept, early_sent)
-    gate_query, early_pair = lax.optimization_barrier((gate_query, early_pair))
-    early = sum_along_x(early_pair)
+    gate_query, early_kept, early_sent = lax.optimization_barrier(
+        (gate_query, early_kept, early_sent)
+    )
     value_key, outgoing = call(
         key_body,
         [((rows_dev, 2 * model_width), bf16), ((slots, model_width), bf16)],
-        all_queries, query_user, att_grad, *later_grads, keys, values, projected, gate_query,
+        all_queries, query_user, att_grad, *later_grads, keys, values, value_key_slope, gate_query,
         w_in, inputs, grad_rows, slot, user,
         core=core, flops=4_000_000_000, moved=8_000_000,
     )
     arrived = lax.all_to_all(
         outgoing.reshape(owners, capacity, model_width), "dp", split_axis=0, concat_axis=0, tiled=True
     ).reshape(slots, model_width)
-    late_block = (X_CHIPS, 2 * model_width // X_CHIPS, half_width)
-    late_kept, late_sent = call(
-        lambda *refs: late_body(piece_in, weight_rows, *refs),
-        [(late_block, bf16), (late_block, bf16)],
-        packed, value_key,
+    piece = piece_in + piece_out
+    z_chips = owners // X_CHIPS
+    weight_block = (X_CHIPS, z_chips * piece, half_width)
+    weight_kept, weight_sent = call(
+        lambda *refs: late_body(piece_in, piece_out, weight_rows, *refs),
+        [(weight_block, bf16), (weight_block, bf16)],
+        packed, value_key, early_kept, early_sent,
         core=core, flops=1_500_000_000, moved=3_000_000,
     )
-    late = sum_along_x(pair_sum(late_kept, late_sent))
-    along_dp = sum_along_z(early, late, piece_in, piece_out, owners)
-    weight_terms = along_dp.T.reshape(chips, weight_rows, piece_in + piece_out)
+    along_x = sum_along_x(pair_sum(weight_kept, weight_sent)).reshape(z_chips, piece, half_width)
+    arrived, along_x = lax.optimization_barrier((arrived, along_x))
+    along_dp = total_of(spread(along_x, "dp", chips_along_z(owners))).astype(bf16)
+    weight_terms = along_dp.T.reshape(chips, weight_rows, piece)
     table_block = (chips, model_width // (2 * chips), table_dev)
     table_kept, table_sent = call(
         table_body, [(table_block, bf16), (table_block, bf16)], asked_row, arrived, core=core

time: 212 us -> 202 us (0.953)
  starting transfers between devices: 95.2 us -> 63.3 us
  waiting for transfers between devices: 46 us -> 65 us
    ppermute x13 -> x3, starting transfers between devices: 44.3 us -> 9.32 us  [sum_along_x(): own = own + lax.ppermute(piece, 'dp', route).astype(f32)]
    ppermute x13 -> x3, waiting for transfers between devices: 10.3 us -> 21.3 us  [sum_along_x(): own = own + lax.ppermute(piece, 'dp', route).astype(f32)]
    all_to_all x0 -> x1, waiting for transfers between devices: none -> 8.17 us  [spread(): lax.all_to_all(block, axis, split_axis=0, concat_axis=0, tiled=True, axis...]
    all_to_all x0 -> x1, starting transfers between devices: none -> 5.36 us  [spread(): lax.all_to_all(block, axis, split_axis=0, concat_axis=0, tiled=True, axis...]
    ppermute x3 -> x2, starting transfers between devices: 8.95 us -> 5.14 us  [pair_sum(): got = lax.ppermute(sent, 'ctx', [(i, i ^ 1) for i in range(devices)])]
    unnamed x15 -> x19, local copies, waits for them, and re-layouts: 3.99 us -> 6.65 us
  transfers between devices with their start and end apart: 32 -> 22, of which waited for: 10 -> 10; matrix products, arithmetic and copies ran while one was open for 2% -> 2% of each run, Pallas kernels for 4% -> 3%
where the time goes in v5:
time: 202 us; the launch traced here: 200 us
  waiting for transfers between devices  65 us (32%)
  starting transfers between devices  63.3 us (31%)
  blocking collectives  40.5 us (20%)
  Pallas kernels  18.3 us (9%)
  local copies, waits for them, and re-layouts  8.14 us (4%)
  other arithmetic  3.72 us (2%)
    all_to_all x1, waiting for transfers between devices, local(): lax.all_to_all(found.reshape(owners, capacity, model_width), 'dp', split_...  25.2 us
    all_to_all x1, blocking collectives, local(): lax.all_to_all(requests, 'dp', split_axis=0, concat_axis=0, tiled=True)  22.1 us
    ppermute x3, waiting for transfers between devices, sum_along_x(): own = own + lax.ppermute(piece, 'dp', route).astype(f32)  21.3 us
    ppermute x8, starting transfers between devices, swapped(): lax.ppermute(block, 'ctx', [(i, i ^ 1) for i in devices if i % 2 in sende...  20.5 us
    all_to_all x1, blocking collectives, spread(): lax.all_to_all(block, axis, split_axis=0, concat_axis=0, tiled=True, axis...  18.4 us
    pallas_call x10, Pallas kernels, call(): pl.pallas_call(body, out_shape=[jax.ShapeDtypeStruct(shape, kind) for sha...  18.3 us
    ppermute x6, starting transfers between devices, passed_along(): return lax.ppermute(block, axis, route)  13.7 us
    ppermute x3, starting transfers between devices, sum_along_x(): own = own + lax.ppermute(piece, 'dp', route).astype(f32)  9.32 us
  transfers between devices with their start and end apart: 22, of which 10 were waited for; matrix products, arithmetic and copies ran while one was open for 2% of the time, Pallas kernels for 3%

profile of v5, /device:TPU:1, one launch (start us, length us, event | category | flops | bytes accessed | tf_op | source)
XLA Modules:
  0.0 200.1 jit_solution(5784263924389435535)
XLA Ops:
  1.9 22.1 %all_to_all.31 = s32[32,1,32]{2,1,0:T(1,128)S(1)} all-to-all(s32[32,1,32]{2,1,0:T(1,128)S(1)} %bitcast.29), channel_id=1, replica_groups=mesh['dp'=32,'ctx'=16] {'dp'}, dimensions={0} | all-to-all | bytes 8192 | tf_op jit(solution)/shard_map/all_to_all | solution.py:486
  25.1 1.9 shard_map.94
  27.0 4.1 %all-to-all-start.1 = ((bf16[32,32,512]{2,1,0:T(8,128)(2,1)}), bf16[32,32,512]{2,1,0:T(8,128)(2,1)S(1)}, u32[]{:S(2)}, u32[]{:S(2)}) async-start(bf16[32,32,512]{2,1,0:T(8,128)(2,1)} %bitcast.5), calls=%async_computation.1 | async-start | bytes 2097152 | tf_op jit(solution)/shard_map/all_to_all | solution.py:490
  31.1 25.2 %all-to-all-done.1 = bf16[32,32,512]{2,1,0:T(8,128)(2,1)S(1)} async-done(((bf16[32,32,512]{2,1,0:T(8,128)(2,1)}), bf16[32,32,512]{2,1,0:T(8,128)(2,1)S(1)}, u32[]{:S(2)}, u32[]{:S(2)}) %all-to-all-start.1) | async-done | bytes 1048608 | tf_op jit(solution)/shard_map/all_to_all | solution.py:490
  56.8 4.2 %collective-permute-start = (bf16[144,512]{1,0:T(8,128)(2,1)S(1)}, bf16[144,512]{1,0:T(8,128)(2,1)S(1)}, u32[]{:S(2)}, u32[]{:S(2)}) collective-permute-start(bf16[144,512]{1,0:T(8,128)(2,1)S(1)} %get-tuple-element.57.packed_ref.refs_1_), channel_id=1, source_target_pairs={{0,4},{1,5},{2,6},{3,7},{4,8},{5,9},{6,10},{7,11},{8,12},{9,13},{1... | collective-permute-start | bytes 442376 | tf_op jit(solution)/shard_map/ppermute | solution.py:24
  63.7 6.3 %collective-permute-start.3 = (bf16[144,512]{1,0:T(8,128)(2,1)S(1)}, bf16[144,512]{1,0:T(8,128)(2,1)S(1)}, u32[]{:S(2)}, u32[]{:S(2)}) collective-permute-start(bf16[144,512]{1,0:T(8,128)(2,1)S(1)} %get-tuple-element.57.packed_ref.refs_1_), channel_id=1, source_target_pairs={{0,1},{1,0},{2,3},{3,2},{4,5},{5,4},{6,7},{7,6},{8,9},{9,8},{10,11... | collective-permute-start | bytes 442376 | tf_op jit(solution)/shard_map/ppermute | solution.py:29
  70.0 4.3 %collective-permute-start.5 = (bf16[144,512]{1,0:T(8,128)(2,1)S(1)}, bf16[144,512]{1,0:T(8,128)(2,1)S(1)}, u32[]{:S(2)}, u32[]{:S(2)}) collective-permute-start(bf16[144,512]{1,0:T(8,128)(2,1)S(1)} %get-tuple-element.57.packed_ref.refs_1_), channel_id=1, source_target_pairs={{0,2},{1,3},{2,4},{3,5},{4,6},{5,7},{6,8},{7,9},{8,10},{9,11},{10,... | collective-permute-start | bytes 442376 | tf_op jit(solution)/shard_map/ppermute | solution.py:24
  76.6 2.2 %collective-permute-start.4 = (bf16[144,512]{1,0:T(8,128)(2,1)S(1)}, bf16[144,512]{1,0:T(8,128)(2,1)S(1)}, u32[]{:S(2)}, u32[]{:S(2)}) collective-permute-start(bf16[144,512]{1,0:T(8,128)(2,1)S(1)} %collective-permute-done.four_ref), channel_id=1, source_target_pairs={{1,0},{3,2},{5,4},{7,6},{9,8},{11,10},{13,12},{15,14},{17,16},{19,... | collective-permute-start | bytes 442376 | tf_op jit(solution)/shard_map/ppermute | solution.py:29
  80.1 3.0 %collective-permute-start.6 = (bf16[144,512]{1,0:T(8,128)(2,1)S(1)}, bf16[144,512]{1,0:T(8,128)(2,1)S(1)}, u32[]{:S(2)}, u32[]{:S(2)}) collective-permute-start(bf16[144,512]{1,0:T(8,128)(2,1)S(1)} %collective-permute-done.5.two_ref), channel_id=1, source_target_pairs={{0,1},{1,0},{2,3},{3,2},{4,5},{5,4},{6,7},{7,6},{8,9},{9,8},{10,11... | collective-permute-start | bytes 442376 | tf_op jit(solution)/shard_map/ppermute | solution.py:29
  83.2 1.9 collective-permute-start.8
  86.4 1.6 copy-done.2
  88.0 3.1 %shard_map.97 = (bf16[128,512]{1,0:T(8,128)(2,1)}, bf16[128,512]{1,0:T(8,128)(2,1)S(1)}, f32[128,512]{1,0:T(8,128)S(1)}, bf16[128,512]{1,0:T(8,128)(2,1)S(1)}, b...) custom-call(s32[1]{0:T(128)} %bitcast.core_ref.refs_0_, ...), custom_call_target="tpu_custom_call" | custom-call | flops 4000000000 | bytes 8000000 | tf_op jit(solution)/shard_map/pallas_call | solution.py:128
  91.1 2.0 %collective-permute-start.9 = (bf16[128,512]{1,0:T(8,128)(2,1)S(1)}, bf16[128,512]{1,0:T(8,128)(2,1)S(1)}, u32[]{:S(2)}, u32[]{:S(2)}) collective-permute-start(bf16[128,512]{1,0:T(8,128)(2,1)S(1)} %get-tuple-element.75.att_grad_ref), channel_id=1, source_target_pairs={{1,0},{3,2},{5,4},{7,6},{9,8},{11,10},{13,12},{15,14},{17,16},{19,... | collective-permute-start | bytes 393224 | tf_op jit(solution)/shard_map/ppermute | solution.py:29
  95.8 5.3 %collective-permute-done.10.two_ref = bf16[128,512]{1,0:T(8,128)(2,1)S(1)} collective-permute-done((bf16[128,512]{1,0:T(8,128)(2,1)S(1)}, bf16[128,512]{1,0:T(8,128)(2,1)S(1)}, u32[]{:S(2)}, u32[]{:S(2)}) %collective-permute-start.10) | collective-permute-done | bytes 131104 | tf_op jit(solution)/shard_map/ppermute | solution.py:24
  101.1 2.2 %collective-permute-start.12 = (bf16[128,512]{1,0:T(8,128)(2,1)S(1)}, bf16[128,512]{1,0:T(8,128)(2,1)S(1)}, u32[]{:S(2)}, u32[]{:S(2)}) collective-permute-start(bf16[128,512]{1,0:T(8,128)(2,1)S(1)} %collective-permute-done.10.two_ref), channel_id=1, source_target_pairs={{0,1},{1,0},{2,3},{3,2},{4,5},{5,4},{6,7},{7,6},{8,9},{9,8},{10,11... | collective-permute-start | bytes 393224 | tf_op jit(solution)/shard_map/ppermute | solution.py:29
  103.3 2.9 %shard_map.98 = (bf16[128,1024]{1,0:T(8,128)(2,1)S(1)}, f32[128,1024]{1,0:T(8,128)S(1)}, bf16[640,512]{1,0:T(8,128)(2,1)S(1)}, f32[640,1]{1,0:T(8,128)S(1)}) custom-call(s32[1]{0:T(128)} %bitcast.core_ref.refs_0_, bf16[128,512]{1,0:T(8,128)(2,1)S(1)} %get-tuple-element.67.queries_ref, bf16[640,512]{1,0:T(8,128)(2,1)S(1)} %get-tuple-element.73.all_keys_ref, ...), custom_call_target="tpu_custom_call" | custom-call | flops 4000000000 | bytes 8000000 | tf_op jit(solution)/shard_map/pallas_call | solution.py:128
  106.2 1.9 collective-permute-done.11.four_ref
  111.4 4.9 %shard_map.100 = (bf16[128,1024]{1,0:T(8,128)(2,1)S(1)}, bf16[1024,512]{1,0:T(8,128)(2,1)}) custom-call(s32[1]{0:T(128)} %bitcast.core_ref.refs_0_, bf16[640,512]{1,0:T(8,128)(2,1)S(1)} %get-tuple-element.81.all_queries_ref, f32[640,1]{1,0:T(8,128)S(1)} %get-tuple-element.82.query_user_ref, bf16[128,512]{1,0:T(8,128)(2,1)S(1)} %get-tuple-element.75.att_grad_ref, ...), custom_call_target="tpu_custom_call" | custom-call | flops 4000000000 | bytes 8000000 | tf_op jit(solution)/shard_map/pallas_call | solution.py:128
  116.3 1.8 shard_map.101
  118.1 2.4 %collective-permute-start.14 = (bf16[4,640,256]{2,1,0:T(8,128)(2,1)}, bf16[4,640,256]{2,1,0:T(8,128)(2,1)}, u32[]{:S(2)}, u32[]{:S(2)}) collective-permute-start(bf16[4,640,256]{2,1,0:T(8,128)(2,1)} %get-tuple-element.99), channel_id=1, source_target_pairs={{0,1},{1,0},{2,3},{3,2},{4,5},{5,4},{6,7},{7,6},{8,9},{9,8},{10,11... | collective-permute-start | bytes 3932168 | tf_op jit(solution)/shard_map/ppermute | solution.py:429
  120.5 5.3 %all-to-all-start.2 = ((bf16[32,32,512]{2,1,0:T(8,128)(2,1)}), bf16[32,32,512]{2,1,0:T(8,128)(2,1)S(1)}, u32[]{:S(2)}, u32[]{:S(2)}) async-start(bf16[32,32,512]{2,1,0:T(8,128)(2,1)} %bitcast.9), calls=%async_computation.2 | async-start | bytes 2097152 | tf_op jit(solution)/shard_map/all_to_all | solution.py:556
  125.9 1.6 add_convert_fusion
  128.7 4.3 %collective-permute-start.17 = (bf16[640,256]{1,0:T(8,128)(2,1)S(1)}, bf16[640,256]{1,0:T(8,128)(2,1)S(1)}, u32[]{:S(2)}, u32[]{:S(2)}) collective-permute-start(bf16[640,256]{1,0:T(8,128)(2,1)S(1)} %get-tuple-element.113), channel_id=1, source_target_pairs={{0,48},{16,0},{32,16},{48,32},{64,112},{80,64},{96,80},{112,96},{1... | collective-permute-start | bytes 983048 | tf_op jit(solution)/shard_map/ppermute | solution.py:455
  133.0 2.5 %collective-permute-start.16 = (bf16[640,256]{1,0:T(8,128)(2,1)S(1)}, bf16[640,256]{1,0:T(8,128)(2,1)S(1)}, u32[]{:S(2)}, u32[]{:S(2)}) collective-permute-start(bf16[640,256]{1,0:T(8,128)(2,1)S(1)} %get-tuple-element.114), channel_id=1, source_target_pairs={{0,32},{16,48},{32,0},{48,16},{64,96},{80,112},{96,64},{112,80},{1... | collective-permute-start | bytes 983048 | tf_op jit(solution)/shard_map/ppermute | solution.py:455
  135.5 2.5 %collective-permute-start.15 = (bf16[640,256]{1,0:T(8,128)(2,1)S(1)}, bf16[640,256]{1,0:T(8,128)(2,1)S(1)}, u32[]{:S(2)}, u32[]{:S(2)}) collective-permute-start(bf16[640,256]{1,0:T(8,128)(2,1)S(1)} %get-tuple-element.112), channel_id=1, source_target_pairs={{0,16},{16,32},{32,48},{48,0},{64,80},{80,96},{96,112},{112,64},{1... | collective-permute-start | bytes 983048 | tf_op jit(solution)/shard_map/ppermute | solution.py:455
  138.0 12.6 %collective-permute-done.17 = bf16[640,256]{1,0:T(8,128)(2,1)S(1)} collective-permute-done((bf16[640,256]{1,0:T(8,128)(2,1)S(1)}, bf16[640,256]{1,0:T(8,128)(2,1)S(1)}, u32[]{:S(2)}, u32[]{:S(2)}) %collective-permute-start.17) | collective-permute-done | bytes 327712 | tf_op jit(solution)/shard_map/ppermute | solution.py:455
  151.1 8.2 %collective-permute-done.15 = bf16[640,256]{1,0:T(8,128)(2,1)S(1)} collective-permute-done((bf16[640,256]{1,0:T(8,128)(2,1)S(1)}, bf16[640,256]{1,0:T(8,128)(2,1)S(1)}, u32[]{:S(2)}, u32[]{:S(2)}) %collective-permute-start.15) | collective-permute-done | bytes 327712 | tf_op jit(solution)/shard_map/ppermute | solution.py:455
  159.3 1.9 fusion.2
  161.2 5.4 %all-to-all-start.3 = ((bf16[8,80,256]{2,1,0:T(8,128)(2,1)}), bf16[8,80,256]{2,1,0:T(8,128)(2,1)S(1)}, u32[]{:S(2)}, u32[]{:S(2)}) async-start(bf16[8,80,256]{2,1,0:T(8,128)(2,1)} %bitcast.15), calls=%async_computation.3 | async-start | bytes 655360 | tf_op jit(solution)/shard_map/all_to_all | solution.py:439
  167.3 2.7 %collective-permute-start.18 = (bf16[8,32,512]{2,1,0:T(8,128)(2,1)S(1)}, bf16[8,32,512]{2,1,0:T(8,128)(2,1)S(1)}, u32[]{:S(2)}, u32[]{:S(2)}) collective-permute-start(bf16[8,32,512]{2,1,0:T(8,128)(2,1)S(1)} %get-tuple-element.102), channel_id=1, source_target_pairs={{0,1},{1,0},{2,3},{3,2},{4,5},{5,4},{6,7},{7,6},{8,9},{9,8},{10,11... | collective-permute-start | bytes 786440 | tf_op jit(solution)/shard_map/ppermute | solution.py:429
  171.3 8.2 %all-to-all-done.3 = bf16[8,80,256]{2,1,0:T(8,128)(2,1)S(1)} async-done(((bf16[8,80,256]{2,1,0:T(8,128)(2,1)}), bf16[8,80,256]{2,1,0:T(8,128)(2,1)S(1)}, u32[]{:S(2)}, u32[]{:S(2)}) %all-to-all-start.3) | async-done | bytes 327712 | tf_op jit(solution)/shard_map/all_to_all | solution.py:439
  179.7 18.4 %all_to_all.32 = bf16[8,32,592]{2,1,0:T(8,128)(2,1)S(1)} all-to-all(bf16[8,32,592]{2,1,0:T(8,128)(2,1)S(1)} %pad_maximum_fusion), channel_id=1, replica_groups={{0,2,4,6,8,10,12,14},{1,3,5,7,9,11,13,15},{16,18,20,22,24,26,28,30},{17..., dimensions={0} | all-to-all | bytes 606208 | tf_op jit(solution)/shard_map/all_to_all | solution.py:439
  (55 shorter events, 22.0 us)
Async XLA Ops:
  0.6 0.7 copy-start.6
  24.0 1.0 copy-start
  25.1 6.0 %copy-start.8 = (s32[1,128]{1,0:T(1,128)S(1)}, s32[1,128]{1,0:T(1,128)}, u32[]{:S(2)}) copy-start(s32[1,128]{1,0:T(1,128)} %param.7) | copy-start | bytes 1540
  27.0 47.3 %copy-start.4 = (bf16[512,512]{1,0:T(8,128)(2,1)S(1)}, bf16[512,512]{1,0:T(8,128)(2,1)}, u32[]{:S(2)}) copy-start(bf16[512,512]{1,0:T(8,128)(2,1)} %w_out_ref.3) | copy-start | bytes 1572868
  27.0 47.3 %copy-start.5 = (bf16[1,128,512]{2,1,0:T(8,128)(2,1)S(1)}, bf16[1,128,512]{2,1,0:T(8,128)(2,1)}, u32[]{:S(2)}) copy-start(bf16[1,128,512]{2,1,0:T(8,128)(2,1)} %param.11) | copy-start | bytes 393220
  27.0 29.3 %all-to-all-start.1 = ((bf16[32,32,512]{2,1,0:T(8,128)(2,1)}), bf16[32,32,512]{2,1,0:T(8,128)(2,1)S(1)}, u32[]{:S(2)}, u32[]{:S(2)}) async-start(bf16[32,32,512]{2,1,0:T(8,128)(2,1)} %bitcast.5), calls=%async_computation.1 | async-start | bytes 2097152 | tf_op jit(solution)/shard_map/all_to_all | solution.py:490
  56.8 19.7 %collective-permute-start = (bf16[144,512]{1,0:T(8,128)(2,1)S(1)}, bf16[144,512]{1,0:T(8,128)(2,1)S(1)}, u32[]{:S(2)}, u32[]{:S(2)}) collective-permute-start(bf16[144,512]{1,0:T(8,128)(2,1)S(1)} %get-tuple-element.57.packed_ref.refs_1_), channel_id=1, source_target_pairs={{0,4},{1,5},{2,6},{3,7},{4,8},{5,9},{6,10},{7,11},{8,12},{9,13},{1... | collective-permute-start | bytes 442376 | tf_op jit(solution)/shard_map/ppermute | solution.py:24
  61.1 15.5 %collective-permute-start.1 = (bf16[144,512]{1,0:T(8,128)(2,1)S(1)}, bf16[144,512]{1,0:T(8,128)(2,1)S(1)}, u32[]{:S(2)}, u32[]{:S(2)}) collective-permute-start(bf16[144,512]{1,0:T(8,128)(2,1)S(1)} %get-tuple-element.57.packed_ref.refs_1_), channel_id=1, source_target_pairs={{4,0},{5,1},{6,2},{7,3},{8,4},{9,5},{10,6},{11,7},{12,8},{13,9},{1... | collective-permute-start | bytes 442376 | tf_op jit(solution)/shard_map/ppermute | solution.py:24
  62.4 14.2 %collective-permute-start.2 = (bf16[144,512]{1,0:T(8,128)(2,1)S(1)}, bf16[144,512]{1,0:T(8,128)(2,1)S(1)}, u32[]{:S(2)}, u32[]{:S(2)}) collective-permute-start(bf16[144,512]{1,0:T(8,128)(2,1)S(1)} %get-tuple-element.57.packed_ref.refs_1_), channel_id=1, source_target_pairs={{2,0},{3,1},{4,2},{5,3},{6,4},{7,5},{8,6},{9,7},{10,8},{11,9},{12,... | collective-permute-start | bytes 442376 | tf_op jit(solution)/shard_map/ppermute | solution.py:24
  63.7 12.9 %collective-permute-start.3 = (bf16[144,512]{1,0:T(8,128)(2,1)S(1)}, bf16[144,512]{1,0:T(8,128)(2,1)S(1)}, u32[]{:S(2)}, u32[]{:S(2)}) collective-permute-start(bf16[144,512]{1,0:T(8,128)(2,1)S(1)} %get-tuple-element.57.packed_ref.refs_1_), channel_id=1, source_target_pairs={{0,1},{1,0},{2,3},{3,2},{4,5},{5,4},{6,7},{7,6},{8,9},{9,8},{10,11... | collective-permute-start | bytes 442376 | tf_op jit(solution)/shard_map/ppermute | solution.py:29
  70.0 10.1 %collective-permute-start.5 = (bf16[144,512]{1,0:T(8,128)(2,1)S(1)}, bf16[144,512]{1,0:T(8,128)(2,1)S(1)}, u32[]{:S(2)}, u32[]{:S(2)}) collective-permute-start(bf16[144,512]{1,0:T(8,128)(2,1)S(1)} %get-tuple-element.57.packed_ref.refs_1_), channel_id=1, source_target_pairs={{0,2},{1,3},{2,4},{3,5},{4,6},{5,7},{6,8},{7,9},{8,10},{9,11},{10,... | collective-permute-start | bytes 442376 | tf_op jit(solution)/shard_map/ppermute | solution.py:24
  74.3 1.6 copy-start.1
  76.6 8.5 %collective-permute-start.4 = (bf16[144,512]{1,0:T(8,128)(2,1)S(1)}, bf16[144,512]{1,0:T(8,128)(2,1)S(1)}, u32[]{:S(2)}, u32[]{:S(2)}) collective-permute-start(bf16[144,512]{1,0:T(8,128)(2,1)S(1)} %collective-permute-done.four_ref), channel_id=1, source_target_pairs={{1,0},{3,2},{5,4},{7,6},{9,8},{11,10},{13,12},{15,14},{17,16},{19,... | collective-permute-start | bytes 442376 | tf_op jit(solution)/shard_map/ppermute | solution.py:29
  78.8 6.3 %collective-permute-start.7 = (bf16[144,512]{1,0:T(8,128)(2,1)S(1)}, bf16[144,512]{1,0:T(8,128)(2,1)S(1)}, u32[]{:S(2)}, u32[]{:S(2)}) collective-permute-start(bf16[144,512]{1,0:T(8,128)(2,1)S(1)} %collective-permute-done.1.four_ref), channel_id=1, source_target_pairs={{0,1},{2,3},{4,5},{6,7},{8,9},{10,11},{12,13},{14,15},{16,17},{18,... | collective-permute-start | bytes 442376 | tf_op jit(solution)/shard_map/ppermute | solution.py:29
  80.1 5.0 %collective-permute-start.6 = (bf16[144,512]{1,0:T(8,128)(2,1)S(1)}, bf16[144,512]{1,0:T(8,128)(2,1)S(1)}, u32[]{:S(2)}, u32[]{:S(2)}) collective-permute-start(bf16[144,512]{1,0:T(8,128)(2,1)S(1)} %collective-permute-done.5.two_ref), channel_id=1, source_target_pairs={{0,1},{1,0},{2,3},{3,2},{4,5},{5,4},{6,7},{7,6},{8,9},{9,8},{10,11... | collective-permute-start | bytes 442376 | tf_op jit(solution)/shard_map/ppermute | solution.py:29
  83.2 3.3 %collective-permute-start.8 = (bf16[144,512]{1,0:T(8,128)(2,1)S(1)}, bf16[144,512]{1,0:T(8,128)(2,1)S(1)}, u32[]{:S(2)}, u32[]{:S(2)}) collective-permute-start(bf16[144,512]{1,0:T(8,128)(2,1)S(1)} %collective-permute-done.2.two_ref), channel_id=1, source_target_pairs={{0,1},{1,0},{2,3},{3,2},{4,5},{5,4},{6,7},{7,6},{8,9},{9,8},{10,11... | collective-permute-start | bytes 442376 | tf_op jit(solution)/shard_map/ppermute | solution.py:29
  86.4 1.6 copy-start.2
  88.0 15.3 %copy-start.3 = (bf16[512,2048]{1,0:T(8,128)(2,1)S(1)}, bf16[512,2048]{1,0:T(8,128)(2,1)}, u32[]{:S(2)}) copy-start(bf16[512,2048]{1,0:T(8,128)(2,1)} %w_in_ref.7) | copy-start | bytes 6291460
  91.1 4.6 %collective-permute-start.9 = (bf16[128,512]{1,0:T(8,128)(2,1)S(1)}, bf16[128,512]{1,0:T(8,128)(2,1)S(1)}, u32[]{:S(2)}, u32[]{:S(2)}) collective-permute-start(bf16[128,512]{1,0:T(8,128)(2,1)S(1)} %get-tuple-element.75.att_grad_ref), channel_id=1, source_target_pairs={{1,0},{3,2},{5,4},{7,6},{9,8},{11,10},{13,12},{15,14},{17,16},{19,... | collective-permute-start | bytes 393224 | tf_op jit(solution)/shard_map/ppermute | solution.py:29
  93.2 7.9 %collective-permute-start.10 = (bf16[128,512]{1,0:T(8,128)(2,1)S(1)}, bf16[128,512]{1,0:T(8,128)(2,1)S(1)}, u32[]{:S(2)}, u32[]{:S(2)}) collective-permute-start(bf16[128,512]{1,0:T(8,128)(2,1)S(1)} %get-tuple-element.75.att_grad_ref), channel_id=1, source_target_pairs={{2,0},{3,1},{4,2},{5,3},{6,4},{7,5},{8,6},{9,7},{10,8},{11,9},{12,... | collective-permute-start | bytes 393224 | tf_op jit(solution)/shard_map/ppermute | solution.py:24
  94.5 13.7 %collective-permute-start.11 = (bf16[128,512]{1,0:T(8,128)(2,1)S(1)}, bf16[128,512]{1,0:T(8,128)(2,1)S(1)}, u32[]{:S(2)}, u32[]{:S(2)}) collective-permute-start(bf16[128,512]{1,0:T(8,128)(2,1)S(1)} %get-tuple-element.75.att_grad_ref), channel_id=1, source_target_pairs={{4,0},{5,1},{6,2},{7,3},{8,4},{9,5},{10,6},{11,7},{12,8},{13,9},{1... | collective-permute-start | bytes 393224 | tf_op jit(solution)/shard_map/ppermute | solution.py:24
  101.1 8.5 %collective-permute-start.12 = (bf16[128,512]{1,0:T(8,128)(2,1)S(1)}, bf16[128,512]{1,0:T(8,128)(2,1)S(1)}, u32[]{:S(2)}, u32[]{:S(2)}) collective-permute-start(bf16[128,512]{1,0:T(8,128)(2,1)S(1)} %collective-permute-done.10.two_ref), channel_id=1, source_target_pairs={{0,1},{1,0},{2,3},{3,2},{4,5},{5,4},{6,7},{7,6},{8,9},{9,8},{10,11... | collective-permute-start | bytes 393224 | tf_op jit(solution)/shard_map/ppermute | solution.py:29
  108.1 3.2 %collective-permute-start.13 = (bf16[128,512]{1,0:T(8,128)(2,1)S(1)}, bf16[128,512]{1,0:T(8,128)(2,1)S(1)}, u32[]{:S(2)}, u32[]{:S(2)}) collective-permute-start(bf16[128,512]{1,0:T(8,128)(2,1)S(1)} %collective-permute-done.11.four_ref), channel_id=1, source_target_pairs={{0,1},{2,3},{4,5},{6,7},{8,9},{10,11},{12,13},{14,15},{16,17},{18,... | collective-permute-start | bytes 393224 | tf_op jit(solution)/shard_map/ppermute | solution.py:29
  118.1 7.8 %collective-permute-start.14 = (bf16[4,640,256]{2,1,0:T(8,128)(2,1)}, bf16[4,640,256]{2,1,0:T(8,128)(2,1)}, u32[]{:S(2)}, u32[]{:S(2)}) collective-permute-start(bf16[4,640,256]{2,1,0:T(8,128)(2,1)} %get-tuple-element.99), channel_id=1, source_target_pairs={{0,1},{1,0},{2,3},{3,2},{4,5},{5,4},{6,7},{7,6},{8,9},{9,8},{10,11... | collective-permute-start | bytes 3932168 | tf_op jit(solution)/shard_map/ppermute | solution.py:429
  120.5 40.7 %all-to-all-start.2 = ((bf16[32,32,512]{2,1,0:T(8,128)(2,1)}), bf16[32,32,512]{2,1,0:T(8,128)(2,1)S(1)}, u32[]{:S(2)}, u32[]{:S(2)}) async-start(bf16[32,32,512]{2,1,0:T(8,128)(2,1)} %bitcast.9), calls=%async_computation.2 | async-start | bytes 2097152 | tf_op jit(solution)/shard_map/all_to_all | solution.py:556
  127.5 1.1 copy-start.7
  128.7 22.0 %collective-permute-start.17 = (bf16[640,256]{1,0:T(8,128)(2,1)S(1)}, bf16[640,256]{1,0:T(8,128)(2,1)S(1)}, u32[]{:S(2)}, u32[]{:S(2)}) collective-permute-start(bf16[640,256]{1,0:T(8,128)(2,1)S(1)} %get-tuple-element.113), channel_id=1, source_target_pairs={{0,48},{16,0},{32,16},{48,32},{64,112},{80,64},{96,80},{112,96},{1... | collective-permute-start | bytes 983048 | tf_op jit(solution)/shard_map/ppermute | solution.py:455
  133.0 18.1 %collective-permute-start.16 = (bf16[640,256]{1,0:T(8,128)(2,1)S(1)}, bf16[640,256]{1,0:T(8,128)(2,1)S(1)}, u32[]{:S(2)}, u32[]{:S(2)}) collective-permute-start(bf16[640,256]{1,0:T(8,128)(2,1)S(1)} %get-tuple-element.114), channel_id=1, source_target_pairs={{0,32},{16,48},{32,0},{48,16},{64,96},{80,112},{96,64},{112,80},{1... | collective-permute-start | bytes 983048 | tf_op jit(solution)/shard_map/ppermute | solution.py:455
  135.5 23.8 %collective-permute-start.15 = (bf16[640,256]{1,0:T(8,128)(2,1)S(1)}, bf16[640,256]{1,0:T(8,128)(2,1)S(1)}, u32[]{:S(2)}, u32[]{:S(2)}) collective-permute-start(bf16[640,256]{1,0:T(8,128)(2,1)S(1)} %get-tuple-element.112), channel_id=1, source_target_pairs={{0,16},{16,32},{32,48},{48,0},{64,80},{80,96},{96,112},{112,64},{1... | collective-permute-start | bytes 983048 | tf_op jit(solution)/shard_map/ppermute | solution.py:455
  161.2 18.3 %all-to-all-start.3 = ((bf16[8,80,256]{2,1,0:T(8,128)(2,1)}), bf16[8,80,256]{2,1,0:T(8,128)(2,1)S(1)}, u32[]{:S(2)}, u32[]{:S(2)}) async-start(bf16[8,80,256]{2,1,0:T(8,128)(2,1)} %bitcast.15), calls=%async_computation.3 | async-start | bytes 655360 | tf_op jit(solution)/shard_map/all_to_all | solution.py:439
  167.3 3.9 %collective-permute-start.18 = (bf16[8,32,512]{2,1,0:T(8,128)(2,1)S(1)}, bf16[8,32,512]{2,1,0:T(8,128)(2,1)S(1)}, u32[]{:S(2)}, u32[]{:S(2)}) collective-permute-start(bf16[8,32,512]{2,1,0:T(8,128)(2,1)S(1)} %get-tuple-element.102), channel_id=1, source_target_pairs={{0,1},{1,0},{2,3},{3,2},{4,5},{5,4},{6,7},{7,6},{8,9},{9,8},{10,11... | collective-permute-start | bytes 786440 | tf_op jit(solution)/shard_map/ppermute | solution.py:429

commit v6 on v5

--- a/solution.py
+++ b/solution.py
@@ -29,16 +29,8 @@
     return lax.ppermute(block, "ctx", [(i, i ^ 1) for i in devices if i % 2 in senders])
 
 
-def halo_across(block, direction):
-    return (
-        passed_along(block, "ctx", 4 * direction),
-        passed_along(block, "ctx", 2 * direction),
-    )
-
-
-def halo_inside(four, two, direction):
-    far_sender = 1 if direction > 0 else 0
-    return (swapped(four, (far_sender,)), swapped(two))
+def mate_of_four(four, direction):
+    return swapped(four, (1,) if direction > 0 else (0,))
 
 
 def nearest_last(core, four, mate_four, two, mate_two, mate_own):
@@ -493,9 +485,7 @@
     inputs, packed = call(
         embed_body, [(block, bf16), (packed_block, bf16)], slot, fetched, user
     )
-    mate_own = swapped(packed)
-    earlier_four, earlier_two = halo_across(packed, 1)
-    later_four, later_two = halo_across(packed, -1)
+    earlier_two = passed_along(packed, "ctx", 2)
     gates, values, queries, keys, mixed_grad = call(
         project_body,
         [
@@ -504,13 +494,19 @@
         packed, w_in, w_out, grad_rows,
         flops=1_500_000_000, moved=6_000_000,
     )
-    earlier_four, later_four, later_two, mate_own, mixed_grad = lax.optimization_barrier(
-        (earlier_four, later_four, later_two, mate_own, mixed_grad)
-    )
-    inside = halo_inside(earlier_four, earlier_two, 1) + halo_inside(later_four, later_two, -1)
-    mate_four, mate_two, later_mate_four, later_mate_two = lax.optimization_barrier(inside)
+    packed_later, mixed_grad = lax.optimization_barrier((packed, mixed_grad))
+    mate_own = swapped(packed_later)
+    later_two = passed_along(packed_later, "ctx", -2)
+    earlier_two, mixed_grad = lax.optimization_barrier((earlier_two, mixed_grad))
+    earlier_four = passed_along(earlier_two, "ctx", 2)
+    earlier_four, mate_two, mate_own = lax.optimization_barrier(
+        (earlier_four, swapped(earlier_two), mate_own)
+    )
+    mate_four, later_mate_two = lax.optimization_barrier(
+        (mate_of_four(earlier_four, 1), swapped(later_two))
+    )
     earlier = (earlier_four, mate_four, earlier_two, mate_two, mate_own)
-    later = (later_four, later_mate_four, later_two, later_mate_two, mate_own)
+    later_four = passed_along(later_two, "ctx", -2)
     layer_out, mixed, gate_grad, att_grad, all_keys, all_values, key_user = call(
         forward_body,
         [
@@ -521,11 +517,12 @@
         core=core, flops=4_000_000_000, moved=8_000_000,
     )
     own_grad = swapped(att_grad, (1,))
-    grad_four, grad_two = halo_across(att_grad, -1)
-    grad_mate_four, grad_mate_two = halo_inside(grad_four, grad_two, -1)
-    gate_grad, own_grad, grad_two = lax.optimization_barrier((gate_grad, own_grad, grad_two))
-    mixed, grad_four, grad_mate_two = lax.optimization_barrier((mixed, grad_four, grad_mate_two))
-    later_grads = (grad_four, grad_mate_four, grad_two, grad_mate_two, own_grad)
+    grad_two = passed_along(att_grad, "ctx", -2)
+    grad_four = passed_along(grad_two, "ctx", -2)
+    later_four, own_grad = lax.optimization_barrier((later_four, own_grad))
+    later = (later_four, mate_of_four(later_four, -1), later_two, later_mate_two, mate_own)
+    grad_mate_two = swapped(grad_two)
+    gate_grad, own_grad, grad_mate_two = lax.optimization_barrier((gate_grad, own_grad, grad_mate_two))
     gate_query, value_key_slope, all_queries, query_user = call(
         query_body,
         [
@@ -534,6 +531,10 @@
         ],
         queries, all_keys, all_values, att_grad, gate_grad, packed, user, key_user, *later, w_in,
         core=core, flops=4_000_000_000, moved=8_000_000,
+    )
+    gate_query, mixed, grad_four = lax.optimization_barrier((gate_query, mixed, grad_four))
+    later_grads = (
+        grad_four, mate_of_four(grad_four, -1), grad_two, grad_mate_two, own_grad,
     )
     half_width = model_width // 2
     early_block = (X_CHIPS, 3 * model_width // X_CHIPS, half_width)

time: 202 us -> 201 us (level)
  starting transfers between devices: 63.3 us -> 61.2 us
  transfers between devices with their start and end apart: 22 -> 22, of which waited for: 10 -> 9; matrix products, arithmetic and copies ran while one was open for 2% -> 2% of each run, Pallas kernels for 3% -> 4%
where the time goes in v6:
time: 201 us; the launch traced here: 199 us
  waiting for transfers between devices  64 us (32%)
  starting transfers between devices  61.2 us (30%)
  blocking collectives  42.2 us (21%)
  Pallas kernels  18.3 us (9%)
  local copies, waits for them, and re-layouts  8.14 us (4%)
  other arithmetic  3.72 us (2%)
    all_to_all x1, waiting for transfers between devices, local(): lax.all_to_all(found.reshape(owners, capacity, model_width), 'dp', split_...  25.2 us
    all_to_all x1, blocking collectives, local(): lax.all_to_all(requests, 'dp', split_axis=0, concat_axis=0, tiled=True)  22.1 us
    ppermute x3, waiting for transfers between devices, sum_along_x(): own = own + lax.ppermute(piece, 'dp', route).astype(f32)  21.3 us
    all_to_all x1, blocking collectives, spread(): lax.all_to_all(block, axis, split_axis=0, concat_axis=0, tiled=True, axis...  20.1 us
    ppermute x8, starting transfers between devices, swapped(): lax.ppermute(block, 'ctx', [(i, i ^ 1) for i in devices if i % 2 in sende...  20 us
    pallas_call x10, Pallas kernels, call(): pl.pallas_call(body, out_shape=[jax.ShapeDtypeStruct(shape, kind) for sha...  18.3 us
    ppermute x6, starting transfers between devices, passed_along(): return lax.ppermute(block, axis, route)  12.4 us
    ppermute x3, starting transfers between devices, sum_along_x(): own = own + lax.ppermute(piece, 'dp', route).astype(f32)  9.32 us
  transfers between devices with their start and end apart: 22, of which 9 were waited for; matrix products, arithmetic and copies ran while one was open for 2% of the time, Pallas kernels for 4%

profile of v6, /device:TPU:1, one launch (start us, length us, event | category | flops | bytes accessed | tf_op | source)
XLA Modules:
  0.0 198.7 jit_solution(2203886449255357096)
XLA Ops:
  1.9 22.1 %all_to_all.31 = s32[32,1,32]{2,1,0:T(1,128)S(1)} all-to-all(s32[32,1,32]{2,1,0:T(1,128)S(1)} %bitcast.29), channel_id=1, replica_groups=mesh['dp'=32,'ctx'=16] {'dp'}, dimensions={0} | all-to-all | bytes 8192 | tf_op jit(solution)/shard_map/all_to_all | solution.py:478
  25.1 1.9 shard_map.94
  27.0 4.1 %all-to-all-start.1 = ((bf16[32,32,512]{2,1,0:T(8,128)(2,1)}), bf16[32,32,512]{2,1,0:T(8,128)(2,1)S(1)}, u32[]{:S(2)}, u32[]{:S(2)}) async-start(bf16[32,32,512]{2,1,0:T(8,128)(2,1)} %bitcast.5), calls=%async_computation.1 | async-start | bytes 2097152 | tf_op jit(solution)/shard_map/all_to_all | solution.py:482
  31.1 25.2 %all-to-all-done.1 = bf16[32,32,512]{2,1,0:T(8,128)(2,1)S(1)} async-done(((bf16[32,32,512]{2,1,0:T(8,128)(2,1)}), bf16[32,32,512]{2,1,0:T(8,128)(2,1)S(1)}, u32[]{:S(2)}, u32[]{:S(2)}) %all-to-all-start.1) | async-done | bytes 1048608 | tf_op jit(solution)/shard_map/all_to_all | solution.py:482
  56.8 3.2 %collective-permute-start = (bf16[144,512]{1,0:T(8,128)(2,1)S(1)}, bf16[144,512]{1,0:T(8,128)(2,1)S(1)}, u32[]{:S(2)}, u32[]{:S(2)}) collective-permute-start(bf16[144,512]{1,0:T(8,128)(2,1)S(1)} %get-tuple-element.63.packed_ref.refs_1_), channel_id=1, source_target_pairs={{0,2},{1,3},{2,4},{3,5},{4,6},{5,7},{6,8},{7,9},{8,10},{9,11},{10,... | collective-permute-start | bytes 442376 | tf_op jit(solution)/shard_map/ppermute | solution.py:24
  60.1 1.6 copy-done.1
  62.3 6.3 %collective-permute-start.3 = (bf16[144,512]{1,0:T(8,128)(2,1)S(1)}, bf16[144,512]{1,0:T(8,128)(2,1)S(1)}, u32[]{:S(2)}, u32[]{:S(2)}) collective-permute-start(bf16[144,512]{1,0:T(8,128)(2,1)S(1)} %get-tuple-element.63.packed_ref.refs_1_), channel_id=1, source_target_pairs={{0,1},{1,0},{2,3},{3,2},{4,5},{5,4},{6,7},{7,6},{8,9},{9,8},{10,11... | collective-permute-start | bytes 442376 | tf_op jit(solution)/shard_map/ppermute | solution.py:29
  69.9 4.0 %collective-permute-start.1 = (bf16[144,512]{1,0:T(8,128)(2,1)S(1)}, bf16[144,512]{1,0:T(8,128)(2,1)S(1)}, u32[]{:S(2)}, u32[]{:S(2)}) collective-permute-start(bf16[144,512]{1,0:T(8,128)(2,1)S(1)} %collective-permute-done.two_ref), channel_id=1, source_target_pairs={{0,2},{1,3},{2,4},{3,5},{4,6},{5,7},{6,8},{7,9},{8,10},{9,11},{10,... | collective-permute-start | bytes 442376 | tf_op jit(solution)/shard_map/ppermute | solution.py:24
  73.9 2.5 %collective-permute-start.2 = (bf16[144,512]{1,0:T(8,128)(2,1)S(1)}, bf16[144,512]{1,0:T(8,128)(2,1)S(1)}, u32[]{:S(2)}, u32[]{:S(2)}) collective-permute-start(bf16[144,512]{1,0:T(8,128)(2,1)S(1)} %collective-permute-done.two_ref), channel_id=1, source_target_pairs={{0,1},{1,0},{2,3},{3,2},{4,5},{5,4},{6,7},{7,6},{8,9},{9,8},{10,11... | collective-permute-start | bytes 442376 | tf_op jit(solution)/shard_map/ppermute | solution.py:29
  76.4 2.2 %collective-permute-start.6 = (bf16[144,512]{1,0:T(8,128)(2,1)S(1)}, bf16[144,512]{1,0:T(8,128)(2,1)S(1)}, u32[]{:S(2)}, u32[]{:S(2)}) collective-permute-start(bf16[144,512]{1,0:T(8,128)(2,1)S(1)} %collective-permute-done.5.two_ref), channel_id=1, source_target_pairs={{0,1},{1,0},{2,3},{3,2},{4,5},{5,4},{6,7},{7,6},{8,9},{9,8},{10,11... | collective-permute-start | bytes 442376 | tf_op jit(solution)/shard_map/ppermute | solution.py:29
  78.7 2.1 %collective-permute-start.4 = (bf16[144,512]{1,0:T(8,128)(2,1)S(1)}, bf16[144,512]{1,0:T(8,128)(2,1)S(1)}, u32[]{:S(2)}, u32[]{:S(2)}) collective-permute-start(bf16[144,512]{1,0:T(8,128)(2,1)S(1)} %collective-permute-done.1.four_ref), channel_id=1, source_target_pairs={{1,0},{3,2},{5,4},{7,6},{9,8},{11,10},{13,12},{15,14},{17,16},{19,... | collective-permute-start | bytes 442376 | tf_op jit(solution)/shard_map/ppermute | solution.py:29
  83.7 3.1 %shard_map.97 = (bf16[128,512]{1,0:T(8,128)(2,1)}, bf16[128,512]{1,0:T(8,128)(2,1)S(1)}, f32[128,512]{1,0:T(8,128)S(1)}, bf16[128,512]{1,0:T(8,128)(2,1)S(1)}, b...) custom-call(s32[1]{0:T(128)} %bitcast.core_ref.refs_0_, ...), custom_call_target="tpu_custom_call" | custom-call | flops 4000000000 | bytes 8000000 | tf_op jit(solution)/shard_map/pallas_call | solution.py:120
  86.8 1.9 collective-permute-start.8
  91.4 4.3 %collective-permute-done.9.two_ref = bf16[128,512]{1,0:T(8,128)(2,1)S(1)} collective-permute-done((bf16[128,512]{1,0:T(8,128)(2,1)S(1)}, bf16[128,512]{1,0:T(8,128)(2,1)S(1)}, u32[]{:S(2)}, u32[]{:S(2)}) %collective-permute-start.9) | collective-permute-done | bytes 131104 | tf_op jit(solution)/shard_map/ppermute | solution.py:24
  95.7 2.2 %collective-permute-start.10 = (bf16[128,512]{1,0:T(8,128)(2,1)S(1)}, bf16[128,512]{1,0:T(8,128)(2,1)S(1)}, u32[]{:S(2)}, u32[]{:S(2)}) collective-permute-start(bf16[128,512]{1,0:T(8,128)(2,1)S(1)} %collective-permute-done.9.two_ref), channel_id=1, source_target_pairs={{0,1},{1,0},{2,3},{3,2},{4,5},{5,4},{6,7},{7,6},{8,9},{9,8},{10,11... | collective-permute-start | bytes 393224 | tf_op jit(solution)/shard_map/ppermute | solution.py:29
  99.3 2.9 %shard_map.98 = (bf16[128,1024]{1,0:T(8,128)(2,1)S(1)}, f32[128,1024]{1,0:T(8,128)S(1)}, bf16[640,512]{1,0:T(8,128)(2,1)S(1)}, f32[640,1]{1,0:T(8,128)S(1)}) custom-call(s32[1]{0:T(128)} %bitcast.core_ref.refs_0_, bf16[128,512]{1,0:T(8,128)(2,1)S(1)} %get-tuple-element.70.queries_ref, bf16[640,512]{1,0:T(8,128)(2,1)S(1)} %get-tuple-element.76.all_keys_ref, ...), custom_call_target="tpu_custom_call" | custom-call | flops 4000000000 | bytes 8000000 | tf_op jit(solution)/shard_map/pallas_call | solution.py:120
  102.1 3.2 %collective-permute-done.12.four_ref = bf16[128,512]{1,0:T(8,128)(2,1)S(1)} collective-permute-done((bf16[128,512]{1,0:T(8,128)(2,1)S(1)}, bf16[128,512]{1,0:T(8,128)(2,1)S(1)}, u32[]{:S(2)}, u32[]{:S(2)}) %collective-permute-start.12) | collective-permute-done | bytes 131104 | tf_op jit(solution)/shard_map/ppermute | solution.py:24
  108.6 4.9 %shard_map.100 = (bf16[128,1024]{1,0:T(8,128)(2,1)S(1)}, bf16[1024,512]{1,0:T(8,128)(2,1)}) custom-call(s32[1]{0:T(128)} %bitcast.core_ref.refs_0_, bf16[640,512]{1,0:T(8,128)(2,1)S(1)} %get-tuple-element.85.all_queries_ref, f32[640,1]{1,0:T(8,128)S(1)} %get-tuple-element.86.query_user_ref, bf16[128,512]{1,0:T(8,128)(2,1)S(1)} %get-tuple-element.78.att_grad_ref, ...), custom_call_target="tpu_custom_call" | custom-call | flops 4000000000 | bytes 8000000 | tf_op jit(solution)/shard_map/pallas_call | solution.py:120
  113.5 1.8 shard_map.101
  115.3 2.4 %collective-permute-start.14 = (bf16[4,640,256]{2,1,0:T(8,128)(2,1)}, bf16[4,640,256]{2,1,0:T(8,128)(2,1)}, u32[]{:S(2)}, u32[]{:S(2)}) collective-permute-start(bf16[4,640,256]{2,1,0:T(8,128)(2,1)} %get-tuple-element.103), channel_id=1, source_target_pairs={{0,1},{1,0},{2,3},{3,2},{4,5},{5,4},{6,7},{7,6},{8,9},{9,8},{10,11... | collective-permute-start | bytes 3932168 | tf_op jit(solution)/shard_map/ppermute | solution.py:421
  117.7 4.9 %all-to-all-start.2 = ((bf16[32,32,512]{2,1,0:T(8,128)(2,1)}), bf16[32,32,512]{2,1,0:T(8,128)(2,1)S(1)}, u32[]{:S(2)}, u32[]{:S(2)}) async-start(bf16[32,32,512]{2,1,0:T(8,128)(2,1)} %bitcast.9), calls=%async_computation.2 | async-start | bytes 2097152 | tf_op jit(solution)/shard_map/all_to_all | solution.py:557
  122.8 1.6 add_convert_fusion
  125.6 4.3 %collective-permute-start.17 = (bf16[640,256]{1,0:T(8,128)(2,1)S(1)}, bf16[640,256]{1,0:T(8,128)(2,1)S(1)}, u32[]{:S(2)}, u32[]{:S(2)}) collective-permute-start(bf16[640,256]{1,0:T(8,128)(2,1)S(1)} %get-tuple-element.117), channel_id=1, source_target_pairs={{0,48},{16,0},{32,16},{48,32},{64,112},{80,64},{96,80},{112,96},{1... | collective-permute-start | bytes 983048 | tf_op jit(solution)/shard_map/ppermute | solution.py:447
  129.9 2.5 %collective-permute-start.16 = (bf16[640,256]{1,0:T(8,128)(2,1)S(1)}, bf16[640,256]{1,0:T(8,128)(2,1)S(1)}, u32[]{:S(2)}, u32[]{:S(2)}) collective-permute-start(bf16[640,256]{1,0:T(8,128)(2,1)S(1)} %get-tuple-element.118), channel_id=1, source_target_pairs={{0,32},{16,48},{32,0},{48,16},{64,96},{80,112},{96,64},{112,80},{1... | collective-permute-start | bytes 983048 | tf_op jit(solution)/shard_map/ppermute | solution.py:447
  132.4 2.5 %collective-permute-start.15 = (bf16[640,256]{1,0:T(8,128)(2,1)S(1)}, bf16[640,256]{1,0:T(8,128)(2,1)S(1)}, u32[]{:S(2)}, u32[]{:S(2)}) collective-permute-start(bf16[640,256]{1,0:T(8,128)(2,1)S(1)} %get-tuple-element.116), channel_id=1, source_target_pairs={{0,16},{16,32},{32,48},{48,0},{64,80},{80,96},{96,112},{112,64},{1... | collective-permute-start | bytes 983048 | tf_op jit(solution)/shard_map/ppermute | solution.py:447
  134.9 12.6 %collective-permute-done.17 = bf16[640,256]{1,0:T(8,128)(2,1)S(1)} collective-permute-done((bf16[640,256]{1,0:T(8,128)(2,1)S(1)}, bf16[640,256]{1,0:T(8,128)(2,1)S(1)}, u32[]{:S(2)}, u32[]{:S(2)}) %collective-permute-start.17) | collective-permute-done | bytes 327712 | tf_op jit(solution)/shard_map/ppermute | solution.py:447
  148.0 8.2 %collective-permute-done.15 = bf16[640,256]{1,0:T(8,128)(2,1)S(1)} collective-permute-done((bf16[640,256]{1,0:T(8,128)(2,1)S(1)}, bf16[640,256]{1,0:T(8,128)(2,1)S(1)}, u32[]{:S(2)}, u32[]{:S(2)}) %collective-permute-start.15) | collective-permute-done | bytes 327712 | tf_op jit(solution)/shard_map/ppermute | solution.py:447
  156.2 1.9 fusion.2
  158.1 5.4 %all-to-all-start.3 = ((bf16[8,80,256]{2,1,0:T(8,128)(2,1)}), bf16[8,80,256]{2,1,0:T(8,128)(2,1)S(1)}, u32[]{:S(2)}, u32[]{:S(2)}) async-start(bf16[8,80,256]{2,1,0:T(8,128)(2,1)} %bitcast.15), calls=%async_computation.3 | async-start | bytes 655360 | tf_op jit(solution)/shard_map/all_to_all | solution.py:431
  164.2 2.7 %collective-permute-start.18 = (bf16[8,32,512]{2,1,0:T(8,128)(2,1)S(1)}, bf16[8,32,512]{2,1,0:T(8,128)(2,1)S(1)}, u32[]{:S(2)}, u32[]{:S(2)}) collective-permute-start(bf16[8,32,512]{2,1,0:T(8,128)(2,1)S(1)} %get-tuple-element.106), channel_id=1, source_target_pairs={{0,1},{1,0},{2,3},{3,2},{4,5},{5,4},{6,7},{7,6},{8,9},{9,8},{10,11... | collective-permute-start | bytes 786440 | tf_op jit(solution)/shard_map/ppermute | solution.py:421
  168.2 8.2 %all-to-all-done.3 = bf16[8,80,256]{2,1,0:T(8,128)(2,1)S(1)} async-done(((bf16[8,80,256]{2,1,0:T(8,128)(2,1)}), bf16[8,80,256]{2,1,0:T(8,128)(2,1)S(1)}, u32[]{:S(2)}, u32[]{:S(2)}) %all-to-all-start.3) | async-done | bytes 327712 | tf_op jit(solution)/shard_map/all_to_all | solution.py:431
  176.5 20.1 %all_to_all.32 = bf16[8,32,592]{2,1,0:T(8,128)(2,1)S(1)} all-to-all(bf16[8,32,592]{2,1,0:T(8,128)(2,1)S(1)} %pad_maximum_fusion), channel_id=1, replica_groups={{0,2,4,6,8,10,12,14},{1,3,5,7,9,11,13,15},{16,18,20,22,24,26,28,30},{17..., dimensions={0} | all-to-all | bytes 606208 | tf_op jit(solution)/shard_map/all_to_all | solution.py:431
  (55 shorter events, 20.7 us)
Async XLA Ops:
  0.6 0.7 copy-start.6
  24.0 1.0 copy-start
  25.1 6.0 %copy-start.8 = (s32[1,128]{1,0:T(1,128)S(1)}, s32[1,128]{1,0:T(1,128)}, u32[]{:S(2)}) copy-start(s32[1,128]{1,0:T(1,128)} %param.7) | copy-start | bytes 1540
  27.0 33.1 %copy-start.4 = (bf16[512,512]{1,0:T(8,128)(2,1)S(1)}, bf16[512,512]{1,0:T(8,128)(2,1)}, u32[]{:S(2)}) copy-start(bf16[512,512]{1,0:T(8,128)(2,1)} %w_out_ref.3) | copy-start | bytes 1572868
  27.0 33.1 %copy-start.5 = (bf16[1,128,512]{2,1,0:T(8,128)(2,1)S(1)}, bf16[1,128,512]{2,1,0:T(8,128)(2,1)}, u32[]{:S(2)}) copy-start(bf16[1,128,512]{2,1,0:T(8,128)(2,1)} %param.11) | copy-start | bytes 393220
  27.0 29.3 %all-to-all-start.1 = ((bf16[32,32,512]{2,1,0:T(8,128)(2,1)}), bf16[32,32,512]{2,1,0:T(8,128)(2,1)S(1)}, u32[]{:S(2)}, u32[]{:S(2)}) async-start(bf16[32,32,512]{2,1,0:T(8,128)(2,1)} %bitcast.5), calls=%async_computation.1 | async-start | bytes 2097152 | tf_op jit(solution)/shard_map/all_to_all | solution.py:482
  56.8 13.1 %collective-permute-start = (bf16[144,512]{1,0:T(8,128)(2,1)S(1)}, bf16[144,512]{1,0:T(8,128)(2,1)S(1)}, u32[]{:S(2)}, u32[]{:S(2)}) collective-permute-start(bf16[144,512]{1,0:T(8,128)(2,1)S(1)} %get-tuple-element.63.packed_ref.refs_1_), channel_id=1, source_target_pairs={{0,2},{1,3},{2,4},{3,5},{4,6},{5,7},{6,8},{7,9},{8,10},{9,11},{10,... | collective-permute-start | bytes 442376 | tf_op jit(solution)/shard_map/ppermute | solution.py:24
  60.1 1.6 copy-start.1
  62.3 16.4 %collective-permute-start.3 = (bf16[144,512]{1,0:T(8,128)(2,1)S(1)}, bf16[144,512]{1,0:T(8,128)(2,1)S(1)}, u32[]{:S(2)}, u32[]{:S(2)}) collective-permute-start(bf16[144,512]{1,0:T(8,128)(2,1)S(1)} %get-tuple-element.63.packed_ref.refs_1_), channel_id=1, source_target_pairs={{0,1},{1,0},{2,3},{3,2},{4,5},{5,4},{6,7},{7,6},{8,9},{9,8},{10,11... | collective-permute-start | bytes 442376 | tf_op jit(solution)/shard_map/ppermute | solution.py:29
  68.6 7.8 %collective-permute-start.5 = (bf16[144,512]{1,0:T(8,128)(2,1)S(1)}, bf16[144,512]{1,0:T(8,128)(2,1)S(1)}, u32[]{:S(2)}, u32[]{:S(2)}) collective-permute-start(bf16[144,512]{1,0:T(8,128)(2,1)S(1)} %get-tuple-element.63.packed_ref.refs_1_), channel_id=1, source_target_pairs={{2,0},{3,1},{4,2},{5,3},{6,4},{7,5},{8,6},{9,7},{10,8},{11,9},{12,... | collective-permute-start | bytes 442376 | tf_op jit(solution)/shard_map/ppermute | solution.py:24
  69.9 8.8 %collective-permute-start.1 = (bf16[144,512]{1,0:T(8,128)(2,1)S(1)}, bf16[144,512]{1,0:T(8,128)(2,1)S(1)}, u32[]{:S(2)}, u32[]{:S(2)}) collective-permute-start(bf16[144,512]{1,0:T(8,128)(2,1)S(1)} %collective-permute-done.two_ref), channel_id=1, source_target_pairs={{0,2},{1,3},{2,4},{3,5},{4,6},{5,7},{6,8},{7,9},{8,10},{9,11},{10,... | collective-permute-start | bytes 442376 | tf_op jit(solution)/shard_map/ppermute | solution.py:24
  73.9 4.8 %collective-permute-start.2 = (bf16[144,512]{1,0:T(8,128)(2,1)S(1)}, bf16[144,512]{1,0:T(8,128)(2,1)S(1)}, u32[]{:S(2)}, u32[]{:S(2)}) collective-permute-start(bf16[144,512]{1,0:T(8,128)(2,1)S(1)} %collective-permute-done.two_ref), channel_id=1, source_target_pairs={{0,1},{1,0},{2,3},{3,2},{4,5},{5,4},{6,7},{7,6},{8,9},{9,8},{10,11... | collective-permute-start | bytes 442376 | tf_op jit(solution)/shard_map/ppermute | solution.py:29
  76.4 5.7 %collective-permute-start.6 = (bf16[144,512]{1,0:T(8,128)(2,1)S(1)}, bf16[144,512]{1,0:T(8,128)(2,1)S(1)}, u32[]{:S(2)}, u32[]{:S(2)}) collective-permute-start(bf16[144,512]{1,0:T(8,128)(2,1)S(1)} %collective-permute-done.5.two_ref), channel_id=1, source_target_pairs={{0,1},{1,0},{2,3},{3,2},{4,5},{5,4},{6,7},{7,6},{8,9},{9,8},{10,11... | collective-permute-start | bytes 442376 | tf_op jit(solution)/shard_map/ppermute | solution.py:29
  78.7 3.4 %collective-permute-start.4 = (bf16[144,512]{1,0:T(8,128)(2,1)S(1)}, bf16[144,512]{1,0:T(8,128)(2,1)S(1)}, u32[]{:S(2)}, u32[]{:S(2)}) collective-permute-start(bf16[144,512]{1,0:T(8,128)(2,1)S(1)} %collective-permute-done.1.four_ref), channel_id=1, source_target_pairs={{1,0},{3,2},{5,4},{7,6},{9,8},{11,10},{13,12},{15,14},{17,16},{19,... | collective-permute-start | bytes 442376 | tf_op jit(solution)/shard_map/ppermute | solution.py:29
  80.8 9.2 %collective-permute-start.7 = (bf16[144,512]{1,0:T(8,128)(2,1)S(1)}, bf16[144,512]{1,0:T(8,128)(2,1)S(1)}, u32[]{:S(2)}, u32[]{:S(2)}) collective-permute-start(bf16[144,512]{1,0:T(8,128)(2,1)S(1)} %collective-permute-done.5.two_ref), channel_id=1, source_target_pairs={{2,0},{3,1},{4,2},{5,3},{6,4},{7,5},{8,6},{9,7},{10,8},{11,9},{12,... | collective-permute-start | bytes 442376 | tf_op jit(solution)/shard_map/ppermute | solution.py:24
  82.1 1.6 copy-start.2
  83.7 15.5 %copy-start.3 = (bf16[512,2048]{1,0:T(8,128)(2,1)S(1)}, bf16[512,2048]{1,0:T(8,128)(2,1)}, u32[]{:S(2)}) copy-start(bf16[512,2048]{1,0:T(8,128)(2,1)} %w_in_ref.7) | copy-start | bytes 6291460
  86.8 3.2 %collective-permute-start.8 = (bf16[128,512]{1,0:T(8,128)(2,1)S(1)}, bf16[128,512]{1,0:T(8,128)(2,1)S(1)}, u32[]{:S(2)}, u32[]{:S(2)}) collective-permute-start(bf16[128,512]{1,0:T(8,128)(2,1)S(1)} %get-tuple-element.78.att_grad_ref), channel_id=1, source_target_pairs={{1,0},{3,2},{5,4},{7,6},{9,8},{11,10},{13,12},{15,14},{17,16},{19,... | collective-permute-start | bytes 393224 | tf_op jit(solution)/shard_map/ppermute | solution.py:29
  88.7 7.0 %collective-permute-start.9 = (bf16[128,512]{1,0:T(8,128)(2,1)S(1)}, bf16[128,512]{1,0:T(8,128)(2,1)S(1)}, u32[]{:S(2)}, u32[]{:S(2)}) collective-permute-start(bf16[128,512]{1,0:T(8,128)(2,1)S(1)} %get-tuple-element.78.att_grad_ref), channel_id=1, source_target_pairs={{2,0},{3,1},{4,2},{5,3},{6,4},{7,5},{8,6},{9,7},{10,8},{11,9},{12,... | collective-permute-start | bytes 393224 | tf_op jit(solution)/shard_map/ppermute | solution.py:24
  90.1 9.2 %collective-permute-start.11 = (bf16[144,512]{1,0:T(8,128)(2,1)S(1)}, bf16[144,512]{1,0:T(8,128)(2,1)S(1)}, u32[]{:S(2)}, u32[]{:S(2)}) collective-permute-start(bf16[144,512]{1,0:T(8,128)(2,1)S(1)} %collective-permute-done.7.four_ref), channel_id=1, source_target_pairs={{0,1},{2,3},{4,5},{6,7},{8,9},{10,11},{12,13},{14,15},{16,17},{18,... | collective-permute-start | bytes 442376 | tf_op jit(solution)/shard_map/ppermute | solution.py:29
  95.7 3.5 %collective-permute-start.10 = (bf16[128,512]{1,0:T(8,128)(2,1)S(1)}, bf16[128,512]{1,0:T(8,128)(2,1)S(1)}, u32[]{:S(2)}, u32[]{:S(2)}) collective-permute-start(bf16[128,512]{1,0:T(8,128)(2,1)S(1)} %collective-permute-done.9.two_ref), channel_id=1, source_target_pairs={{0,1},{1,0},{2,3},{3,2},{4,5},{5,4},{6,7},{7,6},{8,9},{9,8},{10,11... | collective-permute-start | bytes 393224 | tf_op jit(solution)/shard_map/ppermute | solution.py:29
  97.9 7.4 %collective-permute-start.12 = (bf16[128,512]{1,0:T(8,128)(2,1)S(1)}, bf16[128,512]{1,0:T(8,128)(2,1)S(1)}, u32[]{:S(2)}, u32[]{:S(2)}) collective-permute-start(bf16[128,512]{1,0:T(8,128)(2,1)S(1)} %collective-permute-done.9.two_ref), channel_id=1, source_target_pairs={{2,0},{3,1},{4,2},{5,3},{6,4},{7,5},{8,6},{9,7},{10,8},{11,9},{12,... | collective-permute-start | bytes 393224 | tf_op jit(solution)/shard_map/ppermute | solution.py:24
  105.4 3.2 %collective-permute-start.13 = (bf16[128,512]{1,0:T(8,128)(2,1)S(1)}, bf16[128,512]{1,0:T(8,128)(2,1)S(1)}, u32[]{:S(2)}, u32[]{:S(2)}) collective-permute-start(bf16[128,512]{1,0:T(8,128)(2,1)S(1)} %collective-permute-done.12.four_ref), channel_id=1, source_target_pairs={{0,1},{2,3},{4,5},{6,7},{8,9},{10,11},{12,13},{14,15},{16,17},{18,... | collective-permute-start | bytes 393224 | tf_op jit(solution)/shard_map/ppermute | solution.py:29
  115.3 7.4 %collective-permute-start.14 = (bf16[4,640,256]{2,1,0:T(8,128)(2,1)}, bf16[4,640,256]{2,1,0:T(8,128)(2,1)}, u32[]{:S(2)}, u32[]{:S(2)}) collective-permute-start(bf16[4,640,256]{2,1,0:T(8,128)(2,1)} %get-tuple-element.103), channel_id=1, source_target_pairs={{0,1},{1,0},{2,3},{3,2},{4,5},{5,4},{6,7},{7,6},{8,9},{9,8},{10,11... | collective-permute-start | bytes 3932168 | tf_op jit(solution)/shard_map/ppermute | solution.py:421
  117.7 40.3 %all-to-all-start.2 = ((bf16[32,32,512]{2,1,0:T(8,128)(2,1)}), bf16[32,32,512]{2,1,0:T(8,128)(2,1)S(1)}, u32[]{:S(2)}, u32[]{:S(2)}) async-start(bf16[32,32,512]{2,1,0:T(8,128)(2,1)} %bitcast.9), calls=%async_computation.2 | async-start | bytes 2097152 | tf_op jit(solution)/shard_map/all_to_all | solution.py:557
  124.4 1.1 copy-start.7
  125.6 22.0 %collective-permute-start.17 = (bf16[640,256]{1,0:T(8,128)(2,1)S(1)}, bf16[640,256]{1,0:T(8,128)(2,1)S(1)}, u32[]{:S(2)}, u32[]{:S(2)}) collective-permute-start(bf16[640,256]{1,0:T(8,128)(2,1)S(1)} %get-tuple-element.117), channel_id=1, source_target_pairs={{0,48},{16,0},{32,16},{48,32},{64,112},{80,64},{96,80},{112,96},{1... | collective-permute-start | bytes 983048 | tf_op jit(solution)/shard_map/ppermute | solution.py:447
  129.9 18.1 %collective-permute-start.16 = (bf16[640,256]{1,0:T(8,128)(2,1)S(1)}, bf16[640,256]{1,0:T(8,128)(2,1)S(1)}, u32[]{:S(2)}, u32[]{:S(2)}) collective-permute-start(bf16[640,256]{1,0:T(8,128)(2,1)S(1)} %get-tuple-element.118), channel_id=1, source_target_pairs={{0,32},{16,48},{32,0},{48,16},{64,96},{80,112},{96,64},{112,80},{1... | collective-permute-start | bytes 983048 | tf_op jit(solution)/shard_map/ppermute | solution.py:447
  132.4 23.8 %collective-permute-start.15 = (bf16[640,256]{1,0:T(8,128)(2,1)S(1)}, bf16[640,256]{1,0:T(8,128)(2,1)S(1)}, u32[]{:S(2)}, u32[]{:S(2)}) collective-permute-start(bf16[640,256]{1,0:T(8,128)(2,1)S(1)} %get-tuple-element.116), channel_id=1, source_target_pairs={{0,16},{16,32},{32,48},{48,0},{64,80},{80,96},{96,112},{112,64},{1... | collective-permute-start | bytes 983048 | tf_op jit(solution)/shard_map/ppermute | solution.py:447
  158.1 18.3 %all-to-all-start.3 = ((bf16[8,80,256]{2,1,0:T(8,128)(2,1)}), bf16[8,80,256]{2,1,0:T(8,128)(2,1)S(1)}, u32[]{:S(2)}, u32[]{:S(2)}) async-start(bf16[8,80,256]{2,1,0:T(8,128)(2,1)} %bitcast.15), calls=%async_computation.3 | async-start | bytes 655360 | tf_op jit(solution)/shard_map/all_to_all | solution.py:431
  164.2 3.9 %collective-permute-start.18 = (bf16[8,32,512]{2,1,0:T(8,128)(2,1)S(1)}, bf16[8,32,512]{2,1,0:T(8,128)(2,1)S(1)}, u32[]{:S(2)}, u32[]{:S(2)}) collective-permute-start(bf16[8,32,512]{2,1,0:T(8,128)(2,1)S(1)} %get-tuple-element.106), channel_id=1, source_target_pairs={{0,1},{1,0},{2,3},{3,2},{4,5},{5,4},{6,7},{7,6},{8,9},{9,8},{10,11... | collective-permute-start | bytes 786440 | tf_op jit(solution)/shard_map/ppermute | solution.py:421

commit v7 on v6

--- a/solution.py
+++ b/solution.py
@@ -416,10 +416,26 @@
         sent_ref[chip] = jnp.where(even, second, first).astype(bf16)
 
 
-def pair_sum(kept, sent):
-    devices = lax.axis_size("ctx")
-    got = lax.ppermute(sent, "ctx", [(i, i ^ 1) for i in range(devices)])
-    return (kept.astype(f32) + got.astype(f32)).astype(bf16)
+def sum_pieces(kept, sent, axis, stride):
+    devices = range(lax.axis_size(axis))
+    count = kept.shape[0]
+    me = lax.axis_index(axis) // stride % count
+    got = lax.ppermute(sent, "ctx", [(i, i ^ 1) for i in range(lax.axis_size("ctx"))])
+
+    def piece(step):
+        at = (me + step) % count
+        return lax.dynamic_index_in_dim(kept, at, 0, keepdims=False).astype(
+            f32
+        ) + lax.dynamic_index_in_dim(got, at, 0, keepdims=False).astype(f32)
+
+    total = piece(0)
+    for step in range(1, count):
+        route = []
+        for i in devices:
+            at = i // stride % count
+            route.append((i, i + ((at + step) % count - at) * stride))
+        total = total + lax.ppermute(piece(step).astype(bf16), axis, route).astype(f32)
+    return total
 
 
 def chips_along_y():
@@ -435,17 +451,6 @@
 
 def total_of(blocks):
     return jnp.sum(blocks.astype(f32), axis=0)
-
-
-def sum_along_x(block):
-    devices = lax.axis_size("dp")
-    me = lax.axis_index("dp") % X_CHIPS
-    own = lax.dynamic_index_in_dim(block, me, 0, keepdims=False).astype(f32)
-    for step in range(1, X_CHIPS):
-        route = [(i, i - i % X_CHIPS + (i + step) % X_CHIPS) for i in range(devices)]
-        piece = lax.dynamic_index_in_dim(block, (me + step) % X_CHIPS, 0, keepdims=False)
-        own = own + lax.ppermute(piece, "dp", route).astype(f32)
-    return own.astype(bf16)
 
 
 def chips_along_z(owners):
@@ -566,7 +571,8 @@
         packed, value_key, early_kept, early_sent,
         core=core, flops=1_500_000_000, moved=3_000_000,
     )
-    along_x = sum_along_x(pair_sum(weight_kept, weight_sent)).reshape(z_chips, piece, half_width)
+    along_x = sum_pieces(weight_kept, weight_sent, "dp", 1).astype(bf16)
+    along_x = along_x.reshape(z_chips, piece, half_width)
     arrived, along_x = lax.optimization_barrier((arrived, along_x))
     along_dp = total_of(spread(along_x, "dp", chips_along_z(owners))).astype(bf16)
     weight_terms = along_dp.T.reshape(chips, weight_rows, piece)
@@ -574,12 +580,10 @@
     table_kept, table_sent = call(
         table_body, [(table_block, bf16), (table_block, bf16)], asked_row, arrived, core=core
     )
-    table_sum = pair_sum(table_kept, table_sent)
-    last = jnp.concatenate([table_sum, weight_terms], axis=2)
-    summed = total_of(spread(last, "ctx", chips_along_y()))
-    table_grad = summed[:, :table_dev].T
-    w_in_grad = summed[:, table_dev : table_dev + piece_in]
-    w_out_grad = summed[:, table_dev + piece_in :]
+    table_grad = sum_pieces(table_kept, table_sent, "ctx", 2).T
+    weight_grad = total_of(spread(weight_terms, "ctx", chips_along_y()))
+    w_in_grad = weight_grad[:, :piece_in]
+    w_out_grad = weight_grad[:, piece_in:]
     return (layer_out[None], table_grad, w_in_grad, w_out_grad)
 
 

time: 201 us -> 214 us (1.065)
  starting transfers between devices: 61.2 us -> 94.9 us
  blocking collectives: 42.2 us -> 22.1 us
    ppermute x5 -> x12, starting transfers between devices: 14.4 us -> 44.5 us  [the longest x10 39.5 us: sum_pieces(): lax.ppermute(piece(step).astype(bf16), axis, route).astype(f32)]
    all_to_all x1 -> x0, blocking collectives: 20.1 us -> none  [spread(): lax.all_to_all(block, axis, split_axis=0, concat_axis=0, tiled=True, axis...]
    all_to_all x1 -> x2, starting transfers between devices: 5.36 us -> 9.01 us  [spread(): lax.all_to_all(block, axis, split_axis=0, concat_axis=0, tiled=True, axis...]
    all_to_all x1 -> x2, waiting for transfers between devices: 8.17 us -> 6.53 us  [spread(): lax.all_to_all(block, axis, split_axis=0, concat_axis=0, tiled=True, axis...]
    ppermute x5 -> x12, waiting for transfers between devices: 22.4 us -> 23.7 us  [the longest x10 22.7 us: sum_pieces(): lax.ppermute(piece(step).astype(bf16), axis, route).astype(f32)]
  transfers between devices with their start and end apart: 22 -> 30, of which waited for: 9 -> 9; matrix products, arithmetic and copies ran while one was open for 2% -> 2% of each run, Pallas kernels for 4% -> 4%
where the time goes in v7:
time: 214 us; the launch traced here: 211 us
  starting transfers between devices  94.9 us (44%)
  waiting for transfers between devices  63.7 us (30%)
  blocking collectives  22.1 us (10%)
  Pallas kernels  18.3 us (9%)
  local copies, waits for them, and re-layouts  6.37 us (3%)
  other arithmetic  4.44 us (2%)
    ppermute x10, starting transfers between devices, sum_pieces(): lax.ppermute(piece(step).astype(bf16), axis, route).astype(f32)  39.5 us
    all_to_all x1, waiting for transfers between devices, local(): lax.all_to_all(found.reshape(owners, capacity, model_width), 'dp', split_...  25.2 us
    ppermute x10, waiting for transfers between devices, sum_pieces(): lax.ppermute(piece(step).astype(bf16), axis, route).astype(f32)  22.7 us
    all_to_all x1, blocking collectives, local(): lax.all_to_all(requests, 'dp', split_axis=0, concat_axis=0, tiled=True)  22.1 us
    ppermute x8, starting transfers between devices, swapped(): lax.ppermute(block, 'ctx', [(i, i ^ 1) for i in devices if i % 2 in sende...  20 us
    pallas_call x10, Pallas kernels, call(): pl.pallas_call(body, out_shape=[jax.ShapeDtypeStruct(shape, kind) for sha...  18.3 us
    ppermute x6, starting transfers between devices, passed_along(): return lax.ppermute(block, axis, route)  12.4 us
    all_to_all x2, starting transfers between devices, spread(): lax.all_to_all(block, axis, split_axis=0, concat_axis=0, tiled=True, axis...  9.01 us
  transfers between devices with their start and end apart: 30, of which 9 were waited for; matrix products, arithmetic and copies ran while one was open for 2% of the time, Pallas kernels for 4%

profile of v7, /device:TPU:1, one launch (start us, length us, event | category | flops | bytes accessed | tf_op | source)
XLA Modules:
  0.0 211.2 jit_solution(8064464110753522323)
XLA Ops:
  1.9 22.1 %all_to_all.31 = s32[32,1,32]{2,1,0:T(1,128)S(1)} all-to-all(s32[32,1,32]{2,1,0:T(1,128)S(1)} %bitcast.65), channel_id=1, replica_groups=mesh['dp'=32,'ctx'=16] {'dp'}, dimensions={0} | all-to-all | bytes 8192 | tf_op jit(solution)/shard_map/all_to_all | solution.py:483
  27.0 4.1 %all-to-all-start.1 = ((bf16[32,32,512]{2,1,0:T(8,128)(2,1)}), bf16[32,32,512]{2,1,0:T(8,128)(2,1)S(1)}, u32[]{:S(2)}, u32[]{:S(2)}) async-start(bf16[32,32,512]{2,1,0:T(8,128)(2,1)} %bitcast.5), calls=%async_computation.1 | async-start | bytes 2097152 | tf_op jit(solution)/shard_map/all_to_all | solution.py:487
  31.1 25.2 %all-to-all-done.1 = bf16[32,32,512]{2,1,0:T(8,128)(2,1)S(1)} async-done(((bf16[32,32,512]{2,1,0:T(8,128)(2,1)}), bf16[32,32,512]{2,1,0:T(8,128)(2,1)S(1)}, u32[]{:S(2)}, u32[]{:S(2)}) %all-to-all-start.1) | async-done | bytes 1048608 | tf_op jit(solution)/shard_map/all_to_all | solution.py:487
  56.8 3.2 %collective-permute-start = (bf16[144,512]{1,0:T(8,128)(2,1)S(1)}, bf16[144,512]{1,0:T(8,128)(2,1)S(1)}, u32[]{:S(2)}, u32[]{:S(2)}) collective-permute-start(bf16[144,512]{1,0:T(8,128)(2,1)S(1)} %get-tuple-element.63.packed_ref.refs_1_), channel_id=1, source_target_pairs={{0,2},{1,3},{2,4},{3,5},{4,6},{5,7},{6,8},{7,9},{8,10},{9,11},{10,... | collective-permute-start | bytes 442376 | tf_op jit(solution)/shard_map/ppermute | solution.py:24
  62.3 6.3 %collective-permute-start.3 = (bf16[144,512]{1,0:T(8,128)(2,1)S(1)}, bf16[144,512]{1,0:T(8,128)(2,1)S(1)}, u32[]{:S(2)}, u32[]{:S(2)}) collective-permute-start(bf16[144,512]{1,0:T(8,128)(2,1)S(1)} %get-tuple-element.63.packed_ref.refs_1_), channel_id=1, source_target_pairs={{0,1},{1,0},{2,3},{3,2},{4,5},{5,4},{6,7},{7,6},{8,9},{9,8},{10,11... | collective-permute-start | bytes 442376 | tf_op jit(solution)/shard_map/ppermute | solution.py:29
  69.9 4.0 %collective-permute-start.1 = (bf16[144,512]{1,0:T(8,128)(2,1)S(1)}, bf16[144,512]{1,0:T(8,128)(2,1)S(1)}, u32[]{:S(2)}, u32[]{:S(2)}) collective-permute-start(bf16[144,512]{1,0:T(8,128)(2,1)S(1)} %collective-permute-done.two_ref), channel_id=1, source_target_pairs={{0,2},{1,3},{2,4},{3,5},{4,6},{5,7},{6,8},{7,9},{8,10},{9,11},{10,... | collective-permute-start | bytes 442376 | tf_op jit(solution)/shard_map/ppermute | solution.py:24
  73.9 2.5 %collective-permute-start.2 = (bf16[144,512]{1,0:T(8,128)(2,1)S(1)}, bf16[144,512]{1,0:T(8,128)(2,1)S(1)}, u32[]{:S(2)}, u32[]{:S(2)}) collective-permute-start(bf16[144,512]{1,0:T(8,128)(2,1)S(1)} %collective-permute-done.two_ref), channel_id=1, source_target_pairs={{0,1},{1,0},{2,3},{3,2},{4,5},{5,4},{6,7},{7,6},{8,9},{9,8},{10,11... | collective-permute-start | bytes 442376 | tf_op jit(solution)/shard_map/ppermute | solution.py:29
  76.4 2.2 %collective-permute-start.6 = (bf16[144,512]{1,0:T(8,128)(2,1)S(1)}, bf16[144,512]{1,0:T(8,128)(2,1)S(1)}, u32[]{:S(2)}, u32[]{:S(2)}) collective-permute-start(bf16[144,512]{1,0:T(8,128)(2,1)S(1)} %collective-permute-done.5.two_ref), channel_id=1, source_target_pairs={{0,1},{1,0},{2,3},{3,2},{4,5},{5,4},{6,7},{7,6},{8,9},{9,8},{10,11... | collective-permute-start | bytes 442376 | tf_op jit(solution)/shard_map/ppermute | solution.py:29
  83.8 3.1 %shard_map.97 = (bf16[128,512]{1,0:T(8,128)(2,1)}, bf16[128,512]{1,0:T(8,128)(2,1)S(1)}, f32[128,512]{1,0:T(8,128)S(1)}, bf16[128,512]{1,0:T(8,128)(2,1)S(1)}, b...) custom-call(s32[1]{0:T(128)} %bitcast.core_ref.refs_0_, ...), custom_call_target="tpu_custom_call" | custom-call | flops 4000000000 | bytes 8000000 | tf_op jit(solution)/shard_map/pallas_call | solution.py:120
  91.4 4.3 %collective-permute-done.9.two_ref = bf16[128,512]{1,0:T(8,128)(2,1)S(1)} collective-permute-done((bf16[128,512]{1,0:T(8,128)(2,1)S(1)}, bf16[128,512]{1,0:T(8,128)(2,1)S(1)}, u32[]{:S(2)}, u32[]{:S(2)}) %collective-permute-start.9) | collective-permute-done | bytes 131104 | tf_op jit(solution)/shard_map/ppermute | solution.py:24
  99.3 2.8 %shard_map.98 = (bf16[128,1024]{1,0:T(8,128)(2,1)S(1)}, f32[128,1024]{1,0:T(8,128)S(1)}, bf16[640,512]{1,0:T(8,128)(2,1)S(1)}, f32[640,1]{1,0:T(8,128)S(1)}) custom-call(s32[1]{0:T(128)} %bitcast.core_ref.refs_0_, bf16[128,512]{1,0:T(8,128)(2,1)S(1)} %get-tuple-element.70.queries_ref, bf16[640,512]{1,0:T(8,128)(2,1)S(1)} %get-tuple-element.76.all_keys_ref, ...), custom_call_target="tpu_custom_call" | custom-call | flops 4000000000 | bytes 8000000 | tf_op jit(solution)/shard_map/pallas_call | solution.py:120
  102.1 3.3 %collective-permute-done.12.four_ref = bf16[128,512]{1,0:T(8,128)(2,1)S(1)} collective-permute-done((bf16[128,512]{1,0:T(8,128)(2,1)S(1)}, bf16[128,512]{1,0:T(8,128)(2,1)S(1)}, u32[]{:S(2)}, u32[]{:S(2)}) %collective-permute-start.12) | collective-permute-done | bytes 131104 | tf_op jit(solution)/shard_map/ppermute | solution.py:24
  108.6 4.9 %shard_map.100 = (bf16[128,1024]{1,0:T(8,128)(2,1)S(1)}, bf16[1024,512]{1,0:T(8,128)(2,1)}) custom-call(s32[1]{0:T(128)} %bitcast.core_ref.refs_0_, bf16[640,512]{1,0:T(8,128)(2,1)S(1)} %get-tuple-element.85.all_queries_ref, f32[640,1]{1,0:T(8,128)S(1)} %get-tuple-element.86.query_user_ref, bf16[128,512]{1,0:T(8,128)(2,1)S(1)} %get-tuple-element.78.att_grad_ref, ...), custom_call_target="tpu_custom_call" | custom-call | flops 4000000000 | bytes 8000000 | tf_op jit(solution)/shard_map/pallas_call | solution.py:120
  115.3 2.4 %collective-permute-start.14 = (bf16[4,640,256]{2,1,0:T(8,128)(2,1)}, bf16[4,640,256]{2,1,0:T(8,128)(2,1)}, u32[]{:S(2)}, u32[]{:S(2)}) collective-permute-start(bf16[4,640,256]{2,1,0:T(8,128)(2,1)} %get-tuple-element.103), channel_id=1, source_target_pairs={{0,1},{1,0},{2,3},{3,2},{4,5},{5,4},{6,7},{7,6},{8,9},{9,8},{10,11... | collective-permute-start | bytes 3932168 | tf_op jit(solution)/shard_map/ppermute | solution.py:423
  117.7 5.0 %all-to-all-start.2 = ((bf16[32,32,512]{2,1,0:T(8,128)(2,1)}), bf16[32,32,512]{2,1,0:T(8,128)(2,1)S(1)}, u32[]{:S(2)}, u32[]{:S(2)}) async-start(bf16[32,32,512]{2,1,0:T(8,128)(2,1)} %bitcast.9), calls=%async_computation.2 | async-start | bytes 2097152 | tf_op jit(solution)/shard_map/all_to_all | solution.py:562
  124.2 4.4 %collective-permute-start.17 = (bf16[640,256]{1,0:T(8,128)(2,1)S(1)}, bf16[640,256]{1,0:T(8,128)(2,1)}, u32[]{:S(2)}, u32[]{:S(2)}) collective-permute-start(bf16[640,256]{1,0:T(8,128)(2,1)S(1)} %get-tuple-element.121), channel_id=1, source_target_pairs={{0,48},{16,0},{32,16},{48,32},{64,112},{80,64},{96,80},{112,96},{1... | collective-permute-start | bytes 983048 | tf_op jit(solution)/shard_map/ppermute | solution.py:437
  128.6 2.5 %collective-permute-start.16 = (bf16[640,256]{1,0:T(8,128)(2,1)S(1)}, bf16[640,256]{1,0:T(8,128)(2,1)}, u32[]{:S(2)}, u32[]{:S(2)}) collective-permute-start(bf16[640,256]{1,0:T(8,128)(2,1)S(1)} %get-tuple-element.122), channel_id=1, source_target_pairs={{0,32},{16,48},{32,0},{48,16},{64,96},{80,112},{96,64},{112,80},{1... | collective-permute-start | bytes 983048 | tf_op jit(solution)/shard_map/ppermute | solution.py:437
  131.1 2.5 %collective-permute-start.15 = (bf16[640,256]{1,0:T(8,128)(2,1)S(1)}, bf16[640,256]{1,0:T(8,128)(2,1)}, u32[]{:S(2)}, u32[]{:S(2)}) collective-permute-start(bf16[640,256]{1,0:T(8,128)(2,1)S(1)} %get-tuple-element.120), channel_id=1, source_target_pairs={{0,16},{16,32},{32,48},{48,0},{64,80},{80,96},{96,112},{112,64},{1... | collective-permute-start | bytes 983048 | tf_op jit(solution)/shard_map/ppermute | solution.py:437
  133.6 13.1 %collective-permute-done.17 = bf16[640,256]{1,0:T(8,128)(2,1)} collective-permute-done((bf16[640,256]{1,0:T(8,128)(2,1)S(1)}, bf16[640,256]{1,0:T(8,128)(2,1)}, u32[]{:S(2)}, u32[]{:S(2)}) %collective-permute-start.17) | collective-permute-done | bytes 327712 | tf_op jit(solution)/shard_map/ppermute | solution.py:437
  146.7 2.5 %collective-permute-done.16 = bf16[640,256]{1,0:T(8,128)(2,1)} collective-permute-done((bf16[640,256]{1,0:T(8,128)(2,1)S(1)}, bf16[640,256]{1,0:T(8,128)(2,1)}, u32[]{:S(2)}, u32[]{:S(2)}) %collective-permute-start.16) | collective-permute-done | bytes 327712 | tf_op jit(solution)/shard_map/ppermute | solution.py:437
  149.1 7.2 %collective-permute-done.15 = bf16[640,256]{1,0:T(8,128)(2,1)} collective-permute-done((bf16[640,256]{1,0:T(8,128)(2,1)S(1)}, bf16[640,256]{1,0:T(8,128)(2,1)}, u32[]{:S(2)}, u32[]{:S(2)}) %collective-permute-start.15) | collective-permute-done | bytes 327712 | tf_op jit(solution)/shard_map/ppermute | solution.py:437
  156.3 2.2 %fusion.2 = bf16[640,256]{1,0:T(8,128)(2,1)} fusion(bf16[640,256]{1,0:T(8,128)(2,1)} %collective-permute-done.17, bf16[640,256]{1,0:T(8,128)(2,1)} %collective-permute-done.16, bf16[640,256]{1,0:T(8,128)(2,1)} %collective-permute-done.15, bf16[4,640,256]{2,1,0:T(8,128)(2,1)} %collective-permute-done.14, s32[]{:T(128)S(6)} %select_n.121, ...), kind=kLoop, calls=%fused_computation.3 | loop fusion | flops 1638400 | bytes 1966084 | tf_op jit(solution)/shard_map/convert_element_type | solution.py:574
  158.5 5.1 %all-to-all-start.3 = ((bf16[8,80,256]{2,1,0:T(8,128)(2,1)}), bf16[8,80,256]{2,1,0:T(8,128)(2,1)S(1)}, u32[]{:S(2)}, u32[]{:S(2)}) async-start(bf16[8,80,256]{2,1,0:T(8,128)(2,1)} %bitcast.15), calls=%async_computation.3 | async-start | bytes 655360 | tf_op jit(solution)/shard_map/all_to_all | solution.py:447
  164.4 2.6 %collective-permute-start.18 = (bf16[8,32,512]{2,1,0:T(8,128)(2,1)S(1)}, bf16[8,32,512]{2,1,0:T(8,128)(2,1)S(1)}, u32[]{:S(2)}, u32[]{:S(2)}) collective-permute-start(bf16[8,32,512]{2,1,0:T(8,128)(2,1)S(1)} %get-tuple-element.106), channel_id=1, source_target_pairs={{0,1},{1,0},{2,3},{3,2},{4,5},{5,4},{6,7},{7,6},{8,9},{9,8},{10,11... | collective-permute-start | bytes 786440 | tf_op jit(solution)/shard_map/ppermute | solution.py:423
  168.2 6.3 %collective-permute-start.25 = (bf16[32,512]{1,0:T(8,128)(2,1)S(1)}, bf16[32,512]{1,0:T(8,128)(2,1)S(1)}, u32[]{:S(2)}, u32[]{:S(2)}) collective-permute-start(bf16[32,512]{1,0:T(8,128)(2,1)S(1)} %get-tuple-element.124), channel_id=1, source_target_pairs={{0,14},{1,15},{2,0},{3,1},{4,2},{5,3},{6,4},{7,5},{8,6},{9,7},{10,... | collective-permute-start | bytes 98312 | tf_op jit(solution)/shard_map/ppermute | solution.py:437
  174.6 5.9 %collective-permute-start.24 = (bf16[32,512]{1,0:T(8,128)(2,1)S(1)}, bf16[32,512]{1,0:T(8,128)(2,1)S(1)}, u32[]{:S(2)}, u32[]{:S(2)}) collective-permute-start(bf16[32,512]{1,0:T(8,128)(2,1)S(1)} %get-tuple-element.125), channel_id=1, source_target_pairs={{0,12},{1,13},{2,14},{3,15},{4,0},{5,1},{6,2},{7,3},{8,4},{9,5},{1... | collective-permute-start | bytes 98312 | tf_op jit(solution)/shard_map/ppermute | solution.py:437
  180.4 3.5 %collective-permute-start.23 = (bf16[32,512]{1,0:T(8,128)(2,1)S(1)}, bf16[32,512]{1,0:T(8,128)(2,1)S(1)}, u32[]{:S(2)}, u32[]{:S(2)}) collective-permute-start(bf16[32,512]{1,0:T(8,128)(2,1)S(1)} %get-tuple-element.126), channel_id=1, source_target_pairs={{0,10},{1,11},{2,12},{3,13},{4,14},{5,15},{6,0},{7,1},{8,2},{9,3},... | collective-permute-start | bytes 98312 | tf_op jit(solution)/shard_map/ppermute | solution.py:437
  183.9 4.0 %collective-permute-start.22 = (bf16[32,512]{1,0:T(8,128)(2,1)S(1)}, bf16[32,512]{1,0:T(8,128)(2,1)S(1)}, u32[]{:S(2)}, u32[]{:S(2)}) collective-permute-start(bf16[32,512]{1,0:T(8,128)(2,1)S(1)} %get-tuple-element.127), channel_id=1, source_target_pairs={{0,8},{1,9},{2,10},{3,11},{4,12},{5,13},{6,14},{7,15},{8,0},{9,1},... | collective-permute-start | bytes 98312 | tf_op jit(solution)/shard_map/ppermute | solution.py:437
  187.9 3.1 %collective-permute-start.21 = (bf16[32,512]{1,0:T(8,128)(2,1)S(1)}, bf16[32,512]{1,0:T(8,128)(2,1)S(1)}, u32[]{:S(2)}, u32[]{:S(2)}) collective-permute-start(bf16[32,512]{1,0:T(8,128)(2,1)S(1)} %get-tuple-element.128), channel_id=1, source_target_pairs={{0,6},{1,7},{2,8},{3,9},{4,10},{5,11},{6,12},{7,13},{8,14},{9,15},... | collective-permute-start | bytes 98312 | tf_op jit(solution)/shard_map/ppermute | solution.py:437
  191.0 5.5 %collective-permute-start.20 = (bf16[32,512]{1,0:T(8,128)(2,1)S(1)}, bf16[32,512]{1,0:T(8,128)(2,1)S(1)}, u32[]{:S(2)}, u32[]{:S(2)}) collective-permute-start(bf16[32,512]{1,0:T(8,128)(2,1)S(1)} %get-tuple-element.129), channel_id=1, source_target_pairs={{0,4},{1,5},{2,6},{3,7},{4,8},{5,9},{6,10},{7,11},{8,12},{9,13},{1... | collective-permute-start | bytes 98312 | tf_op jit(solution)/shard_map/ppermute | solution.py:437
  199.2 3.9 %all-to-all-start.4 = ((bf16[8,32,80]{2,1,0:T(8,128)(2,1)}), bf16[8,32,80]{2,1,0:T(8,128)(2,1)S(1)}, u32[]{:S(2)}, u32[]{:S(2)}) async-start(bf16[8,32,80]{2,1,0:T(8,128)(2,1)} %bitcast.26), calls=%async_computation.4 | async-start | bytes 131072 | tf_op jit(solution)/shard_map/all_to_all | solution.py:447
  203.9 6.5 %all-to-all-done.4 = bf16[8,32,80]{2,1,0:T(8,128)(2,1)S(1)} async-done(((bf16[8,32,80]{2,1,0:T(8,128)(2,1)}), bf16[8,32,80]{2,1,0:T(8,128)(2,1)S(1)}, u32[]{:S(2)}, u32[]{:S(2)}) %all-to-all-start.4) | async-done | bytes 40992 | tf_op jit(solution)/shard_map/all_to_all | solution.py:447
  (67 shorter events, 33.8 us)
Async XLA Ops:
  27.0 33.0 %copy-start.4 = (bf16[512,512]{1,0:T(8,128)(2,1)S(1)}, bf16[512,512]{1,0:T(8,128)(2,1)}, u32[]{:S(2)}) copy-start(bf16[512,512]{1,0:T(8,128)(2,1)} %w_out_ref.3) | copy-start | bytes 1572868
  27.0 33.1 %copy-start.5 = (bf16[1,128,512]{2,1,0:T(8,128)(2,1)S(1)}, bf16[1,128,512]{2,1,0:T(8,128)(2,1)}, u32[]{:S(2)}) copy-start(bf16[1,128,512]{2,1,0:T(8,128)(2,1)} %param.11) | copy-start | bytes 393220
  27.0 29.3 %all-to-all-start.1 = ((bf16[32,32,512]{2,1,0:T(8,128)(2,1)}), bf16[32,32,512]{2,1,0:T(8,128)(2,1)S(1)}, u32[]{:S(2)}, u32[]{:S(2)}) async-start(bf16[32,32,512]{2,1,0:T(8,128)(2,1)} %bitcast.5), calls=%async_computation.1 | async-start | bytes 2097152 | tf_op jit(solution)/shard_map/all_to_all | solution.py:487
  56.8 13.1 %collective-permute-start = (bf16[144,512]{1,0:T(8,128)(2,1)S(1)}, bf16[144,512]{1,0:T(8,128)(2,1)S(1)}, u32[]{:S(2)}, u32[]{:S(2)}) collective-permute-start(bf16[144,512]{1,0:T(8,128)(2,1)S(1)} %get-tuple-element.63.packed_ref.refs_1_), channel_id=1, source_target_pairs={{0,2},{1,3},{2,4},{3,5},{4,6},{5,7},{6,8},{7,9},{8,10},{9,11},{10,... | collective-permute-start | bytes 442376 | tf_op jit(solution)/shard_map/ppermute | solution.py:24
  62.3 16.4 %collective-permute-start.3 = (bf16[144,512]{1,0:T(8,128)(2,1)S(1)}, bf16[144,512]{1,0:T(8,128)(2,1)S(1)}, u32[]{:S(2)}, u32[]{:S(2)}) collective-permute-start(bf16[144,512]{1,0:T(8,128)(2,1)S(1)} %get-tuple-element.63.packed_ref.refs_1_), channel_id=1, source_target_pairs={{0,1},{1,0},{2,3},{3,2},{4,5},{5,4},{6,7},{7,6},{8,9},{9,8},{10,11... | collective-permute-start | bytes 442376 | tf_op jit(solution)/shard_map/ppermute | solution.py:29
  68.6 7.8 %collective-permute-start.5 = (bf16[144,512]{1,0:T(8,128)(2,1)S(1)}, bf16[144,512]{1,0:T(8,128)(2,1)S(1)}, u32[]{:S(2)}, u32[]{:S(2)}) collective-permute-start(bf16[144,512]{1,0:T(8,128)(2,1)S(1)} %get-tuple-element.63.packed_ref.refs_1_), channel_id=1, source_target_pairs={{2,0},{3,1},{4,2},{5,3},{6,4},{7,5},{8,6},{9,7},{10,8},{11,9},{12,... | collective-permute-start | bytes 442376 | tf_op jit(solution)/shard_map/ppermute | solution.py:24
  69.9 8.8 %collective-permute-start.1 = (bf16[144,512]{1,0:T(8,128)(2,1)S(1)}, bf16[144,512]{1,0:T(8,128)(2,1)S(1)}, u32[]{:S(2)}, u32[]{:S(2)}) collective-permute-start(bf16[144,512]{1,0:T(8,128)(2,1)S(1)} %collective-permute-done.two_ref), channel_id=1, source_target_pairs={{0,2},{1,3},{2,4},{3,5},{4,6},{5,7},{6,8},{7,9},{8,10},{9,11},{10,... | collective-permute-start | bytes 442376 | tf_op jit(solution)/shard_map/ppermute | solution.py:24
  73.9 4.8 %collective-permute-start.2 = (bf16[144,512]{1,0:T(8,128)(2,1)S(1)}, bf16[144,512]{1,0:T(8,128)(2,1)S(1)}, u32[]{:S(2)}, u32[]{:S(2)}) collective-permute-start(bf16[144,512]{1,0:T(8,128)(2,1)S(1)} %collective-permute-done.two_ref), channel_id=1, source_target_pairs={{0,1},{1,0},{2,3},{3,2},{4,5},{5,4},{6,7},{7,6},{8,9},{9,8},{10,11... | collective-permute-start | bytes 442376 | tf_op jit(solution)/shard_map/ppermute | solution.py:29
  76.4 5.7 %collective-permute-start.6 = (bf16[144,512]{1,0:T(8,128)(2,1)S(1)}, bf16[144,512]{1,0:T(8,128)(2,1)S(1)}, u32[]{:S(2)}, u32[]{:S(2)}) collective-permute-start(bf16[144,512]{1,0:T(8,128)(2,1)S(1)} %collective-permute-done.5.two_ref), channel_id=1, source_target_pairs={{0,1},{1,0},{2,3},{3,2},{4,5},{5,4},{6,7},{7,6},{8,9},{9,8},{10,11... | collective-permute-start | bytes 442376 | tf_op jit(solution)/shard_map/ppermute | solution.py:29
  78.7 3.4 %collective-permute-start.4 = (bf16[144,512]{1,0:T(8,128)(2,1)S(1)}, bf16[144,512]{1,0:T(8,128)(2,1)S(1)}, u32[]{:S(2)}, u32[]{:S(2)}) collective-permute-start(bf16[144,512]{1,0:T(8,128)(2,1)S(1)} %collective-permute-done.1.four_ref), channel_id=1, source_target_pairs={{1,0},{3,2},{5,4},{7,6},{9,8},{11,10},{13,12},{15,14},{17,16},{19,... | collective-permute-start | bytes 442376 | tf_op jit(solution)/shard_map/ppermute | solution.py:29
  80.8 9.2 %collective-permute-start.7 = (bf16[144,512]{1,0:T(8,128)(2,1)S(1)}, bf16[144,512]{1,0:T(8,128)(2,1)S(1)}, u32[]{:S(2)}, u32[]{:S(2)}) collective-permute-start(bf16[144,512]{1,0:T(8,128)(2,1)S(1)} %collective-permute-done.5.two_ref), channel_id=1, source_target_pairs={{2,0},{3,1},{4,2},{5,3},{6,4},{7,5},{8,6},{9,7},{10,8},{11,9},{12,... | collective-permute-start | bytes 442376 | tf_op jit(solution)/shard_map/ppermute | solution.py:24
  86.8 3.2 %collective-permute-start.8 = (bf16[128,512]{1,0:T(8,128)(2,1)S(1)}, bf16[128,512]{1,0:T(8,128)(2,1)S(1)}, u32[]{:S(2)}, u32[]{:S(2)}) collective-permute-start(bf16[128,512]{1,0:T(8,128)(2,1)S(1)} %get-tuple-element.78.att_grad_ref), channel_id=1, source_target_pairs={{1,0},{3,2},{5,4},{7,6},{9,8},{11,10},{13,12},{15,14},{17,16},{19,... | collective-permute-start | bytes 393224 | tf_op jit(solution)/shard_map/ppermute | solution.py:29
  88.7 7.0 %collective-permute-start.9 = (bf16[128,512]{1,0:T(8,128)(2,1)S(1)}, bf16[128,512]{1,0:T(8,128)(2,1)S(1)}, u32[]{:S(2)}, u32[]{:S(2)}) collective-permute-start(bf16[128,512]{1,0:T(8,128)(2,1)S(1)} %get-tuple-element.78.att_grad_ref), channel_id=1, source_target_pairs={{2,0},{3,1},{4,2},{5,3},{6,4},{7,5},{8,6},{9,7},{10,8},{11,9},{12,... | collective-permute-start | bytes 393224 | tf_op jit(solution)/shard_map/ppermute | solution.py:24
  90.1 9.2 %collective-permute-start.11 = (bf16[144,512]{1,0:T(8,128)(2,1)S(1)}, bf16[144,512]{1,0:T(8,128)(2,1)S(1)}, u32[]{:S(2)}, u32[]{:S(2)}) collective-permute-start(bf16[144,512]{1,0:T(8,128)(2,1)S(1)} %collective-permute-done.7.four_ref), channel_id=1, source_target_pairs={{0,1},{2,3},{4,5},{6,7},{8,9},{10,11},{12,13},{14,15},{16,17},{18,... | collective-permute-start | bytes 442376 | tf_op jit(solution)/shard_map/ppermute | solution.py:29
  95.7 3.5 %collective-permute-start.10 = (bf16[128,512]{1,0:T(8,128)(2,1)S(1)}, bf16[128,512]{1,0:T(8,128)(2,1)S(1)}, u32[]{:S(2)}, u32[]{:S(2)}) collective-permute-start(bf16[128,512]{1,0:T(8,128)(2,1)S(1)} %collective-permute-done.9.two_ref), channel_id=1, source_target_pairs={{0,1},{1,0},{2,3},{3,2},{4,5},{5,4},{6,7},{7,6},{8,9},{9,8},{10,11... | collective-permute-start | bytes 393224 | tf_op jit(solution)/shard_map/ppermute | solution.py:29
  97.9 7.4 %collective-permute-start.12 = (bf16[128,512]{1,0:T(8,128)(2,1)S(1)}, bf16[128,512]{1,0:T(8,128)(2,1)S(1)}, u32[]{:S(2)}, u32[]{:S(2)}) collective-permute-start(bf16[128,512]{1,0:T(8,128)(2,1)S(1)} %collective-permute-done.9.two_ref), channel_id=1, source_target_pairs={{2,0},{3,1},{4,2},{5,3},{6,4},{7,5},{8,6},{9,7},{10,8},{11,9},{12,... | collective-permute-start | bytes 393224 | tf_op jit(solution)/shard_map/ppermute | solution.py:24
  105.4 3.2 %collective-permute-start.13 = (bf16[128,512]{1,0:T(8,128)(2,1)S(1)}, bf16[128,512]{1,0:T(8,128)(2,1)S(1)}, u32[]{:S(2)}, u32[]{:S(2)}) collective-permute-start(bf16[128,512]{1,0:T(8,128)(2,1)S(1)} %collective-permute-done.12.four_ref), channel_id=1, source_target_pairs={{0,1},{2,3},{4,5},{6,7},{8,9},{10,11},{12,13},{14,15},{16,17},{18,... | collective-permute-start | bytes 393224 | tf_op jit(solution)/shard_map/ppermute | solution.py:29
  115.3 7.5 %collective-permute-start.14 = (bf16[4,640,256]{2,1,0:T(8,128)(2,1)}, bf16[4,640,256]{2,1,0:T(8,128)(2,1)}, u32[]{:S(2)}, u32[]{:S(2)}) collective-permute-start(bf16[4,640,256]{2,1,0:T(8,128)(2,1)} %get-tuple-element.103), channel_id=1, source_target_pairs={{0,1},{1,0},{2,3},{3,2},{4,5},{5,4},{6,7},{7,6},{8,9},{9,8},{10,11... | collective-permute-start | bytes 3932168 | tf_op jit(solution)/shard_map/ppermute | solution.py:423
  117.7 40.8 %all-to-all-start.2 = ((bf16[32,32,512]{2,1,0:T(8,128)(2,1)}), bf16[32,32,512]{2,1,0:T(8,128)(2,1)S(1)}, u32[]{:S(2)}, u32[]{:S(2)}) async-start(bf16[32,32,512]{2,1,0:T(8,128)(2,1)} %bitcast.9), calls=%async_computation.2 | async-start | bytes 2097152 | tf_op jit(solution)/shard_map/all_to_all | solution.py:562
  124.2 22.4 %collective-permute-start.17 = (bf16[640,256]{1,0:T(8,128)(2,1)S(1)}, bf16[640,256]{1,0:T(8,128)(2,1)}, u32[]{:S(2)}, u32[]{:S(2)}) collective-permute-start(bf16[640,256]{1,0:T(8,128)(2,1)S(1)} %get-tuple-element.121), channel_id=1, source_target_pairs={{0,48},{16,0},{32,16},{48,32},{64,112},{80,64},{96,80},{112,96},{1... | collective-permute-start | bytes 983048 | tf_op jit(solution)/shard_map/ppermute | solution.py:437
  128.6 20.6 %collective-permute-start.16 = (bf16[640,256]{1,0:T(8,128)(2,1)S(1)}, bf16[640,256]{1,0:T(8,128)(2,1)}, u32[]{:S(2)}, u32[]{:S(2)}) collective-permute-start(bf16[640,256]{1,0:T(8,128)(2,1)S(1)} %get-tuple-element.122), channel_id=1, source_target_pairs={{0,32},{16,48},{32,0},{48,16},{64,96},{80,112},{96,64},{112,80},{1... | collective-permute-start | bytes 983048 | tf_op jit(solution)/shard_map/ppermute | solution.py:437
  131.1 25.2 %collective-permute-start.15 = (bf16[640,256]{1,0:T(8,128)(2,1)S(1)}, bf16[640,256]{1,0:T(8,128)(2,1)}, u32[]{:S(2)}, u32[]{:S(2)}) collective-permute-start(bf16[640,256]{1,0:T(8,128)(2,1)S(1)} %get-tuple-element.120), channel_id=1, source_target_pairs={{0,16},{16,32},{32,48},{48,0},{64,80},{80,96},{96,112},{112,64},{1... | collective-permute-start | bytes 983048 | tf_op jit(solution)/shard_map/ppermute | solution.py:437
  158.5 39.9 %all-to-all-start.3 = ((bf16[8,80,256]{2,1,0:T(8,128)(2,1)}), bf16[8,80,256]{2,1,0:T(8,128)(2,1)S(1)}, u32[]{:S(2)}, u32[]{:S(2)}) async-start(bf16[8,80,256]{2,1,0:T(8,128)(2,1)} %bitcast.15), calls=%async_computation.3 | async-start | bytes 655360 | tf_op jit(solution)/shard_map/all_to_all | solution.py:447
  164.4 3.7 %collective-permute-start.18 = (bf16[8,32,512]{2,1,0:T(8,128)(2,1)S(1)}, bf16[8,32,512]{2,1,0:T(8,128)(2,1)S(1)}, u32[]{:S(2)}, u32[]{:S(2)}) collective-permute-start(bf16[8,32,512]{2,1,0:T(8,128)(2,1)S(1)} %get-tuple-element.106), channel_id=1, source_target_pairs={{0,1},{1,0},{2,3},{3,2},{4,5},{5,4},{6,7},{7,6},{8,9},{9,8},{10,11... | collective-permute-start | bytes 786440 | tf_op jit(solution)/shard_map/ppermute | solution.py:423
  168.2 22.8 %collective-permute-start.25 = (bf16[32,512]{1,0:T(8,128)(2,1)S(1)}, bf16[32,512]{1,0:T(8,128)(2,1)S(1)}, u32[]{:S(2)}, u32[]{:S(2)}) collective-permute-start(bf16[32,512]{1,0:T(8,128)(2,1)S(1)} %get-tuple-element.124), channel_id=1, source_target_pairs={{0,14},{1,15},{2,0},{3,1},{4,2},{5,3},{6,4},{7,5},{8,6},{9,7},{10,... | collective-permute-start | bytes 98312 | tf_op jit(solution)/shard_map/ppermute | solution.py:437
  174.6 21.9 %collective-permute-start.24 = (bf16[32,512]{1,0:T(8,128)(2,1)S(1)}, bf16[32,512]{1,0:T(8,128)(2,1)S(1)}, u32[]{:S(2)}, u32[]{:S(2)}) collective-permute-start(bf16[32,512]{1,0:T(8,128)(2,1)S(1)} %get-tuple-element.125), channel_id=1, source_target_pairs={{0,12},{1,13},{2,14},{3,15},{4,0},{5,1},{6,2},{7,3},{8,4},{9,5},{1... | collective-permute-start | bytes 98312 | tf_op jit(solution)/shard_map/ppermute | solution.py:437
  180.4 22.7 %collective-permute-start.23 = (bf16[32,512]{1,0:T(8,128)(2,1)S(1)}, bf16[32,512]{1,0:T(8,128)(2,1)S(1)}, u32[]{:S(2)}, u32[]{:S(2)}) collective-permute-start(bf16[32,512]{1,0:T(8,128)(2,1)S(1)} %get-tuple-element.126), channel_id=1, source_target_pairs={{0,10},{1,11},{2,12},{3,13},{4,14},{5,15},{6,0},{7,1},{8,2},{9,3},... | collective-permute-start | bytes 98312 | tf_op jit(solution)/shard_map/ppermute | solution.py:437
  183.9 19.3 %collective-permute-start.22 = (bf16[32,512]{1,0:T(8,128)(2,1)S(1)}, bf16[32,512]{1,0:T(8,128)(2,1)S(1)}, u32[]{:S(2)}, u32[]{:S(2)}) collective-permute-start(bf16[32,512]{1,0:T(8,128)(2,1)S(1)} %get-tuple-element.127), channel_id=1, source_target_pairs={{0,8},{1,9},{2,10},{3,11},{4,12},{5,13},{6,14},{7,15},{8,0},{9,1},... | collective-permute-start | bytes 98312 | tf_op jit(solution)/shard_map/ppermute | solution.py:437
  187.9 15.3 %collective-permute-start.21 = (bf16[32,512]{1,0:T(8,128)(2,1)S(1)}, bf16[32,512]{1,0:T(8,128)(2,1)S(1)}, u32[]{:S(2)}, u32[]{:S(2)}) collective-permute-start(bf16[32,512]{1,0:T(8,128)(2,1)S(1)} %get-tuple-element.128), channel_id=1, source_target_pairs={{0,6},{1,7},{2,8},{3,9},{4,10},{5,11},{6,12},{7,13},{8,14},{9,15},... | collective-permute-start | bytes 98312 | tf_op jit(solution)/shard_map/ppermute | solution.py:437
  191.0 12.2 %collective-permute-start.20 = (bf16[32,512]{1,0:T(8,128)(2,1)S(1)}, bf16[32,512]{1,0:T(8,128)(2,1)S(1)}, u32[]{:S(2)}, u32[]{:S(2)}) collective-permute-start(bf16[32,512]{1,0:T(8,128)(2,1)S(1)} %get-tuple-element.129), channel_id=1, source_target_pairs={{0,4},{1,5},{2,6},{3,7},{4,8},{5,9},{6,10},{7,11},{8,12},{9,13},{1... | collective-permute-start | bytes 98312 | tf_op jit(solution)/shard_map/ppermute | solution.py:437
  196.5 6.7 %collective-permute-start.19 = (bf16[32,512]{1,0:T(8,128)(2,1)S(1)}, bf16[32,512]{1,0:T(8,128)(2,1)S(1)}, u32[]{:S(2)}, u32[]{:S(2)}) collective-permute-start(bf16[32,512]{1,0:T(8,128)(2,1)S(1)} %get-tuple-element.123), channel_id=1, source_target_pairs={{0,2},{1,3},{2,4},{3,5},{4,6},{5,7},{6,8},{7,9},{8,10},{9,11},{10,... | collective-permute-start | bytes 98312 | tf_op jit(solution)/shard_map/ppermute | solution.py:437
  199.2 11.2 %all-to-all-start.4 = ((bf16[8,32,80]{2,1,0:T(8,128)(2,1)}), bf16[8,32,80]{2,1,0:T(8,128)(2,1)S(1)}, u32[]{:S(2)}, u32[]{:S(2)}) async-start(bf16[8,32,80]{2,1,0:T(8,128)(2,1)} %bitcast.26), calls=%async_computation.4 | async-start | bytes 131072 | tf_op jit(solution)/shard_map/all_to_all | solution.py:447
  (7 other events, 27.2 us)

commit v8 on v6

--- a/solution.py
+++ b/solution.py
@@ -9,7 +9,6 @@
 
 H = 8
 DH = 64
-X_CHIPS = 4
 REACH = 4
 USER_ROWS = 16
 
@@ -240,29 +239,16 @@
     att_grad_ref[...] = norm_backward(att_hat, att_inv, mixed_grad * gates).astype(bf16)
 
 
-def core_first(block, rows):
-    width = block.shape[1]
-    old = iota((width, width), 0)
-    new = iota((width, width), 1)
-    inner = jnp.bitwise_and(old, rows - 1)
-    device = jnp.right_shift(old, rows.bit_length() - 1)
-    place = jnp.bitwise_and(device, 1) * (width // 2) + jnp.right_shift(device, 1) * rows + inner
-    return dot(block, hot(new == place)).astype(bf16)
-
-
-def split_by_core(core, terms, first_owner, piece, first_row, stride, kept_ref, sent_ref):
-    half = terms.shape[1] // 2
+def split_by_core(core, terms, first_column, kept_ref, sent_ref):
+    chips = 8
+    rows = terms.shape[0] // (2 * chips)
+    columns = slice(first_column, first_column + terms.shape[1])
     even = core == 0
-    for local_owner in range(terms.shape[0] // piece):
-        owner = first_owner + local_owner
-        rows = terms[local_owner * piece : (local_owner + 1) * piece]
-        place = first_row + (local_owner // X_CHIPS) * stride
-        kept_ref[owner % X_CHIPS, place : place + piece, :] = jnp.where(
-            even, rows[:, :half], rows[:, half:]
-        ).astype(bf16)
-        sent_ref[owner % X_CHIPS, place : place + piece, :] = jnp.where(
-            even, rows[:, half:], rows[:, :half]
-        ).astype(bf16)
+    for chip in range(chips):
+        first = terms[2 * chip * rows : (2 * chip + 1) * rows]
+        second = terms[(2 * chip + 1) * rows : (2 * chip + 2) * rows]
+        kept_ref[chip * rows : (chip + 1) * rows, columns] = jnp.where(even, first, second).astype(bf16)
+        sent_ref[chip * rows : (chip + 1) * rows, columns] = jnp.where(even, second, first).astype(bf16)
 
 
 def query_body(
@@ -358,48 +344,40 @@
     outgoing_ref[...] = dot_tn(places, inputs_grad).astype(bf16)
 
 
-def early_body(
-    piece_in, piece_out, weight_rows,
-    core_ref, packed_ref, gate_query_ref, mixed_ref, grad_ref, kept_ref, sent_ref,
-):
+def early_body(core_ref, packed_ref, gate_query_ref, mixed_ref, grad_ref, kept_ref, sent_ref):
     rows, width = grad_ref.shape
     core = core_ref[0]
-    per_part = width // piece_in
-    in_rows = piece_in * per_part // X_CHIPS
-    normed = core_first(packed_ref[:rows, :], weight_rows)
-    for section, first_owner in ((0, 0), (1, 2 * per_part)):
-        terms = dot_tn(gate_query_ref[:, section * width : (section + 1) * width], normed)
-        split_by_core(
-            core, terms, first_owner, piece_in, section * in_rows, piece_in, kept_ref, sent_ref
-        )
-    terms = dot_tn(grad_ref[...], core_first(mixed_ref[...], weight_rows))
-    split_by_core(core, terms, 0, piece_out, 2 * in_rows, piece_out, kept_ref, sent_ref)
-
-
-def late_body(
-    piece_in, piece_out, weight_rows,
-    core_ref, packed_ref, value_key_ref, early_kept_ref, early_sent_ref, kept_ref, sent_ref,
-):
+    normed = packed_ref[:rows, :]
+    for section in range(2):
+        part = gate_query_ref[:, section * width : (section + 1) * width]
+        split_by_core(core, dot_tn(normed, part), section * width, kept_ref, sent_ref)
+    split_by_core(core, dot_tn(mixed_ref[...], grad_ref[...]), 2 * width, kept_ref, sent_ref)
+
+
+def late_body(core_ref, packed_ref, value_key_ref, early_kept_ref, early_sent_ref, kept_ref, sent_ref):
     rows = value_key_ref.shape[0]
     width = value_key_ref.shape[1] // 2
     core = core_ref[0]
-    piece = piece_in + piece_out
-    z_part = width // piece_in // X_CHIPS
-    z_chips = kept_ref.shape[1] // piece
     for early_ref, ref in ((early_kept_ref, kept_ref), (early_sent_ref, sent_ref)):
-        for z in range(z_chips):
-            section, inner = divmod(z, z_part)
-            if section % 2 == 0:
-                old = (section // 2 * z_part + inner) * piece_in
-                ref[:, z * piece : z * piece + piece_in, :] = early_ref[:, old : old + piece_in, :]
-            old = 2 * z_part * piece_in + z * piece_out
-            ref[:, z * piece + piece_in : (z + 1) * piece, :] = early_ref[:, old : old + piece_out, :]
-    normed = core_first(packed_ref[:rows, :], weight_rows)
+        for section in range(3):
+            ref[:, 2 * section * width : (2 * section + 1) * width] = early_ref[
+                :, section * width : (section + 1) * width
+            ]
+    normed = packed_ref[:rows, :]
     for section in range(2):
-        terms = dot_tn(value_key_ref[:, section * width : (section + 1) * width], normed)
-        split_by_core(
-            core, terms, 0, piece_in, (2 * section + 1) * z_part * piece, piece, kept_ref, sent_ref
-        )
+        part = value_key_ref[:, section * width : (section + 1) * width]
+        split_by_core(core, dot_tn(normed, part), (2 * section + 1) * width, kept_ref, sent_ref)
+
+
+def owners_body(piece_in, piece_out, share_ref, send_ref):
+    owners, rows, lanes = send_ref.shape
+    share = share_ref[...].astype(f32)
+    blank = jnp.zeros((rows, lanes - piece_in - piece_out), f32)
+    start = owners * piece_in
+    for owner in range(owners):
+        wide = share[:, owner * piece_in : (owner + 1) * piece_in]
+        thin = share[:, start + owner * piece_out : start + (owner + 1) * piece_out]
+        send_ref[owner] = jnp.concatenate([wide, thin, blank], axis=1).astype(bf16)
 
 
 def table_body(core_ref, asked_ref, arrived_ref, kept_ref, sent_ref):
@@ -435,21 +413,6 @@
 
 def total_of(blocks):
     return jnp.sum(blocks.astype(f32), axis=0)
-
-
-def sum_along_x(block):
-    devices = lax.axis_size("dp")
-    me = lax.axis_index("dp") % X_CHIPS
-    own = lax.dynamic_index_in_dim(block, me, 0, keepdims=False).astype(f32)
-    for step in range(1, X_CHIPS):
-        route = [(i, i - i % X_CHIPS + (i + step) % X_CHIPS) for i in range(devices)]
-        piece = lax.dynamic_index_in_dim(block, (me + step) % X_CHIPS, 0, keepdims=False)
-        own = own + lax.ppermute(piece, "dp", route).astype(f32)
-    return own.astype(bf16)
-
-
-def chips_along_z(owners):
-    return [list(range(first, owners, X_CHIPS)) for first in range(X_CHIPS)]
 
 
 def local(item_ids, segments, touched_rows, w_in, w_out, out_grad):
@@ -537,9 +500,9 @@
         grad_four, mate_of_four(grad_four, -1), grad_two, grad_mate_two, own_grad,
     )
     half_width = model_width // 2
-    early_block = (X_CHIPS, 3 * model_width // X_CHIPS, half_width)
+    early_block = (half_width, 3 * model_width)
     early_kept, early_sent = call(
-        lambda *refs: early_body(piece_in, piece_out, weight_rows, *refs),
+        early_body,
         [(early_block, bf16), (early_block, bf16)],
         packed, gate_query, mixed, grad_rows,
         core=core, flops=2_000_000_000, moved=4_000_000,
@@ -557,29 +520,32 @@
     arrived = lax.all_to_all(
         outgoing.reshape(owners, capacity, model_width), "dp", split_axis=0, concat_axis=0, tiled=True
     ).reshape(slots, model_width)
-    piece = piece_in + piece_out
-    z_chips = owners // X_CHIPS
-    weight_block = (X_CHIPS, z_chips * piece, half_width)
+    weight_block = (half_width, 5 * model_width)
     weight_kept, weight_sent = call(
-        lambda *refs: late_body(piece_in, piece_out, weight_rows, *refs),
+        late_body,
         [(weight_block, bf16), (weight_block, bf16)],
         packed, value_key, early_kept, early_sent,
         core=core, flops=1_500_000_000, moved=3_000_000,
     )
-    along_x = sum_along_x(pair_sum(weight_kept, weight_sent)).reshape(z_chips, piece, half_width)
-    arrived, along_x = lax.optimization_barrier((arrived, along_x))
-    along_dp = total_of(spread(along_x, "dp", chips_along_z(owners))).astype(bf16)
-    weight_terms = along_dp.T.reshape(chips, weight_rows, piece)
+    share = lax.psum_scatter(
+        pair_sum(weight_kept, weight_sent), "ctx", scatter_dimension=0, tiled=True,
+        axis_index_groups=chips_along_y(),
+    )
+    (weight_send,) = call(
+        lambda *refs: owners_body(piece_in, piece_out, *refs),
+        [((owners, weight_rows, 128), bf16)], share,
+    )
     table_block = (chips, model_width // (2 * chips), table_dev)
     table_kept, table_sent = call(
         table_body, [(table_block, bf16), (table_block, bf16)], asked_row, arrived, core=core
     )
     table_sum = pair_sum(table_kept, table_sent)
-    last = jnp.concatenate([table_sum, weight_terms], axis=2)
-    summed = total_of(spread(last, "ctx", chips_along_y()))
-    table_grad = summed[:, :table_dev].T
-    w_in_grad = summed[:, table_dev : table_dev + piece_in]
-    w_out_grad = summed[:, table_dev + piece_in :]
+    table_spread = spread(table_sum, "ctx", chips_along_y())
+    table_spread, weight_send = lax.optimization_barrier((table_spread, weight_send))
+    table_grad = total_of(table_spread).T
+    weight_grad = total_of(spread(weight_send, "dp", None))
+    w_in_grad = weight_grad[:, :piece_in]
+    w_out_grad = weight_grad[:, piece_in : piece_in + piece_out]
     return (layer_out[None], table_grad, w_in_grad, w_out_grad)
 
 

time: 201 us -> 214 us (1.065)
  blocking collectives: 42.2 us -> 22.1 us
  waiting for transfers between devices: 64 us -> 79.6 us
  between operations: 1.13 us -> 14.4 us
  starting transfers between devices: 61.2 us -> 65 us
    all_to_all x1, waiting for transfers between devices: 0.01 us -> 23.6 us  [local(): lax.all_to_all(outgoing.reshape(owners, capacity, model_width), 'dp', spl...]
    ppermute x3 -> x0, waiting for transfers between devices: 21.3 us -> none  [sum_along_x(): own = own + lax.ppermute(piece, 'dp', route).astype(f32)]
    all_to_all x1 -> x0, blocking collectives: 20.1 us -> none  [spread(): lax.all_to_all(block, axis, split_axis=0, concat_axis=0, tiled=True, axis...]
    all_to_all x1 -> x2, starting transfers between devices: 5.36 us -> 15.7 us  [spread(): lax.all_to_all(block, axis, split_axis=0, concat_axis=0, tiled=True, axis...]
    all_to_all x1 -> x2, waiting for transfers between devices: 8.17 us -> 18.1 us  [spread(): lax.all_to_all(block, axis, split_axis=0, concat_axis=0, tiled=True, axis...]
    ppermute x3 -> x0, starting transfers between devices: 9.32 us -> none  [sum_along_x(): own = own + lax.ppermute(piece, 'dp', route).astype(f32)]
    reduce_scatter x0 -> x1, waiting for transfers between devices: none -> 2.24 us  [local(): lax.psum_scatter(pair_sum(weight_kept, weight_sent), 'ctx', scatter_dimen...]
    unnamed x19 -> x21, local copies, waits for them, and re-layouts: 6.65 us -> 6.5 us
  transfers between devices with their start and end apart: 22 -> 21, of which waited for: 9 -> 9; matrix products, arithmetic and copies ran while one was open for 2% -> 2% of each run, Pallas kernels for 4% -> 4%
where the time goes in v8:
time: 214 us; the launch traced here: 210 us
  waiting for transfers between devices  79.6 us (37%)
  starting transfers between devices  65 us (30%)
  blocking collectives  22.1 us (10%)
  Pallas kernels  18.3 us (9%)
  between operations  14.4 us (7%)
  local copies, waits for them, and re-layouts  6.57 us (3%)
  other arithmetic  4.19 us (2%)
    all_to_all x1, waiting for transfers between devices, local(): lax.all_to_all(found.reshape(owners, capacity, model_width), 'dp', split_...  25.2 us
    all_to_all x1, waiting for transfers between devices, local(): lax.all_to_all(outgoing.reshape(owners, capacity, model_width), 'dp', spl...  23.6 us
    all_to_all x1, blocking collectives, local(): lax.all_to_all(requests, 'dp', split_axis=0, concat_axis=0, tiled=True)  22.1 us
    ppermute x8, starting transfers between devices, swapped(): lax.ppermute(block, 'ctx', [(i, i ^ 1) for i in devices if i % 2 in sende...  21 us
    pallas_call x11, Pallas kernels, call(): pl.pallas_call(body, out_shape=[jax.ShapeDtypeStruct(shape, kind) for sha...  18.3 us
    all_to_all x2, waiting for transfers between devices, spread(): lax.all_to_all(block, axis, split_axis=0, concat_axis=0, tiled=True, axis...  18.1 us
    all_to_all x2, starting transfers between devices, spread(): lax.all_to_all(block, axis, split_axis=0, concat_axis=0, tiled=True, axis...  15.7 us
    ppermute x6, starting transfers between devices, passed_along(): return lax.ppermute(block, axis, route)  12.7 us
  transfers between devices with their start and end apart: 21, of which 9 were waited for; matrix products, arithmetic and copies ran while one was open for 2% of the time, Pallas kernels for 4%

profile of v8, /device:TPU:1, one launch (start us, length us, event | category | flops | bytes accessed | tf_op | source)
XLA Modules:
  0.0 210.1 jit_solution(158446223233053489)
XLA Ops:
  8.5 22.1 %all_to_all.31 = s32[32,1,32]{2,1,0:T(1,128)S(1)} all-to-all(s32[32,1,32]{2,1,0:T(1,128)S(1)} %bitcast.17), channel_id=1, replica_groups=mesh['dp'=32,'ctx'=16] {'dp'}, dimensions={0} | all-to-all | bytes 8192 | tf_op jit(solution)/shard_map/all_to_all | solution.py:441
  31.6 1.9 shard_map.94
  33.5 4.1 %all-to-all-start.1 = ((bf16[32,32,512]{2,1,0:T(8,128)(2,1)}), bf16[32,32,512]{2,1,0:T(8,128)(2,1)S(1)}, u32[]{:S(2)}, u32[]{:S(2)}) async-start(bf16[32,32,512]{2,1,0:T(8,128)(2,1)} %bitcast.5), calls=%async_computation.1 | async-start | bytes 2097152 | tf_op jit(solution)/shard_map/all_to_all | solution.py:445
  37.6 25.2 %all-to-all-done.1 = bf16[32,32,512]{2,1,0:T(8,128)(2,1)S(1)} async-done(((bf16[32,32,512]{2,1,0:T(8,128)(2,1)}), bf16[32,32,512]{2,1,0:T(8,128)(2,1)S(1)}, u32[]{:S(2)}, u32[]{:S(2)}) %all-to-all-start.1) | async-done | bytes 1048608 | tf_op jit(solution)/shard_map/all_to_all | solution.py:445
  63.4 3.2 %collective-permute-start = (bf16[144,512]{1,0:T(8,128)(2,1)S(1)}, bf16[144,512]{1,0:T(8,128)(2,1)S(1)}, u32[]{:S(2)}, u32[]{:S(2)}) collective-permute-start(bf16[144,512]{1,0:T(8,128)(2,1)S(1)} %get-tuple-element.63.packed_ref), channel_id=1, source_target_pairs={{0,2},{1,3},{2,4},{3,5},{4,6},{5,7},{6,8},{7,9},{8,10},{9,11},{10,... | collective-permute-start | bytes 442376 | tf_op jit(solution)/shard_map/ppermute | solution.py:23
  66.6 1.6 copy-done.2
  70.2 6.3 %collective-permute-start.3 = (bf16[144,512]{1,0:T(8,128)(2,1)S(1)}, bf16[144,512]{1,0:T(8,128)(2,1)S(1)}, u32[]{:S(2)}, u32[]{:S(2)}) collective-permute-start(bf16[144,512]{1,0:T(8,128)(2,1)S(1)} %get-tuple-element.63.packed_ref), channel_id=1, source_target_pairs={{0,1},{1,0},{2,3},{3,2},{4,5},{5,4},{6,7},{7,6},{8,9},{9,8},{10,11... | collective-permute-start | bytes 442376 | tf_op jit(solution)/shard_map/ppermute | solution.py:28
  76.5 1.9 collective-permute-start.2
  78.4 4.3 %collective-permute-start.1 = (bf16[144,512]{1,0:T(8,128)(2,1)S(1)}, bf16[144,512]{1,0:T(8,128)(2,1)S(1)}, u32[]{:S(2)}, u32[]{:S(2)}) collective-permute-start(bf16[144,512]{1,0:T(8,128)(2,1)S(1)} %collective-permute-done.two_ref), channel_id=1, source_target_pairs={{0,2},{1,3},{2,4},{3,5},{4,6},{5,7},{6,8},{7,9},{8,10},{9,11},{10,... | collective-permute-start | bytes 442376 | tf_op jit(solution)/shard_map/ppermute | solution.py:23
  82.7 2.7 %collective-permute-start.6 = (bf16[144,512]{1,0:T(8,128)(2,1)S(1)}, bf16[144,512]{1,0:T(8,128)(2,1)S(1)}, u32[]{:S(2)}, u32[]{:S(2)}) collective-permute-start(bf16[144,512]{1,0:T(8,128)(2,1)S(1)} %collective-permute-done.5.two_ref), channel_id=1, source_target_pairs={{0,1},{1,0},{2,3},{3,2},{4,5},{5,4},{6,7},{7,6},{8,9},{9,8},{10,11... | collective-permute-start | bytes 442376 | tf_op jit(solution)/shard_map/ppermute | solution.py:28
  85.4 3.2 %collective-permute-start.4 = (bf16[144,512]{1,0:T(8,128)(2,1)S(1)}, bf16[144,512]{1,0:T(8,128)(2,1)S(1)}, u32[]{:S(2)}, u32[]{:S(2)}) collective-permute-start(bf16[144,512]{1,0:T(8,128)(2,1)S(1)} %collective-permute-done.1.four_ref), channel_id=1, source_target_pairs={{1,0},{3,2},{5,4},{7,6},{9,8},{11,10},{13,12},{15,14},{17,16},{19,... | collective-permute-start | bytes 442376 | tf_op jit(solution)/shard_map/ppermute | solution.py:28
  90.0 1.6 copy-done.3
  91.6 3.1 %shard_map.97 = (bf16[128,512]{1,0:T(8,128)(2,1)}, bf16[128,512]{1,0:T(8,128)(2,1)S(1)}, f32[128,512]{1,0:T(8,128)S(1)}, bf16[128,512]{1,0:T(8,128)(2,1)S(1)}, b...) custom-call(s32[1]{0:T(128)} %bitcast.core_ref, ...), custom_call_target="tpu_custom_call" | custom-call | flops 4000000000 | bytes 8000000 | tf_op jit(solution)/shard_map/pallas_call | solution.py:119
  94.6 1.9 collective-permute-start.8
  99.2 4.8 %collective-permute-done.9.two_ref = bf16[128,512]{1,0:T(8,128)(2,1)S(1)} collective-permute-done((bf16[128,512]{1,0:T(8,128)(2,1)S(1)}, bf16[128,512]{1,0:T(8,128)(2,1)S(1)}, u32[]{:S(2)}, u32[]{:S(2)}) %collective-permute-start.9) | collective-permute-done | bytes 131104 | tf_op jit(solution)/shard_map/ppermute | solution.py:23
  104.0 2.2 %collective-permute-start.10 = (bf16[128,512]{1,0:T(8,128)(2,1)S(1)}, bf16[128,512]{1,0:T(8,128)(2,1)S(1)}, u32[]{:S(2)}, u32[]{:S(2)}) collective-permute-start(bf16[128,512]{1,0:T(8,128)(2,1)S(1)} %collective-permute-done.9.two_ref), channel_id=1, source_target_pairs={{0,1},{1,0},{2,3},{3,2},{4,5},{5,4},{6,7},{7,6},{8,9},{9,8},{10,11... | collective-permute-start | bytes 393224 | tf_op jit(solution)/shard_map/ppermute | solution.py:28
  106.2 1.3 collective-permute-start.12
  107.5 2.8 %shard_map.98 = (bf16[128,1024]{1,0:T(8,128)(2,1)S(1)}, f32[128,1024]{1,0:T(8,128)S(1)}, bf16[640,512]{1,0:T(8,128)(2,1)S(1)}, f32[640,1]{1,0:T(8,128)S(1)}) custom-call(s32[1]{0:T(128)} %bitcast.core_ref, bf16[128,512]{1,0:T(8,128)(2,1)S(1)} %get-tuple-element.70.queries_ref, bf16[640,512]{1,0:T(8,128)(2,1)S(1)} %get-tuple-element.76.all_keys_ref, ...), custom_call_target="tpu_custom_call" | custom-call | flops 4000000000 | bytes 8000000 | tf_op jit(solution)/shard_map/pallas_call | solution.py:119
  110.3 3.3 %collective-permute-done.12.four_ref = bf16[128,512]{1,0:T(8,128)(2,1)S(1)} collective-permute-done((bf16[128,512]{1,0:T(8,128)(2,1)S(1)}, bf16[128,512]{1,0:T(8,128)(2,1)S(1)}, u32[]{:S(2)}, u32[]{:S(2)}) %collective-permute-start.12) | collective-permute-done | bytes 131104 | tf_op jit(solution)/shard_map/ppermute | solution.py:23
  113.6 1.5 collective-permute-start.13
  116.8 4.9 %shard_map.100 = (bf16[128,1024]{1,0:T(8,128)(2,1)S(1)}, bf16[1024,512]{1,0:T(8,128)(2,1)}) custom-call(s32[1]{0:T(128)} %bitcast.core_ref, bf16[640,512]{1,0:T(8,128)(2,1)S(1)} %get-tuple-element.85.all_queries_ref, f32[640,1]{1,0:T(8,128)S(1)} %get-tuple-element.86.query_user_ref, bf16[128,512]{1,0:T(8,128)(2,1)S(1)} %get-tuple-element.78.att_grad_ref, ...), custom_call_target="tpu_custom_call" | custom-call | flops 4000000000 | bytes 8000000 | tf_op jit(solution)/shard_map/pallas_call | solution.py:119
  121.7 1.6 shard_map.102
  123.3 2.0 collective-permute-start.15
  125.4 5.0 %all-to-all-start.2 = ((bf16[32,32,512]{2,1,0:T(8,128)(2,1)}), bf16[32,32,512]{2,1,0:T(8,128)(2,1)S(1)}, u32[]{:S(2)}, u32[]{:S(2)}) async-start(bf16[32,32,512]{2,1,0:T(8,128)(2,1)} %bitcast.9), calls=%async_computation.2 | async-start | bytes 2097152 | tf_op jit(solution)/shard_map/all_to_all | solution.py:520
  130.4 2.7 %add_convert_fusion = bf16[256,2560]{1,0:T(8,128)(2,1)} fusion(bf16[256,2560]{1,0:T(8,128)(2,1)} %collective-permute-done.15, bf16[256,2560]{1,0:T(8,128)(2,1)S(1)} %get-tuple-element.104), kind=kLoop, calls=%fused_computation | loop fusion | flops 2621440 | bytes 3932160 | tf_op jit(solution)/shard_map/convert_element_type | solution.py:400
  133.1 23.6 %all-to-all-done.2 = bf16[32,32,512]{2,1,0:T(8,128)(2,1)S(1)} async-done(((bf16[32,32,512]{2,1,0:T(8,128)(2,1)}), bf16[32,32,512]{2,1,0:T(8,128)(2,1)S(1)}, u32[]{:S(2)}, u32[]{:S(2)}) %all-to-all-start.2) | async-done | bytes 1048608 | tf_op jit(solution)/shard_map/all_to_all | solution.py:520
  157.5 4.5 %collective-permute-start.14 = (bf16[8,32,512]{2,1,0:T(8,128)(2,1)S(1)}, bf16[8,32,512]{2,1,0:T(8,128)(2,1)S(1)}, u32[]{:S(2)}, u32[]{:S(2)}) collective-permute-start(bf16[8,32,512]{2,1,0:T(8,128)(2,1)S(1)} %get-tuple-element.100), channel_id=1, source_target_pairs={{0,1},{1,0},{2,3},{3,2},{4,5},{5,4},{6,7},{7,6},{8,9},{9,8},{10,11... | collective-permute-start | bytes 786440 | tf_op jit(solution)/shard_map/ppermute | solution.py:399
  164.0 9.8 %all-to-all-start.3 = ((bf16[8,32,512]{2,1,0:T(8,128)(2,1)}), bf16[8,32,512]{2,1,0:T(8,128)(2,1)S(1)}, u32[]{:S(2)}, u32[]{:S(2)}) async-start(bf16[8,32,512]{2,1,0:T(8,128)(2,1)} %add_convert_fusion.1), calls=%async_computation.3 | async-start | bytes 524288 | tf_op jit(solution)/shard_map/all_to_all | solution.py:409
  173.8 2.2 %reduce-scatter.2.cloned.1.call-done.refs_0_ = bf16[32,2560]{1,0:T(8,128)(2,1)} async-done(((bf16[256,2560]{1,0:T(8,128)(2,1)}), bf16[32,2560]{1,0:T(8,128)(2,1)}) %reduce-scatter.2.cloned.1.call-update) | async-done | bytes 163856 | tf_op jit(solution)/shard_map/reduce_scatter | solution.py:530
  177.8 8.4 %all-to-all-done.3 = bf16[8,32,512]{2,1,0:T(8,128)(2,1)S(1)} async-done(((bf16[8,32,512]{2,1,0:T(8,128)(2,1)}), bf16[8,32,512]{2,1,0:T(8,128)(2,1)S(1)}, u32[]{:S(2)}, u32[]{:S(2)}) %all-to-all-start.3) | async-done | bytes 262176 | tf_op jit(solution)/shard_map/all_to_all | solution.py:409
  186.2 5.9 %all-to-all-start.4 = ((bf16[32,32,128]{2,1,0:T(8,128)(2,1)}), bf16[32,32,128]{2,1,0:T(8,128)(2,1)S(1)}, u32[]{:S(2)}, u32[]{:S(2)}) async-start(bf16[32,32,128]{2,1,0:T(8,128)(2,1)} %shard_map.103), calls=%async_computation.5 | async-start | bytes 524288 | tf_op jit(solution)/shard_map/all_to_all | solution.py:409
  192.7 9.7 %all-to-all-done.4 = bf16[32,32,128]{2,1,0:T(8,128)(2,1)S(1)} async-done(((bf16[32,32,128]{2,1,0:T(8,128)(2,1)}), bf16[32,32,128]{2,1,0:T(8,128)(2,1)S(1)}, u32[]{:S(2)}, u32[]{:S(2)}) %all-to-all-start.4) | async-done | bytes 262176 | tf_op jit(solution)/shard_map/all_to_all | solution.py:409
  (50 shorter events, 16.5 us)
Async XLA Ops:
  7.2 0.7 copy-start.7
  30.6 1.0 copy-start
  31.6 6.0 %copy-start.9 = (s32[1,128]{1,0:T(1,128)S(1)}, s32[1,128]{1,0:T(1,128)}, u32[]{:S(2)}) copy-start(s32[1,128]{1,0:T(1,128)} %param.7) | copy-start | bytes 1540
  33.5 33.1 %copy-start.5 = (bf16[512,512]{1,0:T(8,128)(2,1)S(1)}, bf16[512,512]{1,0:T(8,128)(2,1)}, u32[]{:S(2)}) copy-start(bf16[512,512]{1,0:T(8,128)(2,1)} %w_out_ref.3) | copy-start | bytes 1572868
  33.5 33.1 %copy-start.6 = (bf16[1,128,512]{2,1,0:T(8,128)(2,1)S(1)}, bf16[1,128,512]{2,1,0:T(8,128)(2,1)}, u32[]{:S(2)}) copy-start(bf16[1,128,512]{2,1,0:T(8,128)(2,1)} %param.11) | copy-start | bytes 393220
  33.5 29.3 %all-to-all-start.1 = ((bf16[32,32,512]{2,1,0:T(8,128)(2,1)}), bf16[32,32,512]{2,1,0:T(8,128)(2,1)S(1)}, u32[]{:S(2)}, u32[]{:S(2)}) async-start(bf16[32,32,512]{2,1,0:T(8,128)(2,1)} %bitcast.5), calls=%async_computation.1 | async-start | bytes 2097152 | tf_op jit(solution)/shard_map/all_to_all | solution.py:445
  63.4 13.1 %collective-permute-start = (bf16[144,512]{1,0:T(8,128)(2,1)S(1)}, bf16[144,512]{1,0:T(8,128)(2,1)S(1)}, u32[]{:S(2)}, u32[]{:S(2)}) collective-permute-start(bf16[144,512]{1,0:T(8,128)(2,1)S(1)} %get-tuple-element.63.packed_ref), channel_id=1, source_target_pairs={{0,2},{1,3},{2,4},{3,5},{4,6},{5,7},{6,8},{7,9},{8,10},{9,11},{10,... | collective-permute-start | bytes 442376 | tf_op jit(solution)/shard_map/ppermute | solution.py:23
  66.6 1.6 copy-start.2
  68.9 13.8 %collective-permute-start.5 = (bf16[144,512]{1,0:T(8,128)(2,1)S(1)}, bf16[144,512]{1,0:T(8,128)(2,1)S(1)}, u32[]{:S(2)}, u32[]{:S(2)}) collective-permute-start(bf16[144,512]{1,0:T(8,128)(2,1)S(1)} %get-tuple-element.63.packed_ref), channel_id=1, source_target_pairs={{2,0},{3,1},{4,2},{5,3},{6,4},{7,5},{8,6},{9,7},{10,8},{11,9},{12,... | collective-permute-start | bytes 442376 | tf_op jit(solution)/shard_map/ppermute | solution.py:23
  70.2 15.2 %collective-permute-start.3 = (bf16[144,512]{1,0:T(8,128)(2,1)S(1)}, bf16[144,512]{1,0:T(8,128)(2,1)S(1)}, u32[]{:S(2)}, u32[]{:S(2)}) collective-permute-start(bf16[144,512]{1,0:T(8,128)(2,1)S(1)} %get-tuple-element.63.packed_ref), channel_id=1, source_target_pairs={{0,1},{1,0},{2,3},{3,2},{4,5},{5,4},{6,7},{7,6},{8,9},{9,8},{10,11... | collective-permute-start | bytes 442376 | tf_op jit(solution)/shard_map/ppermute | solution.py:28
  76.5 8.9 %collective-permute-start.2 = (bf16[144,512]{1,0:T(8,128)(2,1)S(1)}, bf16[144,512]{1,0:T(8,128)(2,1)S(1)}, u32[]{:S(2)}, u32[]{:S(2)}) collective-permute-start(bf16[144,512]{1,0:T(8,128)(2,1)S(1)} %collective-permute-done.two_ref), channel_id=1, source_target_pairs={{0,1},{1,0},{2,3},{3,2},{4,5},{5,4},{6,7},{7,6},{8,9},{9,8},{10,11... | collective-permute-start | bytes 442376 | tf_op jit(solution)/shard_map/ppermute | solution.py:28
  78.4 7.0 %collective-permute-start.1 = (bf16[144,512]{1,0:T(8,128)(2,1)S(1)}, bf16[144,512]{1,0:T(8,128)(2,1)S(1)}, u32[]{:S(2)}, u32[]{:S(2)}) collective-permute-start(bf16[144,512]{1,0:T(8,128)(2,1)S(1)} %collective-permute-done.two_ref), channel_id=1, source_target_pairs={{0,2},{1,3},{2,4},{3,5},{4,6},{5,7},{6,8},{7,9},{8,10},{9,11},{10,... | collective-permute-start | bytes 442376 | tf_op jit(solution)/shard_map/ppermute | solution.py:23
  82.7 7.2 %collective-permute-start.6 = (bf16[144,512]{1,0:T(8,128)(2,1)S(1)}, bf16[144,512]{1,0:T(8,128)(2,1)S(1)}, u32[]{:S(2)}, u32[]{:S(2)}) collective-permute-start(bf16[144,512]{1,0:T(8,128)(2,1)S(1)} %collective-permute-done.5.two_ref), channel_id=1, source_target_pairs={{0,1},{1,0},{2,3},{3,2},{4,5},{5,4},{6,7},{7,6},{8,9},{9,8},{10,11... | collective-permute-start | bytes 442376 | tf_op jit(solution)/shard_map/ppermute | solution.py:28
  85.4 4.5 %collective-permute-start.4 = (bf16[144,512]{1,0:T(8,128)(2,1)S(1)}, bf16[144,512]{1,0:T(8,128)(2,1)S(1)}, u32[]{:S(2)}, u32[]{:S(2)}) collective-permute-start(bf16[144,512]{1,0:T(8,128)(2,1)S(1)} %collective-permute-done.1.four_ref), channel_id=1, source_target_pairs={{1,0},{3,2},{5,4},{7,6},{9,8},{11,10},{13,12},{15,14},{17,16},{19,... | collective-permute-start | bytes 442376 | tf_op jit(solution)/shard_map/ppermute | solution.py:28
  88.6 9.2 %collective-permute-start.7 = (bf16[144,512]{1,0:T(8,128)(2,1)S(1)}, bf16[144,512]{1,0:T(8,128)(2,1)S(1)}, u32[]{:S(2)}, u32[]{:S(2)}) collective-permute-start(bf16[144,512]{1,0:T(8,128)(2,1)S(1)} %collective-permute-done.5.two_ref), channel_id=1, source_target_pairs={{2,0},{3,1},{4,2},{5,3},{6,4},{7,5},{8,6},{9,7},{10,8},{11,9},{12,... | collective-permute-start | bytes 442376 | tf_op jit(solution)/shard_map/ppermute | solution.py:23
  90.0 1.6 copy-start.3
  91.5 16.0 %copy-start.4 = (bf16[512,2048]{1,0:T(8,128)(2,1)S(1)}, bf16[512,2048]{1,0:T(8,128)(2,1)}, u32[]{:S(2)}) copy-start(bf16[512,2048]{1,0:T(8,128)(2,1)} %w_in_ref.7) | copy-start | bytes 6291460
  94.6 3.2 %collective-permute-start.8 = (bf16[128,512]{1,0:T(8,128)(2,1)S(1)}, bf16[128,512]{1,0:T(8,128)(2,1)S(1)}, u32[]{:S(2)}, u32[]{:S(2)}) collective-permute-start(bf16[128,512]{1,0:T(8,128)(2,1)S(1)} %get-tuple-element.78.att_grad_ref), channel_id=1, source_target_pairs={{1,0},{3,2},{5,4},{7,6},{9,8},{11,10},{13,12},{15,14},{17,16},{19,... | collective-permute-start | bytes 393224 | tf_op jit(solution)/shard_map/ppermute | solution.py:28
  96.5 7.4 %collective-permute-start.9 = (bf16[128,512]{1,0:T(8,128)(2,1)S(1)}, bf16[128,512]{1,0:T(8,128)(2,1)S(1)}, u32[]{:S(2)}, u32[]{:S(2)}) collective-permute-start(bf16[128,512]{1,0:T(8,128)(2,1)S(1)} %get-tuple-element.78.att_grad_ref), channel_id=1, source_target_pairs={{2,0},{3,1},{4,2},{5,3},{6,4},{7,5},{8,6},{9,7},{10,8},{11,9},{12,... | collective-permute-start | bytes 393224 | tf_op jit(solution)/shard_map/ppermute | solution.py:23
  97.9 9.6 %collective-permute-start.11 = (bf16[144,512]{1,0:T(8,128)(2,1)S(1)}, bf16[144,512]{1,0:T(8,128)(2,1)S(1)}, u32[]{:S(2)}, u32[]{:S(2)}) collective-permute-start(bf16[144,512]{1,0:T(8,128)(2,1)S(1)} %collective-permute-done.7.four_ref), channel_id=1, source_target_pairs={{0,1},{2,3},{4,5},{6,7},{8,9},{10,11},{12,13},{14,15},{16,17},{18,... | collective-permute-start | bytes 442376 | tf_op jit(solution)/shard_map/ppermute | solution.py:28
  104.0 3.5 %collective-permute-start.10 = (bf16[128,512]{1,0:T(8,128)(2,1)S(1)}, bf16[128,512]{1,0:T(8,128)(2,1)S(1)}, u32[]{:S(2)}, u32[]{:S(2)}) collective-permute-start(bf16[128,512]{1,0:T(8,128)(2,1)S(1)} %collective-permute-done.9.two_ref), channel_id=1, source_target_pairs={{0,1},{1,0},{2,3},{3,2},{4,5},{5,4},{6,7},{7,6},{8,9},{9,8},{10,11... | collective-permute-start | bytes 393224 | tf_op jit(solution)/shard_map/ppermute | solution.py:28
  106.2 7.4 %collective-permute-start.12 = (bf16[128,512]{1,0:T(8,128)(2,1)S(1)}, bf16[128,512]{1,0:T(8,128)(2,1)S(1)}, u32[]{:S(2)}, u32[]{:S(2)}) collective-permute-start(bf16[128,512]{1,0:T(8,128)(2,1)S(1)} %collective-permute-done.9.two_ref), channel_id=1, source_target_pairs={{2,0},{3,1},{4,2},{5,3},{6,4},{7,5},{8,6},{9,7},{10,8},{11,9},{12,... | collective-permute-start | bytes 393224 | tf_op jit(solution)/shard_map/ppermute | solution.py:23
  113.6 3.2 %collective-permute-start.13 = (bf16[128,512]{1,0:T(8,128)(2,1)S(1)}, bf16[128,512]{1,0:T(8,128)(2,1)S(1)}, u32[]{:S(2)}, u32[]{:S(2)}) collective-permute-start(bf16[128,512]{1,0:T(8,128)(2,1)S(1)} %collective-permute-done.12.four_ref), channel_id=1, source_target_pairs={{0,1},{2,3},{4,5},{6,7},{8,9},{10,11},{12,13},{14,15},{16,17},{18,... | collective-permute-start | bytes 393224 | tf_op jit(solution)/shard_map/ppermute | solution.py:28
  123.3 7.1 %collective-permute-start.15 = (bf16[256,2560]{1,0:T(8,128)(2,1)}, bf16[256,2560]{1,0:T(8,128)(2,1)}, u32[]{:S(2)}, u32[]{:S(2)}) collective-permute-start(bf16[256,2560]{1,0:T(8,128)(2,1)} %get-tuple-element.105), channel_id=1, source_target_pairs={{0,1},{1,0},{2,3},{3,2},{4,5},{5,4},{6,7},{7,6},{8,9},{9,8},{10,11... | collective-permute-start | bytes 3932168 | tf_op jit(solution)/shard_map/ppermute | solution.py:399
  125.4 31.4 %all-to-all-start.2 = ((bf16[32,32,512]{2,1,0:T(8,128)(2,1)}), bf16[32,32,512]{2,1,0:T(8,128)(2,1)S(1)}, u32[]{:S(2)}, u32[]{:S(2)}) async-start(bf16[32,32,512]{2,1,0:T(8,128)(2,1)} %bitcast.9), calls=%async_computation.2 | async-start | bytes 2097152 | tf_op jit(solution)/shard_map/all_to_all | solution.py:520
  130.3 45.7 %reduce-scatter.2.cloned.1.call-start = ((), (), s32[]{:S(2)}) async-start(), calls=%async_computation.6 | async-start | bytes 1474560 | tf_op jit(solution)/shard_map/reduce_scatter | solution.py:530
  157.5 5.7 %collective-permute-start.14 = (bf16[8,32,512]{2,1,0:T(8,128)(2,1)S(1)}, bf16[8,32,512]{2,1,0:T(8,128)(2,1)S(1)}, u32[]{:S(2)}, u32[]{:S(2)}) collective-permute-start(bf16[8,32,512]{2,1,0:T(8,128)(2,1)S(1)} %get-tuple-element.100), channel_id=1, source_target_pairs={{0,1},{1,0},{2,3},{3,2},{4,5},{5,4},{6,7},{7,6},{8,9},{9,8},{10,11... | collective-permute-start | bytes 786440 | tf_op jit(solution)/shard_map/ppermute | solution.py:399
  164.0 22.2 %all-to-all-start.3 = ((bf16[8,32,512]{2,1,0:T(8,128)(2,1)}), bf16[8,32,512]{2,1,0:T(8,128)(2,1)S(1)}, u32[]{:S(2)}, u32[]{:S(2)}) async-start(bf16[8,32,512]{2,1,0:T(8,128)(2,1)} %add_convert_fusion.1), calls=%async_computation.3 | async-start | bytes 524288 | tf_op jit(solution)/shard_map/all_to_all | solution.py:409
  176.1 0.9 copy-start.1
  186.2 16.3 %all-to-all-start.4 = ((bf16[32,32,128]{2,1,0:T(8,128)(2,1)}), bf16[32,32,128]{2,1,0:T(8,128)(2,1)S(1)}, u32[]{:S(2)}, u32[]{:S(2)}) async-start(bf16[32,32,128]{2,1,0:T(8,128)(2,1)} %shard_map.103), calls=%async_computation.5 | async-start | bytes 524288 | tf_op jit(solution)/shard_map/all_to_all | solution.py:409
  202.5 0.8 copy-start.8
Sparse Core Ops, SparseCore 0:
  134.0 41.9 reduce-scatter.1

commit v9 on v6

--- a/solution.py
+++ b/solution.py
@@ -308,40 +308,60 @@
     )
 
 
-def key_body(
-    core_ref, all_queries_ref, query_user_ref, att_grad_ref,
-    four_ref, mate_four_ref, two_ref, mate_two_ref, mate_own_ref,
-    keys_ref, values_ref, value_key_slope_ref, gate_query_ref, w_in_ref, inputs_ref, out_grad_ref, slot_ref, user_ref,
-    value_key_ref, outgoing_ref,
-):
-    rows, width = inputs_ref.shape
+def key_terms(queries, query_user, grads, first_row, keys_ref, values_ref, user_row):
     score_scale = 1.0 / math.sqrt(DH)
-    user_row = user_ref[...]
-    query_user = query_user_ref[...]
-    halos = nearest_first(
-        core_ref[0], four_ref[...], mate_four_ref[...], two_ref[...], mate_two_ref[...], mate_own_ref[...]
-    )
-    all_grads = jnp.concatenate((att_grad_ref[...],) + halos, axis=0)
-    total = query_user.shape[0]
-    allowed = (query_user == user_row) & (iota((total, rows), 1) <= iota((total, rows), 0))
+    total = queries.shape[0]
+    rows = user_row.shape[1]
+    allowed = (query_user == user_row) & (
+        iota((total, rows), 1) <= iota((total, rows), 0) + first_row
+    )
     weight = allowed.astype(f32)
     allowed = jnp.concatenate([weight, weight], axis=0) > 0.0
     key_parts = []
     value_parts = []
     for pair in range(H // 2):
         columns = slice(2 * DH * pair, 2 * DH * (pair + 1))
-        queries = both_heads(all_queries_ref[:, columns])
-        grads = both_heads(all_grads[:, columns])
-        scores = dot_nt(queries, keys_ref[:, columns]) * score_scale
+        pair_queries = both_heads(queries[:, columns])
+        pair_grads = both_heads(grads[:, columns])
+        scores = dot_nt(pair_queries, keys_ref[:, columns]) * score_scale
         sig = sigmoid(scores)
         raw = scores * sig
         weights = jnp.where(allowed, raw, 0.0).astype(bf16)
-        prob_grad = dot_nt(grads, values_ref[:, columns])
+        prob_grad = dot_nt(pair_grads, values_ref[:, columns])
         score_grad = jnp.where(allowed, prob_grad * (sig + raw * (1.0 - sig)), 0.0).astype(bf16)
-        key_parts.append(dot_tn(score_grad, queries) * score_scale)
-        value_parts.append(dot_tn(weights, grads))
-    key_grad = jnp.concatenate(key_parts, axis=1)
-    value_grad = jnp.concatenate(value_parts, axis=1)
+        key_parts.append(dot_tn(score_grad, pair_queries) * score_scale)
+        value_parts.append(dot_tn(weights, pair_grads))
+    return jnp.concatenate(key_parts, axis=1), jnp.concatenate(value_parts, axis=1)
+
+
+def near_body(
+    core_ref, all_queries_ref, query_user_ref, att_grad_ref, two_ref, mate_two_ref, mate_own_ref,
+    keys_ref, values_ref, user_ref, key_grad_ref, value_grad_ref,
+):
+    rows = att_grad_ref.shape[0]
+    near = jnp.where(core_ref[0] == 0, mate_own_ref[...], mate_two_ref[...])
+    grads = jnp.concatenate([att_grad_ref[...], near, two_ref[...]], axis=0)
+    key_grad_ref[...], value_grad_ref[...] = key_terms(
+        all_queries_ref[: 3 * rows, :], query_user_ref[: 3 * rows, :], grads, 0,
+        keys_ref, values_ref, user_ref[...],
+    )
+
+
+def key_body(
+    core_ref, all_queries_ref, query_user_ref, four_ref, mate_four_ref, mate_two_ref,
+    keys_ref, values_ref, near_key_ref, near_value_ref, value_key_slope_ref, gate_query_ref,
+    w_in_ref, inputs_ref, out_grad_ref, slot_ref, user_ref,
+    value_key_ref, outgoing_ref,
+):
+    rows, width = inputs_ref.shape
+    third = jnp.where(core_ref[0] == 0, mate_two_ref[...], mate_four_ref[...])
+    far_key, far_value = key_terms(
+        all_queries_ref[3 * rows :, :], query_user_ref[3 * rows :, :],
+        jnp.concatenate([third, four_ref[...]], axis=0), 3 * rows,
+        keys_ref, values_ref, user_ref[...],
+    )
+    key_grad = near_key_ref[...] + far_key
+    value_grad = near_value_ref[...] + far_value
     value_part = (value_grad * value_key_slope_ref[:, :width]).astype(bf16)
     key_part = (key_grad * value_key_slope_ref[:, width:]).astype(bf16)
     value_key_ref[:, :width] = value_part
@@ -437,15 +457,22 @@
     return jnp.sum(blocks.astype(f32), axis=0)
 
 
-def sum_along_x(block):
+def sum_along_x(kept, sent):
     devices = lax.axis_size("dp")
     me = lax.axis_index("dp") % X_CHIPS
-    own = lax.dynamic_index_in_dim(block, me, 0, keepdims=False).astype(f32)
+    got = swapped(sent)
+
+    def piece(step):
+        at = (me + step) % X_CHIPS
+        return lax.dynamic_index_in_dim(kept, at, 0, keepdims=False).astype(
+            f32
+        ) + lax.dynamic_index_in_dim(got, at, 0, keepdims=False).astype(f32)
+
+    total = piece(0)
     for step in range(1, X_CHIPS):
         route = [(i, i - i % X_CHIPS + (i + step) % X_CHIPS) for i in range(devices)]
-        piece = lax.dynamic_index_in_dim(block, (me + step) % X_CHIPS, 0, keepdims=False)
-        own = own + lax.ppermute(piece, "dp", route).astype(f32)
-    return own.astype(bf16)
+        total = total + lax.ppermute(piece(step).astype(bf16), "dp", route).astype(f32)
+    return total.astype(bf16)
 
 
 def chips_along_z(owners):
@@ -532,10 +559,15 @@
         queries, all_keys, all_values, att_grad, gate_grad, packed, user, key_user, *later, w_in,
         core=core, flops=4_000_000_000, moved=8_000_000,
     )
-    gate_query, mixed, grad_four = lax.optimization_barrier((gate_query, mixed, grad_four))
-    later_grads = (
-        grad_four, mate_of_four(grad_four, -1), grad_two, grad_mate_two, own_grad,
-    )
+    near_key, near_value = call(
+        near_body, [(block, f32), (block, f32)],
+        all_queries, query_user, att_grad, grad_two, grad_mate_two, own_grad, keys, values, user,
+        core=core, flops=3_000_000_000, moved=3_000_000,
+    )
+    gate_query, near_key, mixed, grad_four = lax.optimization_barrier(
+        (gate_query, near_key, mixed, grad_four)
+    )
+    grad_mate_four = mate_of_four(grad_four, -1)
     half_width = model_width // 2
     early_block = (X_CHIPS, 3 * model_width // X_CHIPS, half_width)
     early_kept, early_sent = call(
@@ -550,7 +582,8 @@
     value_key, outgoing = call(
         key_body,
         [((rows_dev, 2 * model_width), bf16), ((slots, model_width), bf16)],
-        all_queries, query_user, att_grad, *later_grads, keys, values, value_key_slope, gate_query,
+        all_queries, query_user, grad_four, grad_mate_four, grad_mate_two, keys, values,
+        near_key, near_value, value_key_slope, gate_query,
         w_in, inputs, grad_rows, slot, user,
         core=core, flops=4_000_000_000, moved=8_000_000,
     )
@@ -566,7 +599,7 @@
         packed, value_key, early_kept, early_sent,
         core=core, flops=1_500_000_000, moved=3_000_000,
     )
-    along_x = sum_along_x(pair_sum(weight_kept, weight_sent)).reshape(z_chips, piece, half_width)
+    along_x = sum_along_x(weight_kept, weight_sent).reshape(z_chips, piece, half_width)
     arrived, along_x = lax.optimization_barrier((arrived, along_x))
     along_dp = total_of(spread(along_x, "dp", chips_along_z(owners))).astype(bf16)
     weight_terms = along_dp.T.reshape(chips, weight_rows, piece)

time: 201 us -> 201 us (level)
    ppermute x2 -> x1, starting transfers between devices: 5.12 us -> 2.59 us  [pair_sum(): got = lax.ppermute(sent, 'ctx', [(i, i ^ 1) for i in range(devices)])]
    ppermute x8 -> x9, starting transfers between devices: 20 us -> 22.4 us  [swapped(): lax.ppermute(block, 'ctx', [(i, i ^ 1) for i in devices if i % 2 in sende...]
    unnamed x19 -> x17, local copies, waits for them, and re-layouts: 6.65 us -> 5.57 us
    pallas_call x10 -> x11, Pallas kernels: 18.3 us -> 19.2 us  [call(): pl.pallas_call(body, out_shape=[jax.ShapeDtypeStruct(shape, kind) for sha...]
  transfers between devices with their start and end apart: 22 -> 22, of which waited for: 9 -> 9; matrix products, arithmetic and copies ran while one was open for 2% -> 2% of each run, Pallas kernels for 4% -> 5%
where the time goes in v9:
time: 201 us; the launch traced here: 199 us
  waiting for transfers between devices  64.1 us (32%)
  starting transfers between devices  60.8 us (30%)
  blocking collectives  43.2 us (21%)
  Pallas kernels  19.2 us (10%)
  local copies, waits for them, and re-layouts  7 us (3%)
  other arithmetic  3.82 us (2%)
    all_to_all x1, waiting for transfers between devices, local(): lax.all_to_all(found.reshape(owners, capacity, model_width), 'dp', split_...  25.2 us
    ppermute x3, waiting for transfers between devices, sum_along_x(): lax.ppermute(piece(step).astype(bf16), 'dp', route).astype(f32)  22.7 us
    ppermute x9, starting transfers between devices, swapped(): lax.ppermute(block, 'ctx', [(i, i ^ 1) for i in devices if i % 2 in sende...  22.4 us
    all_to_all x1, blocking collectives, local(): lax.all_to_all(requests, 'dp', split_axis=0, concat_axis=0, tiled=True)  22.1 us
    all_to_all x1, blocking collectives, spread(): lax.all_to_all(block, axis, split_axis=0, concat_axis=0, tiled=True, axis...  21.1 us
    pallas_call x11, Pallas kernels, call(): pl.pallas_call(body, out_shape=[jax.ShapeDtypeStruct(shape, kind) for sha...  19.2 us
    ppermute x6, starting transfers between devices, passed_along(): return lax.ppermute(block, axis, route)  12.4 us
    ppermute x3, starting transfers between devices, sum_along_x(): lax.ppermute(piece(step).astype(bf16), 'dp', route).astype(f32)  9.32 us
  transfers between devices with their start and end apart: 22, of which 9 were waited for; matrix products, arithmetic and copies ran while one was open for 2% of the time, Pallas kernels for 5%

profile of v9, /device:TPU:1, one launch (start us, length us, event | category | flops | bytes accessed | tf_op | source)
XLA Modules:
  0.0 199.3 jit_solution(15007307951701510776)
XLA Ops:
  1.9 22.1 %all_to_all.31 = s32[32,1,32]{2,1,0:T(1,128)S(1)} all-to-all(s32[32,1,32]{2,1,0:T(1,128)S(1)} %bitcast.34), channel_id=1, replica_groups=mesh['dp'=32,'ctx'=16] {'dp'}, dimensions={0} | all-to-all | bytes 8192 | tf_op jit(solution)/shard_map/all_to_all | solution.py:505
  25.1 1.9 shard_map.94
  27.0 4.1 %all-to-all-start.1 = ((bf16[32,32,512]{2,1,0:T(8,128)(2,1)}), bf16[32,32,512]{2,1,0:T(8,128)(2,1)S(1)}, u32[]{:S(2)}, u32[]{:S(2)}) async-start(bf16[32,32,512]{2,1,0:T(8,128)(2,1)} %bitcast.5), calls=%async_computation.1 | async-start | bytes 2097152 | tf_op jit(solution)/shard_map/all_to_all | solution.py:509
  31.1 25.2 %all-to-all-done.1 = bf16[32,32,512]{2,1,0:T(8,128)(2,1)S(1)} async-done(((bf16[32,32,512]{2,1,0:T(8,128)(2,1)}), bf16[32,32,512]{2,1,0:T(8,128)(2,1)S(1)}, u32[]{:S(2)}, u32[]{:S(2)}) %all-to-all-start.1) | async-done | bytes 1048608 | tf_op jit(solution)/shard_map/all_to_all | solution.py:509
  56.8 3.2 %collective-permute-start = (bf16[144,512]{1,0:T(8,128)(2,1)S(1)}, bf16[144,512]{1,0:T(8,128)(2,1)S(1)}, u32[]{:S(2)}, u32[]{:S(2)}) collective-permute-start(bf16[144,512]{1,0:T(8,128)(2,1)S(1)} %get-tuple-element.66.packed_ref.refs_1_), channel_id=1, source_target_pairs={{0,2},{1,3},{2,4},{3,5},{4,6},{5,7},{6,8},{7,9},{8,10},{9,11},{10,... | collective-permute-start | bytes 442376 | tf_op jit(solution)/shard_map/ppermute | solution.py:24
  62.3 6.3 %collective-permute-start.3 = (bf16[144,512]{1,0:T(8,128)(2,1)S(1)}, bf16[144,512]{1,0:T(8,128)(2,1)S(1)}, u32[]{:S(2)}, u32[]{:S(2)}) collective-permute-start(bf16[144,512]{1,0:T(8,128)(2,1)S(1)} %get-tuple-element.66.packed_ref.refs_1_), channel_id=1, source_target_pairs={{0,1},{1,0},{2,3},{3,2},{4,5},{5,4},{6,7},{7,6},{8,9},{9,8},{10,11... | collective-permute-start | bytes 442376 | tf_op jit(solution)/shard_map/ppermute | solution.py:29
  69.9 4.0 %collective-permute-start.1 = (bf16[144,512]{1,0:T(8,128)(2,1)S(1)}, bf16[144,512]{1,0:T(8,128)(2,1)S(1)}, u32[]{:S(2)}, u32[]{:S(2)}) collective-permute-start(bf16[144,512]{1,0:T(8,128)(2,1)S(1)} %collective-permute-done.two_ref), channel_id=1, source_target_pairs={{0,2},{1,3},{2,4},{3,5},{4,6},{5,7},{6,8},{7,9},{8,10},{9,11},{10,... | collective-permute-start | bytes 442376 | tf_op jit(solution)/shard_map/ppermute | solution.py:24
  73.9 2.5 %collective-permute-start.2 = (bf16[144,512]{1,0:T(8,128)(2,1)S(1)}, bf16[144,512]{1,0:T(8,128)(2,1)S(1)}, u32[]{:S(2)}, u32[]{:S(2)}) collective-permute-start(bf16[144,512]{1,0:T(8,128)(2,1)S(1)} %collective-permute-done.two_ref), channel_id=1, source_target_pairs={{0,1},{1,0},{2,3},{3,2},{4,5},{5,4},{6,7},{7,6},{8,9},{9,8},{10,11... | collective-permute-start | bytes 442376 | tf_op jit(solution)/shard_map/ppermute | solution.py:29
  76.4 2.2 %collective-permute-start.6 = (bf16[144,512]{1,0:T(8,128)(2,1)S(1)}, bf16[144,512]{1,0:T(8,128)(2,1)S(1)}, u32[]{:S(2)}, u32[]{:S(2)}) collective-permute-start(bf16[144,512]{1,0:T(8,128)(2,1)S(1)} %collective-permute-done.5.two_ref), channel_id=1, source_target_pairs={{0,1},{1,0},{2,3},{3,2},{4,5},{5,4},{6,7},{7,6},{8,9},{9,8},{10,11... | collective-permute-start | bytes 442376 | tf_op jit(solution)/shard_map/ppermute | solution.py:29
  78.7 2.1 %collective-permute-start.4 = (bf16[144,512]{1,0:T(8,128)(2,1)S(1)}, bf16[144,512]{1,0:T(8,128)(2,1)S(1)}, u32[]{:S(2)}, u32[]{:S(2)}) collective-permute-start(bf16[144,512]{1,0:T(8,128)(2,1)S(1)} %collective-permute-done.1.four_ref), channel_id=1, source_target_pairs={{1,0},{3,2},{5,4},{7,6},{9,8},{11,10},{13,12},{15,14},{17,16},{19,... | collective-permute-start | bytes 442376 | tf_op jit(solution)/shard_map/ppermute | solution.py:29
  82.1 1.6 copy-done.2
  83.7 3.1 %shard_map.97 = (bf16[128,512]{1,0:T(8,128)(2,1)}, bf16[128,512]{1,0:T(8,128)(2,1)S(1)}, f32[128,512]{1,0:T(8,128)S(1)}, bf16[128,512]{1,0:T(8,128)(2,1)S(1)}, b...) custom-call(s32[1]{0:T(128)} %bitcast.core_ref.refs_0_, ...), custom_call_target="tpu_custom_call" | custom-call | flops 4000000000 | bytes 8000000 | tf_op jit(solution)/shard_map/pallas_call | solution.py:120
  86.8 1.9 collective-permute-start.8
  91.3 4.3 %collective-permute-done.9.two_ref = bf16[128,512]{1,0:T(8,128)(2,1)S(1)} collective-permute-done((bf16[128,512]{1,0:T(8,128)(2,1)S(1)}, bf16[128,512]{1,0:T(8,128)(2,1)S(1)}, u32[]{:S(2)}, u32[]{:S(2)}) %collective-permute-start.9) | collective-permute-done | bytes 131104 | tf_op jit(solution)/shard_map/ppermute | solution.py:24
  95.7 2.2 %collective-permute-start.10 = (bf16[128,512]{1,0:T(8,128)(2,1)S(1)}, bf16[128,512]{1,0:T(8,128)(2,1)S(1)}, u32[]{:S(2)}, u32[]{:S(2)}) collective-permute-start(bf16[128,512]{1,0:T(8,128)(2,1)S(1)} %collective-permute-done.9.two_ref), channel_id=1, source_target_pairs={{0,1},{1,0},{2,3},{3,2},{4,5},{5,4},{6,7},{7,6},{8,9},{9,8},{10,11... | collective-permute-start | bytes 393224 | tf_op jit(solution)/shard_map/ppermute | solution.py:29
  99.2 2.8 %shard_map.98 = (bf16[128,1024]{1,0:T(8,128)(2,1)S(1)}, f32[128,1024]{1,0:T(8,128)S(1)}, bf16[640,512]{1,0:T(8,128)(2,1)S(1)}, f32[640,1]{1,0:T(8,128)S(1)}) custom-call(s32[1]{0:T(128)} %bitcast.core_ref.refs_0_, bf16[128,512]{1,0:T(8,128)(2,1)S(1)} %get-tuple-element.73.queries_ref, bf16[640,512]{1,0:T(8,128)(2,1)S(1)} %get-tuple-element.79.all_keys_ref, ...), custom_call_target="tpu_custom_call" | custom-call | flops 4000000000 | bytes 8000000 | tf_op jit(solution)/shard_map/pallas_call | solution.py:120
  102.1 2.0 shard_map.99
  108.6 3.8 %shard_map.101 = (bf16[128,1024]{1,0:T(8,128)(2,1)S(1)}, bf16[1024,512]{1,0:T(8,128)(2,1)}) custom-call(s32[1]{0:T(128)} %bitcast.core_ref.refs_0_, bf16[640,512]{1,0:T(8,128)(2,1)S(1)} %get-tuple-element.88.all_queries_ref, f32[640,1]{1,0:T(8,128)S(1)} %get-tuple-element.89.query_user_ref, bf16[128,512]{1,0:T(8,128)(2,1)S(1)} %collective-permute-done.12.four_ref, ...), custom_call_target="tpu_custom_call" | custom-call | flops 4000000000 | bytes 8000000 | tf_op jit(solution)/shard_map/pallas_call | solution.py:120
  112.4 1.8 shard_map.102
  114.3 2.4 %collective-permute-start.14 = (bf16[4,640,256]{2,1,0:T(8,128)(2,1)}, bf16[4,640,256]{2,1,0:T(8,128)(2,1)}, u32[]{:S(2)}, u32[]{:S(2)}) collective-permute-start(bf16[4,640,256]{2,1,0:T(8,128)(2,1)} %get-tuple-element.109), channel_id=1, source_target_pairs={{0,1},{1,0},{2,3},{3,2},{4,5},{5,4},{6,7},{7,6},{8,9},{9,8},{10,11... | collective-permute-start | bytes 3932168 | tf_op jit(solution)/shard_map/ppermute | solution.py:29
  116.7 5.0 %all-to-all-start.2 = ((bf16[32,32,512]{2,1,0:T(8,128)(2,1)}), bf16[32,32,512]{2,1,0:T(8,128)(2,1)S(1)}, u32[]{:S(2)}, u32[]{:S(2)}) async-start(bf16[32,32,512]{2,1,0:T(8,128)(2,1)} %bitcast.9), calls=%async_computation.2 | async-start | bytes 2097152 | tf_op jit(solution)/shard_map/all_to_all | solution.py:590
  123.1 4.4 %collective-permute-start.17 = (bf16[640,256]{1,0:T(8,128)(2,1)S(1)}, bf16[640,256]{1,0:T(8,128)(2,1)}, u32[]{:S(2)}, u32[]{:S(2)}) collective-permute-start(bf16[640,256]{1,0:T(8,128)(2,1)S(1)} %get-tuple-element.123), channel_id=1, source_target_pairs={{0,48},{16,0},{32,16},{48,32},{64,112},{80,64},{96,80},{112,96},{1... | collective-permute-start | bytes 983048 | tf_op jit(solution)/shard_map/ppermute | solution.py:474
  127.5 2.5 %collective-permute-start.16 = (bf16[640,256]{1,0:T(8,128)(2,1)S(1)}, bf16[640,256]{1,0:T(8,128)(2,1)}, u32[]{:S(2)}, u32[]{:S(2)}) collective-permute-start(bf16[640,256]{1,0:T(8,128)(2,1)S(1)} %get-tuple-element.124), channel_id=1, source_target_pairs={{0,32},{16,48},{32,0},{48,16},{64,96},{80,112},{96,64},{112,80},{1... | collective-permute-start | bytes 983048 | tf_op jit(solution)/shard_map/ppermute | solution.py:474
  130.0 2.5 %collective-permute-start.15 = (bf16[640,256]{1,0:T(8,128)(2,1)S(1)}, bf16[640,256]{1,0:T(8,128)(2,1)}, u32[]{:S(2)}, u32[]{:S(2)}) collective-permute-start(bf16[640,256]{1,0:T(8,128)(2,1)S(1)} %get-tuple-element.122), channel_id=1, source_target_pairs={{0,16},{16,32},{32,48},{48,0},{64,80},{80,96},{96,112},{112,64},{1... | collective-permute-start | bytes 983048 | tf_op jit(solution)/shard_map/ppermute | solution.py:474
  132.5 13.1 %collective-permute-done.17 = bf16[640,256]{1,0:T(8,128)(2,1)} collective-permute-done((bf16[640,256]{1,0:T(8,128)(2,1)S(1)}, bf16[640,256]{1,0:T(8,128)(2,1)}, u32[]{:S(2)}, u32[]{:S(2)}) %collective-permute-start.17) | collective-permute-done | bytes 327712 | tf_op jit(solution)/shard_map/ppermute | solution.py:474
  145.6 2.5 %collective-permute-done.16 = bf16[640,256]{1,0:T(8,128)(2,1)} collective-permute-done((bf16[640,256]{1,0:T(8,128)(2,1)S(1)}, bf16[640,256]{1,0:T(8,128)(2,1)}, u32[]{:S(2)}, u32[]{:S(2)}) %collective-permute-start.16) | collective-permute-done | bytes 327712 | tf_op jit(solution)/shard_map/ppermute | solution.py:474
  148.1 7.2 %collective-permute-done.15 = bf16[640,256]{1,0:T(8,128)(2,1)} collective-permute-done((bf16[640,256]{1,0:T(8,128)(2,1)S(1)}, bf16[640,256]{1,0:T(8,128)(2,1)}, u32[]{:S(2)}, u32[]{:S(2)}) %collective-permute-start.15) | collective-permute-done | bytes 327712 | tf_op jit(solution)/shard_map/ppermute | solution.py:474
  155.2 2.2 %fusion.2 = bf16[640,256]{1,0:T(8,128)(2,1)} fusion(bf16[640,256]{1,0:T(8,128)(2,1)} %collective-permute-done.17, bf16[640,256]{1,0:T(8,128)(2,1)} %collective-permute-done.16, bf16[640,256]{1,0:T(8,128)(2,1)} %collective-permute-done.15, bf16[4,640,256]{2,1,0:T(8,128)(2,1)} %collective-permute-done.14, s32[]{:T(128)S(6)} %select_n.47, ...), kind=kLoop, calls=%fused_computation.3 | loop fusion | flops 1638400 | bytes 1966084 | tf_op jit(solution)/shard_map/convert_element_type | solution.py:475
  157.4 5.1 %all-to-all-start.3 = ((bf16[8,80,256]{2,1,0:T(8,128)(2,1)}), bf16[8,80,256]{2,1,0:T(8,128)(2,1)S(1)}, u32[]{:S(2)}, u32[]{:S(2)}) async-start(bf16[8,80,256]{2,1,0:T(8,128)(2,1)} %bitcast.15), calls=%async_computation.3 | async-start | bytes 655360 | tf_op jit(solution)/shard_map/all_to_all | solution.py:451
  163.3 2.6 %collective-permute-start.18 = (bf16[8,32,512]{2,1,0:T(8,128)(2,1)S(1)}, bf16[8,32,512]{2,1,0:T(8,128)(2,1)S(1)}, u32[]{:S(2)}, u32[]{:S(2)}) collective-permute-start(bf16[8,32,512]{2,1,0:T(8,128)(2,1)S(1)} %get-tuple-element.112), channel_id=1, source_target_pairs={{0,1},{1,0},{2,3},{3,2},{4,5},{5,4},{6,7},{7,6},{8,9},{9,8},{10,11... | collective-permute-start | bytes 786440 | tf_op jit(solution)/shard_map/ppermute | solution.py:441
  167.1 8.8 %all-to-all-done.3 = bf16[8,80,256]{2,1,0:T(8,128)(2,1)S(1)} async-done(((bf16[8,80,256]{2,1,0:T(8,128)(2,1)}), bf16[8,80,256]{2,1,0:T(8,128)(2,1)S(1)}, u32[]{:S(2)}, u32[]{:S(2)}) %all-to-all-start.3) | async-done | bytes 327712 | tf_op jit(solution)/shard_map/all_to_all | solution.py:451
  176.1 21.1 %all_to_all.32 = bf16[8,32,592]{2,1,0:T(8,128)(2,1)S(1)} all-to-all(bf16[8,32,592]{2,1,0:T(8,128)(2,1)S(1)} %pad_maximum_fusion), channel_id=1, replica_groups={{0,2,4,6,8,10,12,14},{1,3,5,7,9,11,13,15},{16,18,20,22,24,26,28,30},{17..., dimensions={0} | all-to-all | bytes 606208 | tf_op jit(solution)/shard_map/all_to_all | solution.py:451
  (53 shorter events, 21.7 us)
Async XLA Ops:
  0.6 0.7 copy-start.6
  24.0 1.0 copy-start
  25.1 6.0 %copy-start.7 = (s32[1,128]{1,0:T(1,128)S(1)}, s32[1,128]{1,0:T(1,128)}, u32[]{:S(2)}) copy-start(s32[1,128]{1,0:T(1,128)} %param.7) | copy-start | bytes 1540
  27.0 33.1 %copy-start.4 = (bf16[512,512]{1,0:T(8,128)(2,1)S(1)}, bf16[512,512]{1,0:T(8,128)(2,1)}, u32[]{:S(2)}) copy-start(bf16[512,512]{1,0:T(8,128)(2,1)} %w_out_ref.3) | copy-start | bytes 1572868
  27.0 33.1 %copy-start.5 = (bf16[1,128,512]{2,1,0:T(8,128)(2,1)S(1)}, bf16[1,128,512]{2,1,0:T(8,128)(2,1)}, u32[]{:S(2)}) copy-start(bf16[1,128,512]{2,1,0:T(8,128)(2,1)} %param.11) | copy-start | bytes 393220
  27.0 29.3 %all-to-all-start.1 = ((bf16[32,32,512]{2,1,0:T(8,128)(2,1)}), bf16[32,32,512]{2,1,0:T(8,128)(2,1)S(1)}, u32[]{:S(2)}, u32[]{:S(2)}) async-start(bf16[32,32,512]{2,1,0:T(8,128)(2,1)} %bitcast.5), calls=%async_computation.1 | async-start | bytes 2097152 | tf_op jit(solution)/shard_map/all_to_all | solution.py:509
  56.8 13.1 %collective-permute-start = (bf16[144,512]{1,0:T(8,128)(2,1)S(1)}, bf16[144,512]{1,0:T(8,128)(2,1)S(1)}, u32[]{:S(2)}, u32[]{:S(2)}) collective-permute-start(bf16[144,512]{1,0:T(8,128)(2,1)S(1)} %get-tuple-element.66.packed_ref.refs_1_), channel_id=1, source_target_pairs={{0,2},{1,3},{2,4},{3,5},{4,6},{5,7},{6,8},{7,9},{8,10},{9,11},{10,... | collective-permute-start | bytes 442376 | tf_op jit(solution)/shard_map/ppermute | solution.py:24
  60.1 1.6 copy-start.1
  62.3 16.4 %collective-permute-start.3 = (bf16[144,512]{1,0:T(8,128)(2,1)S(1)}, bf16[144,512]{1,0:T(8,128)(2,1)S(1)}, u32[]{:S(2)}, u32[]{:S(2)}) collective-permute-start(bf16[144,512]{1,0:T(8,128)(2,1)S(1)} %get-tuple-element.66.packed_ref.refs_1_), channel_id=1, source_target_pairs={{0,1},{1,0},{2,3},{3,2},{4,5},{5,4},{6,7},{7,6},{8,9},{9,8},{10,11... | collective-permute-start | bytes 442376 | tf_op jit(solution)/shard_map/ppermute | solution.py:29
  68.6 7.8 %collective-permute-start.5 = (bf16[144,512]{1,0:T(8,128)(2,1)S(1)}, bf16[144,512]{1,0:T(8,128)(2,1)S(1)}, u32[]{:S(2)}, u32[]{:S(2)}) collective-permute-start(bf16[144,512]{1,0:T(8,128)(2,1)S(1)} %get-tuple-element.66.packed_ref.refs_1_), channel_id=1, source_target_pairs={{2,0},{3,1},{4,2},{5,3},{6,4},{7,5},{8,6},{9,7},{10,8},{11,9},{12,... | collective-permute-start | bytes 442376 | tf_op jit(solution)/shard_map/ppermute | solution.py:24
  69.9 8.8 %collective-permute-start.1 = (bf16[144,512]{1,0:T(8,128)(2,1)S(1)}, bf16[144,512]{1,0:T(8,128)(2,1)S(1)}, u32[]{:S(2)}, u32[]{:S(2)}) collective-permute-start(bf16[144,512]{1,0:T(8,128)(2,1)S(1)} %collective-permute-done.two_ref), channel_id=1, source_target_pairs={{0,2},{1,3},{2,4},{3,5},{4,6},{5,7},{6,8},{7,9},{8,10},{9,11},{10,... | collective-permute-start | bytes 442376 | tf_op jit(solution)/shard_map/ppermute | solution.py:24
  73.9 4.8 %collective-permute-start.2 = (bf16[144,512]{1,0:T(8,128)(2,1)S(1)}, bf16[144,512]{1,0:T(8,128)(2,1)S(1)}, u32[]{:S(2)}, u32[]{:S(2)}) collective-permute-start(bf16[144,512]{1,0:T(8,128)(2,1)S(1)} %collective-permute-done.two_ref), channel_id=1, source_target_pairs={{0,1},{1,0},{2,3},{3,2},{4,5},{5,4},{6,7},{7,6},{8,9},{9,8},{10,11... | collective-permute-start | bytes 442376 | tf_op jit(solution)/shard_map/ppermute | solution.py:29
  76.4 5.7 %collective-permute-start.6 = (bf16[144,512]{1,0:T(8,128)(2,1)S(1)}, bf16[144,512]{1,0:T(8,128)(2,1)S(1)}, u32[]{:S(2)}, u32[]{:S(2)}) collective-permute-start(bf16[144,512]{1,0:T(8,128)(2,1)S(1)} %collective-permute-done.5.two_ref), channel_id=1, source_target_pairs={{0,1},{1,0},{2,3},{3,2},{4,5},{5,4},{6,7},{7,6},{8,9},{9,8},{10,11... | collective-permute-start | bytes 442376 | tf_op jit(solution)/shard_map/ppermute | solution.py:29
  78.7 3.4 %collective-permute-start.4 = (bf16[144,512]{1,0:T(8,128)(2,1)S(1)}, bf16[144,512]{1,0:T(8,128)(2,1)S(1)}, u32[]{:S(2)}, u32[]{:S(2)}) collective-permute-start(bf16[144,512]{1,0:T(8,128)(2,1)S(1)} %collective-permute-done.1.four_ref), channel_id=1, source_target_pairs={{1,0},{3,2},{5,4},{7,6},{9,8},{11,10},{13,12},{15,14},{17,16},{19,... | collective-permute-start | bytes 442376 | tf_op jit(solution)/shard_map/ppermute | solution.py:29
  80.8 9.2 %collective-permute-start.7 = (bf16[144,512]{1,0:T(8,128)(2,1)S(1)}, bf16[144,512]{1,0:T(8,128)(2,1)S(1)}, u32[]{:S(2)}, u32[]{:S(2)}) collective-permute-start(bf16[144,512]{1,0:T(8,128)(2,1)S(1)} %collective-permute-done.5.two_ref), channel_id=1, source_target_pairs={{2,0},{3,1},{4,2},{5,3},{6,4},{7,5},{8,6},{9,7},{10,8},{11,9},{12,... | collective-permute-start | bytes 442376 | tf_op jit(solution)/shard_map/ppermute | solution.py:24
  82.1 1.6 copy-start.2
  83.7 15.5 %copy-start.3 = (bf16[512,2048]{1,0:T(8,128)(2,1)S(1)}, bf16[512,2048]{1,0:T(8,128)(2,1)}, u32[]{:S(2)}) copy-start(bf16[512,2048]{1,0:T(8,128)(2,1)} %w_in_ref.7) | copy-start | bytes 6291460
  86.8 3.2 %collective-permute-start.8 = (bf16[128,512]{1,0:T(8,128)(2,1)S(1)}, bf16[128,512]{1,0:T(8,128)(2,1)S(1)}, u32[]{:S(2)}, u32[]{:S(2)}) collective-permute-start(bf16[128,512]{1,0:T(8,128)(2,1)S(1)} %get-tuple-element.81.att_grad_ref), channel_id=1, source_target_pairs={{1,0},{3,2},{5,4},{7,6},{9,8},{11,10},{13,12},{15,14},{17,16},{19,... | collective-permute-start | bytes 393224 | tf_op jit(solution)/shard_map/ppermute | solution.py:29
  88.7 7.0 %collective-permute-start.9 = (bf16[128,512]{1,0:T(8,128)(2,1)S(1)}, bf16[128,512]{1,0:T(8,128)(2,1)S(1)}, u32[]{:S(2)}, u32[]{:S(2)}) collective-permute-start(bf16[128,512]{1,0:T(8,128)(2,1)S(1)} %get-tuple-element.81.att_grad_ref), channel_id=1, source_target_pairs={{2,0},{3,1},{4,2},{5,3},{6,4},{7,5},{8,6},{9,7},{10,8},{11,9},{12,... | collective-permute-start | bytes 393224 | tf_op jit(solution)/shard_map/ppermute | solution.py:24
  90.0 9.2 %collective-permute-start.11 = (bf16[144,512]{1,0:T(8,128)(2,1)S(1)}, bf16[144,512]{1,0:T(8,128)(2,1)S(1)}, u32[]{:S(2)}, u32[]{:S(2)}) collective-permute-start(bf16[144,512]{1,0:T(8,128)(2,1)S(1)} %collective-permute-done.7.four_ref), channel_id=1, source_target_pairs={{0,1},{2,3},{4,5},{6,7},{8,9},{10,11},{12,13},{14,15},{16,17},{18,... | collective-permute-start | bytes 442376 | tf_op jit(solution)/shard_map/ppermute | solution.py:29
  95.7 3.5 %collective-permute-start.10 = (bf16[128,512]{1,0:T(8,128)(2,1)S(1)}, bf16[128,512]{1,0:T(8,128)(2,1)S(1)}, u32[]{:S(2)}, u32[]{:S(2)}) collective-permute-start(bf16[128,512]{1,0:T(8,128)(2,1)S(1)} %collective-permute-done.9.two_ref), channel_id=1, source_target_pairs={{0,1},{1,0},{2,3},{3,2},{4,5},{5,4},{6,7},{7,6},{8,9},{9,8},{10,11... | collective-permute-start | bytes 393224 | tf_op jit(solution)/shard_map/ppermute | solution.py:29
  97.9 7.4 %collective-permute-start.12 = (bf16[128,512]{1,0:T(8,128)(2,1)S(1)}, bf16[128,512]{1,0:T(8,128)(2,1)S(1)}, u32[]{:S(2)}, u32[]{:S(2)}) collective-permute-start(bf16[128,512]{1,0:T(8,128)(2,1)S(1)} %collective-permute-done.9.two_ref), channel_id=1, source_target_pairs={{2,0},{3,1},{4,2},{5,3},{6,4},{7,5},{8,6},{9,7},{10,8},{11,9},{12,... | collective-permute-start | bytes 393224 | tf_op jit(solution)/shard_map/ppermute | solution.py:24
  105.4 3.2 %collective-permute-start.13 = (bf16[128,512]{1,0:T(8,128)(2,1)S(1)}, bf16[128,512]{1,0:T(8,128)(2,1)S(1)}, u32[]{:S(2)}, u32[]{:S(2)}) collective-permute-start(bf16[128,512]{1,0:T(8,128)(2,1)S(1)} %collective-permute-done.12.four_ref), channel_id=1, source_target_pairs={{0,1},{2,3},{4,5},{6,7},{8,9},{10,11},{12,13},{14,15},{16,17},{18,... | collective-permute-start | bytes 393224 | tf_op jit(solution)/shard_map/ppermute | solution.py:29
  114.3 7.5 %collective-permute-start.14 = (bf16[4,640,256]{2,1,0:T(8,128)(2,1)}, bf16[4,640,256]{2,1,0:T(8,128)(2,1)}, u32[]{:S(2)}, u32[]{:S(2)}) collective-permute-start(bf16[4,640,256]{2,1,0:T(8,128)(2,1)} %get-tuple-element.109), channel_id=1, source_target_pairs={{0,1},{1,0},{2,3},{3,2},{4,5},{5,4},{6,7},{7,6},{8,9},{9,8},{10,11... | collective-permute-start | bytes 3932168 | tf_op jit(solution)/shard_map/ppermute | solution.py:29
  116.7 40.8 %all-to-all-start.2 = ((bf16[32,32,512]{2,1,0:T(8,128)(2,1)}), bf16[32,32,512]{2,1,0:T(8,128)(2,1)S(1)}, u32[]{:S(2)}, u32[]{:S(2)}) async-start(bf16[32,32,512]{2,1,0:T(8,128)(2,1)} %bitcast.9), calls=%async_computation.2 | async-start | bytes 2097152 | tf_op jit(solution)/shard_map/all_to_all | solution.py:590
  123.1 22.4 %collective-permute-start.17 = (bf16[640,256]{1,0:T(8,128)(2,1)S(1)}, bf16[640,256]{1,0:T(8,128)(2,1)}, u32[]{:S(2)}, u32[]{:S(2)}) collective-permute-start(bf16[640,256]{1,0:T(8,128)(2,1)S(1)} %get-tuple-element.123), channel_id=1, source_target_pairs={{0,48},{16,0},{32,16},{48,32},{64,112},{80,64},{96,80},{112,96},{1... | collective-permute-start | bytes 983048 | tf_op jit(solution)/shard_map/ppermute | solution.py:474
  127.5 20.6 %collective-permute-start.16 = (bf16[640,256]{1,0:T(8,128)(2,1)S(1)}, bf16[640,256]{1,0:T(8,128)(2,1)}, u32[]{:S(2)}, u32[]{:S(2)}) collective-permute-start(bf16[640,256]{1,0:T(8,128)(2,1)S(1)} %get-tuple-element.124), channel_id=1, source_target_pairs={{0,32},{16,48},{32,0},{48,16},{64,96},{80,112},{96,64},{112,80},{1... | collective-permute-start | bytes 983048 | tf_op jit(solution)/shard_map/ppermute | solution.py:474
  130.0 25.2 %collective-permute-start.15 = (bf16[640,256]{1,0:T(8,128)(2,1)S(1)}, bf16[640,256]{1,0:T(8,128)(2,1)}, u32[]{:S(2)}, u32[]{:S(2)}) collective-permute-start(bf16[640,256]{1,0:T(8,128)(2,1)S(1)} %get-tuple-element.122), channel_id=1, source_target_pairs={{0,16},{16,32},{32,48},{48,0},{64,80},{80,96},{96,112},{112,64},{1... | collective-permute-start | bytes 983048 | tf_op jit(solution)/shard_map/ppermute | solution.py:474
  157.4 18.5 %all-to-all-start.3 = ((bf16[8,80,256]{2,1,0:T(8,128)(2,1)}), bf16[8,80,256]{2,1,0:T(8,128)(2,1)S(1)}, u32[]{:S(2)}, u32[]{:S(2)}) async-start(bf16[8,80,256]{2,1,0:T(8,128)(2,1)} %bitcast.15), calls=%async_computation.3 | async-start | bytes 655360 | tf_op jit(solution)/shard_map/all_to_all | solution.py:451
  163.3 3.7 %collective-permute-start.18 = (bf16[8,32,512]{2,1,0:T(8,128)(2,1)S(1)}, bf16[8,32,512]{2,1,0:T(8,128)(2,1)S(1)}, u32[]{:S(2)}, u32[]{:S(2)}) collective-permute-start(bf16[8,32,512]{2,1,0:T(8,128)(2,1)S(1)} %get-tuple-element.112), channel_id=1, source_target_pairs={{0,1},{1,0},{2,3},{3,2},{4,5},{5,4},{6,7},{7,6},{8,9},{9,8},{10,11... | collective-permute-start | bytes 786440 | tf_op jit(solution)/shard_map/ppermute | solution.py:441

commit v10 on v9

--- a/solution.py
+++ b/solution.py
@@ -529,10 +529,7 @@
     earlier_four, mate_two, mate_own = lax.optimization_barrier(
         (earlier_four, swapped(earlier_two), mate_own)
     )
-    mate_four, later_mate_two = lax.optimization_barrier(
-        (mate_of_four(earlier_four, 1), swapped(later_two))
-    )
-    earlier = (earlier_four, mate_four, earlier_two, mate_two, mate_own)
+    earlier = (earlier_four, mate_of_four(earlier_four, 1), earlier_two, mate_two, mate_own)
     later_four = passed_along(later_two, "ctx", -2)
     layer_out, mixed, gate_grad, att_grad, all_keys, all_values, key_user = call(
         forward_body,
@@ -546,8 +543,8 @@
     own_grad = swapped(att_grad, (1,))
     grad_two = passed_along(att_grad, "ctx", -2)
     grad_four = passed_along(grad_two, "ctx", -2)
-    later_four, own_grad = lax.optimization_barrier((later_four, own_grad))
-    later = (later_four, mate_of_four(later_four, -1), later_two, later_mate_two, mate_own)
+    later_four, later_two, own_grad = lax.optimization_barrier((later_four, later_two, own_grad))
+    later = (later_four, mate_of_four(later_four, -1), later_two, swapped(later_two), mate_own)
     grad_mate_two = swapped(grad_two)
     gate_grad, own_grad, grad_mate_two = lax.optimization_barrier((gate_grad, own_grad, grad_mate_two))
     gate_query, value_key_slope, all_queries, query_user = call(

time: 201 us -> 203 us (level)
  transfers between devices with their start and end apart: 22 -> 22, of which waited for: 9 -> 10; matrix products, arithmetic and copies ran while one was open for 2% -> 2% of each run, Pallas kernels for 5% -> 5%
where the time goes in v10:
time: 203 us; the launch traced here: 202 us
  waiting for transfers between devices  65.8 us (32%)
  starting transfers between devices  61.9 us (30%)
  blocking collectives  43.1 us (21%)
  Pallas kernels  19.2 us (9%)
  local copies, waits for them, and re-layouts  7 us (3%)
  other arithmetic  3.82 us (2%)
    all_to_all x1, waiting for transfers between devices, local(): lax.all_to_all(found.reshape(owners, capacity, model_width), 'dp', split_...  25.2 us
    ppermute x9, starting transfers between devices, swapped(): lax.ppermute(block, 'ctx', [(i, i ^ 1) for i in devices if i % 2 in sende...  24.2 us
    ppermute x3, waiting for transfers between devices, sum_along_x(): lax.ppermute(piece(step).astype(bf16), 'dp', route).astype(f32)  22.7 us
    all_to_all x1, blocking collectives, local(): lax.all_to_all(requests, 'dp', split_axis=0, concat_axis=0, tiled=True)  22.1 us
    all_to_all x1, blocking collectives, spread(): lax.all_to_all(block, axis, split_axis=0, concat_axis=0, tiled=True, axis...  21 us
    pallas_call x11, Pallas kernels, call(): pl.pallas_call(body, out_shape=[jax.ShapeDtypeStruct(shape, kind) for sha...  19.2 us
    ppermute x6, starting transfers between devices, passed_along(): return lax.ppermute(block, axis, route)  11.6 us
    ppermute x3, starting transfers between devices, sum_along_x(): lax.ppermute(piece(step).astype(bf16), 'dp', route).astype(f32)  9.32 us
  transfers between devices with their start and end apart: 22, of which 10 were waited for; matrix products, arithmetic and copies ran while one was open for 2% of the time, Pallas kernels for 5%

profile of v10, /device:TPU:1, one launch (start us, length us, event | category | flops | bytes accessed | tf_op | source)
XLA Modules:
  0.0 201.8 jit_solution(8684359154327488220)
XLA Ops:
  1.9 22.1 %all_to_all.31 = s32[32,1,32]{2,1,0:T(1,128)S(1)} all-to-all(s32[32,1,32]{2,1,0:T(1,128)S(1)} %bitcast.34), channel_id=1, replica_groups=mesh['dp'=32,'ctx'=16] {'dp'}, dimensions={0} | all-to-all | bytes 8192 | tf_op jit(solution)/shard_map/all_to_all | solution.py:505
  25.1 1.9 shard_map.94
  27.0 4.1 %all-to-all-start.1 = ((bf16[32,32,512]{2,1,0:T(8,128)(2,1)}), bf16[32,32,512]{2,1,0:T(8,128)(2,1)S(1)}, u32[]{:S(2)}, u32[]{:S(2)}) async-start(bf16[32,32,512]{2,1,0:T(8,128)(2,1)} %bitcast.5), calls=%async_computation.1 | async-start | bytes 2097152 | tf_op jit(solution)/shard_map/all_to_all | solution.py:509
  31.1 25.2 %all-to-all-done.1 = bf16[32,32,512]{2,1,0:T(8,128)(2,1)S(1)} async-done(((bf16[32,32,512]{2,1,0:T(8,128)(2,1)}), bf16[32,32,512]{2,1,0:T(8,128)(2,1)S(1)}, u32[]{:S(2)}, u32[]{:S(2)}) %all-to-all-start.1) | async-done | bytes 1048608 | tf_op jit(solution)/shard_map/all_to_all | solution.py:509
  56.8 3.2 %collective-permute-start = (bf16[144,512]{1,0:T(8,128)(2,1)S(1)}, bf16[144,512]{1,0:T(8,128)(2,1)S(1)}, u32[]{:S(2)}, u32[]{:S(2)}) collective-permute-start(bf16[144,512]{1,0:T(8,128)(2,1)S(1)} %get-tuple-element.65.packed_ref.refs_1_), channel_id=1, source_target_pairs={{0,2},{1,3},{2,4},{3,5},{4,6},{5,7},{6,8},{7,9},{8,10},{9,11},{10,... | collective-permute-start | bytes 442376 | tf_op jit(solution)/shard_map/ppermute | solution.py:24
  62.3 6.3 %collective-permute-start.3 = (bf16[144,512]{1,0:T(8,128)(2,1)S(1)}, bf16[144,512]{1,0:T(8,128)(2,1)S(1)}, u32[]{:S(2)}, u32[]{:S(2)}) collective-permute-start(bf16[144,512]{1,0:T(8,128)(2,1)S(1)} %get-tuple-element.65.packed_ref.refs_1_), channel_id=1, source_target_pairs={{0,1},{1,0},{2,3},{3,2},{4,5},{5,4},{6,7},{7,6},{8,9},{9,8},{10,11... | collective-permute-start | bytes 442376 | tf_op jit(solution)/shard_map/ppermute | solution.py:29
  68.6 3.2 %collective-permute-start.1 = (bf16[144,512]{1,0:T(8,128)(2,1)S(1)}, bf16[144,512]{1,0:T(8,128)(2,1)S(1)}, u32[]{:S(2)}, u32[]{:S(2)}) collective-permute-start(bf16[144,512]{1,0:T(8,128)(2,1)S(1)} %collective-permute-done.two_ref), channel_id=1, source_target_pairs={{0,2},{1,3},{2,4},{3,5},{4,6},{5,7},{6,8},{7,9},{8,10},{9,11},{10,... | collective-permute-start | bytes 442376 | tf_op jit(solution)/shard_map/ppermute | solution.py:24
  71.9 2.2 %collective-permute-start.2 = (bf16[144,512]{1,0:T(8,128)(2,1)S(1)}, bf16[144,512]{1,0:T(8,128)(2,1)S(1)}, u32[]{:S(2)}, u32[]{:S(2)}) collective-permute-start(bf16[144,512]{1,0:T(8,128)(2,1)S(1)} %collective-permute-done.two_ref), channel_id=1, source_target_pairs={{0,1},{1,0},{2,3},{3,2},{4,5},{5,4},{6,7},{7,6},{8,9},{9,8},{10,11... | collective-permute-start | bytes 442376 | tf_op jit(solution)/shard_map/ppermute | solution.py:29
  75.4 2.4 %collective-permute-start.4 = (bf16[144,512]{1,0:T(8,128)(2,1)S(1)}, bf16[144,512]{1,0:T(8,128)(2,1)S(1)}, u32[]{:S(2)}, u32[]{:S(2)}) collective-permute-start(bf16[144,512]{1,0:T(8,128)(2,1)S(1)} %collective-permute-done.1.four_ref), channel_id=1, source_target_pairs={{1,0},{3,2},{5,4},{7,6},{9,8},{11,10},{13,12},{15,14},{17,16},{19,... | collective-permute-start | bytes 442376 | tf_op jit(solution)/shard_map/ppermute | solution.py:29
  77.8 3.4 %collective-permute-done.5.two_ref = bf16[144,512]{1,0:T(8,128)(2,1)S(1)} collective-permute-done((bf16[144,512]{1,0:T(8,128)(2,1)S(1)}, bf16[144,512]{1,0:T(8,128)(2,1)S(1)}, u32[]{:S(2)}, u32[]{:S(2)}) %collective-permute-start.5) | collective-permute-done | bytes 147488 | tf_op jit(solution)/shard_map/ppermute | solution.py:24
  84.1 3.1 %shard_map.97 = (bf16[128,512]{1,0:T(8,128)(2,1)}, bf16[128,512]{1,0:T(8,128)(2,1)S(1)}, f32[128,512]{1,0:T(8,128)S(1)}, bf16[128,512]{1,0:T(8,128)(2,1)S(1)}, b...) custom-call(s32[1]{0:T(128)} %bitcast.core_ref.refs_0_, ...), custom_call_target="tpu_custom_call" | custom-call | flops 4000000000 | bytes 8000000 | tf_op jit(solution)/shard_map/pallas_call | solution.py:120
  87.2 2.9 %collective-permute-start.7 = (bf16[128,512]{1,0:T(8,128)(2,1)S(1)}, bf16[128,512]{1,0:T(8,128)(2,1)S(1)}, u32[]{:S(2)}, u32[]{:S(2)}) collective-permute-start(bf16[128,512]{1,0:T(8,128)(2,1)S(1)} %get-tuple-element.79.att_grad_ref), channel_id=1, source_target_pairs={{1,0},{3,2},{5,4},{7,6},{9,8},{11,10},{13,12},{15,14},{17,16},{19,... | collective-permute-start | bytes 393224 | tf_op jit(solution)/shard_map/ppermute | solution.py:29
  92.7 3.0 %collective-permute-start.11 = (bf16[144,512]{1,0:T(8,128)(2,1)S(1)}, bf16[144,512]{1,0:T(8,128)(2,1)S(1)}, u32[]{:S(2)}, u32[]{:S(2)}) collective-permute-start(bf16[144,512]{1,0:T(8,128)(2,1)S(1)} %collective-permute-done.5.two_ref), channel_id=1, source_target_pairs={{0,1},{1,0},{2,3},{3,2},{4,5},{5,4},{6,7},{7,6},{8,9},{9,8},{10,11... | collective-permute-start | bytes 442376 | tf_op jit(solution)/shard_map/ppermute | solution.py:29
  95.8 2.5 %collective-permute-done.8.two_ref = bf16[128,512]{1,0:T(8,128)(2,1)S(1)} collective-permute-done((bf16[128,512]{1,0:T(8,128)(2,1)S(1)}, bf16[128,512]{1,0:T(8,128)(2,1)S(1)}, u32[]{:S(2)}, u32[]{:S(2)}) %collective-permute-start.8) | collective-permute-done | bytes 131104 | tf_op jit(solution)/shard_map/ppermute | solution.py:24
  98.3 2.2 %collective-permute-start.9 = (bf16[128,512]{1,0:T(8,128)(2,1)S(1)}, bf16[128,512]{1,0:T(8,128)(2,1)S(1)}, u32[]{:S(2)}, u32[]{:S(2)}) collective-permute-start(bf16[128,512]{1,0:T(8,128)(2,1)S(1)} %collective-permute-done.8.two_ref), channel_id=1, source_target_pairs={{0,1},{1,0},{2,3},{3,2},{4,5},{5,4},{6,7},{7,6},{8,9},{9,8},{10,11... | collective-permute-start | bytes 393224 | tf_op jit(solution)/shard_map/ppermute | solution.py:29
  101.9 2.8 %shard_map.98 = (bf16[128,1024]{1,0:T(8,128)(2,1)S(1)}, f32[128,1024]{1,0:T(8,128)S(1)}, bf16[640,512]{1,0:T(8,128)(2,1)S(1)}, f32[640,1]{1,0:T(8,128)S(1)}) custom-call(s32[1]{0:T(128)} %bitcast.core_ref.refs_0_, bf16[128,512]{1,0:T(8,128)(2,1)S(1)} %get-tuple-element.71.queries_ref, bf16[640,512]{1,0:T(8,128)(2,1)S(1)} %get-tuple-element.77.all_keys_ref, ...), custom_call_target="tpu_custom_call" | custom-call | flops 4000000000 | bytes 8000000 | tf_op jit(solution)/shard_map/pallas_call | solution.py:120
  104.7 2.0 shard_map.99
  111.3 3.8 %shard_map.101 = (bf16[128,1024]{1,0:T(8,128)(2,1)S(1)}, bf16[1024,512]{1,0:T(8,128)(2,1)}) custom-call(s32[1]{0:T(128)} %bitcast.core_ref.refs_0_, bf16[640,512]{1,0:T(8,128)(2,1)S(1)} %get-tuple-element.86.all_queries_ref, f32[640,1]{1,0:T(8,128)S(1)} %get-tuple-element.87.query_user_ref, bf16[128,512]{1,0:T(8,128)(2,1)S(1)} %collective-permute-done.12.four_ref, ...), custom_call_target="tpu_custom_call" | custom-call | flops 4000000000 | bytes 8000000 | tf_op jit(solution)/shard_map/pallas_call | solution.py:120
  115.1 1.8 shard_map.102
  116.9 2.4 %collective-permute-start.14 = (bf16[4,640,256]{2,1,0:T(8,128)(2,1)}, bf16[4,640,256]{2,1,0:T(8,128)(2,1)}, u32[]{:S(2)}, u32[]{:S(2)}) collective-permute-start(bf16[4,640,256]{2,1,0:T(8,128)(2,1)} %get-tuple-element.107), channel_id=1, source_target_pairs={{0,1},{1,0},{2,3},{3,2},{4,5},{5,4},{6,7},{7,6},{8,9},{9,8},{10,11... | collective-permute-start | bytes 3932168 | tf_op jit(solution)/shard_map/ppermute | solution.py:29
  119.4 5.0 %all-to-all-start.2 = ((bf16[32,32,512]{2,1,0:T(8,128)(2,1)}), bf16[32,32,512]{2,1,0:T(8,128)(2,1)S(1)}, u32[]{:S(2)}, u32[]{:S(2)}) async-start(bf16[32,32,512]{2,1,0:T(8,128)(2,1)} %bitcast.9), calls=%async_computation.2 | async-start | bytes 2097152 | tf_op jit(solution)/shard_map/all_to_all | solution.py:587
  125.8 4.4 %collective-permute-start.17 = (bf16[640,256]{1,0:T(8,128)(2,1)S(1)}, bf16[640,256]{1,0:T(8,128)(2,1)}, u32[]{:S(2)}, u32[]{:S(2)}) collective-permute-start(bf16[640,256]{1,0:T(8,128)(2,1)S(1)} %get-tuple-element.121), channel_id=1, source_target_pairs={{0,48},{16,0},{32,16},{48,32},{64,112},{80,64},{96,80},{112,96},{1... | collective-permute-start | bytes 983048 | tf_op jit(solution)/shard_map/ppermute | solution.py:474
  130.2 2.5 %collective-permute-start.16 = (bf16[640,256]{1,0:T(8,128)(2,1)S(1)}, bf16[640,256]{1,0:T(8,128)(2,1)}, u32[]{:S(2)}, u32[]{:S(2)}) collective-permute-start(bf16[640,256]{1,0:T(8,128)(2,1)S(1)} %get-tuple-element.122), channel_id=1, source_target_pairs={{0,32},{16,48},{32,0},{48,16},{64,96},{80,112},{96,64},{112,80},{1... | collective-permute-start | bytes 983048 | tf_op jit(solution)/shard_map/ppermute | solution.py:474
  132.7 2.5 %collective-permute-start.15 = (bf16[640,256]{1,0:T(8,128)(2,1)S(1)}, bf16[640,256]{1,0:T(8,128)(2,1)}, u32[]{:S(2)}, u32[]{:S(2)}) collective-permute-start(bf16[640,256]{1,0:T(8,128)(2,1)S(1)} %get-tuple-element.120), channel_id=1, source_target_pairs={{0,16},{16,32},{32,48},{48,0},{64,80},{80,96},{96,112},{112,64},{1... | collective-permute-start | bytes 983048 | tf_op jit(solution)/shard_map/ppermute | solution.py:474
  135.2 13.1 %collective-permute-done.17 = bf16[640,256]{1,0:T(8,128)(2,1)} collective-permute-done((bf16[640,256]{1,0:T(8,128)(2,1)S(1)}, bf16[640,256]{1,0:T(8,128)(2,1)}, u32[]{:S(2)}, u32[]{:S(2)}) %collective-permute-start.17) | collective-permute-done | bytes 327712 | tf_op jit(solution)/shard_map/ppermute | solution.py:474
  148.3 2.5 %collective-permute-done.16 = bf16[640,256]{1,0:T(8,128)(2,1)} collective-permute-done((bf16[640,256]{1,0:T(8,128)(2,1)S(1)}, bf16[640,256]{1,0:T(8,128)(2,1)}, u32[]{:S(2)}, u32[]{:S(2)}) %collective-permute-start.16) | collective-permute-done | bytes 327712 | tf_op jit(solution)/shard_map/ppermute | solution.py:474
  150.7 7.2 %collective-permute-done.15 = bf16[640,256]{1,0:T(8,128)(2,1)} collective-permute-done((bf16[640,256]{1,0:T(8,128)(2,1)S(1)}, bf16[640,256]{1,0:T(8,128)(2,1)}, u32[]{:S(2)}, u32[]{:S(2)}) %collective-permute-start.15) | collective-permute-done | bytes 327712 | tf_op jit(solution)/shard_map/ppermute | solution.py:474
  157.9 2.2 %fusion.2 = bf16[640,256]{1,0:T(8,128)(2,1)} fusion(bf16[640,256]{1,0:T(8,128)(2,1)} %collective-permute-done.17, bf16[640,256]{1,0:T(8,128)(2,1)} %collective-permute-done.16, bf16[640,256]{1,0:T(8,128)(2,1)} %collective-permute-done.15, bf16[4,640,256]{2,1,0:T(8,128)(2,1)} %collective-permute-done.14, s32[]{:T(128)S(6)} %select_n.47, ...), kind=kLoop, calls=%fused_computation.3 | loop fusion | flops 1638400 | bytes 1966084 | tf_op jit(solution)/shard_map/convert_element_type | solution.py:475
  160.1 5.1 %all-to-all-start.3 = ((bf16[8,80,256]{2,1,0:T(8,128)(2,1)}), bf16[8,80,256]{2,1,0:T(8,128)(2,1)S(1)}, u32[]{:S(2)}, u32[]{:S(2)}) async-start(bf16[8,80,256]{2,1,0:T(8,128)(2,1)} %bitcast.15), calls=%async_computation.3 | async-start | bytes 655360 | tf_op jit(solution)/shard_map/all_to_all | solution.py:451
  166.0 2.6 %collective-permute-start.18 = (bf16[8,32,512]{2,1,0:T(8,128)(2,1)S(1)}, bf16[8,32,512]{2,1,0:T(8,128)(2,1)S(1)}, u32[]{:S(2)}, u32[]{:S(2)}) collective-permute-start(bf16[8,32,512]{2,1,0:T(8,128)(2,1)S(1)} %get-tuple-element.110), channel_id=1, source_target_pairs={{0,1},{1,0},{2,3},{3,2},{4,5},{5,4},{6,7},{7,6},{8,9},{9,8},{10,11... | collective-permute-start | bytes 786440 | tf_op jit(solution)/shard_map/ppermute | solution.py:441
  169.8 8.8 %all-to-all-done.3 = bf16[8,80,256]{2,1,0:T(8,128)(2,1)S(1)} async-done(((bf16[8,80,256]{2,1,0:T(8,128)(2,1)}), bf16[8,80,256]{2,1,0:T(8,128)(2,1)S(1)}, u32[]{:S(2)}, u32[]{:S(2)}) %all-to-all-start.3) | async-done | bytes 327712 | tf_op jit(solution)/shard_map/all_to_all | solution.py:451
  178.8 21.0 %all_to_all.32 = bf16[8,32,592]{2,1,0:T(8,128)(2,1)S(1)} all-to-all(bf16[8,32,592]{2,1,0:T(8,128)(2,1)S(1)} %pad_maximum_fusion), channel_id=1, replica_groups={{0,2,4,6,8,10,12,14},{1,3,5,7,9,11,13,15},{16,18,20,22,24,26,28,30},{17..., dimensions={0} | all-to-all | bytes 606208 | tf_op jit(solution)/shard_map/all_to_all | solution.py:451
  (53 shorter events, 23.4 us)
Async XLA Ops:
  0.6 0.7 copy-start.6
  24.0 1.0 copy-start
  25.1 6.0 %copy-start.7 = (s32[1,128]{1,0:T(1,128)S(1)}, s32[1,128]{1,0:T(1,128)}, u32[]{:S(2)}) copy-start(s32[1,128]{1,0:T(1,128)} %param.7) | copy-start | bytes 1540
  27.0 33.1 %copy-start.4 = (bf16[512,512]{1,0:T(8,128)(2,1)S(1)}, bf16[512,512]{1,0:T(8,128)(2,1)}, u32[]{:S(2)}) copy-start(bf16[512,512]{1,0:T(8,128)(2,1)} %w_out_ref.3) | copy-start | bytes 1572868
  27.0 33.1 %copy-start.5 = (bf16[1,128,512]{2,1,0:T(8,128)(2,1)S(1)}, bf16[1,128,512]{2,1,0:T(8,128)(2,1)}, u32[]{:S(2)}) copy-start(bf16[1,128,512]{2,1,0:T(8,128)(2,1)} %param.11) | copy-start | bytes 393220
  27.0 29.3 %all-to-all-start.1 = ((bf16[32,32,512]{2,1,0:T(8,128)(2,1)}), bf16[32,32,512]{2,1,0:T(8,128)(2,1)S(1)}, u32[]{:S(2)}, u32[]{:S(2)}) async-start(bf16[32,32,512]{2,1,0:T(8,128)(2,1)} %bitcast.5), calls=%async_computation.1 | async-start | bytes 2097152 | tf_op jit(solution)/shard_map/all_to_all | solution.py:509
  56.8 11.8 %collective-permute-start = (bf16[144,512]{1,0:T(8,128)(2,1)S(1)}, bf16[144,512]{1,0:T(8,128)(2,1)S(1)}, u32[]{:S(2)}, u32[]{:S(2)}) collective-permute-start(bf16[144,512]{1,0:T(8,128)(2,1)S(1)} %get-tuple-element.65.packed_ref.refs_1_), channel_id=1, source_target_pairs={{0,2},{1,3},{2,4},{3,5},{4,6},{5,7},{6,8},{7,9},{8,10},{9,11},{10,... | collective-permute-start | bytes 442376 | tf_op jit(solution)/shard_map/ppermute | solution.py:24
  60.1 1.6 copy-start.1
  62.3 13.0 %collective-permute-start.3 = (bf16[144,512]{1,0:T(8,128)(2,1)S(1)}, bf16[144,512]{1,0:T(8,128)(2,1)S(1)}, u32[]{:S(2)}, u32[]{:S(2)}) collective-permute-start(bf16[144,512]{1,0:T(8,128)(2,1)S(1)} %get-tuple-element.65.packed_ref.refs_1_), channel_id=1, source_target_pairs={{0,1},{1,0},{2,3},{3,2},{4,5},{5,4},{6,7},{7,6},{8,9},{9,8},{10,11... | collective-permute-start | bytes 442376 | tf_op jit(solution)/shard_map/ppermute | solution.py:29
  68.6 6.8 %collective-permute-start.1 = (bf16[144,512]{1,0:T(8,128)(2,1)S(1)}, bf16[144,512]{1,0:T(8,128)(2,1)S(1)}, u32[]{:S(2)}, u32[]{:S(2)}) collective-permute-start(bf16[144,512]{1,0:T(8,128)(2,1)S(1)} %collective-permute-done.two_ref), channel_id=1, source_target_pairs={{0,2},{1,3},{2,4},{3,5},{4,6},{5,7},{6,8},{7,9},{8,10},{9,11},{10,... | collective-permute-start | bytes 442376 | tf_op jit(solution)/shard_map/ppermute | solution.py:24
  71.9 3.5 %collective-permute-start.2 = (bf16[144,512]{1,0:T(8,128)(2,1)S(1)}, bf16[144,512]{1,0:T(8,128)(2,1)S(1)}, u32[]{:S(2)}, u32[]{:S(2)}) collective-permute-start(bf16[144,512]{1,0:T(8,128)(2,1)S(1)} %collective-permute-done.two_ref), channel_id=1, source_target_pairs={{0,1},{1,0},{2,3},{3,2},{4,5},{5,4},{6,7},{7,6},{8,9},{9,8},{10,11... | collective-permute-start | bytes 442376 | tf_op jit(solution)/shard_map/ppermute | solution.py:29
  74.1 7.1 %collective-permute-start.5 = (bf16[144,512]{1,0:T(8,128)(2,1)S(1)}, bf16[144,512]{1,0:T(8,128)(2,1)S(1)}, u32[]{:S(2)}, u32[]{:S(2)}) collective-permute-start(bf16[144,512]{1,0:T(8,128)(2,1)S(1)} %get-tuple-element.65.packed_ref.refs_1_), channel_id=1, source_target_pairs={{2,0},{3,1},{4,2},{5,3},{6,4},{7,5},{8,6},{9,7},{10,8},{11,9},{12,... | collective-permute-start | bytes 442376 | tf_op jit(solution)/shard_map/ppermute | solution.py:24
  75.4 7.1 %collective-permute-start.4 = (bf16[144,512]{1,0:T(8,128)(2,1)S(1)}, bf16[144,512]{1,0:T(8,128)(2,1)S(1)}, u32[]{:S(2)}, u32[]{:S(2)}) collective-permute-start(bf16[144,512]{1,0:T(8,128)(2,1)S(1)} %collective-permute-done.1.four_ref), channel_id=1, source_target_pairs={{1,0},{3,2},{5,4},{7,6},{9,8},{11,10},{13,12},{15,14},{17,16},{19,... | collective-permute-start | bytes 442376 | tf_op jit(solution)/shard_map/ppermute | solution.py:29
  81.2 10.2 %collective-permute-start.6 = (bf16[144,512]{1,0:T(8,128)(2,1)S(1)}, bf16[144,512]{1,0:T(8,128)(2,1)S(1)}, u32[]{:S(2)}, u32[]{:S(2)}) collective-permute-start(bf16[144,512]{1,0:T(8,128)(2,1)S(1)} %collective-permute-done.5.two_ref), channel_id=1, source_target_pairs={{2,0},{3,1},{4,2},{5,3},{6,4},{7,5},{8,6},{9,7},{10,8},{11,9},{12,... | collective-permute-start | bytes 442376 | tf_op jit(solution)/shard_map/ppermute | solution.py:24
  82.5 1.6 copy-start.2
  84.1 17.8 %copy-start.3 = (bf16[512,2048]{1,0:T(8,128)(2,1)S(1)}, bf16[512,2048]{1,0:T(8,128)(2,1)}, u32[]{:S(2)}) copy-start(bf16[512,2048]{1,0:T(8,128)(2,1)} %w_in_ref.7) | copy-start | bytes 6291460
  87.2 4.2 %collective-permute-start.7 = (bf16[128,512]{1,0:T(8,128)(2,1)S(1)}, bf16[128,512]{1,0:T(8,128)(2,1)S(1)}, u32[]{:S(2)}, u32[]{:S(2)}) collective-permute-start(bf16[128,512]{1,0:T(8,128)(2,1)S(1)} %get-tuple-element.79.att_grad_ref), channel_id=1, source_target_pairs={{1,0},{3,2},{5,4},{7,6},{9,8},{11,10},{13,12},{15,14},{17,16},{19,... | collective-permute-start | bytes 393224 | tf_op jit(solution)/shard_map/ppermute | solution.py:29
  90.1 8.2 %collective-permute-start.8 = (bf16[128,512]{1,0:T(8,128)(2,1)S(1)}, bf16[128,512]{1,0:T(8,128)(2,1)S(1)}, u32[]{:S(2)}, u32[]{:S(2)}) collective-permute-start(bf16[128,512]{1,0:T(8,128)(2,1)S(1)} %get-tuple-element.79.att_grad_ref), channel_id=1, source_target_pairs={{2,0},{3,1},{4,2},{5,3},{6,4},{7,5},{8,6},{9,7},{10,8},{11,9},{12,... | collective-permute-start | bytes 393224 | tf_op jit(solution)/shard_map/ppermute | solution.py:24
  91.4 10.4 %collective-permute-start.10 = (bf16[144,512]{1,0:T(8,128)(2,1)S(1)}, bf16[144,512]{1,0:T(8,128)(2,1)S(1)}, u32[]{:S(2)}, u32[]{:S(2)}) collective-permute-start(bf16[144,512]{1,0:T(8,128)(2,1)S(1)} %collective-permute-done.6.four_ref), channel_id=1, source_target_pairs={{0,1},{2,3},{4,5},{6,7},{8,9},{10,11},{12,13},{14,15},{16,17},{18,... | collective-permute-start | bytes 442376 | tf_op jit(solution)/shard_map/ppermute | solution.py:29
  92.7 9.1 %collective-permute-start.11 = (bf16[144,512]{1,0:T(8,128)(2,1)S(1)}, bf16[144,512]{1,0:T(8,128)(2,1)S(1)}, u32[]{:S(2)}, u32[]{:S(2)}) collective-permute-start(bf16[144,512]{1,0:T(8,128)(2,1)S(1)} %collective-permute-done.5.two_ref), channel_id=1, source_target_pairs={{0,1},{1,0},{2,3},{3,2},{4,5},{5,4},{6,7},{7,6},{8,9},{9,8},{10,11... | collective-permute-start | bytes 442376 | tf_op jit(solution)/shard_map/ppermute | solution.py:29
  98.3 3.5 %collective-permute-start.9 = (bf16[128,512]{1,0:T(8,128)(2,1)S(1)}, bf16[128,512]{1,0:T(8,128)(2,1)S(1)}, u32[]{:S(2)}, u32[]{:S(2)}) collective-permute-start(bf16[128,512]{1,0:T(8,128)(2,1)S(1)} %collective-permute-done.8.two_ref), channel_id=1, source_target_pairs={{0,1},{1,0},{2,3},{3,2},{4,5},{5,4},{6,7},{7,6},{8,9},{9,8},{10,11... | collective-permute-start | bytes 393224 | tf_op jit(solution)/shard_map/ppermute | solution.py:29
  100.5 7.5 %collective-permute-start.12 = (bf16[128,512]{1,0:T(8,128)(2,1)S(1)}, bf16[128,512]{1,0:T(8,128)(2,1)S(1)}, u32[]{:S(2)}, u32[]{:S(2)}) collective-permute-start(bf16[128,512]{1,0:T(8,128)(2,1)S(1)} %collective-permute-done.8.two_ref), channel_id=1, source_target_pairs={{2,0},{3,1},{4,2},{5,3},{6,4},{7,5},{8,6},{9,7},{10,8},{11,9},{12,... | collective-permute-start | bytes 393224 | tf_op jit(solution)/shard_map/ppermute | solution.py:24
  108.0 3.2 %collective-permute-start.13 = (bf16[128,512]{1,0:T(8,128)(2,1)S(1)}, bf16[128,512]{1,0:T(8,128)(2,1)S(1)}, u32[]{:S(2)}, u32[]{:S(2)}) collective-permute-start(bf16[128,512]{1,0:T(8,128)(2,1)S(1)} %collective-permute-done.12.four_ref), channel_id=1, source_target_pairs={{0,1},{2,3},{4,5},{6,7},{8,9},{10,11},{12,13},{14,15},{16,17},{18,... | collective-permute-start | bytes 393224 | tf_op jit(solution)/shard_map/ppermute | solution.py:29
  116.9 7.5 %collective-permute-start.14 = (bf16[4,640,256]{2,1,0:T(8,128)(2,1)}, bf16[4,640,256]{2,1,0:T(8,128)(2,1)}, u32[]{:S(2)}, u32[]{:S(2)}) collective-permute-start(bf16[4,640,256]{2,1,0:T(8,128)(2,1)} %get-tuple-element.107), channel_id=1, source_target_pairs={{0,1},{1,0},{2,3},{3,2},{4,5},{5,4},{6,7},{7,6},{8,9},{9,8},{10,11... | collective-permute-start | bytes 3932168 | tf_op jit(solution)/shard_map/ppermute | solution.py:29
  119.4 40.8 %all-to-all-start.2 = ((bf16[32,32,512]{2,1,0:T(8,128)(2,1)}), bf16[32,32,512]{2,1,0:T(8,128)(2,1)S(1)}, u32[]{:S(2)}, u32[]{:S(2)}) async-start(bf16[32,32,512]{2,1,0:T(8,128)(2,1)} %bitcast.9), calls=%async_computation.2 | async-start | bytes 2097152 | tf_op jit(solution)/shard_map/all_to_all | solution.py:587
  125.8 22.4 %collective-permute-start.17 = (bf16[640,256]{1,0:T(8,128)(2,1)S(1)}, bf16[640,256]{1,0:T(8,128)(2,1)}, u32[]{:S(2)}, u32[]{:S(2)}) collective-permute-start(bf16[640,256]{1,0:T(8,128)(2,1)S(1)} %get-tuple-element.121), channel_id=1, source_target_pairs={{0,48},{16,0},{32,16},{48,32},{64,112},{80,64},{96,80},{112,96},{1... | collective-permute-start | bytes 983048 | tf_op jit(solution)/shard_map/ppermute | solution.py:474
  130.2 20.6 %collective-permute-start.16 = (bf16[640,256]{1,0:T(8,128)(2,1)S(1)}, bf16[640,256]{1,0:T(8,128)(2,1)}, u32[]{:S(2)}, u32[]{:S(2)}) collective-permute-start(bf16[640,256]{1,0:T(8,128)(2,1)S(1)} %get-tuple-element.122), channel_id=1, source_target_pairs={{0,32},{16,48},{32,0},{48,16},{64,96},{80,112},{96,64},{112,80},{1... | collective-permute-start | bytes 983048 | tf_op jit(solution)/shard_map/ppermute | solution.py:474
  132.7 25.2 %collective-permute-start.15 = (bf16[640,256]{1,0:T(8,128)(2,1)S(1)}, bf16[640,256]{1,0:T(8,128)(2,1)}, u32[]{:S(2)}, u32[]{:S(2)}) collective-permute-start(bf16[640,256]{1,0:T(8,128)(2,1)S(1)} %get-tuple-element.120), channel_id=1, source_target_pairs={{0,16},{16,32},{32,48},{48,0},{64,80},{80,96},{96,112},{112,64},{1... | collective-permute-start | bytes 983048 | tf_op jit(solution)/shard_map/ppermute | solution.py:474
  160.1 18.5 %all-to-all-start.3 = ((bf16[8,80,256]{2,1,0:T(8,128)(2,1)}), bf16[8,80,256]{2,1,0:T(8,128)(2,1)S(1)}, u32[]{:S(2)}, u32[]{:S(2)}) async-start(bf16[8,80,256]{2,1,0:T(8,128)(2,1)} %bitcast.15), calls=%async_computation.3 | async-start | bytes 655360 | tf_op jit(solution)/shard_map/all_to_all | solution.py:451
  166.0 3.7 %collective-permute-start.18 = (bf16[8,32,512]{2,1,0:T(8,128)(2,1)S(1)}, bf16[8,32,512]{2,1,0:T(8,128)(2,1)S(1)}, u32[]{:S(2)}, u32[]{:S(2)}) collective-permute-start(bf16[8,32,512]{2,1,0:T(8,128)(2,1)S(1)} %get-tuple-element.110), channel_id=1, source_target_pairs={{0,1},{1,0},{2,3},{3,2},{4,5},{5,4},{6,7},{7,6},{8,9},{9,8},{10,11... | collective-permute-start | bytes 786440 | tf_op jit(solution)/shard_map/ppermute | solution.py:441
